TPU v7x, 128 devices: a whole 4x4x4 slice. The times are simulated.
128 devices in a mesh: gx: 8 (over y, core), gy: 16 (over z, x).
Axes of the slice: x: 4, y: 4, z: 4, core: 2. Of those that a mesh axis runs over, the one named last changes fastest.
Arguments:
- pressure: float32 [8, 512, 4096], P(None, 'gx', 'gy'), may hold values from -4 to 4
- sat_water: float32 [8, 512, 4096], P(None, 'gx', 'gy'), may hold values from 0.1 to 0.4
- sat_gas: float32 [8, 512, 4096], P(None, 'gx', 'gy'), may hold values from 0.1 to 0.4
- old_mass: float32 [3, 8, 512, 4096], P(None, None, 'gx', 'gy'), may hold values from 0.02 to 0.2
- perm: bfloat16 [3, 8, 512, 4096], P(None, None, 'gx', 'gy'), may hold values from 0.099609375 to 10
- porosity: float32 [8, 512, 4096], P(None, 'gx', 'gy'), may hold values from 0.1 to 0.3
- perf_well: int32 [32768], P(('gx', 'gy')), may hold values from 0 to 2047, as said below
- perf_cell: int32 [32768], P(('gx', 'gy')), may hold values from 0 to 131071
- perf_index: float32 [32768], P(('gx', 'gy')), may hold values from 0.5 to 5
- well_pressure: float32 [2048], P(('gx', 'gy')), may hold values from -4 to 4
- well_rate: float32 [2048], P(('gx', 'gy')), may hold values from -3 to 3
Outputs:
- residual: float32 [3, 8, 512, 4096], P(None, None, 'gx', 'gy')
- well_residual: float32 [2048], P(('gx', 'gy'))
- update: float32 [3, 8, 512, 4096], P(None, None, 'gx', 'gy')
- well_update: float32 [2048], P(('gx', 'gy'))
Inputs may be any that keep to these rules, and one draw needn't show every extreme that they name: Every well has a perforation on the device that holds its state, the one with index perf_well // 16 along gx+gy, and one on the device 2048 // 32 indices after that one, counted cyclically; its other perforations lie on devices at most 39 indices after the holding device along gx+gy, counted cyclically. perf_cell is layer-major within the device's block of 8 x 64 x 256 cells.
All inputs are finite; a program needn't handle non-finite values.
Results may differ from a plain program's by a relative error of at most 0.0003.
Values sent between devices are 32-bit elements; how exact they have to be, the bound alone decides.
No kernel may reach another device: no remote copies, remote signals or barrier semaphores. Data moves between devices by JAX's collectives and lax.ppermute only.
A program may use at most 192 MiB of HBM per device.

v0:
```python
import jax
import jax.numpy as jnp
from jax import lax
from jax.sharding import PartitionSpec as P

SWEEPS = 4


compress = (0.05, 0.02, 0.2)
viscosity = (0.5, 2.0, 0.1)
volume_scale = 4.0
layer_ratio = 0.1
directions = (
    (-3, -1, 2, layer_ratio),
    (-3, 1, 2, layer_ratio),
    (-2, -1, 0, 1.0),
    (-2, 1, 0, 1.0),
    (-1, -1, 1, 1.0),
    (-1, 1, 1, 1.0),
)


def extended(array, sides, width):
    for axis, dim in sides:
        count, length = (lax.axis_size(axis), array.shape[dim])
        up = [(i, (i + 1) % count) for i in range(count - 1)]
        down = [(j, i) for i, j in up]
        last = lax.slice_in_dim(array, length - width, length, axis=dim)
        leading = lax.slice_in_dim(array, 0, width, axis=dim)
        before = lax.ppermute(last, axis, up)
        after = lax.ppermute(leading, axis, down)
        array = jnp.concatenate([before, array, after], axis=dim)
    return array


def phase_coeffs(pressure, sat_water, sat_gas):
    sat_oil = 1.0 - sat_water - sat_gas
    sats = (sat_water, sat_oil, sat_gas)
    return jnp.stack(
        [
            sats[phase_index]
            * sats[phase_index]
            / viscosity[phase_index]
            * (1.0 + compress[phase_index] * pressure)
            for phase_index in range(3)
        ]
    )


def shifted(values, dimension, offset):
    dimension = dimension % values.ndim
    length = values.shape[dimension]
    widths = [(0, 0)] * values.ndim
    if offset > 0:
        widths[dimension] = (0, 1)
        padded = jnp.pad(values, widths)
        return lax.slice_in_dim(padded, 1, length + 1, axis=dimension)
    widths[dimension] = (1, 0)
    padded = jnp.pad(values, widths)
    return lax.slice_in_dim(padded, 0, length, axis=dimension)


def face_coefficient(coeffs, perm_here, coeffs_next, perm_next, factor):
    transmit = factor * 2.0 * perm_here * perm_next / (perm_here + perm_next)
    return transmit * 0.5 * (coeffs + coeffs_next)


def block_solve(right_terms, diagonal, inverse_b, inverse_total):
    pressure_step = (
        right_terms[0] * inverse_b[0]
        + right_terms[1] * inverse_b[1]
        + right_terms[2] * inverse_b[2]
    ) * inverse_total
    water_step = (right_terms[0] - diagonal[0] * pressure_step) * inverse_b[0]
    gas_step = (right_terms[2] - diagonal[2] * pressure_step) * inverse_b[2]
    return jnp.stack([pressure_step, water_step, gas_step])


def local(
    pressure,
    sat_water,
    sat_gas,
    old_mass,
    perm,
    porosity,
    perf_well,
    perf_cell,
    perf_index,
    well_pressure,
    well_rate,
):
    layers, row_count, column_count = pressure.shape
    cell_count = layers * row_count * column_count
    perm_all = perm.astype(jnp.float32)
    coeffs = phase_coeffs(pressure, sat_water, sat_gas)
    stacked = jnp.stack([pressure, sat_water, sat_gas, perm_all[0], perm_all[1]])
    widened = extended(stacked, (("gx", 2), ("gy", 3)), 1)
    lateral = [
        widened[:, :, :-2, 1:-1],
        widened[:, :, 2:, 1:-1],
        widened[:, :, 1:-1, :-2],
        widened[:, :, 1:-1, 2:],
    ]
    perm_slots = (3, 3, 4, 4)
    saturations = jnp.stack([sat_water, 1.0 - sat_water - sat_gas, sat_gas])
    densities = jnp.stack([1.0 + compress[phase_index] * pressure for phase_index in range(3)])
    diagonal = jnp.stack(
        [
            volume_scale * porosity * compress[phase_index] * saturations[phase_index]
            for phase_index in range(3)
        ]
    )
    net_flux = jnp.zeros_like(coeffs)
    face_terms = []
    for direction_index, (dimension, offset, component, factor) in enumerate(directions):
        perm_here = perm_all[component]
        if direction_index < 2:
            pressure_next = shifted(pressure, dimension, offset)
            coeffs_next = shifted(coeffs, dimension, offset)
            perm_next = shifted(perm_here, dimension, offset)
        else:
            fields = lateral[direction_index - 2]
            pressure_next = fields[0]
            coeffs_next = phase_coeffs(fields[0], fields[1], fields[2])
            perm_next = fields[perm_slots[direction_index - 2]]
        face_term = face_coefficient(coeffs, perm_here, coeffs_next, perm_next, factor)
        face_terms.append(face_term)
        net_flux = net_flux + face_term * (pressure - pressure_next)
        diagonal = diagonal + face_term

    def cell_sum(values):
        return jax.ops.segment_sum(values, perf_cell, num_segments=cell_count).reshape(
            pressure.shape
        )

    all_heads = lax.all_gather(well_pressure, ("gx", "gy"), axis=0, tiled=True)
    well_count = all_heads.shape[0]
    perf_coeffs = coeffs.reshape(3, -1)[:, perf_cell]
    perf_pressure = pressure.reshape(-1)[perf_cell]
    perf_rates = perf_index * perf_coeffs * (perf_pressure - all_heads[perf_well])
    well_rates = jnp.stack([cell_sum(perf_rates[phase_index]) for phase_index in range(3)])
    residual = (
        volume_scale * (porosity * densities * saturations - old_mass) + net_flux + well_rates
    )
    diagonal = diagonal + coeffs * cell_sum(perf_index)
    inverse_b = 1.0 / (volume_scale * porosity * densities)
    inverse_total = 1.0 / jnp.sum(diagonal * inverse_b, axis=0)
    perf_total = perf_index * jnp.sum(perf_coeffs, axis=0)
    part_rate = jax.ops.segment_sum(jnp.sum(perf_rates, axis=0), perf_well, num_segments=well_count)
    part_total = jax.ops.segment_sum(perf_total, perf_well, num_segments=well_count)
    total_rate, well_total = (
        lax.psum_scatter(part_rate, ("gx", "gy"), scatter_dimension=0, tiled=True),
        lax.psum_scatter(part_total, ("gx", "gy"), scatter_dimension=0, tiled=True),
    )
    well_residual = total_rate - well_rate
    head_moves = well_residual / well_total
    right_side = -residual
    update = block_solve(right_side, diagonal, inverse_b, inverse_total)
    for sweep_number in range(SWEEPS - 1):
        pressure_step = update[0]
        widened_step = extended(pressure_step, (("gx", 1), ("gy", 2)), 1)
        step_lateral = [
            widened_step[:, :-2, 1:-1],
            widened_step[:, 2:, 1:-1],
            widened_step[:, 1:-1, :-2],
            widened_step[:, 1:-1, 2:],
        ]
        right_terms = (
            right_side
            + face_terms[0] * shifted(pressure_step, -3, -1)
            + face_terms[1] * shifted(pressure_step, -3, 1)
        )
        for lateral_index in range(4):
            right_terms = right_terms + face_terms[2 + lateral_index] * step_lateral[lateral_index]
        all_moves = lax.all_gather(head_moves, ("gx", "gy"), axis=0, tiled=True)
        right_terms = right_terms + coeffs * cell_sum(perf_index * all_moves[perf_well])
        part_flow = jax.ops.segment_sum(
            perf_total * pressure_step.reshape(-1)[perf_cell], perf_well, num_segments=well_count
        )
        well_flow = lax.psum_scatter(part_flow, ("gx", "gy"), scatter_dimension=0, tiled=True)
        head_moves = (well_flow + well_residual) / well_total
        update = block_solve(right_terms, diagonal, inverse_b, inverse_total)
    return (residual, well_residual, update, head_moves)


def solution(mesh):
    return jax.shard_map(
        local,
        mesh=mesh,
        in_specs=(
            P(None, "gx", "gy"),
            P(None, "gx", "gy"),
            P(None, "gx", "gy"),
            P(None, None, "gx", "gy"),
            P(None, None, "gx", "gy"),
            P(None, "gx", "gy"),
            P(("gx", "gy")),
            P(("gx", "gy")),
            P(("gx", "gy")),
            P(("gx", "gy")),
            P(("gx", "gy")),
        ),
        out_specs=(
            P(None, None, "gx", "gy"),
            P(("gx", "gy")),
            P(None, None, "gx", "gy"),
            P(("gx", "gy")),
        ),
        check_vma=False,
    )
```

profile of v0, /device:TPU:6, one launch (start us, length us, event | category | flops | bytes accessed | tf_op | source)
XLA Modules:
  0.0 556.6 jit_solution(11416502893124814795)
XLA Ops:
  7.0 2.7 scatter_custom_fusion.4
  13.8 68.2 %all-reduce.12 = f32[2048]{0:T(1024)S(1)} all-reduce(f32[2048]{0:T(1024)S(1)} %dynamic-update-slice), channel_id=1, replica_groups=mesh['gx'=8,'gy'=16] {'gx','gy'}, use_global_device_ids=true, to_apply=%add.12 | all-reduce | flops 2048 | bytes 16384
  83.7 4.6 fusion.63
  88.3 2.4 stack.118
  90.7 2.4 stack.117
  93.0 2.4 stack.116
  95.4 4.2 pad_maximum_fusion.1
  99.6 30.2 %copy.55 = f32[3,131072]{0,1:T(8,128)} copy(f32[3,131072]{1,0:T(4,128)} %pad_maximum_fusion.1) | data formatting | bytes 3145728 | tf_op jit(solution)/shard_map/stack | solution.py:39
  129.9 2.3 gather_fusion
  132.5 2.1 fusion.77
  136.5 3.3 collective-permute-start.3
  141.7 5.1 collective-permute-start.2
  147.1 2.1 add_multiply_fusion.8
  150.5 2.5 multiply_bitcast_fusion.5
  156.3 2.1 scatter_custom_fusion.2
  159.4 2.1 scatter_custom_fusion.1
  162.4 2.1 scatter_custom_fusion
  165.4 2.3 scatter_custom_fusion.3
  179.2 5.2 multiply_reduce_fusion
  184.5 7.3 %fusion.75 = (f32[3,8,64,256]{3,2,1,0:T(8,128)S(1)}, f32[3,8,64,256]{3,2,1,0:T(8,128)}) fusion(f32[1,8,64,256]{3,2,1,0:T(8,128)S(1)} %copy-done.52, f32[1,8,64,256]{3,2,1,0:T(8,128)S(1)} %copy-done.53, f32[1,8,64,256]{3,2,1,0:T(8,128)S(1)} %copy-done.54, f32[3,8,64,256]{3,2,1,0:T(8,128)S(1)} %get-tuple-element.37, f32[8,64,256]{2,1,0:T(8,128)S(1)} %get-tuple-element.49, ...), kind=kLoop, calls=%fused_computation.243 | loop fusion | flops 11010048 | bytes 22020096 | tf_op jit(solution)/shard_map/neg | solution.py:157
  196.7 3.0 collective-permute-start.4
  199.7 2.2 scatter_custom_fusion.5
  201.9 64.0 %all-reduce.24 = (f32[2048]{0:T(1024)S(1)}, f32[2048]{0:T(1024)S(1)}) all-reduce(f32[2048]{0:T(1024)S(1)} %scatter_custom_fusion.3, f32[2048]{0:T(1024)S(1)} %scatter_custom_fusion.5), channel_id=2, replica_groups=mesh['gx'=8,'gy'=16] {'gx','gy'}, use_global_device_ids=true, to_apply=%region_5.6.clone | all-reduce | flops 4096 | bytes 32768
  266.1 2.2 scatter_custom_fusion.7
  269.2 3.7 collective-permute-start.6
  272.9 2.1 collective-permute-start.7
  275.1 65.6 %all-reduce.23 = (f32[2048]{0:T(1024)S(1)}, f32[2048]{0:T(1024)}) all-reduce(f32[2048]{0:T(1024)S(1)} %get-tuple-element.40, f32[2048]{0:T(1024)S(1)} %scatter_custom_fusion.7), channel_id=1, replica_groups=mesh['gx'=8,'gy'=16] {'gx','gy'}, use_global_device_ids=true, to_apply=%add.13 | all-reduce | flops 4096 | bytes 32768
  342.4 2.2 scatter_custom_fusion.6
  347.8 3.9 multiply_add_fusion.2
  354.1 3.0 collective-permute-start.8
  359.1 3.3 gather_fusion.6
  362.4 2.3 scatter_custom_fusion.9
  366.8 3.6 collective-permute-start.10
  370.3 2.3 collective-permute-start.11
  372.6 66.4 %all-reduce.22 = (f32[2048]{0:T(1024)S(1)}, f32[2048]{0:T(1024)S(1)}) all-reduce(f32[2048]{0:T(1024)S(1)} %scatter_custom_fusion.9, f32[2048]{0:T(1024)S(1)} %divide_dynamic-update-slice_fusion.1), channel_id=5, replica_groups=mesh['gx'=8,'gy'=16] {'gx','gy'}, use_global_device_ids=true, to_apply=%region_16.17.clone | all-reduce | flops 4096 | bytes 32768
  440.7 3.1 scatter_custom_fusion.8
  445.9 3.1 pad_maximum_fusion.19
  449.0 3.8 multiply_add_fusion.1
  455.2 3.0 collective-permute-start.12
  459.6 3.2 gather_fusion.8
  462.9 2.3 scatter_custom_fusion.11
  465.2 63.9 %all-reduce.21 = (f32[2048]{0:T(1024)S(1)}, f32[2048]{0:T(1024)S(1)}) all-reduce(f32[2048]{0:T(1024)S(1)} %divide_dynamic-update-slice_fusion, f32[2048]{0:T(1024)S(1)} %scatter_custom_fusion.11), channel_id=1, replica_groups=mesh['gx'=8,'gy'=16] {'gx','gy'}, use_global_device_ids=true, to_apply=%add.15 | all-reduce | flops 4096 | bytes 32768
  531.1 3.6 collective-permute-start.14
  534.7 2.2 collective-permute-start.15
  539.3 2.9 scatter_custom_fusion.10
  544.2 3.4 collective-permute-done.15
  547.5 2.8 pad_maximum_fusion.11
  550.4 3.9 multiply_add_fusion
  (218 shorter events, 67.6 us)
Async XLA Ops:
  1.9 3.3 copy-start.58
  1.9 3.4 copy-start.57
  2.0 3.4 copy-start.46
  2.2 81.5 %collective-permute-start = (f32[5,8,1,256]{3,2,1,0:T(1,128)S(1)}, f32[5,8,1,256]{3,2,1,0:T(1,128)S(1)}, u32[]{:S(2)}, u32[]{:S(2)}) collective-permute-start(f32[5,8,1,256]{3,2,1,0:T(1,128)S(1)} %get-tuple-element.86), channel_id=1, source_target_pairs={{0,16},{16,32},{32,48},{48,64},{64,80},{80,96},{96,112},{1,17},{17... | collective-permute-start | bytes 122888 | tf_op jit(solution)/shard_map/ppermute | solution.py:30
  4.0 79.8 %collective-permute-start.1 = (f32[5,8,1,256]{3,2,1,0:T(1,128)S(1)}, f32[5,8,1,256]{3,2,1,0:T(1,128)S(1)}, u32[]{:S(2)}, u32[]{:S(2)}) collective-permute-start(f32[5,8,1,256]{3,2,1,0:T(1,128)S(1)} %get-tuple-element.85), channel_id=1, source_target_pairs={{16,0},{32,16},{48,32},{64,48},{80,64},{96,80},{112,96},{17,1},{33... | collective-permute-start | bytes 122888 | tf_op jit(solution)/shard_map/ppermute | solution.py:31
  7.0 6.5 %copy-start.60 = (f32[16]{0:T(128)S(1)}, f32[16]{0:T(128)}, u32[]{:S(2)}) copy-start(f32[16]{0:T(128)} %param.20) | copy-start | bytes 196
  136.5 31.2 %collective-permute-start.3 = (f32[5,8,66,1]{2,1,3,0:T(8,128)S(1)}, f32[5,8,66,1]{2,1,3,0:T(8,128)S(1)}, u32[]{:S(2)}, u32[]{:S(2)}) collective-permute-start(f32[5,8,66,1]{2,1,3,0:T(8,128)S(1)} %copy.53), channel_id=1, source_target_pairs={{1,0},{2,1},{3,2},{4,3},{5,4},{6,5},{7,6},{8,7},{9,8},{10,9},{11,1... | collective-permute-start | bytes 31688 | tf_op jit(solution)/shard_map/ppermute | solution.py:31
  141.7 27.8 %collective-permute-start.2 = (f32[5,8,66,1]{2,1,3,0:T(8,128)S(1)}, f32[5,8,66,1]{2,1,3,0:T(8,128)S(1)}, u32[]{:S(2)}, u32[]{:S(2)}) collective-permute-start(f32[5,8,66,1]{2,1,3,0:T(8,128)S(1)} %copy.51), channel_id=1, source_target_pairs={{0,1},{1,2},{2,3},{3,4},{4,5},{5,6},{6,7},{7,8},{8,9},{9,10},{10,1... | collective-permute-start | bytes 31688 | tf_op jit(solution)/shard_map/ppermute | solution.py:30
  174.6 9.9 %copy-start.18 = (f32[8,64,256]{2,1,0:T(8,128)}, f32[8,64,256]{2,1,0:T(8,128)S(1)}, u32[]{:S(2)}) copy-start(f32[8,64,256]{2,1,0:T(8,128)S(1)} %get-tuple-element.136) | copy-start | bytes 1572868
  174.6 9.9 %copy-start.22 = (f32[8,64,256]{2,1,0:T(8,128)}, f32[8,64,256]{2,1,0:T(8,128)S(1)}, u32[]{:S(2)}) copy-start(f32[8,64,256]{2,1,0:T(8,128)S(1)} %get-tuple-element.137) | copy-start | bytes 1572868
  179.2 5.3 copy-start.52
  179.2 5.3 copy-start.53
  179.2 5.3 copy-start.54
  184.4 7.4 %copy-start.6 = (f32[3,8,64,256]{3,2,1,0:T(8,128)}, f32[3,8,64,256]{3,2,1,0:T(8,128)S(1)}, u32[]{:S(2)}) copy-start(f32[3,8,64,256]{3,2,1,0:T(8,128)S(1)} %get-tuple-element.34) | copy-start | bytes 4718596
  184.4 7.4 %copy-start.10 = (f32[3,8,64,256]{3,2,1,0:T(8,128)}, f32[3,8,64,256]{3,2,1,0:T(8,128)S(1)}, u32[]{:S(2)}) copy-start(f32[3,8,64,256]{3,2,1,0:T(8,128)S(1)} %get-tuple-element.35) | copy-start | bytes 4718596
  184.4 7.4 %copy-start.14 = (f32[3,8,64,256]{3,2,1,0:T(8,128)}, f32[3,8,64,256]{3,2,1,0:T(8,128)S(1)}, u32[]{:S(2)}) copy-start(f32[3,8,64,256]{3,2,1,0:T(8,128)S(1)} %get-tuple-element.36) | copy-start | bytes 4718596
  184.4 7.4 %copy-start.15 = (f32[3,8,64,256]{3,2,1,0:T(8,128)}, f32[3,8,64,256]{3,2,1,0:T(8,128)S(1)}, u32[]{:S(2)}) copy-start(f32[3,8,64,256]{3,2,1,0:T(8,128)S(1)} %get-tuple-element.37) | copy-start | bytes 4718596
  184.4 7.4 %copy-start.4 = (f32[3,8,64,256]{3,2,1,0:T(8,128)}, f32[3,8,64,256]{3,2,1,0:T(8,128)S(1)}, u32[]{:S(2)}) copy-start(f32[3,8,64,256]{3,2,1,0:T(8,128)S(1)} %get-tuple-element.33) | copy-start | bytes 4718596
  184.5 7.4 %copy-start.26 = (f32[8,64,256]{2,1,0:T(8,128)}, f32[8,64,256]{2,1,0:T(8,128)S(1)}, u32[]{:S(2)}) copy-start(f32[8,64,256]{2,1,0:T(8,128)S(1)} %get-tuple-element.31) | copy-start | bytes 1572868
  192.8 73.1 %copy-start.59 = (f32[16]{0:T(128)S(1)}, f32[16]{0:T(128)}, u32[]{:S(2)}) copy-start(f32[16]{0:T(128)} %param.21) | copy-start | bytes 196
  195.4 72.9 %collective-permute-start.5 = (f32[8,1,256]{2,1,0:T(1,128)S(1)}, f32[8,1,256]{2,1,0:T(1,128)S(1)}, u32[]{:S(2)}, u32[]{:S(2)}) collective-permute-start(f32[8,1,256]{2,1,0:T(1,128)S(1)} %get-tuple-element.134), channel_id=1, source_target_pairs={{16,0},{32,16},{48,32},{64,48},{80,64},{96,80},{112,96},{17,1},{33... | collective-permute-start | bytes 24584 | tf_op jit(solution)/shard_map/ppermute | solution.py:31
  196.7 71.6 %collective-permute-start.4 = (f32[8,1,256]{2,1,0:T(1,128)S(1)}, f32[8,1,256]{2,1,0:T(1,128)S(1)}, u32[]{:S(2)}, u32[]{:S(2)}) collective-permute-start(f32[8,1,256]{2,1,0:T(1,128)S(1)} %get-tuple-element.133), channel_id=1, source_target_pairs={{0,16},{16,32},{32,48},{48,64},{64,80},{80,96},{96,112},{1,17},{17... | collective-permute-start | bytes 24584 | tf_op jit(solution)/shard_map/ppermute | solution.py:30
  266.1 270.9 %copy-start.56 = (f32[16]{0:T(128)}, f32[16]{0:T(128)S(1)}, u32[]{:S(2)}) copy-start(f32[16]{0:T(128)S(1)} %get-tuple-element.42) | copy-start | bytes 196
  269.2 76.4 %collective-permute-start.6 = (f32[8,66,1]{2,1,0:T(8,128)}, f32[8,66,1]{2,1,0:T(8,128)S(1)}, u32[]{:S(2)}, u32[]{:S(2)}) collective-permute-start(f32[8,66,1]{2,1,0:T(8,128)} %get-tuple-element.99), channel_id=1, source_target_pairs={{0,1},{1,2},{2,3},{3,4},{4,5},{5,6},{6,7},{7,8},{8,9},{9,10},{10,1... | collective-permute-start | bytes 6344 | tf_op jit(solution)/shard_map/ppermute | solution.py:30
  272.9 72.7 %collective-permute-start.7 = (f32[8,66,1]{2,1,0:T(8,128)S(1)}, f32[8,66,1]{2,1,0:T(8,128)S(1)}, u32[]{:S(2)}, u32[]{:S(2)}) collective-permute-start(f32[8,66,1]{2,1,0:T(8,128)S(1)} %get-tuple-element.100), channel_id=1, source_target_pairs={{1,0},{2,1},{3,2},{4,3},{5,4},{6,5},{7,6},{8,7},{9,8},{10,9},{11,1... | collective-permute-start | bytes 6344 | tf_op jit(solution)/shard_map/ppermute | solution.py:31
  347.8 3.9 copy-start.5
  347.8 3.9 copy-start.27
  351.7 6.6 %copy-start.31 = (f32[64,2,8,128]{3,1,2,0:T(2,128)S(1)}, f32[64,2,8,128]{3,1,2,0:T(2,128)}, u32[]{:S(2)}) copy-start(f32[64,2,8,128]{3,1,2,0:T(2,128)} %copy-done.30) | copy-start | bytes 1572868
  352.8 12.0 %collective-permute-start.9 = (f32[8,1,256]{2,1,0:T(1,128)S(1)}, f32[8,1,256]{2,1,0:T(1,128)S(1)}, u32[]{:S(2)}, u32[]{:S(2)}) collective-permute-start(f32[8,1,256]{2,1,0:T(1,128)S(1)} %get-tuple-element.132), channel_id=1, source_target_pairs={{16,0},{32,16},{48,32},{64,48},{80,64},{96,80},{112,96},{17,1},{33... | collective-permute-start | bytes 24584 | tf_op jit(solution)/shard_map/ppermute | solution.py:31
  354.1 10.7 %collective-permute-start.8 = (f32[8,1,256]{2,1,0:T(1,128)S(1)}, f32[8,1,256]{2,1,0:T(1,128)S(1)}, u32[]{:S(2)}, u32[]{:S(2)}) collective-permute-start(f32[8,1,256]{2,1,0:T(1,128)S(1)} %get-tuple-element.131), channel_id=1, source_target_pairs={{0,16},{16,32},{32,48},{48,64},{64,80},{80,96},{96,112},{1,17},{17... | collective-permute-start | bytes 24584 | tf_op jit(solution)/shard_map/ppermute | solution.py:30
  366.8 79.1 %collective-permute-start.10 = (f32[8,66,1]{2,1,0:T(8,128)}, f32[8,66,1]{2,1,0:T(8,128)S(1)}, u32[]{:S(2)}, u32[]{:S(2)}) collective-permute-start(f32[8,66,1]{2,1,0:T(8,128)} %get-tuple-element.97), channel_id=1, source_target_pairs={{0,1},{1,2},{2,3},{3,4},{4,5},{5,6},{6,7},{7,8},{8,9},{9,10},{10,1... | collective-permute-start | bytes 6344 | tf_op jit(solution)/shard_map/ppermute | solution.py:30
  370.3 75.5 %collective-permute-start.11 = (f32[8,66,1]{2,1,0:T(8,128)}, f32[8,66,1]{2,1,0:T(8,128)}, u32[]{:S(2)}, u32[]{:S(2)}) collective-permute-start(f32[8,66,1]{2,1,0:T(8,128)} %get-tuple-element.98), channel_id=1, source_target_pairs={{1,0},{2,1},{3,2},{4,3},{5,4},{6,5},{7,6},{8,7},{9,8},{10,9},{11,1... | collective-permute-start | bytes 6344 | tf_op jit(solution)/shard_map/ppermute | solution.py:31
  445.8 3.1 copy-start.8
  445.9 3.1 copy-start.12
  445.9 3.1 copy-start.20
  445.9 3.1 copy-start.24
  449.0 3.8 copy-start.28
  452.9 5.9 %copy-start.32 = (f32[64,2,8,128]{3,1,2,0:T(2,128)S(1)}, f32[64,2,8,128]{3,1,2,0:T(2,128)}, u32[]{:S(2)}) copy-start(f32[64,2,8,128]{3,1,2,0:T(2,128)} %copy-done.30) | copy-start | bytes 1572868
  453.9 75.1 %collective-permute-start.13 = (f32[8,1,256]{2,1,0:T(1,128)S(1)}, f32[8,1,256]{2,1,0:T(1,128)S(1)}, u32[]{:S(2)}, u32[]{:S(2)}) collective-permute-start(f32[8,1,256]{2,1,0:T(1,128)S(1)} %get-tuple-element.130), channel_id=1, source_target_pairs={{16,0},{32,16},{48,32},{64,48},{80,64},{96,80},{112,96},{17,1},{33... | collective-permute-start | bytes 24584 | tf_op jit(solution)/shard_map/ppermute | solution.py:31
  455.2 73.8 %collective-permute-start.12 = (f32[8,1,256]{2,1,0:T(1,128)S(1)}, f32[8,1,256]{2,1,0:T(1,128)S(1)}, u32[]{:S(2)}, u32[]{:S(2)}) collective-permute-start(f32[8,1,256]{2,1,0:T(1,128)S(1)} %get-tuple-element.129), channel_id=1, source_target_pairs={{0,16},{16,32},{32,48},{48,64},{64,80},{80,96},{96,112},{1,17},{17... | collective-permute-start | bytes 24584 | tf_op jit(solution)/shard_map/ppermute | solution.py:30
  531.1 13.1 %collective-permute-start.14 = (f32[8,66,1]{2,1,0:T(8,128)}, f32[8,66,1]{2,1,0:T(8,128)S(1)}, u32[]{:S(2)}, u32[]{:S(2)}) collective-permute-start(f32[8,66,1]{2,1,0:T(8,128)} %get-tuple-element.95), channel_id=1, source_target_pairs={{0,1},{1,2},{2,3},{3,4},{4,5},{5,6},{6,7},{7,8},{8,9},{9,10},{10,1... | collective-permute-start | bytes 6344 | tf_op jit(solution)/shard_map/ppermute | solution.py:30
  534.7 12.8 %collective-permute-start.15 = (f32[8,66,1]{2,1,0:T(8,128)}, f32[8,66,1]{2,1,0:T(8,128)}, u32[]{:S(2)}, u32[]{:S(2)}) collective-permute-start(f32[8,66,1]{2,1,0:T(8,128)} %get-tuple-element.96), channel_id=1, source_target_pairs={{1,0},{2,1},{3,2},{4,3},{5,4},{6,5},{7,6},{8,7},{9,8},{10,9},{11,1... | collective-permute-start | bytes 6344 | tf_op jit(solution)/shard_map/ppermute | solution.py:31
  544.2 6.2 %copy-start.9 = (f32[3,8,64,256]{3,2,1,0:T(8,128)S(1)}, f32[3,8,64,256]{3,2,1,0:T(8,128)}, u32[]{:S(2)}) copy-start(f32[3,8,64,256]{3,2,1,0:T(8,128)} %copy-done.6) | copy-start | bytes 4718596
  544.2 6.2 %copy-start.13 = (f32[3,8,64,256]{3,2,1,0:T(8,128)S(1)}, f32[3,8,64,256]{3,2,1,0:T(8,128)}, u32[]{:S(2)}) copy-start(f32[3,8,64,256]{3,2,1,0:T(8,128)} %copy-done.10) | copy-start | bytes 4718596
  544.2 6.2 %copy-start.21 = (f32[8,64,256]{2,1,0:T(8,128)S(1)}, f32[8,64,256]{2,1,0:T(8,128)}, u32[]{:S(2)}) copy-start(f32[8,64,256]{2,1,0:T(8,128)} %copy-done.18) | copy-start | bytes 1572868
  544.2 6.2 %copy-start.25 = (f32[8,64,256]{2,1,0:T(8,128)S(1)}, f32[8,64,256]{2,1,0:T(8,128)}, u32[]{:S(2)}) copy-start(f32[8,64,256]{2,1,0:T(8,128)} %copy-done.22) | copy-start | bytes 1572868
  550.4 3.9 copy-start.29
  550.4 3.9 copy-start.45
  (29 other events, 52.3 us)
where the time goes:
time: 566 us; the launch traced here: 557 us
  blocking collectives  328 us (58%)
  other arithmetic  91.6 us (16%)
  local copies, waits for them, and re-layouts  89.3 us (16%)
  starting transfers between devices  41.9 us (7%)
    unnamed x5, blocking collectives  328 us
    another operation x4, local copies, waits for them, and re-layouts, phase_coeffs(): jnp.stack([sats[phase_index] * sats[phase_index] / viscosity[phase_index]...  37.4 us
    ppermute x8, starting transfers between devices, extended(): before = lax.ppermute(last, axis, up)  26.9 us
    scatter-add x7, other arithmetic, cell_sum(): jax.ops.segment_sum(values, perf_cell, num_segments=cell_count)  17.2 us
    ppermute x8, starting transfers between devices, extended(): after = lax.ppermute(leading, axis, down)  15.1 us
    add x3, other arithmetic, local(): right_terms + coeffs * cell_sum(perf_index * all_moves[perf_well])  11.6 us
  transfers between devices with their start and end apart: 16, of which 1 were waited for; matrix products, arithmetic and copies ran while one was open for 13% of the time, Pallas kernels for 0%

commit v1 on v0

v1 whole, which is shorter than its diff:
```python
import jax
import jax.numpy as jnp
from jax import lax
from jax.experimental import pallas as pl
from jax.experimental.pallas import tpu as pltpu
from jax.sharding import PartitionSpec as P

f32 = jnp.float32
bf16 = jnp.bfloat16
i32 = jnp.int32

compress = (0.05, 0.02, 0.2)
viscosity = (0.5, 2.0, 0.1)
volume_scale = 4.0
layer_ratio = 0.1
AXES = ("gx", "gy")
DEVICES = 128
WELL_DEV = 16
REACH = 40
FAR = 64
TAIL = REACH * WELL_DEV
WIDTH = TAIL + 128
LANES = 128
L, R, C = 8, 64, 256
PERFS = 256
VM = pl.BlockSpec(memory_space=pltpu.VMEM)
SM = pl.BlockSpec(memory_space=pltpu.SMEM)


def iota(shape, dim):
    return lax.broadcasted_iota(i32, shape, dim)


def split3(x):
    high = x.astype(bf16)
    rest = x - high.astype(f32)
    middle = rest.astype(bf16)
    low = (rest - middle.astype(f32)).astype(bf16)
    return high, middle, low


def dot(a, b):
    return jnp.dot(a, b, preferred_element_type=f32)


def to_column(row):
    n = row.shape[1]
    return jnp.sum(jnp.where(iota((n, n), 0) == iota((n, n), 1), row, 0.0), axis=1, keepdims=True)


def to_row(column):
    n = column.shape[0]
    return jnp.sum(jnp.where(iota((n, n), 0) == iota((n, n), 1), column, 0.0), axis=0, keepdims=True)


def coeffs_of(p, sw, sg):
    so = 1.0 - sw - sg
    return tuple(
        s * s * (1.0 / viscosity[a]) * (1.0 + compress[a] * p) for a, s in enumerate((sw, so, sg))
    )


def scatter(cell_row, values):
    match = iota((L * R, PERFS), 0) == (cell_row >> 8)
    column = to_column(cell_row.astype(f32)).astype(i32) & (C - 1)
    spread = (iota((PERFS, C), 1) == column).astype(bf16)
    return sum(
        dot(jnp.where(match, part.astype(f32), 0.0).astype(bf16), spread) for part in split3(values)
    )


def gather_cells(cells, refs, rows):
    def body(block, carry):
        for u in range(8):
            k = block * 8 + u
            cell = cells[k]
            layer = cell >> 14
            line = (cell >> 8) & (R - 1)
            for n, ref in enumerate(refs):
                rows[n, pl.ds(k, 1), :] = ref[layer, pl.ds(line, 1), :]
        return carry

    lax.fori_loop(0, PERFS // 8, body, 0)


def pick_columns(rows, n, column):
    return jnp.sum(jnp.where(iota((PERFS, C), 1) == column, rows[n], 0.0), axis=1, keepdims=True)


def gather_wells(table, holder, slot):
    onehot = (iota((DEVICES, PERFS), 0) == holder).astype(bf16)
    wide = sum(dot(part, onehot) for part in split3(table.T))
    return jnp.sum(jnp.where(iota((LANES, PERFS), 0) == slot, wide, 0.0), axis=0, keepdims=True)


def to_holders(holder, slot_column, columns):
    lane = iota((PERFS, LANES), 1)
    group = lane >> 4
    values = jnp.zeros((PERFS, LANES), f32)
    for g, column in columns:
        values = jnp.where(group == g, column, values)
    values = jnp.where((lane & 15) == slot_column, values, 0.0)
    onehot = (iota((DEVICES, PERFS), 0) == holder).astype(bf16)
    return sum(dot(onehot, part) for part in split3(values))


def parts_by_offset(me, well_row, values):
    offset = (me - (well_row >> 4)) & (DEVICES - 1)
    lane = jnp.where(offset == FAR, TAIL, offset * WELL_DEV) + (well_row & 15)
    column = to_column(lane.astype(f32)).astype(i32)
    onehot = (iota((PERFS, WIDTH), 1) == column).astype(bf16)
    high, middle, low = split3(values)
    rows = jnp.concatenate([high.astype(f32), middle.astype(f32), low.astype(f32), jnp.zeros((5, PERFS), f32)], axis=0)
    return jnp.sum(dot(rows.astype(bf16), onehot), axis=0, keepdims=True)


def sum_parts(got):
    aligned = got[:, :LANES]
    for t in range(1, TAIL // LANES):
        aligned = aligned + pltpu.roll(got[:, t * LANES : (t + 1) * LANES], DEVICES - 8 * t, 0)
    total = aligned + pltpu.roll(got[:, TAIL:], DEVICES - FAR, 0)
    for u in range(1, 8):
        total = total + pltpu.roll(pltpu.roll(aligned, DEVICES - u, 0), LANES - 16 * u, 1)
    return total


def shift_rows(x, first, last):
    return (
        jnp.concatenate([first, x[:-1]], axis=0),
        jnp.concatenate([x[1:], last], axis=0),
    )


def shift_columns(x, first, last):
    lane = iota(x.shape, 1)
    return (
        jnp.where(lane == 0, first, pltpu.roll(x, 1, 1)),
        jnp.where(lane == C - 1, last, pltpu.roll(x, C - 1, 1)),
    )


def lane_of(ref, index):
    return pltpu.roll(ref, (LANES - index) % LANES, 1)[:, 0:1]


def write_faces(read, outs):
    row_lo, row_hi, col_lo, col_hi = outs
    lane = iota((R, LANES), 1)
    low = jnp.zeros((R, LANES), f32)
    high = jnp.zeros((R, LANES), f32)
    for l in range(L):
        x = read(l)
        row_lo[l : l + 1, :] = x[0:1]
        row_hi[l : l + 1, :] = x[R - 1 : R]
        low = jnp.where(lane == l, x[:, 0:1], low)
        high = jnp.where(lane == l, x[:, C - 1 : C], high)
    col_lo[...] = low
    col_hi[...] = high


def start_kernel(cells, info, own, p, sw, sg, perm, row_lo, row_hi, col_lo, col_hi, pay, perf, rows):
    lane = iota((R, LANES), 1)
    low = jnp.zeros((R, LANES), f32)
    high = jnp.zeros((R, LANES), f32)
    for l in range(L):
        for f, ref in enumerate((p, sw, sg)):
            x = ref[l]
            n = f * L + l
            row_lo[n : n + 1, :] = x[0:1]
            row_hi[n : n + 1, :] = x[R - 1 : R]
            low = jnp.where(lane == n, x[:, 0:1], low)
            high = jnp.where(lane == n, x[:, C - 1 : C], high)
        n = 3 * L + l
        row_lo[n : n + 1, :] = perm[0, l, 0:16, :].astype(f32)[0:1]
        row_hi[n : n + 1, :] = perm[0, l, R - 16 : R, :].astype(f32)[15:16]
        k = perm[1, l].astype(f32)
        low = jnp.where(lane == n, k[:, 0:1], low)
        high = jnp.where(lane == n, k[:, C - 1 : C], high)
    col_lo[...] = low
    col_hi[...] = high
    gather_cells(cells, (p, sw, sg), rows)
    cell_row = info[0:1].astype(i32)
    well_row = info[1:2].astype(i32)
    index_row = info[2:3]
    column = to_column(info[0:1]).astype(i32) & (C - 1)
    here = [pick_columns(rows, n, column) for n in range(3)]
    coeffs = coeffs_of(*here)
    total = to_column(index_row) * (coeffs[0] + coeffs[1] + coeffs[2])
    slot_column = to_column(info[1:2]).astype(i32) & 15
    sums = to_holders(well_row >> 4, slot_column, ((0, total), (1, total * here[0])))
    wide = pltpu.roll(jnp.broadcast_to(own[0:1], (8, LANES)), 32, 1)[0:1]
    pay[...] = sums + wide
    perf[...] = jnp.broadcast_to(to_row(total), (8, PERFS))


def transmit(k, k_next):
    return k * k_next / (k + k_next)


def setup_kernel(
    info, p, sw, sg, por, mass, perm, row_lo, row_hi, col_lo, col_hi,
    coef, coef_row, coef_col, tx, ty, tz, base, head, weight, res, diag, index_sum,
):
    for side, ref in enumerate((row_lo, row_hi)):
        for a, c in enumerate(coeffs_of(ref[0:L], ref[L : 2 * L], ref[2 * L : 3 * L])):
            coef_row[side, a] = c
    for side, ref in enumerate((col_lo, col_hi)):
        x = ref[...]
        for a, c in enumerate(coeffs_of(x, pltpu.roll(x, LANES - L, 1), pltpu.roll(x, LANES - 2 * L, 1))):
            coef_col[side, a] = c
    index_sum[...] = scatter(info[0:1].astype(i32), info[2:3]).reshape(L, R, C)
    lane = iota((R, C), 1)

    def first(l, carry):
        for a, c in enumerate(coeffs_of(p[l], sw[l], sg[l])):
            coef[a, l] = c
        k = perm[0, l].astype(f32)
        n = 3 * L + l
        before = transmit(k, jnp.concatenate([row_lo[pl.ds(n, 1), :], k[:-1]], axis=0))
        tx[0, l] = before
        tx[1, l] = jnp.concatenate([before[1:], transmit(k[R - 1 : R], row_hi[pl.ds(n, 1), :])], axis=0)
        k = perm[1, l].astype(f32)
        before = transmit(k, jnp.where(lane == 0, lane_of(col_lo[...], n), pltpu.roll(k, 1, 1)))
        ty[0, l] = before
        last = transmit(k[:, C - 1 : C], lane_of(col_hi[...], n))
        ty[1, l] = jnp.where(lane == C - 1, last, pltpu.roll(before, C - 1, 1))
        k = perm[2, l].astype(f32)
        under = perm[2, jnp.maximum(l - 1, 0)].astype(f32)
        tz[l] = jnp.where(l > 0, layer_ratio, 0.0) * transmit(k, under)
        return carry

    lax.fori_loop(0, L, first, 0)
    tz[L] = jnp.zeros((R, C), f32)

    def second(l, carry):
        down, up = (jnp.maximum(l - 1, 0), jnp.minimum(l + 1, L - 1))
        here = p[l]
        nexts = shift_rows(here, row_lo[pl.ds(l, 1), :], row_hi[pl.ds(l, 1), :])
        nexts += shift_columns(here, lane_of(col_lo[...], l), lane_of(col_hi[...], l))
        nexts += (p[down], p[up])
        faces = (tx[0, l], tx[1, l], ty[0, l], ty[1, l], tz[l], tz[l + 1])
        drops = [t * (here - q) for t, q in zip(faces, nexts)]
        face_sum = sum(faces)
        drop_sum = sum(drops)
        porous = volume_scale * por[l]
        sats = (sw[l], 1.0 - sw[l] - sg[l], sg[l])
        indices = index_sum[l]
        diagonals, residuals, inverses, cs = [], [], [], []
        for a in range(3):
            c = coef[a, l]
            sides = shift_rows(c, coef_row[0, a, pl.ds(l, 1), :], coef_row[1, a, pl.ds(l, 1), :])
            sides += shift_columns(c, lane_of(coef_col[0, a], l), lane_of(coef_col[1, a], l))
            sides += (coef[a, down], coef[a, up])
            ab = c * face_sum
            net = c * drop_sum
            for t, d, s in zip(faces, drops, sides):
                ab = ab + t * s
                net = net + d * s
            b = 1.0 + compress[a] * here
            stored = porous * sats[a]
            diagonals.append(compress[a] * stored + ab + c * indices)
            residuals.append(b * stored - volume_scale * mass[a, l] + net + c * (indices * here))
            inverses.append(1.0 / (porous * b))
            cs.append(c)
        inverse_total = 1.0 / sum(d * v for d, v in zip(diagonals, inverses))
        weights = [v * inverse_total for v in inverses]
        base[l] = -sum(w * r for w, r in zip(weights, residuals))
        head[l] = sum(w * c for w, c in zip(weights, cs))
        for a in range(3):
            weight[a, l] = weights[a]
            res[a, l] = residuals[a]
        diag[0, l] = diagonals[0]
        diag[1, l] = diagonals[2]
        return carry

    lax.fori_loop(0, L, second, 0)


def first_kernel(
    cells, me, got, info, own, perf, base, head,
    spread, step, row_lo, row_hi, col_lo, col_hi, pay, mine, rows,
):
    lane = iota((1, LANES), 1)
    sums = jnp.sum(got[...], axis=0, keepdims=True)
    total = jnp.where(lane < WELL_DEV, sums, 1.0)
    flow = pltpu.roll(jnp.broadcast_to(sums, (8, LANES)), LANES - 16, 1)[0:1]
    residual = jnp.where(lane < WELL_DEV, flow - total * own[0:1] - own[1:2], 0.0)
    inverse = jnp.where(lane < WELL_DEV, 1.0 / total, 0.0)
    mine[0:1] = residual
    mine[1:2] = inverse
    cell_row = info[0:1].astype(i32)
    well_row = info[1:2].astype(i32)
    heads = gather_wells(got[...], well_row >> 4, (well_row & 15) + 32)
    wells = scatter(cell_row, info[2:3] * heads).reshape(L, R, C)
    spread[...] = wells
    step[...] = base[...] + head[...] * wells
    write_faces(lambda l: step[l], (row_lo, row_hi, col_lo, col_hi))
    gather_cells(cells, (step,), rows)
    column = to_column(info[0:1]).astype(i32) & (C - 1)
    here = to_row(pick_columns(rows, 0, column))
    parts = parts_by_offset(me[0], well_row, perf[0:1] * here)
    pay[:, :TAIL] = jnp.broadcast_to(parts[:, :TAIL], (DEVICES, TAIL))
    packed = parts[:, TAIL:]
    for n, row in enumerate((residual * inverse, residual, inverse)):
        packed = packed + pltpu.roll(jnp.broadcast_to(row, (8, LANES)), 16 * (n + 1), 1)[0:1]
    pay[:, TAIL:] = jnp.broadcast_to(packed, (DEVICES, LANES))


def step_faces(l, down, up, refs, halo):
    step = refs
    row_lo, row_hi, col_lo, col_hi = halo
    here = step[l]
    nexts = shift_rows(here, row_lo[pl.ds(l, 1), :], row_hi[pl.ds(l, 1), :])
    nexts += shift_columns(here, lane_of(col_lo[...], l), lane_of(col_hi[...], l))
    return nexts + (step[down], step[up])


def grid_kernel(
    coef, coef_row, coef_col, tx, ty, tz, head, weight, res, spread, step, row_lo, row_hi, col_lo, col_hi,
    residual, gain, ahead,
):
    def layer(l, carry):
        down, up = (jnp.maximum(l - 1, 0), jnp.minimum(l + 1, L - 1))
        nexts = step_faces(l, down, up, step, (row_lo, row_hi, col_lo, col_hi))
        faces = (tx[0, l], tx[1, l], ty[0, l], ty[1, l], tz[l], tz[l + 1])
        wells = spread[l]
        mixes = [head[l]] * 6
        for a in range(3):
            c = coef[a, l]
            w = weight[a, l]
            sides = shift_rows(c, coef_row[0, a, pl.ds(l, 1), :], coef_row[1, a, pl.ds(l, 1), :])
            sides += shift_columns(c, lane_of(coef_col[0, a], l), lane_of(coef_col[1, a], l))
            sides += (coef[a, down], coef[a, up])
            mixes = [m + w * s for m, s in zip(mixes, sides)]
            residual[a, l] = res[a, l] - c * wells
        total = step[l]
        for j in range(6):
            g = faces[j] * mixes[j]
            gain[j, l] = g
            total = total + g * nexts[j]
        ahead[l] = total
        return carry

    lax.fori_loop(0, L, layer, 0)


def second_kernel(got, info, ahead, head, step, row_lo, row_hi, col_lo, col_hi):
    cell_row = info[0:1].astype(i32)
    well_row = info[1:2].astype(i32)
    moves = gather_wells(got[:, TAIL:], well_row >> 4, (well_row & 15) + 16)
    wells = scatter(cell_row, info[2:3] * moves).reshape(L, R, C)
    step[...] = ahead[...] + head[...] * wells
    write_faces(lambda l: step[l], (row_lo, row_hi, col_lo, col_hi))


def wells_kernel(cells, me, got, info, perf, step, table, spread, parts, rows):
    tail = got[:, TAIL:]
    residuals = pltpu.roll(tail, LANES - 32, 1)
    inverses = pltpu.roll(tail, LANES - 48, 1)
    table[0] = residuals
    table[1] = inverses
    cell_row = info[0:1].astype(i32)
    well_row = info[1:2].astype(i32)
    valid = iota((DEVICES, LANES), 1) < WELL_DEV
    moves = jnp.where(valid, (sum_parts(got[...]) + residuals) * inverses, 0.0)
    values = gather_wells(moves, well_row >> 4, well_row & 15)
    spread[...] = scatter(cell_row, info[2:3] * values).reshape(L, R, C)
    gather_cells(cells, (step,), rows)
    column = to_column(info[0:1]).astype(i32) & (C - 1)
    here = to_row(pick_columns(rows, 0, column))
    parts[...] = jnp.broadcast_to(parts_by_offset(me[0], well_row, perf[0:1] * here), (8, WIDTH))


def third_kernel(
    cells, info, perf, parts, base, gain, head, spread, old, row_lo, row_hi, col_lo, col_hi,
    step, out_row_lo, out_row_hi, out_col_lo, out_col_hi, pay, rows,
):
    def layer(l, carry):
        down, up = (jnp.maximum(l - 1, 0), jnp.minimum(l + 1, L - 1))
        nexts = step_faces(l, down, up, old, (row_lo, row_hi, col_lo, col_hi))
        total = base[l] + head[l] * spread[l]
        for j in range(6):
            total = total + gain[j, l] * nexts[j]
        step[l] = total
        return carry

    lax.fori_loop(0, L, layer, 0)
    write_faces(lambda l: step[l], (out_row_lo, out_row_hi, out_col_lo, out_col_hi))
    gather_cells(cells, (step,), rows)
    column = to_column(info[0:1]).astype(i32) & (C - 1)
    here = pick_columns(rows, 0, column)
    well_row = info[1:2].astype(i32)
    slot_column = to_column(info[1:2]).astype(i32) & 15
    flows = to_holders(well_row >> 4, slot_column, ((1, to_column(perf[0:1]) * here),))
    pay[:, :TAIL] = jnp.broadcast_to(parts[0:1, :TAIL], (DEVICES, TAIL))
    pay[:, TAIL:] = parts[0:1, TAIL:] + flows


def last_grid_kernel(
    p, por, coef, coef_row, coef_col, tx, ty, tz, head, weight, diag, residual, step, row_lo, row_hi, col_lo, col_hi,
    ahead, slope,
):
    def layer(l, carry):
        down, up = (jnp.maximum(l - 1, 0), jnp.minimum(l + 1, L - 1))
        nexts = step_faces(l, down, up, step, (row_lo, row_hi, col_lo, col_hi))
        faces = (tx[0, l], tx[1, l], ty[0, l], ty[1, l], tz[l], tz[l + 1])
        flows = [t * q for t, q in zip(faces, nexts)]
        flow_sum = sum(flows)
        rights, cs = [], []
        for a in range(3):
            c = coef[a, l]
            sides = shift_rows(c, coef_row[0, a, pl.ds(l, 1), :], coef_row[1, a, pl.ds(l, 1), :])
            sides += shift_columns(c, lane_of(coef_col[0, a], l), lane_of(coef_col[1, a], l))
            sides += (coef[a, down], coef[a, up])
            total = c * flow_sum - residual[a, l]
            for v, s in zip(flows, sides):
                total = total + v * s
            rights.append(total)
            cs.append(c)
        z = sum(weight[a, l] * rights[a] for a in range(3))
        h = head[l]
        porous = volume_scale * por[l]
        inverse_water = 1.0 / (porous * (1.0 + compress[0] * p[l]))
        inverse_gas = 1.0 / (porous * (1.0 + compress[2] * p[l]))
        ahead[0, l] = z
        ahead[1, l] = (rights[0] - diag[0, l] * z) * inverse_water
        ahead[2, l] = (rights[2] - diag[1, l] * z) * inverse_gas
        slope[0, l] = (cs[0] - diag[0, l] * h) * inverse_water
        slope[1, l] = (cs[2] - diag[1, l] * h) * inverse_gas
        return carry

    lax.fori_loop(0, L, layer, 0)


def final_kernel(got, info, table, mine, ahead, head, slope, update, moved):
    cell_row = info[0:1].astype(i32)
    well_row = info[1:2].astype(i32)
    valid = iota((DEVICES, LANES), 1) < WELL_DEV
    moves = jnp.where(valid, (sum_parts(got[...]) + table[0]) * table[1], 0.0)
    values = gather_wells(moves, well_row >> 4, well_row & 15)
    wells = scatter(cell_row, info[2:3] * values).reshape(L, R, C)
    update[0] = ahead[0] + head[...] * wells
    update[1] = ahead[1] + slope[0] * wells
    update[2] = ahead[2] + slope[1] * wells
    flow = jnp.sum(got[:, TAIL:], axis=0, keepdims=True)
    flow = pltpu.roll(jnp.broadcast_to(flow, (8, LANES)), LANES - 16, 1)[0:1]
    moved[...] = jnp.broadcast_to((flow + mine[0:1]) * mine[1:2], (8, LANES))


def call(kernel, outs, ins, operands, scratch=(), flops=0, hbm=()):
    shapes = tuple(
        jax.ShapeDtypeStruct(s, f32) if n in hbm else pltpu.VMEM(s, f32) for n, s in enumerate(outs)
    )
    moved = 4 * sum(int(x.size) for x in operands)
    return pl.pallas_call(
        kernel,
        out_shape=shapes,
        in_specs=ins,
        out_specs=tuple(VM for _ in outs),
        scratch_shapes=list(scratch),
        compiler_params=pltpu.CompilerParams(vmem_limit_bytes=40 * 1024 * 1024),
        cost_estimate=pl.CostEstimate(flops=flops, bytes_accessed=moved, transcendentals=0),
    )(*operands)


FIELD = (L, R, C)
ROW, COLUMN = ((L, C), (R, LANES))
FACES = (ROW, ROW, COLUMN, COLUMN)
GATHERED = pltpu.VMEM((1, PERFS, C), f32)


def exchange(array):
    return lax.all_to_all(array, AXES, split_axis=0, concat_axis=0, tiled=True)


def halo_of(faces):
    row_lo, row_hi, col_lo, col_hi = faces
    got = []
    for axis, low, high in (("gx", row_lo, row_hi), ("gy", col_lo, col_hi)):
        count = lax.axis_size(axis)
        up = [(i, i + 1) for i in range(count - 1)]
        got.append(lax.ppermute(high, axis, up))
        got.append(lax.ppermute(low, axis, [(j, i) for i, j in up]))
    return got


def local(
    pressure, sat_water, sat_gas, old_mass, perm, porosity,
    perf_well, perf_cell, perf_index, well_pressure, well_rate,
):
    me = (lax.axis_index("gx") * lax.axis_size("gy") + lax.axis_index("gy")).astype(i32).reshape(1)
    info = jnp.pad(
        jnp.stack([perf_cell.astype(f32), perf_well.astype(f32), perf_index]), ((0, 5), (0, 0))
    )
    own = jnp.pad(jnp.stack([well_pressure, well_rate]), ((0, 6), (0, LANES - WELL_DEV)))
    wide_row, wide_column = ((4 * L, C), (R, LANES))
    *faces, pay, perf = call(
        start_kernel,
        (wide_row, wide_row, wide_column, wide_column, (DEVICES, LANES), (8, PERFS)),
        [SM] + [VM] * 6,
        (perf_cell, info, own, pressure, sat_water, sat_gas, perm),
        [pltpu.VMEM((3, PERFS, C), f32)],
    )
    halo = halo_of(faces)
    got = exchange(pay)
    coef, coef_row, coef_col, tx, ty, tz, base, head, weight, res, diag, _ = call(
        setup_kernel,
        (
            (3,) + FIELD, (2, 3) + ROW, (2, 3) + COLUMN, (2,) + FIELD, (2,) + FIELD, (L + 1, R, C),
            FIELD, FIELD, (3,) + FIELD, (3,) + FIELD, (2,) + FIELD, FIELD,
        ),
        [VM] * 11,
        (info, pressure, sat_water, sat_gas, porosity, old_mass, perm, *halo),
        flops=400 * L * R * C,
    )
    spread, start, *faces, pay, mine = call(
        first_kernel,
        (FIELD, FIELD) + FACES + ((DEVICES, WIDTH), (8, LANES)),
        [SM, SM] + [VM] * 6,
        (perf_cell, me, got, info, own, perf, base, head),
        [GATHERED],
    )
    halo = halo_of(faces)
    got = exchange(pay)
    fields = (coef, coef_row, coef_col, tx, ty, tz, head, weight)
    residual, gain, ahead = call(
        grid_kernel,
        ((3,) + FIELD, (6,) + FIELD, FIELD),
        [VM] * 15,
        (*fields, res, spread, start, *halo),
        flops=100 * L * R * C,
        hbm=(0,),
    )
    step, *faces = call(second_kernel, (FIELD,) + FACES, [VM] * 4, (got, info, ahead, head))
    halo = halo_of(faces)
    table, spread, parts = call(
        wells_kernel,
        ((2, DEVICES, LANES), FIELD, (8, WIDTH)),
        [SM, SM] + [VM] * 4,
        (perf_cell, me, got, info, perf, step),
        [GATHERED],
    )
    step, *faces, pay = call(
        third_kernel,
        (FIELD,) + FACES + ((DEVICES, WIDTH),),
        [SM] + [VM] * 12,
        (perf_cell, info, perf, parts, start, gain, head, spread, step, *halo),
        [GATHERED],
    )
    halo = halo_of(faces)
    got = exchange(pay)
    ahead, slope = call(
        last_grid_kernel,
        ((3,) + FIELD, (2,) + FIELD),
        [VM] * 17,
        (pressure, porosity, *fields, diag, residual, step, *halo),
        flops=150 * L * R * C,
    )
    update, moved = call(
        final_kernel,
        ((3,) + FIELD, (8, LANES)),
        [VM] * 7,
        (got, info, table, mine, ahead, head, slope),
        hbm=(0, 1),
    )
    return residual, mine[0, :WELL_DEV], update, moved[0, :WELL_DEV]


def solution(mesh):
    return jax.shard_map(
        local,
        mesh=mesh,
        in_specs=(
            P(None, "gx", "gy"),
            P(None, "gx", "gy"),
            P(None, "gx", "gy"),
            P(None, None, "gx", "gy"),
            P(None, None, "gx", "gy"),
            P(None, "gx", "gy"),
            P(("gx", "gy")),
            P(("gx", "gy")),
            P(("gx", "gy")),
            P(("gx", "gy")),
            P(("gx", "gy")),
        ),
        out_specs=(
            P(None, None, "gx", "gy"),
            P(("gx", "gy")),
            P(None, None, "gx", "gy"),
            P(("gx", "gy")),
        ),
        check_vma=False,
    )
```

time: 566 us -> 190 us (0.34)
  the two profiles are of different devices: /device:TPU:6 before, /device:TPU:33 now
where the time goes in v1:
time: 190 us; the launch traced here: 188 us
  starting transfers between devices  81.7 us (43%)
  local copies, waits for them, and re-layouts  59.2 us (31%)
  Pallas kernels  37.3 us (20%)
  waiting for transfers between devices  5.6 us (3%)
  other arithmetic  2.73 us (1%)
    unnamed x132, local copies, waits for them, and re-layouts  55.9 us
    pallas_call x9, Pallas kernels, call(): pl.pallas_call(kernel, out_shape=shapes, in_specs=ins, out_specs=tuple((V...  37.3 us
    all_to_all x3, starting transfers between devices, exchange(): return lax.all_to_all(array, AXES, split_axis=0, concat_axis=0, tiled=True)  30.6 us
    ppermute x8, starting transfers between devices, halo_of(): got.append(lax.ppermute(low, axis, [(j, i) for i, j in up]))  26 us
    ppermute x8, starting transfers between devices, halo_of(): got.append(lax.ppermute(high, axis, up))  25.1 us
    ppermute x8, waiting for transfers between devices, halo_of(): got.append(lax.ppermute(low, axis, [(j, i) for i, j in up]))  5.57 us
  transfers between devices with their start and end apart: 19, of which 2 were waited for; matrix products, arithmetic and copies ran while one was open for 0% of the time, Pallas kernels for 12%

profile of v1, /device:TPU:33, one launch (start us, length us, event | category | flops | bytes accessed | tf_op | source)
XLA Modules:
  0.0 187.6 jit_solution(2754762419698544862)
XLA Ops:
  4.4 1.1 copy-done.13
  8.3 4.0 %shard_map.138 = (f32[32,256]{1,0:T(8,128)S(1)}, f32[32,256]{1,0:T(8,128)S(1)}, f32[64,128]{1,0:T(8,128)S(1)}, f32[64,128]{1,0:T(8,128)S(1)}, f32[128,128]{1,0:T(8,128)}, /*index=5*/f32[8,256]{1,0:T(8,128)S(1)}) custom-call(s32[256]{0:T(256)S(1)} %copy-done.55, f32[8,256]{1,0:T(8,128)S(1)} %select_maximum_fusion.info, ...), custom_call_target="tpu_custom_call" | custom-call | bytes 3159040 | tf_op jit(solution)/shard_map/pallas_call | solution.py:455
  12.3 10.5 %all-to-all-start = ((f32[128,1,128]{2,1,0:T(1,128)}), f32[128,1,128]{2,1,0:T(1,128)S(1)}, u32[]{:S(2)}, u32[]{:S(2)}) async-start(f32[128,1,128]{2,1,0:T(1,128)} %bitcast.7), calls=%async_computation | async-start | bytes 131072 | tf_op jit(solution)/shard_map/all_to_all | solution.py:473
  22.8 3.4 %collective-permute-start = (f32[32,256]{1,0:T(8,128)S(1)}, f32[32,256]{1,0:T(8,128)S(1)}, u32[]{:S(2)}, u32[]{:S(2)}) collective-permute-start(f32[32,256]{1,0:T(8,128)S(1)} %get-tuple-element.50), channel_id=1, source_target_pairs={{0,16},{16,32},{32,48},{48,64},{64,80},{80,96},{96,112},{1,17},{17... | collective-permute-start | bytes 98312 | tf_op jit(solution)/shard_map/ppermute | solution.py:482
  26.3 1.9 %collective-permute-start.1 = (f32[32,256]{1,0:T(8,128)S(1)}, f32[32,256]{1,0:T(8,128)S(1)}, u32[]{:S(2)}, u32[]{:S(2)}) collective-permute-start(f32[32,256]{1,0:T(8,128)S(1)} %get-tuple-element.51), channel_id=1, source_target_pairs={{16,0},{32,16},{48,32},{64,48},{80,64},{96,80},{112,96},{17,1},{33... | collective-permute-start | bytes 98312 | tf_op jit(solution)/shard_map/ppermute | solution.py:483
  28.2 3.1 %collective-permute-start.2 = (f32[64,128]{1,0:T(8,128)S(1)}, f32[64,128]{1,0:T(8,128)S(1)}, u32[]{:S(2)}, u32[]{:S(2)}) collective-permute-start(f32[64,128]{1,0:T(8,128)S(1)} %get-tuple-element.52), channel_id=1, source_target_pairs={{0,1},{1,2},{2,3},{3,4},{4,5},{5,6},{6,7},{7,8},{8,9},{9,10},{10,1... | collective-permute-start | bytes 98312 | tf_op jit(solution)/shard_map/ppermute | solution.py:482
  31.3 4.3 %collective-permute-start.3 = (f32[64,128]{1,0:T(8,128)S(1)}, f32[64,128]{1,0:T(8,128)S(1)}, u32[]{:S(2)}, u32[]{:S(2)}) collective-permute-start(f32[64,128]{1,0:T(8,128)S(1)} %get-tuple-element.53), channel_id=1, source_target_pairs={{1,0},{2,1},{3,2},{4,3},{5,4},{6,5},{7,6},{8,7},{9,8},{10,9},{11,1... | collective-permute-start | bytes 98312 | tf_op jit(solution)/shard_map/ppermute | solution.py:483
  44.2 10.4 %shard_map.139 = (f32[3,8,64,256]{3,2,1,0:T(8,128)S(1)}, f32[2,3,8,256]{3,2,1,0:T(8,128)S(1)}, f32[2,3,64,128]{3,2,1,0:T(8,128)S(1)}, f32[2,8,64,256]{3,2,1,0:T(...) custom-call(f32[8,256]{1,0:T(8,128)S(1)} %select_maximum_fusion.info, ...), custom_call_target="tpu_custom_call" | custom-call | flops 52428800 | bytes 5382144 | tf_op jit(solution)/shard_map/pallas_call | solution.py:455
  54.6 1.1 copy-done
  58.6 1.1 copy-done.26
  63.3 3.1 %shard_map.140 = (f32[8,64,256]{2,1,0:T(8,128)S(1)}, f32[8,64,256]{2,1,0:T(8,128)S(1)}, f32[8,256]{1,0:T(8,128)S(1)}, f32[8,256]{1,0:T(8,128)S(1)}, f32[64,128]{...) custom-call(s32[256]{0:T(256)S(1)} %copy-done.56, s32[1]{0:T(128)} %bitcast.5.me, ...), custom_call_target="tpu_custom_call" | custom-call | bytes 1135620 | tf_op jit(solution)/shard_map/pallas_call | solution.py:455
  70.4 1.2 copy.16
  71.6 12.1 %all-to-all-start.1 = ((f32[128,1,768]{2,1,0:T(1,128)}), f32[128,1,768]{2,1,0:T(1,128)}, u32[]{:S(2)}, u32[]{:S(2)}) async-start(f32[128,1,768]{2,1,0:T(1,128)} %copy.16), calls=%async_computation.1 | async-start | bytes 786432 | tf_op jit(solution)/shard_map/all_to_all | solution.py:473
  83.7 3.1 %collective-permute-start.6 = (f32[64,128]{1,0:T(8,128)S(1)}, f32[64,128]{1,0:T(8,128)S(1)}, u32[]{:S(2)}, u32[]{:S(2)}) collective-permute-start(f32[64,128]{1,0:T(8,128)S(1)} %copy-done.60), channel_id=1, source_target_pairs={{0,1},{1,2},{2,3},{3,4},{4,5},{5,6},{6,7},{7,8},{8,9},{9,10},{10,1... | collective-permute-start | bytes 98312 | tf_op jit(solution)/shard_map/ppermute | solution.py:482
  86.8 4.3 %collective-permute-start.7 = (f32[64,128]{1,0:T(8,128)S(1)}, f32[64,128]{1,0:T(8,128)S(1)}, u32[]{:S(2)}, u32[]{:S(2)}) collective-permute-start(f32[64,128]{1,0:T(8,128)S(1)} %copy-done.58), channel_id=1, source_target_pairs={{1,0},{2,1},{3,2},{4,3},{5,4},{6,5},{7,6},{8,7},{9,8},{10,9},{11,1... | collective-permute-start | bytes 98312 | tf_op jit(solution)/shard_map/ppermute | solution.py:483
  91.1 4.0 %collective-permute-start.4 = (f32[8,256]{1,0:T(8,128)}, f32[8,256]{1,0:T(8,128)S(1)}, u32[]{:S(2)}, u32[]{:S(2)}) collective-permute-start(f32[8,256]{1,0:T(8,128)} %copy-done.64), channel_id=1, source_target_pairs={{0,16},{16,32},{32,48},{48,64},{64,80},{80,96},{96,112},{1,17},{17... | collective-permute-start | bytes 24584 | tf_op jit(solution)/shard_map/ppermute | solution.py:482
  95.1 1.9 %collective-permute-start.5 = (f32[8,256]{1,0:T(8,128)S(1)}, f32[8,256]{1,0:T(8,128)S(1)}, u32[]{:S(2)}, u32[]{:S(2)}) collective-permute-start(f32[8,256]{1,0:T(8,128)S(1)} %copy-done.63), channel_id=1, source_target_pairs={{16,0},{32,16},{48,32},{64,48},{80,64},{96,80},{112,96},{17,1},{33... | collective-permute-start | bytes 24584 | tf_op jit(solution)/shard_map/ppermute | solution.py:483
  97.0 3.0 %collective-permute-done.5.row_hi = f32[8,256]{1,0:T(8,128)S(1)} collective-permute-done((f32[8,256]{1,0:T(8,128)S(1)}, f32[8,256]{1,0:T(8,128)S(1)}, u32[]{:S(2)}, u32[]{:S(2)}) %collective-permute-start.5) | collective-permute-done | bytes 8224 | tf_op jit(solution)/shard_map/ppermute | solution.py:483
  100.1 1.4 copy-done.1
  101.5 1.2 copy-done.6
  102.7 1.2 copy-done.9
  105.0 1.4 copy-done.27
  107.4 5.4 %shard_map.141 = (f32[3,8,64,256]{3,2,1,0:T(8,128)}, f32[6,8,64,256]{3,2,1,0:T(8,128)S(1)}, f32[8,64,256]{2,1,0:T(8,128)S(1)}) custom-call(f32[3,8,64,256]{3,2,1,0:T(8,128)S(1)} %get-tuple-element.54.coef, f32[2,3,8,256]{3,2,1,0:T(8,128)S(1)} %get-tuple-element.55.coef_row, f32[2,3,64,128]{3,2,1,0:T(8,128)S(1)} %copy-done.36, ...), custom_call_target="tpu_custom_call" | custom-call | flops 13107200 | bytes 9306112 | tf_op jit(solution)/shard_map/pallas_call | solution.py:455
  112.9 1.6 copy-done.11
  115.3 1.2 copy.23
  118.4 1.9 %collective-permute-start.10 = (f32[64,128]{1,0:T(8,128)S(1)}, f32[64,128]{1,0:T(8,128)S(1)}, u32[]{:S(2)}, u32[]{:S(2)}) collective-permute-start(f32[64,128]{1,0:T(8,128)S(1)} %get-tuple-element.82), channel_id=1, source_target_pairs={{0,1},{1,2},{2,3},{3,4},{4,5},{5,6},{6,7},{7,8},{8,9},{9,10},{10,1... | collective-permute-start | bytes 98312 | tf_op jit(solution)/shard_map/ppermute | solution.py:482
  120.3 5.5 %collective-permute-start.11 = (f32[64,128]{1,0:T(8,128)S(1)}, f32[64,128]{1,0:T(8,128)S(1)}, u32[]{:S(2)}, u32[]{:S(2)}) collective-permute-start(f32[64,128]{1,0:T(8,128)S(1)} %get-tuple-element.83), channel_id=1, source_target_pairs={{1,0},{2,1},{3,2},{4,3},{5,4},{6,5},{7,6},{8,7},{9,8},{10,9},{11,1... | collective-permute-start | bytes 98312 | tf_op jit(solution)/shard_map/ppermute | solution.py:483
  125.8 2.5 %collective-permute-start.8 = (f32[8,256]{1,0:T(8,128)S(1)}, f32[8,256]{1,0:T(8,128)S(1)}, u32[]{:S(2)}, u32[]{:S(2)}) collective-permute-start(f32[8,256]{1,0:T(8,128)S(1)} %get-tuple-element.80), channel_id=1, source_target_pairs={{0,16},{16,32},{32,48},{48,64},{64,80},{80,96},{96,112},{1,17},{17... | collective-permute-start | bytes 24584 | tf_op jit(solution)/shard_map/ppermute | solution.py:482
  128.3 1.9 %collective-permute-start.9 = (f32[8,256]{1,0:T(8,128)S(1)}, f32[8,256]{1,0:T(8,128)S(1)}, u32[]{:S(2)}, u32[]{:S(2)}) collective-permute-start(f32[8,256]{1,0:T(8,128)S(1)} %get-tuple-element.81), channel_id=1, source_target_pairs={{16,0},{32,16},{48,32},{64,48},{80,64},{96,80},{112,96},{17,1},{33... | collective-permute-start | bytes 24584 | tf_op jit(solution)/shard_map/ppermute | solution.py:483
  130.2 3.2 %shard_map.143 = (f32[2,128,128]{2,1,0:T(8,128)S(1)}, f32[8,64,256]{2,1,0:T(8,128)S(1)}, f32[8,768]{1,0:T(8,128)S(1)}) custom-call(s32[256]{0:T(256)S(1)} %copy-done.56, s32[1]{0:T(128)} %bitcast.5.me, f32[128,768]{1,0:T(8,128)S(1)} %bitcast.23, f32[8,256]{1,0:T(8,128)S(1)} %select_maximum_fusion.info, f32[8,256]{1,0:T(8,128)S(1)} %get-tuple-element.64.perf, ...), custom_call_target="tpu_custom_call" | custom-call | bytes 934916 | tf_op jit(solution)/shard_map/pallas_call | solution.py:455
  134.5 3.8 %shard_map.144 = (f32[8,64,256]{2,1,0:T(8,128)S(1)}, f32[8,256]{1,0:T(8,128)S(1)}, f32[8,256]{1,0:T(8,128)S(1)}, f32[64,128]{1,0:T(8,128)S(1)}, f32[64,128]{1,0:T(8,128)S(1)}, /*index=5*/f32[128,768]{1,0:T(8,128)S(1)}) custom-call(s32[256]{0:T(256)S(1)} %copy-done.56, f32[8,256]{1,0:T(8,128)S(1)} %select_maximum_fusion.info, ...), custom_call_target="tpu_custom_call" | custom-call | bytes 5366784 | tf_op jit(solution)/shard_map/pallas_call | solution.py:455
  139.8 1.2 copy.17
  140.9 8.0 %all-to-all-start.2 = ((f32[128,1,768]{2,1,0:T(1,128)}), f32[128,1,768]{2,1,0:T(1,128)}, u32[]{:S(2)}, u32[]{:S(2)}) async-start(f32[128,1,768]{2,1,0:T(1,128)} %copy.17), calls=%async_computation.2 | async-start | bytes 786432 | tf_op jit(solution)/shard_map/all_to_all | solution.py:473
  148.9 3.1 %collective-permute-start.14 = (f32[64,128]{1,0:T(8,128)S(1)}, f32[64,128]{1,0:T(8,128)S(1)}, u32[]{:S(2)}, u32[]{:S(2)}) collective-permute-start(f32[64,128]{1,0:T(8,128)S(1)} %get-tuple-element.90), channel_id=1, source_target_pairs={{0,1},{1,2},{2,3},{3,4},{4,5},{5,6},{6,7},{7,8},{8,9},{9,10},{10,1... | collective-permute-start | bytes 98312 | tf_op jit(solution)/shard_map/ppermute | solution.py:482
  152.0 4.3 %collective-permute-start.15 = (f32[64,128]{1,0:T(8,128)S(1)}, f32[64,128]{1,0:T(8,128)S(1)}, u32[]{:S(2)}, u32[]{:S(2)}) collective-permute-start(f32[64,128]{1,0:T(8,128)S(1)} %get-tuple-element.91), channel_id=1, source_target_pairs={{1,0},{2,1},{3,2},{4,3},{5,4},{6,5},{7,6},{8,7},{9,8},{10,9},{11,1... | collective-permute-start | bytes 98312 | tf_op jit(solution)/shard_map/ppermute | solution.py:483
  156.3 4.0 %collective-permute-start.12 = (f32[8,256]{1,0:T(8,128)}, f32[8,256]{1,0:T(8,128)S(1)}, u32[]{:S(2)}, u32[]{:S(2)}) collective-permute-start(f32[8,256]{1,0:T(8,128)} %copy-done.61), channel_id=1, source_target_pairs={{0,16},{16,32},{32,48},{48,64},{64,80},{80,96},{96,112},{1,17},{17... | collective-permute-start | bytes 24584 | tf_op jit(solution)/shard_map/ppermute | solution.py:482
  160.3 1.9 %collective-permute-start.13 = (f32[8,256]{1,0:T(8,128)S(1)}, f32[8,256]{1,0:T(8,128)S(1)}, u32[]{:S(2)}, u32[]{:S(2)}) collective-permute-start(f32[8,256]{1,0:T(8,128)S(1)} %get-tuple-element.89), channel_id=1, source_target_pairs={{16,0},{32,16},{48,32},{64,48},{80,64},{96,80},{112,96},{17,1},{33... | collective-permute-start | bytes 24584 | tf_op jit(solution)/shard_map/ppermute | solution.py:483
  162.7 2.5 %collective-permute-done.13.row_hi = f32[8,256]{1,0:T(8,128)S(1)} collective-permute-done((f32[8,256]{1,0:T(8,128)S(1)}, f32[8,256]{1,0:T(8,128)S(1)}, u32[]{:S(2)}, u32[]{:S(2)}) %collective-permute-start.13) | collective-permute-done | bytes 8224 | tf_op jit(solution)/shard_map/ppermute | solution.py:483
  165.3 1.4 copy-done.2
  166.7 1.2 copy-done.7
  167.9 1.2 copy-done.10
  170.2 1.4 copy-done.30
  171.6 1.2 copy-done.34
  173.8 4.4 %shard_map.145 = (f32[3,8,64,256]{3,2,1,0:T(8,128)S(1)}, f32[2,8,64,256]{3,2,1,0:T(8,128)S(1)}) custom-call(f32[8,64,256]{2,1,0:T(8,128)S(1)} %copy-done.4, f32[8,64,256]{2,1,0:T(8,128)S(1)} %copy-done.25, f32[3,8,64,256]{3,2,1,0:T(8,128)S(1)} %get-tuple-element.54.coef, f32[2,3,8,256]{3,2,1,0:T(8,128)S(1)} %get-tuple-element.55.coef_row, ...), custom_call_target="tpu_custom_call" | custom-call | flops 19660800 | bytes 10878976 | tf_op jit(solution)/shard_map/pallas_call | solution.py:455
  178.3 1.1 copy-done.28
  181.4 1.4 copy-done.29
  182.8 1.2 copy-done.32
  185.0 2.1 %shard_map.146 = (f32[3,8,64,256]{3,2,1,0:T(8,128)}, f32[8,128]{1,0:T(8,128)S(1)}) custom-call(f32[128,768]{1,0:T(8,128)S(1)} %bitcast.24, f32[8,256]{1,0:T(8,128)S(1)} %select_maximum_fusion.info, f32[2,128,128]{2,1,0:T(8,128)S(1)} %copy-done.46, f32[8,128]{1,0:T(8,128)S(1)} %get-tuple-element.73.mine, f32[3,8,64,256]{3,2,1,0:T(8,128)S(1)} %copy-done.29, ...), custom_call_target="tpu_custom_call" | custom-call | bytes 3682304 | tf_op jit(solution)/shard_map/pallas_call | solution.py:455
  (139 shorter events, 38.8 us)
Async XLA Ops:
  4.4 1.1 copy-start.13
  8.3 29.8 %copy-start.4 = (f32[8,64,256]{2,1,0:T(8,128)S(1)}, f32[8,64,256]{2,1,0:T(8,128)}, u32[]{:S(2)}) copy-start(f32[8,64,256]{2,1,0:T(8,128)} %p.5) | copy-start | bytes 1572868
  8.3 29.8 %copy-start.14 = (bf16[3,8,64,256]{3,2,1,0:T(8,128)(2,1)S(1)}, bf16[3,8,64,256]{3,2,1,0:T(8,128)(2,1)}, u32[]{:S(2)}) copy-start(bf16[3,8,64,256]{3,2,1,0:T(8,128)(2,1)} %perm.3) | copy-start | bytes 2359300
  12.3 49.9 %all-to-all-start = ((f32[128,1,128]{2,1,0:T(1,128)}), f32[128,1,128]{2,1,0:T(1,128)S(1)}, u32[]{:S(2)}, u32[]{:S(2)}) async-start(f32[128,1,128]{2,1,0:T(1,128)} %bitcast.7), calls=%async_computation | async-start | bytes 131072 | tf_op jit(solution)/shard_map/all_to_all | solution.py:473
  22.8 12.8 %collective-permute-start = (f32[32,256]{1,0:T(8,128)S(1)}, f32[32,256]{1,0:T(8,128)S(1)}, u32[]{:S(2)}, u32[]{:S(2)}) collective-permute-start(f32[32,256]{1,0:T(8,128)S(1)} %get-tuple-element.50), channel_id=1, source_target_pairs={{0,16},{16,32},{32,48},{48,64},{64,80},{80,96},{96,112},{1,17},{17... | collective-permute-start | bytes 98312 | tf_op jit(solution)/shard_map/ppermute | solution.py:482
  26.3 10.0 %collective-permute-start.1 = (f32[32,256]{1,0:T(8,128)S(1)}, f32[32,256]{1,0:T(8,128)S(1)}, u32[]{:S(2)}, u32[]{:S(2)}) collective-permute-start(f32[32,256]{1,0:T(8,128)S(1)} %get-tuple-element.51), channel_id=1, source_target_pairs={{16,0},{32,16},{48,32},{64,48},{80,64},{96,80},{112,96},{17,1},{33... | collective-permute-start | bytes 98312 | tf_op jit(solution)/shard_map/ppermute | solution.py:483
  28.2 8.7 %collective-permute-start.2 = (f32[64,128]{1,0:T(8,128)S(1)}, f32[64,128]{1,0:T(8,128)S(1)}, u32[]{:S(2)}, u32[]{:S(2)}) collective-permute-start(f32[64,128]{1,0:T(8,128)S(1)} %get-tuple-element.52), channel_id=1, source_target_pairs={{0,1},{1,2},{2,3},{3,4},{4,5},{5,6},{6,7},{7,8},{8,9},{9,10},{10,1... | collective-permute-start | bytes 98312 | tf_op jit(solution)/shard_map/ppermute | solution.py:482
  31.3 6.2 %collective-permute-start.3 = (f32[64,128]{1,0:T(8,128)S(1)}, f32[64,128]{1,0:T(8,128)S(1)}, u32[]{:S(2)}, u32[]{:S(2)}) collective-permute-start(f32[64,128]{1,0:T(8,128)S(1)} %get-tuple-element.53), channel_id=1, source_target_pairs={{1,0},{2,1},{3,2},{4,3},{5,4},{6,5},{7,6},{8,7},{9,8},{10,9},{11,1... | collective-permute-start | bytes 98312 | tf_op jit(solution)/shard_map/ppermute | solution.py:483
  35.6 26.6 %copy-start.56 = (s32[256]{0:T(256)S(1)}, s32[256]{0:T(256)}, u32[]{:S(2)}) copy-start(s32[256]{0:T(256)} %cells.7) | copy-start | bytes 3076
  38.1 1.0 copy-start.21
  54.6 1.1 copy-start
  58.6 1.1 copy-start.26
  62.2 37.9 %copy-start.16 = (f32[9,64,256]{2,1,0:T(8,128)S(1)}, f32[9,64,256]{2,1,0:T(8,128)}, u32[]{:S(2)}) copy-start(f32[9,64,256]{2,1,0:T(8,128)} %copy-done.15) | copy-start | bytes 1769476
  62.2 37.9 %copy-start.36 = (f32[2,3,64,128]{3,2,1,0:T(8,128)S(1)}, f32[2,3,64,128]{3,2,1,0:T(8,128)}, u32[]{:S(2)}) copy-start(f32[2,3,64,128]{3,2,1,0:T(8,128)} %copy-done.35) | copy-start | bytes 589828
  62.2 1.1 copy-start.40
  70.4 13.2 %copy-start.60 = (f32[64,128]{1,0:T(8,128)S(1)}, f32[64,128]{1,0:T(8,128)}, u32[]{:S(2)}) copy-start(f32[64,128]{1,0:T(8,128)} %copy-done.59) | copy-start | bytes 98308
  70.4 16.4 %copy-start.58 = (f32[64,128]{1,0:T(8,128)S(1)}, f32[64,128]{1,0:T(8,128)}, u32[]{:S(2)}) copy-start(f32[64,128]{1,0:T(8,128)} %copy-done.57) | copy-start | bytes 98308
  70.4 24.6 %copy-start.63 = (f32[8,256]{1,0:T(8,128)S(1)}, f32[8,256]{1,0:T(8,128)}, u32[]{:S(2)}) copy-start(f32[8,256]{1,0:T(8,128)} %copy-done.62) | copy-start | bytes 24580
  71.6 43.7 %all-to-all-start.1 = ((f32[128,1,768]{2,1,0:T(1,128)}), f32[128,1,768]{2,1,0:T(1,128)}, u32[]{:S(2)}, u32[]{:S(2)}) async-start(f32[128,1,768]{2,1,0:T(1,128)} %copy.16), calls=%async_computation.1 | async-start | bytes 786432 | tf_op jit(solution)/shard_map/all_to_all | solution.py:473
  83.7 16.4 %collective-permute-start.6 = (f32[64,128]{1,0:T(8,128)S(1)}, f32[64,128]{1,0:T(8,128)S(1)}, u32[]{:S(2)}, u32[]{:S(2)}) collective-permute-start(f32[64,128]{1,0:T(8,128)S(1)} %copy-done.60), channel_id=1, source_target_pairs={{0,1},{1,2},{2,3},{3,4},{4,5},{5,6},{6,7},{7,8},{8,9},{9,10},{10,1... | collective-permute-start | bytes 98312 | tf_op jit(solution)/shard_map/ppermute | solution.py:482
  86.8 13.3 %collective-permute-start.7 = (f32[64,128]{1,0:T(8,128)S(1)}, f32[64,128]{1,0:T(8,128)S(1)}, u32[]{:S(2)}, u32[]{:S(2)}) collective-permute-start(f32[64,128]{1,0:T(8,128)S(1)} %copy-done.58), channel_id=1, source_target_pairs={{1,0},{2,1},{3,2},{4,3},{5,4},{6,5},{7,6},{8,7},{9,8},{10,9},{11,1... | collective-permute-start | bytes 98312 | tf_op jit(solution)/shard_map/ppermute | solution.py:483
  91.1 5.9 %collective-permute-start.4 = (f32[8,256]{1,0:T(8,128)}, f32[8,256]{1,0:T(8,128)S(1)}, u32[]{:S(2)}, u32[]{:S(2)}) collective-permute-start(f32[8,256]{1,0:T(8,128)} %copy-done.64), channel_id=1, source_target_pairs={{0,16},{16,32},{32,48},{48,64},{64,80},{80,96},{96,112},{1,17},{17... | collective-permute-start | bytes 24584 | tf_op jit(solution)/shard_map/ppermute | solution.py:482
  95.1 5.0 %collective-permute-start.5 = (f32[8,256]{1,0:T(8,128)S(1)}, f32[8,256]{1,0:T(8,128)S(1)}, u32[]{:S(2)}, u32[]{:S(2)}) collective-permute-start(f32[8,256]{1,0:T(8,128)S(1)} %copy-done.63), channel_id=1, source_target_pairs={{16,0},{32,16},{48,32},{64,48},{80,64},{96,80},{112,96},{17,1},{33... | collective-permute-start | bytes 24584 | tf_op jit(solution)/shard_map/ppermute | solution.py:483
  100.1 1.4 copy-start.1
  101.5 1.2 copy-start.6
  102.7 1.2 copy-start.9
  105.0 1.4 copy-start.27
  112.9 1.6 copy-start.11
  115.3 18.1 %copy-start.12 = (f32[6,8,64,256]{3,2,1,0:T(8,128)S(1)}, f32[6,8,64,256]{3,2,1,0:T(8,128)}, u32[]{:S(2)}) copy-start(f32[6,8,64,256]{3,2,1,0:T(8,128)} %copy-done.11) | copy-start | bytes 9437188
  118.4 15.0 %collective-permute-start.10 = (f32[64,128]{1,0:T(8,128)S(1)}, f32[64,128]{1,0:T(8,128)S(1)}, u32[]{:S(2)}, u32[]{:S(2)}) collective-permute-start(f32[64,128]{1,0:T(8,128)S(1)} %get-tuple-element.82), channel_id=1, source_target_pairs={{0,1},{1,2},{2,3},{3,4},{4,5},{5,6},{6,7},{7,8},{8,9},{9,10},{10,1... | collective-permute-start | bytes 98312 | tf_op jit(solution)/shard_map/ppermute | solution.py:482
  120.3 13.1 %collective-permute-start.11 = (f32[64,128]{1,0:T(8,128)S(1)}, f32[64,128]{1,0:T(8,128)S(1)}, u32[]{:S(2)}, u32[]{:S(2)}) collective-permute-start(f32[64,128]{1,0:T(8,128)S(1)} %get-tuple-element.83), channel_id=1, source_target_pairs={{1,0},{2,1},{3,2},{4,3},{5,4},{6,5},{7,6},{8,7},{9,8},{10,9},{11,1... | collective-permute-start | bytes 98312 | tf_op jit(solution)/shard_map/ppermute | solution.py:483
  125.8 7.6 %collective-permute-start.8 = (f32[8,256]{1,0:T(8,128)S(1)}, f32[8,256]{1,0:T(8,128)S(1)}, u32[]{:S(2)}, u32[]{:S(2)}) collective-permute-start(f32[8,256]{1,0:T(8,128)S(1)} %get-tuple-element.80), channel_id=1, source_target_pairs={{0,16},{16,32},{32,48},{48,64},{64,80},{80,96},{96,112},{1,17},{17... | collective-permute-start | bytes 24584 | tf_op jit(solution)/shard_map/ppermute | solution.py:482
  128.3 5.1 %collective-permute-start.9 = (f32[8,256]{1,0:T(8,128)S(1)}, f32[8,256]{1,0:T(8,128)S(1)}, u32[]{:S(2)}, u32[]{:S(2)}) collective-permute-start(f32[8,256]{1,0:T(8,128)S(1)} %get-tuple-element.81), channel_id=1, source_target_pairs={{16,0},{32,16},{48,32},{64,48},{80,64},{96,80},{112,96},{17,1},{33... | collective-permute-start | bytes 24584 | tf_op jit(solution)/shard_map/ppermute | solution.py:483
  133.4 4.9 %copy-start.45 = (f32[2,128,128]{2,1,0:T(8,128)}, f32[2,128,128]{2,1,0:T(8,128)S(1)}, u32[]{:S(2)}) copy-start(f32[2,128,128]{2,1,0:T(8,128)S(1)} %get-tuple-element.85.table) | copy-start | bytes 393220
  133.5 1.1 copy-start.19
  140.9 39.5 %all-to-all-start.2 = ((f32[128,1,768]{2,1,0:T(1,128)}), f32[128,1,768]{2,1,0:T(1,128)}, u32[]{:S(2)}, u32[]{:S(2)}) async-start(f32[128,1,768]{2,1,0:T(1,128)} %copy.17), calls=%async_computation.2 | async-start | bytes 786432 | tf_op jit(solution)/shard_map/all_to_all | solution.py:473
  148.9 16.4 %collective-permute-start.14 = (f32[64,128]{1,0:T(8,128)S(1)}, f32[64,128]{1,0:T(8,128)S(1)}, u32[]{:S(2)}, u32[]{:S(2)}) collective-permute-start(f32[64,128]{1,0:T(8,128)S(1)} %get-tuple-element.90), channel_id=1, source_target_pairs={{0,1},{1,2},{2,3},{3,4},{4,5},{5,6},{6,7},{7,8},{8,9},{9,10},{10,1... | collective-permute-start | bytes 98312 | tf_op jit(solution)/shard_map/ppermute | solution.py:482
  152.0 13.2 %collective-permute-start.15 = (f32[64,128]{1,0:T(8,128)S(1)}, f32[64,128]{1,0:T(8,128)S(1)}, u32[]{:S(2)}, u32[]{:S(2)}) collective-permute-start(f32[64,128]{1,0:T(8,128)S(1)} %get-tuple-element.91), channel_id=1, source_target_pairs={{1,0},{2,1},{3,2},{4,3},{5,4},{6,5},{7,6},{8,7},{9,8},{10,9},{11,1... | collective-permute-start | bytes 98312 | tf_op jit(solution)/shard_map/ppermute | solution.py:483
  156.3 6.4 %collective-permute-start.12 = (f32[8,256]{1,0:T(8,128)}, f32[8,256]{1,0:T(8,128)S(1)}, u32[]{:S(2)}, u32[]{:S(2)}) collective-permute-start(f32[8,256]{1,0:T(8,128)} %copy-done.61), channel_id=1, source_target_pairs={{0,16},{16,32},{32,48},{48,64},{64,80},{80,96},{96,112},{1,17},{17... | collective-permute-start | bytes 24584 | tf_op jit(solution)/shard_map/ppermute | solution.py:482
  160.3 5.0 %collective-permute-start.13 = (f32[8,256]{1,0:T(8,128)S(1)}, f32[8,256]{1,0:T(8,128)S(1)}, u32[]{:S(2)}, u32[]{:S(2)}) collective-permute-start(f32[8,256]{1,0:T(8,128)S(1)} %get-tuple-element.89), channel_id=1, source_target_pairs={{16,0},{32,16},{48,32},{64,48},{80,64},{96,80},{112,96},{17,1},{33... | collective-permute-start | bytes 24584 | tf_op jit(solution)/shard_map/ppermute | solution.py:483
  165.3 1.4 copy-start.2
  166.7 1.2 copy-start.7
  167.9 1.2 copy-start.10
  170.2 1.4 copy-start.30
  171.6 1.2 copy-start.34
  178.3 1.1 copy-start.28
  181.4 1.4 copy-start.29
  182.8 1.2 copy-start.32
  (36 other events, 29.9 us)

commit v2 on v1

v2 whole, which is shorter than its diff:
```python
import jax
import jax.numpy as jnp
from jax import lax
from jax.experimental import pallas as pl
from jax.experimental.pallas import tpu as pltpu
from jax.sharding import PartitionSpec as P

f32 = jnp.float32
bf16 = jnp.bfloat16
i32 = jnp.int32

compress = (0.05, 0.02, 0.2)
viscosity = (0.5, 2.0, 0.1)
volume_scale = 4.0
layer_ratio = 0.1
AXES = ("gx", "gy")
DEVICES = 128
WELL_DEV = 16
REACH = 40
FAR = 64
TAIL = REACH * WELL_DEV
WIDTH = TAIL + 128
LANES = 128
L, R, C = 8, 64, 256
PERFS = 256
VM = pl.BlockSpec(memory_space=pltpu.VMEM)
SM = pl.BlockSpec(memory_space=pltpu.SMEM)
HB = pl.BlockSpec(memory_space=pltpu.HBM)


def iota(shape, dim):
    return lax.broadcasted_iota(i32, shape, dim)


def split3(x):
    high = x.astype(bf16)
    rest = x - high.astype(f32)
    middle = rest.astype(bf16)
    low = (rest - middle.astype(f32)).astype(bf16)
    return high, middle, low


def dot(a, b):
    return jnp.dot(a, b, preferred_element_type=f32)


def to_column(row):
    n = row.shape[1]
    return jnp.sum(jnp.where(iota((n, n), 0) == iota((n, n), 1), row, 0.0), axis=1, keepdims=True)


def to_row(column):
    n = column.shape[0]
    return jnp.sum(jnp.where(iota((n, n), 0) == iota((n, n), 1), column, 0.0), axis=0, keepdims=True)


def coeffs_of(p, sw, sg):
    so = 1.0 - sw - sg
    return tuple(
        s * s * (1.0 / viscosity[a]) * (1.0 + compress[a] * p) for a, s in enumerate((sw, so, sg))
    )


def scatter(cell_row, values):
    match = iota((L * R, PERFS), 0) == (cell_row >> 8)
    column = to_column(cell_row.astype(f32)).astype(i32) & (C - 1)
    spread = (iota((PERFS, C), 1) == column).astype(bf16)
    return sum(
        dot(jnp.where(match, part.astype(f32), 0.0).astype(bf16), spread) for part in split3(values)
    )


def gather_cells(cells, refs, rows):
    def body(block, carry):
        for u in range(8):
            k = block * 8 + u
            cell = cells[k]
            layer = cell >> 14
            line = (cell >> 8) & (R - 1)
            for n, ref in enumerate(refs):
                rows[n, pl.ds(k, 1), :] = ref[layer, pl.ds(line, 1), :]
        return carry

    lax.fori_loop(0, PERFS // 8, body, 0)


def pick_columns(rows, n, column):
    return jnp.sum(jnp.where(iota((PERFS, C), 1) == column, rows[n], 0.0), axis=1, keepdims=True)


def gather_wells(table, holder, slot):
    onehot = (iota((DEVICES, PERFS), 0) == holder).astype(bf16)
    wide = sum(dot(part, onehot) for part in split3(table.T))
    return jnp.sum(jnp.where(iota((LANES, PERFS), 0) == slot, wide, 0.0), axis=0, keepdims=True)


def to_holders(holder, slot_column, columns):
    lane = iota((PERFS, LANES), 1)
    group = lane >> 4
    values = jnp.zeros((PERFS, LANES), f32)
    for g, column in columns:
        values = jnp.where(group == g, column, values)
    values = jnp.where((lane & 15) == slot_column, values, 0.0)
    onehot = (iota((DEVICES, PERFS), 0) == holder).astype(bf16)
    return sum(dot(onehot, part) for part in split3(values))


def parts_by_offset(me, well_row, values):
    offset = (me - (well_row >> 4)) & (DEVICES - 1)
    lane = jnp.where(offset == FAR, TAIL, offset * WELL_DEV) + (well_row & 15)
    column = to_column(lane.astype(f32)).astype(i32)
    onehot = (iota((PERFS, WIDTH), 1) == column).astype(bf16)
    high, middle, low = split3(values)
    rows = jnp.concatenate([high.astype(f32), middle.astype(f32), low.astype(f32), jnp.zeros((5, PERFS), f32)], axis=0)
    return jnp.sum(dot(rows.astype(bf16), onehot), axis=0, keepdims=True)


def tile_of(got, t):
    return got[pl.ds(t, DEVICES, stride=8), :]


def sum_parts(got):
    aligned = tile_of(got, 0)
    for t in range(1, TAIL // LANES):
        aligned = aligned + pltpu.roll(tile_of(got, t), DEVICES - 8 * t, 0)
    total = aligned + pltpu.roll(tile_of(got, 5), DEVICES - FAR, 0)
    for u in range(1, 8):
        total = total + pltpu.roll(pltpu.roll(aligned, DEVICES - u, 0), LANES - 16 * u, 1)
    return total


def to_everyone(tile):
    return jnp.broadcast_to(tile[None], (DEVICES, 8, LANES)).reshape(8 * DEVICES, LANES)


def rolled_row(row, shift):
    return pltpu.roll(jnp.broadcast_to(row, (8, LANES)), shift, 1)[0:1]


def shift_rows(x, first, last):
    return (
        jnp.concatenate([first, x[:-1]], axis=0),
        jnp.concatenate([x[1:], last], axis=0),
    )


def shift_columns(x, first, last):
    lane = iota(x.shape, 1)
    return (
        jnp.where(lane == 0, first, pltpu.roll(x, 1, 1)),
        jnp.where(lane == C - 1, last, pltpu.roll(x, C - 1, 1)),
    )


def lane_of(x, index):
    return pltpu.roll(x, (LANES - index) % LANES, 1)[:, 0:1]


def pack_columns(columns, low, high):
    n = low.shape[0]
    turned = jnp.concatenate([columns, jnp.zeros((LANES - R, LANES), f32)], axis=0).T
    low[...] = turned[0:n]
    high[...] = turned[n : 2 * n]


def unpack_columns(low, high):
    n = low.shape[0]
    rows = jnp.concatenate([low[...], high[...], jnp.zeros((LANES - 2 * n, LANES), f32)], axis=0)
    return rows.T[0:R]


def write_faces(step, outs):
    row_lo, row_hi, col_lo, col_hi = outs
    lane = iota((R, LANES), 1)
    columns = jnp.zeros((R, LANES), f32)
    for l in range(L):
        x = step[l]
        row_lo[l : l + 1, :] = x[0:1]
        row_hi[l : l + 1, :] = x[R - 1 : R]
        columns = jnp.where(lane == l, x[:, 0:1], columns)
        columns = jnp.where(lane == L + l, x[:, C - 1 : C], columns)
    pack_columns(columns, col_lo, col_hi)


def start_copies(pairs, sems):
    copies = [pltpu.make_async_copy(a, b, sems.at[n]) for n, (a, b) in enumerate(pairs)]
    for c in copies:
        c.start()
    return copies


def wait_copies(copies):
    for c in copies:
        c.wait()


def layer_copies(pairs, sems, l):
    return [pltpu.make_async_copy(a, b, sems.at[n, l]) for n, (a, b) in enumerate(pairs(l))]


def start_kernel(
    cells, cell_in, well_in, index_in, pressure_in, rate_in, p_h, sw_h, sg_h, perm_h,
    row_lo, row_hi, col_lo, col_hi, pay, perf, info, own,
    p, sw, sg, perm, rows, sems,
):
    copies = start_copies(
        ((p_h, p), (sw_h, sw), (sg_h, sg), (perm_h.at[0:2], perm)), sems
    )
    cell_row = cell_in[...]
    well_row = well_in[...]
    index_row = index_in[...]
    cell_float = cell_row.astype(f32)
    well_float = well_row.astype(f32)
    info[...] = jnp.concatenate([cell_float, well_float, index_row, jnp.zeros((5, PERFS), f32)], axis=0)
    blank = jnp.zeros((1, LANES - WELL_DEV), f32)
    heads = jnp.concatenate([pressure_in[...], blank], axis=1)
    rates = jnp.concatenate([rate_in[...], blank], axis=1)
    own[...] = jnp.concatenate([heads, rates, jnp.zeros((6, LANES), f32)], axis=0)
    column = to_column(cell_float).astype(i32) & (C - 1)
    slot_column = to_column(well_float).astype(i32) & 15
    index_column = to_column(index_row)
    wait_copies(copies)
    lane = iota((R, LANES), 1)
    columns = jnp.zeros((R, LANES), f32)
    for l in range(L):
        for f, ref in enumerate((p, sw, sg)):
            x = ref[l]
            n = f * L + l
            row_lo[n : n + 1, :] = x[0:1]
            row_hi[n : n + 1, :] = x[R - 1 : R]
            columns = jnp.where(lane == n, x[:, 0:1], columns)
            columns = jnp.where(lane == 4 * L + n, x[:, C - 1 : C], columns)
        n = 3 * L + l
        row_lo[n : n + 1, :] = perm[0, l, 0:16, :].astype(f32)[0:1]
        row_hi[n : n + 1, :] = perm[0, l, R - 16 : R, :].astype(f32)[15:16]
        k = perm[1, l].astype(f32)
        columns = jnp.where(lane == n, k[:, 0:1], columns)
        columns = jnp.where(lane == 4 * L + n, k[:, C - 1 : C], columns)
    pack_columns(columns, col_lo, col_hi)
    gather_cells(cells, (p, sw, sg), rows)
    here = [pick_columns(rows, n, column) for n in range(3)]
    coeffs = coeffs_of(*here)
    total = index_column * (coeffs[0] + coeffs[1] + coeffs[2])
    sums = to_holders(well_row >> 4, slot_column, ((0, total), (1, total * here[0])))
    pay[...] = sums + rolled_row(heads, 32)
    perf[...] = jnp.broadcast_to(to_row(total), (8, PERFS))


def transmit(k, k_next):
    return k * k_next / (k + k_next)


def neighbours(field, l, rows, columns, first, last):
    here = field(l)
    nexts = shift_rows(here, *rows)
    nexts += shift_columns(here, lane_of(columns, first), lane_of(columns, last))
    return nexts + (field(jnp.maximum(l - 1, 0)), field(jnp.minimum(l + 1, L - 1)))


def coeff_neighbours(coef, coef_row, coef_col, a, l):
    rows = (coef_row[0, a, pl.ds(l, 1), :], coef_row[1, a, pl.ds(l, 1), :])
    return neighbours(lambda m: coef[a, m], l, rows, coef_col[a], l, 4 * L + l)


def step_neighbours(step, row_lo, row_hi, columns, l):
    rows = (row_lo[pl.ds(l, 1), :], row_hi[pl.ds(l, 1), :])
    return neighbours(lambda m: step[m], l, rows, columns, l, L + l)


def setup_kernel(
    me, info, row_lo, row_hi, col_lo, col_hi, p_h, sw_h, sg_h, por_h, mass_h, perm_h,
    coef_row, coef_col, coef_h, tx_h, ty_h, tz_h, base_h, head_h, weight_h, res_h, diag_h,
    p, sw, sg, por, mass, perm, coef, tx, ty, tz, base, head, weight, res, diag, index_sum,
    sems, sems_t, sems_out,
):
    copies = start_copies(
        ((p_h, p), (sw_h, sw), (sg_h, sg), (perm_h, perm), (por_h, por), (mass_h, mass)), sems
    )
    index_sum[...] = scatter(info[0:1].astype(i32), info[2:3]).reshape(L, R, C)
    for side, ref in enumerate((row_lo, row_hi)):
        for a, c in enumerate(coeffs_of(ref[0:L], ref[L : 2 * L], ref[2 * L : 3 * L])):
            coef_row[side, a] = c
    columns = unpack_columns(col_lo, col_hi)
    for a, c in enumerate(
        coeffs_of(columns, pltpu.roll(columns, LANES - L, 1), pltpu.roll(columns, LANES - 2 * L, 1))
    ):
        coef_col[a] = c
    lane = iota((R, C), 1)
    gx = me[0] >> 4
    gy = me[0] & 15
    inside = [jnp.where(t, 1.0, 0.0) for t in (gx > 0, gx < 7, gy > 0, gy < 15)]
    wait_copies(copies[:4])

    def first(l, carry):
        for a, c in enumerate(coeffs_of(p[l], sw[l], sg[l])):
            coef[a, l] = c
        k = perm[0, l].astype(f32)
        n = 3 * L + l
        edge = row_lo[pl.ds(n, 1), :] * inside[0]
        before = transmit(k, jnp.concatenate([edge, k[:-1]], axis=0))
        edge = row_hi[pl.ds(n, 1), :] * inside[1]
        tx[0, l] = before
        tx[1, l] = jnp.concatenate([before[1:], transmit(k[R - 1 : R], edge)], axis=0)
        k = perm[1, l].astype(f32)
        edge = lane_of(columns, n) * inside[2]
        before = transmit(k, jnp.where(lane == 0, edge, pltpu.roll(k, 1, 1)))
        edge = lane_of(columns, 4 * L + n) * inside[3]
        ty[0, l] = before
        ty[1, l] = jnp.where(lane == C - 1, transmit(k[:, C - 1 : C], edge), pltpu.roll(before, C - 1, 1))
        k = perm[2, l].astype(f32)
        under = perm[2, jnp.maximum(l - 1, 0)].astype(f32)
        tz[l] = jnp.where(l > 0, layer_ratio, 0.0) * transmit(k, under)
        return carry

    lax.fori_loop(0, L, first, 0)
    tz[L] = jnp.zeros((R, C), f32)
    saved = start_copies(((coef, coef_h), (tx, tx_h), (ty, ty_h), (tz, tz_h)), sems_t)
    wait_copies(copies[4:])

    def outs(l):
        return (
            (base.at[l], base_h.at[l]), (head.at[l], head_h.at[l]), (weight.at[:, l], weight_h.at[:, l]),
            (res.at[:, l], res_h.at[:, l]), (diag.at[:, l], diag_h.at[:, l]),
        )

    def second(l, carry):
        here = p[l]
        rows = (row_lo[pl.ds(l, 1), :], row_hi[pl.ds(l, 1), :])
        nexts = neighbours(lambda m: p[m], l, rows, columns, l, 4 * L + l)
        faces = (tx[0, l], tx[1, l], ty[0, l], ty[1, l], tz[l], tz[l + 1])
        drops = [t * (here - q) for t, q in zip(faces, nexts)]
        face_sum = sum(faces)
        drop_sum = sum(drops)
        porous = volume_scale * por[l]
        sats = (sw[l], 1.0 - sw[l] - sg[l], sg[l])
        indices = index_sum[l]
        diagonals, residuals, inverses, cs = [], [], [], []
        for a in range(3):
            c = coef[a, l]
            ab = c * face_sum
            net = c * drop_sum
            for t, d, s in zip(faces, drops, coeff_neighbours(coef, coef_row, coef_col, a, l)):
                ab = ab + t * s
                net = net + d * s
            b = 1.0 + compress[a] * here
            stored = porous * sats[a]
            diagonals.append(compress[a] * stored + ab + c * indices)
            residuals.append(b * stored - volume_scale * mass[a, l] + net + c * (indices * here))
            inverses.append(1.0 / (porous * b))
            cs.append(c)
        inverse_total = 1.0 / sum(d * v for d, v in zip(diagonals, inverses))
        weights = [v * inverse_total for v in inverses]
        base[l] = -sum(w * r for w, r in zip(weights, residuals))
        head[l] = sum(w * c for w, c in zip(weights, cs))
        for a in range(3):
            weight[a, l] = weights[a]
            res[a, l] = residuals[a]
        diag[0, l] = diagonals[0]
        diag[1, l] = diagonals[2]
        for c in layer_copies(outs, sems_out, l):
            c.start()
        return carry

    lax.fori_loop(0, L, second, 0)
    wait_copies(saved)
    for l in range(L):
        wait_copies(layer_copies(outs, sems_out, l))


def first_kernel(
    cells, me, got, info, own, perf, base_h, head_h,
    row_lo, row_hi, col_lo, col_hi, pay, mine, well_residual, spread_h, step_h,
    base, head, spread, step, rows, sems,
):
    copies = start_copies(((base_h, base), (head_h, head)), sems)
    lane = iota((1, LANES), 1)
    sums = jnp.sum(got[...], axis=0, keepdims=True)
    total = jnp.where(lane < WELL_DEV, sums, 1.0)
    flow = rolled_row(sums, LANES - 16)
    residual = jnp.where(lane < WELL_DEV, flow - total * own[0:1] - own[1:2], 0.0)
    inverse = jnp.where(lane < WELL_DEV, 1.0 / total, 0.0)
    mine[...] = jnp.concatenate([residual, inverse, jnp.zeros((6, LANES), f32)], axis=0)
    well_residual[...] = residual[:, 0:WELL_DEV]
    cell_row = info[0:1].astype(i32)
    well_row = info[1:2].astype(i32)
    heads = gather_wells(got[...], well_row >> 4, (well_row & 15) + 32)
    spread[...] = scatter(cell_row, info[2:3] * heads).reshape(L, R, C)
    wait_copies(copies)
    step[...] = base[...] + head[...] * spread[...]
    copies = start_copies(((spread, spread_h), (step, step_h)), sems)
    write_faces(step, (row_lo, row_hi, col_lo, col_hi))
    gather_cells(cells, (step,), rows)
    column = to_column(info[0:1]).astype(i32) & (C - 1)
    here = to_row(pick_columns(rows, 0, column))
    parts = parts_by_offset(me[0], well_row, perf[0:1] * here)
    packed = parts[:, TAIL:]
    for n, row in enumerate((residual * inverse, residual, inverse)):
        packed = packed + rolled_row(row, 16 * (n + 1))
    tiles = [parts[:, LANES * t : LANES * (t + 1)] for t in range(5)]
    pay[...] = to_everyone(jnp.concatenate(tiles + [packed, jnp.zeros((2, LANES), f32)], axis=0))
    wait_copies(copies)


def grid_kernel(
    coef_row, coef_col, row_lo, row_hi, col_lo, col_hi,
    coef_h, tx_h, ty_h, tz_h, head_h, weight_h, res_h, spread_h, step_h,
    residual_h, gain_h, ahead_h,
    coef, tx, ty, tz, head, weight, res, spread, step, residual, gain, ahead, sems, sems_out,
):
    copies = start_copies(
        (
            (coef_h, coef), (tx_h, tx), (ty_h, ty), (tz_h, tz), (head_h, head), (weight_h, weight),
            (res_h, res), (spread_h, spread), (step_h, step),
        ),
        sems,
    )
    columns = unpack_columns(col_lo, col_hi)
    wait_copies(copies)

    def outs(l):
        return (
            (residual.at[:, l], residual_h.at[:, l]), (gain.at[:, l], gain_h.at[:, l]),
            (ahead.at[l], ahead_h.at[l]),
        )

    def layer(l, carry):
        nexts = step_neighbours(step, row_lo, row_hi, columns, l)
        faces = (tx[0, l], tx[1, l], ty[0, l], ty[1, l], tz[l], tz[l + 1])
        wells = spread[l]
        mixes = [head[l]] * 6
        for a in range(3):
            w = weight[a, l]
            sides = coeff_neighbours(coef, coef_row, coef_col, a, l)
            mixes = [m + w * s for m, s in zip(mixes, sides)]
            residual[a, l] = res[a, l] - coef[a, l] * wells
        total = step[l]
        for j in range(6):
            g = faces[j] * mixes[j]
            gain[j, l] = g
            total = total + g * nexts[j]
        ahead[l] = total
        for c in layer_copies(outs, sems_out, l):
            c.start()
        return carry

    lax.fori_loop(0, L, layer, 0)
    for l in range(L):
        wait_copies(layer_copies(outs, sems_out, l))


def second_kernel(got, info, ahead_h, head_h, row_lo, row_hi, col_lo, col_hi, step, ahead, head, sems):
    copies = start_copies(((ahead_h, ahead), (head_h, head)), sems)
    cell_row = info[0:1].astype(i32)
    well_row = info[1:2].astype(i32)
    moves = gather_wells(tile_of(got, 5), well_row >> 4, (well_row & 15) + 16)
    wells = scatter(cell_row, info[2:3] * moves).reshape(L, R, C)
    wait_copies(copies)
    step[...] = ahead[...] + head[...] * wells
    write_faces(step, (row_lo, row_hi, col_lo, col_hi))


def wells_kernel(
    cells, me, got, info, perf, step, base_h, gain_h, head_h, table, parts, spread, base, gain, head, rows, sems,
):
    copies = start_copies(((base_h, base), (gain_h, gain), (head_h, head)), sems)
    tail = tile_of(got, 5)
    residuals = pltpu.roll(tail, LANES - 32, 1)
    inverses = pltpu.roll(tail, LANES - 48, 1)
    table[0] = residuals
    table[1] = inverses
    cell_row = info[0:1].astype(i32)
    well_row = info[1:2].astype(i32)
    valid = iota((DEVICES, LANES), 1) < WELL_DEV
    moves = jnp.where(valid, (sum_parts(got) + residuals) * inverses, 0.0)
    values = gather_wells(moves, well_row >> 4, well_row & 15)
    spread[...] = scatter(cell_row, info[2:3] * values).reshape(L, R, C)
    gather_cells(cells, (step,), rows)
    column = to_column(info[0:1]).astype(i32) & (C - 1)
    here = to_row(pick_columns(rows, 0, column))
    flows = parts_by_offset(me[0], well_row, perf[0:1] * here)
    tiles = [flows[:, LANES * t : LANES * (t + 1)] for t in range(6)]
    parts[...] = jnp.concatenate(tiles + [jnp.zeros((2, LANES), f32)], axis=0)
    wait_copies(copies)


def third_kernel(
    cells, info, perf, parts, spread, old, base, gain, head, row_lo, row_hi, col_lo, col_hi,
    out_row_lo, out_row_hi, out_col_lo, out_col_hi, pay, step_h, step, rows, sems,
):
    columns = unpack_columns(col_lo, col_hi)

    def layer(l, carry):
        nexts = step_neighbours(old, row_lo, row_hi, columns, l)
        total = base[l] + head[l] * spread[l]
        for j in range(6):
            total = total + gain[j, l] * nexts[j]
        step[l] = total
        return carry

    lax.fori_loop(0, L, layer, 0)
    copies = start_copies(((step, step_h),), sems)
    write_faces(step, (out_row_lo, out_row_hi, out_col_lo, out_col_hi))
    gather_cells(cells, (step,), rows)
    column = to_column(info[0:1]).astype(i32) & (C - 1)
    here = pick_columns(rows, 0, column)
    well_row = info[1:2].astype(i32)
    slot_column = to_column(info[1:2]).astype(i32) & 15
    pay[...] = to_everyone(parts[...])
    pay[pl.ds(6, DEVICES, stride=8), :] = to_holders(
        well_row >> 4, slot_column, ((0, to_column(perf[0:1]) * here),)
    )
    wait_copies(copies)


def last_grid_kernel(
    coef_row, coef_col, row_lo, row_hi, col_lo, col_hi,
    p_h, por_h, coef_h, tx_h, ty_h, tz_h, head_h, weight_h, diag_h, residual_h, step_h,
    ahead_h, slope_h,
    p, por, coef, tx, ty, tz, head, weight, diag, residual, step, ahead, slope, sems, sems_out,
):
    copies = start_copies(
        (
            (p_h, p), (por_h, por), (coef_h, coef), (tx_h, tx), (ty_h, ty), (tz_h, tz), (head_h, head),
            (weight_h, weight), (diag_h, diag), (residual_h, residual), (step_h, step),
        ),
        sems,
    )
    columns = unpack_columns(col_lo, col_hi)
    wait_copies(copies)

    def outs(l):
        return ((ahead.at[:, l], ahead_h.at[:, l]), (slope.at[:, l], slope_h.at[:, l]))

    def layer(l, carry):
        nexts = step_neighbours(step, row_lo, row_hi, columns, l)
        faces = (tx[0, l], tx[1, l], ty[0, l], ty[1, l], tz[l], tz[l + 1])
        flows = [t * q for t, q in zip(faces, nexts)]
        flow_sum = sum(flows)
        rights, cs = [], []
        for a in range(3):
            c = coef[a, l]
            total = c * flow_sum - residual[a, l]
            for v, s in zip(flows, coeff_neighbours(coef, coef_row, coef_col, a, l)):
                total = total + v * s
            rights.append(total)
            cs.append(c)
        z = sum(weight[a, l] * rights[a] for a in range(3))
        h = head[l]
        porous = volume_scale * por[l]
        inverse_water = 1.0 / (porous * (1.0 + compress[0] * p[l]))
        inverse_gas = 1.0 / (porous * (1.0 + compress[2] * p[l]))
        ahead[0, l] = z
        ahead[1, l] = (rights[0] - diag[0, l] * z) * inverse_water
        ahead[2, l] = (rights[2] - diag[1, l] * z) * inverse_gas
        slope[0, l] = (cs[0] - diag[0, l] * h) * inverse_water
        slope[1, l] = (cs[2] - diag[1, l] * h) * inverse_gas
        for c in layer_copies(outs, sems_out, l):
            c.start()
        return carry

    lax.fori_loop(0, L, layer, 0)
    for l in range(L):
        wait_copies(layer_copies(outs, sems_out, l))


def final_kernel(
    got, info, table, mine, ahead_h, head_h, slope_h, update_h, moved, ahead, head, slope, update, sems, sems_out,
):
    copies = start_copies(((head_h, head), (ahead_h, ahead), (slope_h, slope)), sems)
    flow = jnp.sum(tile_of(got, 6), axis=0, keepdims=True)
    moved[...] = ((flow + mine[0:1]) * mine[1:2])[:, 0:WELL_DEV]
    cell_row = info[0:1].astype(i32)
    well_row = info[1:2].astype(i32)
    valid = iota((DEVICES, LANES), 1) < WELL_DEV
    moves = jnp.where(valid, (sum_parts(got) + table[0]) * table[1], 0.0)
    values = gather_wells(moves, well_row >> 4, well_row & 15)
    wells = scatter(cell_row, info[2:3] * values).reshape(L, R, C)
    wait_copies(copies)

    def outs(l):
        return ((update.at[:, l], update_h.at[:, l]),)

    for l in range(L):
        update[0, l] = ahead[0, l] + head[l] * wells[l]
        update[1, l] = ahead[1, l] + slope[0, l] * wells[l]
        update[2, l] = ahead[2, l] + slope[1, l] * wells[l]
        layer_copies(outs, sems_out, l)[0].start()
    for l in range(L):
        wait_copies(layer_copies(outs, sems_out, l))


def call(kernel, outs, ins, operands, scratch=(), flops=0):
    shapes = tuple(pltpu.VMEM(s, f32) if w is VM else jax.ShapeDtypeStruct(s, f32) for s, w in outs)
    moved = 4 * sum(int(x.size) for x in operands)
    return pl.pallas_call(
        kernel,
        out_shape=shapes,
        in_specs=ins,
        out_specs=tuple(w or VM for _, w in outs),
        scratch_shapes=[pltpu.VMEM(x, f32) if type(x) is tuple else x for x in scratch],
        compiler_params=pltpu.CompilerParams(vmem_limit_bytes=40 * 1024 * 1024),
        cost_estimate=pl.CostEstimate(flops=flops, bytes_accessed=moved, transcendentals=0),
    )(*operands)


FIELD = (L, R, C)
TWO, THREE, SIX, FACED = ((2,) + FIELD, (3,) + FIELD, (6,) + FIELD, (L + 1, R, C))
FACES = (((L, C), VM), ((L, C), VM), ((L, LANES), VM), ((L, LANES), VM))
WIDE_FACES = (((4 * L, C), VM), ((4 * L, C), VM), ((4 * L, LANES), VM), ((4 * L, LANES), VM))
SMALL = (8, LANES)
ROWS = (1, PERFS, C)
PAY = ((8 * DEVICES, LANES), None)
sem = pltpu.SemaphoreType.DMA


def exchange(array):
    return lax.all_to_all(array, AXES, split_axis=0, concat_axis=0, tiled=True)


def exchange_tiles(array):
    return exchange(array.reshape(DEVICES, 8, LANES)).reshape(8 * DEVICES, LANES)


def halo_of(faces):
    row_lo, row_hi, col_lo, col_hi = faces
    got = []
    for axis, low, high in (("gx", row_lo, row_hi), ("gy", col_lo, col_hi)):
        count = lax.axis_size(axis)
        up = [(i, (i + 1) % count) for i in range(count)]
        got.append(lax.ppermute(high, axis, up))
        got.append(lax.ppermute(low, axis, [(j, i) for i, j in up]))
    return got


def local(
    pressure, sat_water, sat_gas, old_mass, perm, porosity,
    perf_well, perf_cell, perf_index, well_pressure, well_rate,
):
    me = (lax.axis_index("gx") * lax.axis_size("gy") + lax.axis_index("gy")).astype(i32).reshape(1)
    *faces, pay, perf, info, own = call(
        start_kernel,
        WIDE_FACES + (((DEVICES, LANES), None), ((8, PERFS), VM), ((8, PERFS), VM), (SMALL, VM)),
        [SM] + [VM] * 5 + [HB] * 4,
        (
            perf_cell, perf_cell.reshape(1, PERFS), perf_well.reshape(1, PERFS), perf_index.reshape(1, PERFS),
            well_pressure.reshape(1, WELL_DEV), well_rate.reshape(1, WELL_DEV), pressure, sat_water, sat_gas, perm,
        ),
        [FIELD, FIELD, FIELD, pltpu.VMEM(TWO, bf16), (3, PERFS, C), sem((4,))],
    )
    halo = halo_of(faces)
    got = exchange(pay)
    coef_row, coef_col, coef, tx, ty, tz, base, head, weight, res, diag = call(
        setup_kernel,
        (
            ((2, 3, L, C), VM), ((3, R, LANES), VM), (THREE, HB), (TWO, HB), (TWO, HB), (FACED, HB),
            (FIELD, HB), (FIELD, HB), (THREE, HB), (THREE, HB), (TWO, HB),
        ),
        [SM] + [VM] * 5 + [HB] * 6,
        (me, info, *halo, pressure, sat_water, sat_gas, porosity, old_mass, perm),
        [
            FIELD, FIELD, FIELD, FIELD, THREE, pltpu.VMEM(THREE, bf16), THREE, TWO, TWO, FACED,
            FIELD, FIELD, THREE, THREE, TWO, FIELD, sem((6,)), sem((4,)), sem((5, L)),
        ],
        flops=400 * L * R * C,
    )
    *faces, pay, mine, well_residual, spread, start = call(
        first_kernel,
        FACES + (PAY, (SMALL, VM), ((1, WELL_DEV), None), (FIELD, HB), (FIELD, HB)),
        [SM, SM] + [VM] * 4 + [HB] * 2,
        (perf_cell, me, got, info, own, perf, base, head),
        [FIELD, FIELD, FIELD, FIELD, ROWS, sem((2,))],
    )
    halo = halo_of(faces)
    got = exchange_tiles(pay)
    fields = (coef, tx, ty, tz, head, weight)
    residual, gain, ahead = call(
        grid_kernel,
        ((THREE, HB), (SIX, HB), (FIELD, HB)),
        [VM] * 6 + [HB] * 9,
        (coef_row, coef_col, *halo, *fields, res, spread, start),
        [
            THREE, TWO, TWO, FACED, FIELD, THREE, THREE, FIELD, FIELD, THREE, SIX, FIELD,
            sem((9,)), sem((3, L)),
        ],
        flops=100 * L * R * C,
    )
    *faces, step = call(
        second_kernel,
        FACES + ((FIELD, VM),),
        [VM] * 2 + [HB] * 2,
        (got, info, ahead, head),
        [FIELD, FIELD, sem((2,))],
    )
    halo = halo_of(faces)
    table, parts, spread, base, gain_near, head_near = call(
        wells_kernel,
        (((2, DEVICES, LANES), None), (SMALL, VM), (FIELD, VM), (FIELD, VM), (SIX, VM), (FIELD, VM)),
        [SM, SM] + [VM] * 4 + [HB] * 3,
        (perf_cell, me, got, info, perf, step, start, gain, head),
        [ROWS, sem((3,))],
    )
    *faces, pay, step = call(
        third_kernel,
        FACES + (PAY, (FIELD, HB)),
        [SM] + [VM] * 12,
        (perf_cell, info, perf, parts, spread, step, base, gain_near, head_near, *halo),
        [FIELD, ROWS, sem((1,))],
    )
    halo = halo_of(faces)
    got = exchange_tiles(pay)
    ahead, slope = call(
        last_grid_kernel,
        ((THREE, HB), (TWO, HB)),
        [VM] * 6 + [HB] * 11,
        (coef_row, coef_col, *halo, pressure, porosity, *fields, diag, residual, step),
        [
            FIELD, FIELD, THREE, TWO, TWO, FACED, FIELD, THREE, TWO, THREE, FIELD, THREE, TWO,
            sem((11,)), sem((2, L)),
        ],
        flops=150 * L * R * C,
    )
    update, moved = call(
        final_kernel,
        ((THREE, HB), ((1, WELL_DEV), None)),
        [VM] * 4 + [HB] * 3,
        (got, info, table, mine, ahead, head, slope),
        [THREE, FIELD, TWO, THREE, sem((3,)), sem((1, L))],
    )
    return residual, well_residual.reshape(WELL_DEV), update, moved.reshape(WELL_DEV)


def solution(mesh):
    return jax.shard_map(
        local,
        mesh=mesh,
        in_specs=(
            P(None, "gx", "gy"),
            P(None, "gx", "gy"),
            P(None, "gx", "gy"),
            P(None, None, "gx", "gy"),
            P(None, None, "gx", "gy"),
            P(None, "gx", "gy"),
            P(("gx", "gy")),
            P(("gx", "gy")),
            P(("gx", "gy")),
            P(("gx", "gy")),
            P(("gx", "gy")),
        ),
        out_specs=(
            P(None, None, "gx", "gy"),
            P(("gx", "gy")),
            P(None, None, "gx", "gy"),
            P(("gx", "gy")),
        ),
        check_vma=False,
    )
```

time: 190 us -> 165 us (0.87)
  the two profiles are of different devices: /device:TPU:33 before, /device:TPU:1 now
where the time goes in v2:
time: 165 us; the launch traced here: 164 us
  starting transfers between devices  56.7 us (34%)
  local copies, waits for them, and re-layouts  51.4 us (31%)
  Pallas kernels  46.1 us (28%)
  waiting for transfers between devices  8.62 us (5%)
    unnamed x106, local copies, waits for them, and re-layouts  51.4 us
    pallas_call x9, Pallas kernels, call(): pl.pallas_call(kernel, out_shape=shapes, in_specs=ins, out_specs=tuple((w...  46.1 us
    all_to_all x3, starting transfers between devices, exchange(): return lax.all_to_all(array, AXES, split_axis=0, concat_axis=0, tiled=True)  28.6 us
    ppermute x8, starting transfers between devices, halo_of(): got.append(lax.ppermute(low, axis, [(j, i) for i, j in up]))  17.2 us
    ppermute x8, starting transfers between devices, halo_of(): got.append(lax.ppermute(high, axis, up))  10.9 us
    ppermute x8, waiting for transfers between devices, halo_of(): got.append(lax.ppermute(high, axis, up))  8.59 us
  transfers between devices with their start and end apart: 19, of which 3 were waited for; matrix products, arithmetic and copies ran while one was open for 0% of the time, Pallas kernels for 18%

profile of v2, /device:TPU:1, one launch (start us, length us, event | category | flops | bytes accessed | tf_op | source)
XLA Modules:
  0.0 163.9 jit_solution(5296743222984005407)
XLA Ops:
  1.7 1.1 copy-done.13
  8.2 4.4 %shard_map.138 = (f32[32,256]{1,0:T(8,128)S(1)}, f32[32,256]{1,0:T(8,128)S(1)}, f32[32,128]{1,0:T(8,128)S(1)}, f32[32,128]{1,0:T(8,128)S(1)}, f32[128,128]{1,0:T...) custom-call(s32[256]{0:T(256)S(1)} %copy-done.47, s32[1,256]{1,0:T(1,128)S(1)} %bitcast.21, ...), custom_call_target="tpu_custom_call" | custom-call | bytes 3149952 | tf_op jit(solution)/shard_map/pallas_call | solution.py:595
  12.7 11.5 %all-to-all-start = ((f32[128,1,128]{2,1,0:T(1,128)}), f32[128,1,128]{2,1,0:T(1,128)S(1)}, u32[]{:S(2)}, u32[]{:S(2)}) async-start(f32[128,1,128]{2,1,0:T(1,128)} %bitcast.7), calls=%async_computation | async-start | bytes 131072 | tf_op jit(solution)/shard_map/all_to_all | solution.py:617
  24.2 1.6 %collective-permute-start = (f32[32,256]{1,0:T(8,128)S(1)}, f32[32,256]{1,0:T(8,128)S(1)}, u32[]{:S(2)}, u32[]{:S(2)}) collective-permute-start(f32[32,256]{1,0:T(8,128)S(1)} %get-tuple-element.57), channel_id=1, source_target_pairs={{0,16},{16,32},{32,48},{48,64},{64,80},{80,96},{96,112},{112,0},{1... | collective-permute-start | bytes 98312 | tf_op jit(solution)/shard_map/ppermute | solution.py:630
  25.9 1.2 collective-permute-start.2
  27.0 4.1 %collective-permute-start.3 = (f32[32,128]{1,0:T(8,128)S(1)}, f32[32,128]{1,0:T(8,128)S(1)}, u32[]{:S(2)}, u32[]{:S(2)}) collective-permute-start(f32[32,128]{1,0:T(8,128)S(1)} %get-tuple-element.60), channel_id=1, source_target_pairs={{1,0},{2,1},{3,2},{4,3},{5,4},{6,5},{7,6},{8,7},{9,8},{10,9},{11,1... | collective-permute-start | bytes 49160 | tf_op jit(solution)/shard_map/ppermute | solution.py:631
  31.1 1.4 collective-permute-done.2.col_lo
  32.6 1.1 copy-done.14
  35.8 1.4 copy-done.28
  37.2 12.2 %shard_map.139 = (f32[2,3,8,256]{3,2,1,0:T(8,128)S(1)}, f32[3,64,128]{2,1,0:T(8,128)S(1)}, f32[3,8,64,256]{3,2,1,0:T(8,128)S(1)}, f32[2,8,64,256]{3,2,1,0:T(8,12...) custom-call(s32[1]{0:T(128)} %bitcast.me, ...), custom_call_target="tpu_custom_call" | custom-call | flops 52428800 | bytes 5349380 | tf_op jit(solution)/shard_map/pallas_call | solution.py:595
  49.4 1.1 copy-done
  53.4 1.1 copy-done.31
  57.4 4.0 %shard_map.140 = (f32[8,256]{1,0:T(8,128)S(1)}, f32[8,256]{1,0:T(8,128)S(1)}, f32[8,128]{1,0:T(8,128)S(1)}, f32[8,128]{1,0:T(8,128)S(1)}, f32[1024,128]{1,0:T(8,...) custom-call(s32[256]{0:T(256)S(1)} %copy-done.48, ...), custom_call_target="tpu_custom_call" | custom-call | bytes 1135620 | tf_op jit(solution)/shard_map/pallas_call | solution.py:595
  63.9 10.1 %all-to-all-start.1 = ((f32[128,8,128]{2,1,0:T(8,128)}), f32[128,8,128]{2,1,0:T(8,128)S(1)}, u32[]{:S(2)}, u32[]{:S(2)}) async-start(f32[128,8,128]{2,1,0:T(8,128)} %bitcast.19), calls=%async_computation.1 | async-start | bytes 1048576 | tf_op jit(solution)/shard_map/all_to_all | solution.py:617
  74.0 1.6 %collective-permute-start.4 = (f32[8,256]{1,0:T(8,128)S(1)}, f32[8,256]{1,0:T(8,128)S(1)}, u32[]{:S(2)}, u32[]{:S(2)}) collective-permute-start(f32[8,256]{1,0:T(8,128)S(1)} %get-tuple-element.68), channel_id=1, source_target_pairs={{0,16},{16,32},{32,48},{48,64},{64,80},{80,96},{96,112},{112,0},{1... | collective-permute-start | bytes 24584 | tf_op jit(solution)/shard_map/ppermute | solution.py:630
  75.7 1.2 collective-permute-start.6
  76.9 4.1 %collective-permute-start.7 = (f32[8,128]{1,0:T(8,128)S(1)}, f32[8,128]{1,0:T(8,128)S(1)}, u32[]{:S(2)}, u32[]{:S(2)}) collective-permute-start(f32[8,128]{1,0:T(8,128)S(1)} %get-tuple-element.71), channel_id=1, source_target_pairs={{1,0},{2,1},{3,2},{4,3},{5,4},{6,5},{7,6},{8,7},{9,8},{10,9},{11,1... | collective-permute-start | bytes 12296 | tf_op jit(solution)/shard_map/ppermute | solution.py:631
  81.0 3.8 %collective-permute-done.6.col_lo = f32[8,128]{1,0:T(8,128)S(1)} collective-permute-done((f32[8,128]{1,0:T(8,128)S(1)}, f32[8,128]{1,0:T(8,128)S(1)}, u32[]{:S(2)}, u32[]{:S(2)}) %collective-permute-start.6) | collective-permute-done | bytes 4128 | tf_op jit(solution)/shard_map/ppermute | solution.py:630
  84.7 1.4 copy-done.1
  86.1 1.2 copy-done.6
  87.4 1.2 copy-done.9
  88.6 1.1 copy-done.16
  90.7 1.4 copy-done.32
  93.2 6.5 %shard_map.141 = (f32[3,8,64,256]{3,2,1,0:T(8,128)}, f32[6,8,64,256]{3,2,1,0:T(8,128)S(1)}, f32[8,64,256]{2,1,0:T(8,128)S(1)}) custom-call(f32[2,3,8,256]{3,2,1,0:T(8,128)S(1)} %get-tuple-element.61.coef_row, f32[3,64,128]{2,1,0:T(8,128)S(1)} %get-tuple-element.62.coef_col, f32[8,256]{1,0:T(8,128)S(1)} %collective-permute-done.4.row_lo, ...), custom_call_target="tpu_custom_call" | custom-call | flops 13107200 | bytes 9150464 | tf_op jit(solution)/shard_map/pallas_call | solution.py:595
  99.7 1.6 copy-done.11
  102.1 1.1 copy-done.40
  103.2 1.1 shard_map.142
  104.3 2.3 %collective-permute-start.8 = (f32[8,256]{1,0:T(8,128)S(1)}, f32[8,256]{1,0:T(8,128)S(1)}, u32[]{:S(2)}, u32[]{:S(2)}) collective-permute-start(f32[8,256]{1,0:T(8,128)S(1)} %get-tuple-element.91), channel_id=1, source_target_pairs={{0,16},{16,32},{32,48},{48,64},{64,80},{80,96},{96,112},{112,0},{1... | collective-permute-start | bytes 24584 | tf_op jit(solution)/shard_map/ppermute | solution.py:630
  106.7 4.8 %collective-permute-start.11 = (f32[8,128]{1,0:T(8,128)S(1)}, f32[8,128]{1,0:T(8,128)S(1)}, u32[]{:S(2)}, u32[]{:S(2)}) collective-permute-start(f32[8,128]{1,0:T(8,128)S(1)} %get-tuple-element.94), channel_id=1, source_target_pairs={{1,0},{2,1},{3,2},{4,3},{5,4},{6,5},{7,6},{8,7},{9,8},{10,9},{11,1... | collective-permute-start | bytes 12296 | tf_op jit(solution)/shard_map/ppermute | solution.py:631
  111.4 1.9 %copy-done.12 = f32[6,8,64,256]{3,2,1,0:T(8,128)S(1)} copy-done((f32[6,8,64,256]{3,2,1,0:T(8,128)S(1)}, f32[6,8,64,256]{3,2,1,0:T(8,128)}, u32[]{:S(2)}) %copy-start.12) | copy-done | bytes 3145752
  113.3 3.5 %shard_map.143 = (f32[2,128,128]{2,1,0:T(8,128)S(1)}, f32[8,128]{1,0:T(8,128)S(1)}, f32[8,64,256]{2,1,0:T(8,128)S(1)}, f32[8,64,256]{2,1,0:T(8,128)S(1)}, f32[6,...) custom-call(s32[256]{0:T(256)S(1)} %copy-done.48, s32[1]{0:T(128)} %bitcast.me, f32[1024,128]{1,0:T(8,128)S(1)} %bitcast.17, ...), custom_call_target="tpu_custom_call" | custom-call | bytes 5260292 | tf_op jit(solution)/shard_map/pallas_call | solution.py:595
  116.9 3.9 %shard_map.144 = (f32[8,256]{1,0:T(8,128)S(1)}, f32[8,256]{1,0:T(8,128)S(1)}, f32[8,128]{1,0:T(8,128)S(1)}, f32[8,128]{1,0:T(8,128)S(1)}, f32[1024,128]{1,0:T(8,128)S(1)}, /*index=5*/f32[8,64,256]{2,1,0:T(8,128)S(1)}) custom-call(s32[256]{0:T(256)S(1)} %copy-done.48, f32[8,256]{1,0:T(8,128)S(1)} %get-tuple-element.56.info, ...), custom_call_target="tpu_custom_call" | custom-call | bytes 5288960 | tf_op jit(solution)/shard_map/pallas_call | solution.py:595
  122.4 7.0 %all-to-all-start.2 = ((f32[128,8,128]{2,1,0:T(8,128)}), f32[128,8,128]{2,1,0:T(8,128)}, u32[]{:S(2)}, u32[]{:S(2)}) async-start(f32[128,8,128]{2,1,0:T(8,128)} %bitcast.18), calls=%async_computation.2 | async-start | bytes 1048576 | tf_op jit(solution)/shard_map/all_to_all | solution.py:617
  129.4 1.7 %collective-permute-start.12 = (f32[8,256]{1,0:T(8,128)S(1)}, f32[8,256]{1,0:T(8,128)S(1)}, u32[]{:S(2)}, u32[]{:S(2)}) collective-permute-start(f32[8,256]{1,0:T(8,128)S(1)} %get-tuple-element.98), channel_id=1, source_target_pairs={{0,16},{16,32},{32,48},{48,64},{64,80},{80,96},{96,112},{112,0},{1... | collective-permute-start | bytes 24584 | tf_op jit(solution)/shard_map/ppermute | solution.py:630
  131.1 1.2 collective-permute-start.14
  132.3 4.2 %collective-permute-start.15 = (f32[8,128]{1,0:T(8,128)S(1)}, f32[8,128]{1,0:T(8,128)S(1)}, u32[]{:S(2)}, u32[]{:S(2)}) collective-permute-start(f32[8,128]{1,0:T(8,128)S(1)} %get-tuple-element.101), channel_id=1, source_target_pairs={{1,0},{2,1},{3,2},{4,3},{5,4},{6,5},{7,6},{8,7},{9,8},{10,9},{11,1... | collective-permute-start | bytes 12296 | tf_op jit(solution)/shard_map/ppermute | solution.py:631
  136.5 3.4 %collective-permute-done.14.col_lo = f32[8,128]{1,0:T(8,128)S(1)} collective-permute-done((f32[8,128]{1,0:T(8,128)S(1)}, f32[8,128]{1,0:T(8,128)S(1)}, u32[]{:S(2)}, u32[]{:S(2)}) %collective-permute-start.14) | collective-permute-done | bytes 4128 | tf_op jit(solution)/shard_map/ppermute | solution.py:630
  139.9 1.4 copy-done.2
  141.3 1.2 copy-done.7
  142.6 1.2 copy-done.10
  143.8 1.1 copy-done.17
  144.9 1.4 copy-done.27
  146.3 1.2 copy-done.34
  148.5 6.6 %shard_map.145 = (f32[3,8,64,256]{3,2,1,0:T(8,128)S(1)}, f32[2,8,64,256]{3,2,1,0:T(8,128)S(1)}) custom-call(f32[2,3,8,256]{3,2,1,0:T(8,128)S(1)} %get-tuple-element.61.coef_row, f32[3,64,128]{2,1,0:T(8,128)S(1)} %get-tuple-element.62.coef_col, f32[8,256]{1,0:T(8,128)S(1)} %collective-permute-done.12.row_lo, f32[8,256]{1,0:T(8,128)S(1)} %collective-permute-done.13.row_hi, ...), custom_call_target="tpu_custom_call" | custom-call | flops 19660800 | bytes 10723328 | tf_op jit(solution)/shard_map/pallas_call | solution.py:595
  155.1 1.1 copy-done.29
  157.2 1.4 copy-done.30
  158.6 1.2 copy-done.36
  159.9 3.9 %shard_map.146 = (f32[3,8,64,256]{3,2,1,0:T(8,128)}, f32[1,16]{1,0:T(1,128)}) custom-call(f32[1024,128]{1,0:T(8,128)} %bitcast.13.got, f32[8,256]{1,0:T(8,128)S(1)} %get-tuple-element.56.info, f32[2,128,128]{2,1,0:T(8,128)S(1)} %get-tuple-element.96.table, f32[8,128]{1,0:T(8,128)S(1)} %get-tuple-element.97.mine, f32[3,8,64,256]{3,2,1,0:T(8,128)S(1)} %copy-done.30, ...), custom_call_target="tpu_custom_call" | custom-call | bytes 3813376 | tf_op jit(solution)/shard_map/pallas_call | solution.py:595
  (105 shorter events, 23.3 us)
Async XLA Ops:
  0.6 1.0 copy-start.3
  1.7 1.1 copy-start.13
  8.2 24.3 %copy-start.4 = (f32[8,64,256]{2,1,0:T(8,128)S(1)}, f32[8,64,256]{2,1,0:T(8,128)}, u32[]{:S(2)}) copy-start(f32[8,64,256]{2,1,0:T(8,128)} %p_h.5) | copy-start | bytes 1572868
  8.2 24.3 %copy-start.18 = (f32[8,64,256]{2,1,0:T(8,128)S(1)}, f32[8,64,256]{2,1,0:T(8,128)}, u32[]{:S(2)}) copy-start(f32[8,64,256]{2,1,0:T(8,128)} %por_h.3) | copy-start | bytes 1572868
  12.7 43.6 %all-to-all-start = ((f32[128,1,128]{2,1,0:T(1,128)}), f32[128,1,128]{2,1,0:T(1,128)S(1)}, u32[]{:S(2)}, u32[]{:S(2)}) async-start(f32[128,1,128]{2,1,0:T(1,128)} %bitcast.7), calls=%async_computation | async-start | bytes 131072 | tf_op jit(solution)/shard_map/all_to_all | solution.py:617
  24.2 8.4 %collective-permute-start = (f32[32,256]{1,0:T(8,128)S(1)}, f32[32,256]{1,0:T(8,128)S(1)}, u32[]{:S(2)}, u32[]{:S(2)}) collective-permute-start(f32[32,256]{1,0:T(8,128)S(1)} %get-tuple-element.57), channel_id=1, source_target_pairs={{0,16},{16,32},{32,48},{48,64},{64,80},{80,96},{96,112},{112,0},{1... | collective-permute-start | bytes 98312 | tf_op jit(solution)/shard_map/ppermute | solution.py:630
  25.9 6.7 %collective-permute-start.1 = (f32[32,256]{1,0:T(8,128)S(1)}, f32[32,256]{1,0:T(8,128)S(1)}, u32[]{:S(2)}, u32[]{:S(2)}) collective-permute-start(f32[32,256]{1,0:T(8,128)S(1)} %get-tuple-element.58), channel_id=1, source_target_pairs={{16,0},{32,16},{48,32},{64,48},{80,64},{96,80},{112,96},{0,112},{1... | collective-permute-start | bytes 98312 | tf_op jit(solution)/shard_map/ppermute | solution.py:631
  25.9 6.7 %collective-permute-start.2 = (f32[32,128]{1,0:T(8,128)S(1)}, f32[32,128]{1,0:T(8,128)S(1)}, u32[]{:S(2)}, u32[]{:S(2)}) collective-permute-start(f32[32,128]{1,0:T(8,128)S(1)} %get-tuple-element.59), channel_id=1, source_target_pairs={{0,1},{1,2},{2,3},{3,4},{4,5},{5,6},{6,7},{7,8},{8,9},{9,10},{10,1... | collective-permute-start | bytes 49160 | tf_op jit(solution)/shard_map/ppermute | solution.py:630
  27.0 5.5 %collective-permute-start.3 = (f32[32,128]{1,0:T(8,128)S(1)}, f32[32,128]{1,0:T(8,128)S(1)}, u32[]{:S(2)}, u32[]{:S(2)}) collective-permute-start(f32[32,128]{1,0:T(8,128)S(1)} %get-tuple-element.60), channel_id=1, source_target_pairs={{1,0},{2,1},{3,2},{4,3},{5,4},{6,5},{7,6},{8,7},{9,8},{10,9},{11,1... | collective-permute-start | bytes 49160 | tf_op jit(solution)/shard_map/ppermute | solution.py:631
  32.6 1.1 copy-start.14
  35.8 1.4 copy-start.28
  37.2 19.1 %copy-start.48 = (s32[256]{0:T(256)S(1)}, s32[256]{0:T(256)}, u32[]{:S(2)}) copy-start(s32[256]{0:T(256)} %cells.7) | copy-start | bytes 3076
  49.4 1.1 copy-start
  53.4 1.1 copy-start.31
  56.3 1.0 copy-start.42
  63.9 38.2 %all-to-all-start.1 = ((f32[128,8,128]{2,1,0:T(8,128)}), f32[128,8,128]{2,1,0:T(8,128)S(1)}, u32[]{:S(2)}, u32[]{:S(2)}) async-start(f32[128,8,128]{2,1,0:T(8,128)} %bitcast.19), calls=%async_computation.1 | async-start | bytes 1048576 | tf_op jit(solution)/shard_map/all_to_all | solution.py:617
  74.0 10.7 %collective-permute-start.4 = (f32[8,256]{1,0:T(8,128)S(1)}, f32[8,256]{1,0:T(8,128)S(1)}, u32[]{:S(2)}, u32[]{:S(2)}) collective-permute-start(f32[8,256]{1,0:T(8,128)S(1)} %get-tuple-element.68), channel_id=1, source_target_pairs={{0,16},{16,32},{32,48},{48,64},{64,80},{80,96},{96,112},{112,0},{1... | collective-permute-start | bytes 24584 | tf_op jit(solution)/shard_map/ppermute | solution.py:630
  75.7 9.1 %collective-permute-start.5 = (f32[8,256]{1,0:T(8,128)S(1)}, f32[8,256]{1,0:T(8,128)S(1)}, u32[]{:S(2)}, u32[]{:S(2)}) collective-permute-start(f32[8,256]{1,0:T(8,128)S(1)} %get-tuple-element.69), channel_id=1, source_target_pairs={{16,0},{32,16},{48,32},{64,48},{80,64},{96,80},{112,96},{0,112},{1... | collective-permute-start | bytes 24584 | tf_op jit(solution)/shard_map/ppermute | solution.py:631
  75.7 9.0 %collective-permute-start.6 = (f32[8,128]{1,0:T(8,128)S(1)}, f32[8,128]{1,0:T(8,128)S(1)}, u32[]{:S(2)}, u32[]{:S(2)}) collective-permute-start(f32[8,128]{1,0:T(8,128)S(1)} %get-tuple-element.70), channel_id=1, source_target_pairs={{0,1},{1,2},{2,3},{3,4},{4,5},{5,6},{6,7},{7,8},{8,9},{9,10},{10,1... | collective-permute-start | bytes 12296 | tf_op jit(solution)/shard_map/ppermute | solution.py:630
  76.9 7.9 %collective-permute-start.7 = (f32[8,128]{1,0:T(8,128)S(1)}, f32[8,128]{1,0:T(8,128)S(1)}, u32[]{:S(2)}, u32[]{:S(2)}) collective-permute-start(f32[8,128]{1,0:T(8,128)S(1)} %get-tuple-element.71), channel_id=1, source_target_pairs={{1,0},{2,1},{3,2},{4,3},{5,4},{6,5},{7,6},{8,7},{9,8},{10,9},{11,1... | collective-permute-start | bytes 12296 | tf_op jit(solution)/shard_map/ppermute | solution.py:631
  84.7 1.4 copy-start.1
  86.1 1.2 copy-start.6
  87.4 1.2 copy-start.9
  88.6 1.1 copy-start.16
  90.7 1.4 copy-start.32
  99.7 1.6 %copy-start.11 = (f32[6,8,64,256]{3,2,1,0:T(8,128)}, f32[6,8,64,256]{3,2,1,0:T(8,128)S(1)}, u32[]{:S(2)}) copy-start(f32[6,8,64,256]{3,2,1,0:T(8,128)S(1)} %get-tuple-element.85.gain_h) | copy-start | bytes 9437188
  102.1 9.3 %copy-start.26 = (f32[8,64,256]{2,1,0:T(8,128)S(1)}, f32[8,64,256]{2,1,0:T(8,128)}, u32[]{:S(2)}) copy-start(f32[8,64,256]{2,1,0:T(8,128)} %copy-done.24) | copy-start | bytes 1572868
  102.1 1.1 copy-start.40
  104.3 12.5 %collective-permute-start.8 = (f32[8,256]{1,0:T(8,128)S(1)}, f32[8,256]{1,0:T(8,128)S(1)}, u32[]{:S(2)}, u32[]{:S(2)}) collective-permute-start(f32[8,256]{1,0:T(8,128)S(1)} %get-tuple-element.91), channel_id=1, source_target_pairs={{0,16},{16,32},{32,48},{48,64},{64,80},{80,96},{96,112},{112,0},{1... | collective-permute-start | bytes 24584 | tf_op jit(solution)/shard_map/ppermute | solution.py:630
  106.6 10.2 %collective-permute-start.9 = (f32[8,256]{1,0:T(8,128)S(1)}, f32[8,256]{1,0:T(8,128)S(1)}, u32[]{:S(2)}, u32[]{:S(2)}) collective-permute-start(f32[8,256]{1,0:T(8,128)S(1)} %get-tuple-element.92), channel_id=1, source_target_pairs={{16,0},{32,16},{48,32},{64,48},{80,64},{96,80},{112,96},{0,112},{1... | collective-permute-start | bytes 24584 | tf_op jit(solution)/shard_map/ppermute | solution.py:631
  106.6 10.2 %collective-permute-start.10 = (f32[8,128]{1,0:T(8,128)S(1)}, f32[8,128]{1,0:T(8,128)S(1)}, u32[]{:S(2)}, u32[]{:S(2)}) collective-permute-start(f32[8,128]{1,0:T(8,128)S(1)} %get-tuple-element.93), channel_id=1, source_target_pairs={{0,1},{1,2},{2,3},{3,4},{4,5},{5,6},{6,7},{7,8},{8,9},{9,10},{10,1... | collective-permute-start | bytes 12296 | tf_op jit(solution)/shard_map/ppermute | solution.py:630
  106.7 10.2 %collective-permute-start.11 = (f32[8,128]{1,0:T(8,128)S(1)}, f32[8,128]{1,0:T(8,128)S(1)}, u32[]{:S(2)}, u32[]{:S(2)}) collective-permute-start(f32[8,128]{1,0:T(8,128)S(1)} %get-tuple-element.94), channel_id=1, source_target_pairs={{1,0},{2,1},{3,2},{4,3},{5,4},{6,5},{7,6},{8,7},{9,8},{10,9},{11,1... | collective-permute-start | bytes 12296 | tf_op jit(solution)/shard_map/ppermute | solution.py:631
  111.4 1.9 %copy-start.12 = (f32[6,8,64,256]{3,2,1,0:T(8,128)S(1)}, f32[6,8,64,256]{3,2,1,0:T(8,128)}, u32[]{:S(2)}) copy-start(f32[6,8,64,256]{3,2,1,0:T(8,128)} %copy-done.11) | copy-start | bytes 9437188
  116.9 23.0 %copy-start.19 = (f32[8,64,256]{2,1,0:T(8,128)S(1)}, f32[8,64,256]{2,1,0:T(8,128)}, u32[]{:S(2)}) copy-start(f32[8,64,256]{2,1,0:T(8,128)} %por_h.3) | copy-start | bytes 1572868
  122.4 34.8 %all-to-all-start.2 = ((f32[128,8,128]{2,1,0:T(8,128)}), f32[128,8,128]{2,1,0:T(8,128)}, u32[]{:S(2)}, u32[]{:S(2)}) async-start(f32[128,8,128]{2,1,0:T(8,128)} %bitcast.18), calls=%async_computation.2 | async-start | bytes 1048576 | tf_op jit(solution)/shard_map/all_to_all | solution.py:617
  129.4 10.5 %collective-permute-start.12 = (f32[8,256]{1,0:T(8,128)S(1)}, f32[8,256]{1,0:T(8,128)S(1)}, u32[]{:S(2)}, u32[]{:S(2)}) collective-permute-start(f32[8,256]{1,0:T(8,128)S(1)} %get-tuple-element.98), channel_id=1, source_target_pairs={{0,16},{16,32},{32,48},{48,64},{64,80},{80,96},{96,112},{112,0},{1... | collective-permute-start | bytes 24584 | tf_op jit(solution)/shard_map/ppermute | solution.py:630
  131.1 8.8 %collective-permute-start.13 = (f32[8,256]{1,0:T(8,128)S(1)}, f32[8,256]{1,0:T(8,128)S(1)}, u32[]{:S(2)}, u32[]{:S(2)}) collective-permute-start(f32[8,256]{1,0:T(8,128)S(1)} %get-tuple-element.99), channel_id=1, source_target_pairs={{16,0},{32,16},{48,32},{64,48},{80,64},{96,80},{112,96},{0,112},{1... | collective-permute-start | bytes 24584 | tf_op jit(solution)/shard_map/ppermute | solution.py:631
  131.1 8.8 %collective-permute-start.14 = (f32[8,128]{1,0:T(8,128)S(1)}, f32[8,128]{1,0:T(8,128)S(1)}, u32[]{:S(2)}, u32[]{:S(2)}) collective-permute-start(f32[8,128]{1,0:T(8,128)S(1)} %get-tuple-element.100), channel_id=1, source_target_pairs={{0,1},{1,2},{2,3},{3,4},{4,5},{5,6},{6,7},{7,8},{8,9},{9,10},{10,1... | collective-permute-start | bytes 12296 | tf_op jit(solution)/shard_map/ppermute | solution.py:630
  132.3 7.6 %collective-permute-start.15 = (f32[8,128]{1,0:T(8,128)S(1)}, f32[8,128]{1,0:T(8,128)S(1)}, u32[]{:S(2)}, u32[]{:S(2)}) collective-permute-start(f32[8,128]{1,0:T(8,128)S(1)} %get-tuple-element.101), channel_id=1, source_target_pairs={{1,0},{2,1},{3,2},{4,3},{5,4},{6,5},{7,6},{8,7},{9,8},{10,9},{11,1... | collective-permute-start | bytes 12296 | tf_op jit(solution)/shard_map/ppermute | solution.py:631
  139.9 1.4 copy-start.2
  141.3 1.2 copy-start.7
  142.6 1.2 copy-start.10
  143.8 1.1 copy-start.17
  144.9 1.4 copy-start.27
  146.3 1.2 copy-start.34
  155.1 1.1 copy-start.29
  157.2 1.4 copy-start.30
  158.6 1.2 copy-start.36
  (24 other events, 21.1 us)

commit v3 on v2

--- a/solution.py
+++ b/solution.py
@@ -74,7 +74,7 @@
     def body(block, carry):
         for u in range(8):
             k = block * 8 + u
-            cell = cells[k]
+            cell = cells[0, k]
             layer = cell >> 14
             line = (cell >> 8) & (R - 1)
             for n, ref in enumerate(refs):
@@ -199,13 +199,19 @@
 
 
 def start_kernel(
-    cells, cell_in, well_in, index_in, pressure_in, rate_in, p_h, sw_h, sg_h, perm_h,
+    cell_h, well_h, index_h, pressure_h, rate_h, p_h, sw_h, sg_h, perm_h,
     row_lo, row_hi, col_lo, col_hi, pay, perf, info, own,
-    p, sw, sg, perm, rows, sems,
+    cells, cell_in, well_in, index_in, pressure_in, rate_in, p, sw, sg, perm, rows, sems,
 ):
     copies = start_copies(
-        ((p_h, p), (sw_h, sw), (sg_h, sg), (perm_h.at[0:2], perm)), sems
-    )
+        (
+            (cell_h, cells), (cell_h, cell_in), (well_h, well_in), (index_h, index_in),
+            (pressure_h, pressure_in), (rate_h, rate_in),
+            (p_h, p), (sw_h, sw), (sg_h, sg), (perm_h.at[0:2], perm),
+        ),
+        sems,
+    )
+    wait_copies(copies[:6])
     cell_row = cell_in[...]
     well_row = well_in[...]
     index_row = index_in[...]
@@ -219,7 +225,7 @@
     column = to_column(cell_float).astype(i32) & (C - 1)
     slot_column = to_column(well_float).astype(i32) & 15
     index_column = to_column(index_row)
-    wait_copies(copies)
+    wait_copies(copies[6:])
     lane = iota((R, LANES), 1)
     columns = jnp.zeros((R, LANES), f32)
     for l in range(L):
@@ -590,8 +596,14 @@
 
 
 def call(kernel, outs, ins, operands, scratch=(), flops=0):
-    shapes = tuple(pltpu.VMEM(s, f32) if w is VM else jax.ShapeDtypeStruct(s, f32) for s, w in outs)
+    shapes = tuple(
+        pltpu.VMEM(s, f32) if w is VM else pltpu.HBM(s, f32) if w is HB else jax.ShapeDtypeStruct(s, f32)
+        for s, w in outs
+    )
     moved = 4 * sum(int(x.size) for x in operands)
+    operands = [
+        pltpu.with_memory_space_constraint(x, pltpu.HBM) if w is HB else x for x, w in zip(operands, ins)
+    ]
     return pl.pallas_call(
         kernel,
         out_shape=shapes,
@@ -637,15 +649,19 @@
     perf_well, perf_cell, perf_index, well_pressure, well_rate,
 ):
     me = (lax.axis_index("gx") * lax.axis_size("gy") + lax.axis_index("gy")).astype(i32).reshape(1)
+    cells = perf_cell.reshape(1, PERFS)
     *faces, pay, perf, info, own = call(
         start_kernel,
         WIDE_FACES + (((DEVICES, LANES), None), ((8, PERFS), VM), ((8, PERFS), VM), (SMALL, VM)),
-        [SM] + [VM] * 5 + [HB] * 4,
+        [HB] * 9,
         (
-            perf_cell, perf_cell.reshape(1, PERFS), perf_well.reshape(1, PERFS), perf_index.reshape(1, PERFS),
+            cells, perf_well.reshape(1, PERFS), perf_index.reshape(1, PERFS),
             well_pressure.reshape(1, WELL_DEV), well_rate.reshape(1, WELL_DEV), pressure, sat_water, sat_gas, perm,
         ),
-        [FIELD, FIELD, FIELD, pltpu.VMEM(TWO, bf16), (3, PERFS, C), sem((4,))],
+        [
+            pltpu.SMEM((1, PERFS), i32), pltpu.VMEM((1, PERFS), i32), pltpu.VMEM((1, PERFS), i32), (1, PERFS),
+            (1, WELL_DEV), (1, WELL_DEV), FIELD, FIELD, FIELD, pltpu.VMEM(TWO, bf16), (3, PERFS, C), sem((10,)),
+        ],
     )
     halo = halo_of(faces)
     got = exchange(pay)
@@ -667,7 +683,7 @@
         first_kernel,
         FACES + (PAY, (SMALL, VM), ((1, WELL_DEV), None), (FIELD, HB), (FIELD, HB)),
         [SM, SM] + [VM] * 4 + [HB] * 2,
-        (perf_cell, me, got, info, own, perf, base, head),
+        (cells, me, got, info, own, perf, base, head),
         [FIELD, FIELD, FIELD, FIELD, ROWS, sem((2,))],
     )
     halo = halo_of(faces)
@@ -696,14 +712,14 @@
         wells_kernel,
         (((2, DEVICES, LANES), None), (SMALL, VM), (FIELD, VM), (FIELD, VM), (SIX, VM), (FIELD, VM)),
         [SM, SM] + [VM] * 4 + [HB] * 3,
-        (perf_cell, me, got, info, perf, step, start, gain, head),
+        (cells, me, got, info, perf, step, start, gain, head),
         [ROWS, sem((3,))],
     )
     *faces, pay, step = call(
         third_kernel,
         FACES + (PAY, (FIELD, HB)),
         [SM] + [VM] * 12,
-        (perf_cell, info, perf, parts, spread, step, base, gain_near, head_near, *halo),
+        (cells, info, perf, parts, spread, step, base, gain_near, head_near, *halo),
         [FIELD, ROWS, sem((1,))],
     )
     halo = halo_of(faces)

time: 165 us -> 120 us (0.73)
  local copies, waits for them, and re-layouts: 51.4 us -> 0.01 us
  Pallas kernels: 46.1 us -> 51.9 us
    unnamed x106 -> x2, local copies, waits for them, and re-layouts: 51.4 us -> 0.01 us
    pallas_call x9, Pallas kernels: 46.1 us -> 51.9 us  [call(): pl.pallas_call(kernel, out_shape=shapes, in_specs=ins, out_specs=tuple((w...]
  transfers between devices with their start and end apart: 19 -> 19, of which waited for: 3 -> 3; matrix products, arithmetic and copies ran while one was open for 0% -> 0% of each run, Pallas kernels for 18% -> 26%
where the time goes in v3:
time: 120 us
  starting transfers between devices  57.8 us (48%)
  Pallas kernels  51.9 us (43%)
  waiting for transfers between devices  8.97 us (7%)
    pallas_call x9, Pallas kernels, call(): pl.pallas_call(kernel, out_shape=shapes, in_specs=ins, out_specs=tuple((w...  51.9 us
    all_to_all x3, starting transfers between devices, exchange(): return lax.all_to_all(array, AXES, split_axis=0, concat_axis=0, tiled=True)  29.9 us
    ppermute x8, starting transfers between devices, halo_of(): got.append(lax.ppermute(low, axis, [(j, i) for i, j in up]))  17.1 us
    ppermute x8, starting transfers between devices, halo_of(): got.append(lax.ppermute(high, axis, up))  10.8 us
    ppermute x8, waiting for transfers between devices, halo_of(): got.append(lax.ppermute(high, axis, up))  8.94 us
  transfers between devices with their start and end apart: 19, of which 3 were waited for; matrix products, arithmetic and copies ran while one was open for 0% of the time, Pallas kernels for 26%

profile of v3, /device:TPU:1, one launch (start us, length us, event | category | flops | bytes accessed | tf_op | source)
XLA Modules:
  0.0 119.5 jit_solution(3946102812393633836)
XLA Ops:
  0.6 5.2 %shard_map.138 = (f32[32,256]{1,0:T(8,128)S(1)}, f32[32,256]{1,0:T(8,128)S(1)}, f32[32,128]{1,0:T(8,128)S(1)}, f32[32,128]{1,0:T(8,128)S(1)}, f32[128,128]{1,0:T...) custom-call(s32[1,256]{1,0:T(1,128)} %bitcast.20, s32[1,256]{1,0:T(1,128)} %bitcast.24, ...), custom_call_target="tpu_custom_call" | custom-call | bytes 3148928 | tf_op jit(solution)/shard_map/pallas_call | solution.py:607
  5.9 11.5 %all-to-all-start = ((f32[128,1,128]{2,1,0:T(1,128)}), f32[128,1,128]{2,1,0:T(1,128)S(1)}, u32[]{:S(2)}, u32[]{:S(2)}) async-start(f32[128,1,128]{2,1,0:T(1,128)} %bitcast.7), calls=%async_computation | async-start | bytes 131072 | tf_op jit(solution)/shard_map/all_to_all | solution.py:629
  17.4 1.6 %collective-permute-start = (f32[32,256]{1,0:T(8,128)S(1)}, f32[32,256]{1,0:T(8,128)S(1)}, u32[]{:S(2)}, u32[]{:S(2)}) collective-permute-start(f32[32,256]{1,0:T(8,128)S(1)} %get-tuple-element.57), channel_id=1, source_target_pairs={{0,16},{16,32},{32,48},{48,64},{64,80},{80,96},{96,112},{112,0},{1... | collective-permute-start | bytes 98312 | tf_op jit(solution)/shard_map/ppermute | solution.py:642
  19.0 0.0 collective-permute-start.1
  19.0 1.2 collective-permute-start.2
  20.2 4.1 %collective-permute-start.3 = (f32[32,128]{1,0:T(8,128)S(1)}, f32[32,128]{1,0:T(8,128)S(1)}, u32[]{:S(2)}, u32[]{:S(2)}) collective-permute-start(f32[32,128]{1,0:T(8,128)S(1)} %get-tuple-element.60), channel_id=1, source_target_pairs={{1,0},{2,1},{3,2},{4,3},{5,4},{6,5},{7,6},{8,7},{9,8},{10,9},{11,1... | collective-permute-start | bytes 49160 | tf_op jit(solution)/shard_map/ppermute | solution.py:643
  24.3 1.4 %collective-permute-done.2.col_lo = f32[32,128]{1,0:T(8,128)S(1)} collective-permute-done((f32[32,128]{1,0:T(8,128)S(1)}, f32[32,128]{1,0:T(8,128)S(1)}, u32[]{:S(2)}, u32[]{:S(2)}) %collective-permute-start.2) | collective-permute-done | bytes 16416 | tf_op jit(solution)/shard_map/ppermute | solution.py:642
  25.7 0.0 collective-permute-done.3.col_hi
  25.7 0.0 collective-permute-done.row_lo
  25.7 0.0 collective-permute-done.1.row_hi
  25.7 0.0 copy-start
  25.8 10.2 %shard_map.139 = (f32[2,3,8,256]{3,2,1,0:T(8,128)S(1)}, f32[3,64,128]{2,1,0:T(8,128)S(1)}, f32[3,8,64,256]{3,2,1,0:T(8,128)}, f32[2,8,64,256]{3,2,1,0:T(8,128)},...) custom-call(s32[1]{0:T(128)} %bitcast.me, ...), custom_call_target="tpu_custom_call" | custom-call | flops 52428800 | bytes 5349380 | tf_op jit(solution)/shard_map/pallas_call | solution.py:607
  35.9 0.0 all-to-all-done
  35.9 5.1 %shard_map.140 = (f32[8,256]{1,0:T(8,128)S(1)}, f32[8,256]{1,0:T(8,128)S(1)}, f32[8,128]{1,0:T(8,128)S(1)}, f32[8,128]{1,0:T(8,128)S(1)}, f32[1024,128]{1,0:T(8,...) custom-call(s32[1,256]{1,0:T(1,128)S(1)} %bitcast.21, ...), custom_call_target="tpu_custom_call" | custom-call | bytes 1135620 | tf_op jit(solution)/shard_map/pallas_call | solution.py:607
  41.1 10.1 %all-to-all-start.1 = ((f32[128,8,128]{2,1,0:T(8,128)}), f32[128,8,128]{2,1,0:T(8,128)S(1)}, u32[]{:S(2)}, u32[]{:S(2)}) async-start(f32[128,8,128]{2,1,0:T(8,128)} %bitcast.10), calls=%async_computation.1 | async-start | bytes 1048576 | tf_op jit(solution)/shard_map/all_to_all | solution.py:629
  51.2 1.6 %collective-permute-start.4 = (f32[8,256]{1,0:T(8,128)S(1)}, f32[8,256]{1,0:T(8,128)S(1)}, u32[]{:S(2)}, u32[]{:S(2)}) collective-permute-start(f32[8,256]{1,0:T(8,128)S(1)} %get-tuple-element.68), channel_id=1, source_target_pairs={{0,16},{16,32},{32,48},{48,64},{64,80},{80,96},{96,112},{112,0},{1... | collective-permute-start | bytes 24584 | tf_op jit(solution)/shard_map/ppermute | solution.py:642
  52.8 0.0 collective-permute-start.5
  52.8 1.2 collective-permute-start.6
  54.0 4.1 %collective-permute-start.7 = (f32[8,128]{1,0:T(8,128)S(1)}, f32[8,128]{1,0:T(8,128)S(1)}, u32[]{:S(2)}, u32[]{:S(2)}) collective-permute-start(f32[8,128]{1,0:T(8,128)S(1)} %get-tuple-element.71), channel_id=1, source_target_pairs={{1,0},{2,1},{3,2},{4,3},{5,4},{6,5},{7,6},{8,7},{9,8},{10,9},{11,1... | collective-permute-start | bytes 12296 | tf_op jit(solution)/shard_map/ppermute | solution.py:643
  58.1 3.8 %collective-permute-done.6.col_lo = f32[8,128]{1,0:T(8,128)S(1)} collective-permute-done((f32[8,128]{1,0:T(8,128)S(1)}, f32[8,128]{1,0:T(8,128)S(1)}, u32[]{:S(2)}, u32[]{:S(2)}) %collective-permute-start.6) | collective-permute-done | bytes 4128 | tf_op jit(solution)/shard_map/ppermute | solution.py:642
  61.9 0.0 collective-permute-done.7.col_hi
  61.9 0.0 collective-permute-done.4.row_lo
  61.9 0.0 collective-permute-done.5.row_hi
  61.9 8.6 %shard_map.141 = (f32[3,8,64,256]{3,2,1,0:T(8,128)}, f32[6,8,64,256]{3,2,1,0:T(8,128)}, f32[8,64,256]{2,1,0:T(8,128)}) custom-call(f32[2,3,8,256]{3,2,1,0:T(8,128)S(1)} %get-tuple-element.61.coef_row, f32[3,64,128]{2,1,0:T(8,128)S(1)} %get-tuple-element.62.coef_col, f32[8,256]{1,0:T(8,128)S(1)} %collective-permute-done.4.row_lo, ...), custom_call_target="tpu_custom_call" | custom-call | flops 13107200 | bytes 9150464 | tf_op jit(solution)/shard_map/pallas_call | solution.py:607
  70.5 0.0 all-to-all-done.1
  70.5 1.8 %shard_map.142 = (f32[8,256]{1,0:T(8,128)S(1)}, f32[8,256]{1,0:T(8,128)S(1)}, f32[8,128]{1,0:T(8,128)S(1)}, f32[8,128]{1,0:T(8,128)S(1)}, f32[8,64,256]{2,1,0:T(8,128)S(1)}) custom-call(f32[1024,128]{1,0:T(8,128)S(1)} %bitcast.16, f32[8,256]{1,0:T(8,128)S(1)} %get-tuple-element.56.info, f32[8,64,256]{2,1,0:T(8,128)} %get-tuple-element.83.ahead_h, ...), custom_call_target="tpu_custom_call" | custom-call | bytes 1581056 | tf_op jit(solution)/shard_map/pallas_call | solution.py:607
  72.3 2.3 %collective-permute-start.8 = (f32[8,256]{1,0:T(8,128)S(1)}, f32[8,256]{1,0:T(8,128)S(1)}, u32[]{:S(2)}, u32[]{:S(2)}) collective-permute-start(f32[8,256]{1,0:T(8,128)S(1)} %get-tuple-element.91), channel_id=1, source_target_pairs={{0,16},{16,32},{32,48},{48,64},{64,80},{80,96},{96,112},{112,0},{1... | collective-permute-start | bytes 24584 | tf_op jit(solution)/shard_map/ppermute | solution.py:642
  74.7 0.0 collective-permute-start.9
  74.7 0.0 collective-permute-start.10
  74.7 4.8 %collective-permute-start.11 = (f32[8,128]{1,0:T(8,128)S(1)}, f32[8,128]{1,0:T(8,128)S(1)}, u32[]{:S(2)}, u32[]{:S(2)}) collective-permute-start(f32[8,128]{1,0:T(8,128)S(1)} %get-tuple-element.94), channel_id=1, source_target_pairs={{1,0},{2,1},{3,2},{4,3},{5,4},{6,5},{7,6},{8,7},{9,8},{10,9},{11,1... | collective-permute-start | bytes 12296 | tf_op jit(solution)/shard_map/ppermute | solution.py:643
  79.5 3.2 %shard_map.143 = (f32[2,128,128]{2,1,0:T(8,128)S(1)}, f32[8,128]{1,0:T(8,128)S(1)}, f32[8,64,256]{2,1,0:T(8,128)S(1)}, f32[8,64,256]{2,1,0:T(8,128)S(1)}, f32[6,...) custom-call(s32[1,256]{1,0:T(1,128)S(1)} %bitcast.22, s32[1]{0:T(128)} %bitcast.me, f32[1024,128]{1,0:T(8,128)S(1)} %bitcast.17, ...), custom_call_target="tpu_custom_call" | custom-call | bytes 5260292 | tf_op jit(solution)/shard_map/pallas_call | solution.py:607
  82.7 0.0 collective-permute-done.10.col_lo
  82.7 0.0 collective-permute-done.11.col_hi
  82.7 0.0 collective-permute-done.8.row_lo
  82.7 0.0 collective-permute-done.9.row_hi
  82.7 4.7 %shard_map.144 = (f32[8,256]{1,0:T(8,128)S(1)}, f32[8,256]{1,0:T(8,128)S(1)}, f32[8,128]{1,0:T(8,128)S(1)}, f32[8,128]{1,0:T(8,128)S(1)}, f32[1024,128]{1,0:T(8,128)}, /*index=5*/f32[8,64,256]{2,1,0:T(8,128)}) custom-call(s32[1,256]{1,0:T(1,128)S(1)} %bitcast.23, f32[8,256]{1,0:T(8,128)S(1)} %get-tuple-element.56.info, f32[8,256]{1,0:T(8,128)S(1)} %get-tuple-element.65.perf, ...), custom_call_target="tpu_custom_call" | custom-call | bytes 5288960 | tf_op jit(solution)/shard_map/pallas_call | solution.py:607
  87.4 8.3 %all-to-all-start.2 = ((f32[128,8,128]{2,1,0:T(8,128)}), f32[128,8,128]{2,1,0:T(8,128)S(1)}, u32[]{:S(2)}, u32[]{:S(2)}) async-start(f32[128,8,128]{2,1,0:T(8,128)} %bitcast.12), calls=%async_computation.2 | async-start | bytes 1048576 | tf_op jit(solution)/shard_map/all_to_all | solution.py:629
  95.7 1.6 %collective-permute-start.12 = (f32[8,256]{1,0:T(8,128)S(1)}, f32[8,256]{1,0:T(8,128)S(1)}, u32[]{:S(2)}, u32[]{:S(2)}) collective-permute-start(f32[8,256]{1,0:T(8,128)S(1)} %get-tuple-element.98), channel_id=1, source_target_pairs={{0,16},{16,32},{32,48},{48,64},{64,80},{80,96},{96,112},{112,0},{1... | collective-permute-start | bytes 24584 | tf_op jit(solution)/shard_map/ppermute | solution.py:642
  97.3 0.0 collective-permute-start.13
  97.3 1.2 collective-permute-start.14
  98.5 4.1 %collective-permute-start.15 = (f32[8,128]{1,0:T(8,128)S(1)}, f32[8,128]{1,0:T(8,128)S(1)}, u32[]{:S(2)}, u32[]{:S(2)}) collective-permute-start(f32[8,128]{1,0:T(8,128)S(1)} %get-tuple-element.101), channel_id=1, source_target_pairs={{1,0},{2,1},{3,2},{4,3},{5,4},{6,5},{7,6},{8,7},{9,8},{10,9},{11,1... | collective-permute-start | bytes 12296 | tf_op jit(solution)/shard_map/ppermute | solution.py:643
  102.6 3.8 %collective-permute-done.14.col_lo = f32[8,128]{1,0:T(8,128)S(1)} collective-permute-done((f32[8,128]{1,0:T(8,128)S(1)}, f32[8,128]{1,0:T(8,128)S(1)}, u32[]{:S(2)}, u32[]{:S(2)}) %collective-permute-start.14) | collective-permute-done | bytes 4128 | tf_op jit(solution)/shard_map/ppermute | solution.py:642
  106.4 0.0 collective-permute-done.15.col_hi
  106.4 0.0 collective-permute-done.12.row_lo
  106.4 0.0 collective-permute-done.13.row_hi
  106.4 9.0 %shard_map.145 = (f32[3,8,64,256]{3,2,1,0:T(8,128)}, f32[2,8,64,256]{3,2,1,0:T(8,128)}) custom-call(f32[2,3,8,256]{3,2,1,0:T(8,128)S(1)} %get-tuple-element.61.coef_row, f32[3,64,128]{2,1,0:T(8,128)S(1)} %get-tuple-element.62.coef_col, f32[8,256]{1,0:T(8,128)S(1)} %collective-permute-done.12.row_lo, f32[8,256]{1,0:T(8,128)S(1)} %collective-permute-done.13.row_hi, ...), custom_call_target="tpu_custom_call" | custom-call | flops 19660800 | bytes 10723328 | tf_op jit(solution)/shard_map/pallas_call | solution.py:607
  115.4 0.0 all-to-all-done.2
  115.4 4.1 %shard_map.146 = (f32[3,8,64,256]{3,2,1,0:T(8,128)}, f32[1,16]{1,0:T(1,128)}) custom-call(f32[1024,128]{1,0:T(8,128)S(1)} %bitcast.18, f32[8,256]{1,0:T(8,128)S(1)} %get-tuple-element.56.info, f32[2,128,128]{2,1,0:T(8,128)S(1)} %get-tuple-element.96.table, f32[8,128]{1,0:T(8,128)S(1)} %get-tuple-element.97.mine, ...), custom_call_target="tpu_custom_call" | custom-call | bytes 3813376 | tf_op jit(solution)/shard_map/pallas_call | solution.py:607
  (1 shorter events, 0.0 us)
Async XLA Ops:
  5.9 30.1 %all-to-all-start = ((f32[128,1,128]{2,1,0:T(1,128)}), f32[128,1,128]{2,1,0:T(1,128)S(1)}, u32[]{:S(2)}, u32[]{:S(2)}) async-start(f32[128,1,128]{2,1,0:T(1,128)} %bitcast.7), calls=%async_computation | async-start | bytes 131072 | tf_op jit(solution)/shard_map/all_to_all | solution.py:629
  17.4 8.4 %collective-permute-start = (f32[32,256]{1,0:T(8,128)S(1)}, f32[32,256]{1,0:T(8,128)S(1)}, u32[]{:S(2)}, u32[]{:S(2)}) collective-permute-start(f32[32,256]{1,0:T(8,128)S(1)} %get-tuple-element.57), channel_id=1, source_target_pairs={{0,16},{16,32},{32,48},{48,64},{64,80},{80,96},{96,112},{112,0},{1... | collective-permute-start | bytes 98312 | tf_op jit(solution)/shard_map/ppermute | solution.py:642
  19.0 6.7 %collective-permute-start.1 = (f32[32,256]{1,0:T(8,128)S(1)}, f32[32,256]{1,0:T(8,128)S(1)}, u32[]{:S(2)}, u32[]{:S(2)}) collective-permute-start(f32[32,256]{1,0:T(8,128)S(1)} %get-tuple-element.58), channel_id=1, source_target_pairs={{16,0},{32,16},{48,32},{64,48},{80,64},{96,80},{112,96},{0,112},{1... | collective-permute-start | bytes 98312 | tf_op jit(solution)/shard_map/ppermute | solution.py:643
  19.0 6.7 %collective-permute-start.2 = (f32[32,128]{1,0:T(8,128)S(1)}, f32[32,128]{1,0:T(8,128)S(1)}, u32[]{:S(2)}, u32[]{:S(2)}) collective-permute-start(f32[32,128]{1,0:T(8,128)S(1)} %get-tuple-element.59), channel_id=1, source_target_pairs={{0,1},{1,2},{2,3},{3,4},{4,5},{5,6},{6,7},{7,8},{8,9},{9,10},{10,1... | collective-permute-start | bytes 49160 | tf_op jit(solution)/shard_map/ppermute | solution.py:642
  20.2 5.5 %collective-permute-start.3 = (f32[32,128]{1,0:T(8,128)S(1)}, f32[32,128]{1,0:T(8,128)S(1)}, u32[]{:S(2)}, u32[]{:S(2)}) collective-permute-start(f32[32,128]{1,0:T(8,128)S(1)} %get-tuple-element.60), channel_id=1, source_target_pairs={{1,0},{2,1},{3,2},{4,3},{5,4},{6,5},{7,6},{8,7},{9,8},{10,9},{11,1... | collective-permute-start | bytes 49160 | tf_op jit(solution)/shard_map/ppermute | solution.py:643
  25.7 10.2 %copy-start = (s32[256]{0:T(256)S(1)}, s32[256]{0:T(256)}, u32[]{:S(2)}) copy-start(s32[256]{0:T(256)} %param.18) | copy-start | bytes 3076
  41.1 29.5 %all-to-all-start.1 = ((f32[128,8,128]{2,1,0:T(8,128)}), f32[128,8,128]{2,1,0:T(8,128)S(1)}, u32[]{:S(2)}, u32[]{:S(2)}) async-start(f32[128,8,128]{2,1,0:T(8,128)} %bitcast.10), calls=%async_computation.1 | async-start | bytes 1048576 | tf_op jit(solution)/shard_map/all_to_all | solution.py:629
  51.2 10.7 %collective-permute-start.4 = (f32[8,256]{1,0:T(8,128)S(1)}, f32[8,256]{1,0:T(8,128)S(1)}, u32[]{:S(2)}, u32[]{:S(2)}) collective-permute-start(f32[8,256]{1,0:T(8,128)S(1)} %get-tuple-element.68), channel_id=1, source_target_pairs={{0,16},{16,32},{32,48},{48,64},{64,80},{80,96},{96,112},{112,0},{1... | collective-permute-start | bytes 24584 | tf_op jit(solution)/shard_map/ppermute | solution.py:642
  52.8 9.1 %collective-permute-start.5 = (f32[8,256]{1,0:T(8,128)S(1)}, f32[8,256]{1,0:T(8,128)S(1)}, u32[]{:S(2)}, u32[]{:S(2)}) collective-permute-start(f32[8,256]{1,0:T(8,128)S(1)} %get-tuple-element.69), channel_id=1, source_target_pairs={{16,0},{32,16},{48,32},{64,48},{80,64},{96,80},{112,96},{0,112},{1... | collective-permute-start | bytes 24584 | tf_op jit(solution)/shard_map/ppermute | solution.py:643
  52.8 9.0 %collective-permute-start.6 = (f32[8,128]{1,0:T(8,128)S(1)}, f32[8,128]{1,0:T(8,128)S(1)}, u32[]{:S(2)}, u32[]{:S(2)}) collective-permute-start(f32[8,128]{1,0:T(8,128)S(1)} %get-tuple-element.70), channel_id=1, source_target_pairs={{0,1},{1,2},{2,3},{3,4},{4,5},{5,6},{6,7},{7,8},{8,9},{9,10},{10,1... | collective-permute-start | bytes 12296 | tf_op jit(solution)/shard_map/ppermute | solution.py:642
  54.0 7.9 %collective-permute-start.7 = (f32[8,128]{1,0:T(8,128)S(1)}, f32[8,128]{1,0:T(8,128)S(1)}, u32[]{:S(2)}, u32[]{:S(2)}) collective-permute-start(f32[8,128]{1,0:T(8,128)S(1)} %get-tuple-element.71), channel_id=1, source_target_pairs={{1,0},{2,1},{3,2},{4,3},{5,4},{6,5},{7,6},{8,7},{9,8},{10,9},{11,1... | collective-permute-start | bytes 12296 | tf_op jit(solution)/shard_map/ppermute | solution.py:643
  72.3 10.4 %collective-permute-start.8 = (f32[8,256]{1,0:T(8,128)S(1)}, f32[8,256]{1,0:T(8,128)S(1)}, u32[]{:S(2)}, u32[]{:S(2)}) collective-permute-start(f32[8,256]{1,0:T(8,128)S(1)} %get-tuple-element.91), channel_id=1, source_target_pairs={{0,16},{16,32},{32,48},{48,64},{64,80},{80,96},{96,112},{112,0},{1... | collective-permute-start | bytes 24584 | tf_op jit(solution)/shard_map/ppermute | solution.py:642
  74.7 8.0 %collective-permute-start.9 = (f32[8,256]{1,0:T(8,128)S(1)}, f32[8,256]{1,0:T(8,128)S(1)}, u32[]{:S(2)}, u32[]{:S(2)}) collective-permute-start(f32[8,256]{1,0:T(8,128)S(1)} %get-tuple-element.92), channel_id=1, source_target_pairs={{16,0},{32,16},{48,32},{64,48},{80,64},{96,80},{112,96},{0,112},{1... | collective-permute-start | bytes 24584 | tf_op jit(solution)/shard_map/ppermute | solution.py:643
  74.7 8.0 %collective-permute-start.10 = (f32[8,128]{1,0:T(8,128)S(1)}, f32[8,128]{1,0:T(8,128)S(1)}, u32[]{:S(2)}, u32[]{:S(2)}) collective-permute-start(f32[8,128]{1,0:T(8,128)S(1)} %get-tuple-element.93), channel_id=1, source_target_pairs={{0,1},{1,2},{2,3},{3,4},{4,5},{5,6},{6,7},{7,8},{8,9},{9,10},{10,1... | collective-permute-start | bytes 12296 | tf_op jit(solution)/shard_map/ppermute | solution.py:642
  74.7 8.0 %collective-permute-start.11 = (f32[8,128]{1,0:T(8,128)S(1)}, f32[8,128]{1,0:T(8,128)S(1)}, u32[]{:S(2)}, u32[]{:S(2)}) collective-permute-start(f32[8,128]{1,0:T(8,128)S(1)} %get-tuple-element.94), channel_id=1, source_target_pairs={{1,0},{2,1},{3,2},{4,3},{5,4},{6,5},{7,6},{8,7},{9,8},{10,9},{11,1... | collective-permute-start | bytes 12296 | tf_op jit(solution)/shard_map/ppermute | solution.py:643
  87.4 28.0 %all-to-all-start.2 = ((f32[128,8,128]{2,1,0:T(8,128)}), f32[128,8,128]{2,1,0:T(8,128)S(1)}, u32[]{:S(2)}, u32[]{:S(2)}) async-start(f32[128,8,128]{2,1,0:T(8,128)} %bitcast.12), calls=%async_computation.2 | async-start | bytes 1048576 | tf_op jit(solution)/shard_map/all_to_all | solution.py:629
  95.7 10.7 %collective-permute-start.12 = (f32[8,256]{1,0:T(8,128)S(1)}, f32[8,256]{1,0:T(8,128)S(1)}, u32[]{:S(2)}, u32[]{:S(2)}) collective-permute-start(f32[8,256]{1,0:T(8,128)S(1)} %get-tuple-element.98), channel_id=1, source_target_pairs={{0,16},{16,32},{32,48},{48,64},{64,80},{80,96},{96,112},{112,0},{1... | collective-permute-start | bytes 24584 | tf_op jit(solution)/shard_map/ppermute | solution.py:642
  97.3 9.1 %collective-permute-start.13 = (f32[8,256]{1,0:T(8,128)S(1)}, f32[8,256]{1,0:T(8,128)S(1)}, u32[]{:S(2)}, u32[]{:S(2)}) collective-permute-start(f32[8,256]{1,0:T(8,128)S(1)} %get-tuple-element.99), channel_id=1, source_target_pairs={{16,0},{32,16},{48,32},{64,48},{80,64},{96,80},{112,96},{0,112},{1... | collective-permute-start | bytes 24584 | tf_op jit(solution)/shard_map/ppermute | solution.py:643
  97.3 9.0 %collective-permute-start.14 = (f32[8,128]{1,0:T(8,128)S(1)}, f32[8,128]{1,0:T(8,128)S(1)}, u32[]{:S(2)}, u32[]{:S(2)}) collective-permute-start(f32[8,128]{1,0:T(8,128)S(1)} %get-tuple-element.100), channel_id=1, source_target_pairs={{0,1},{1,2},{2,3},{3,4},{4,5},{5,6},{6,7},{7,8},{8,9},{9,10},{10,1... | collective-permute-start | bytes 12296 | tf_op jit(solution)/shard_map/ppermute | solution.py:642
  98.5 7.9 %collective-permute-start.15 = (f32[8,128]{1,0:T(8,128)S(1)}, f32[8,128]{1,0:T(8,128)S(1)}, u32[]{:S(2)}, u32[]{:S(2)}) collective-permute-start(f32[8,128]{1,0:T(8,128)S(1)} %get-tuple-element.101), channel_id=1, source_target_pairs={{1,0},{2,1},{3,2},{4,3},{5,4},{6,5},{7,6},{8,7},{9,8},{10,9},{11,1... | collective-permute-start | bytes 12296 | tf_op jit(solution)/shard_map/ppermute | solution.py:643

commit v4 on v3

--- a/solution.py
+++ b/solution.py
@@ -198,20 +198,45 @@
     return [pltpu.make_async_copy(a, b, sems.at[n, l]) for n, (a, b) in enumerate(pairs(l))]
 
 
+def faces_kernel(
+    p_h, sw_h, sg_h, perm_h, row_lo, row_hi, col_lo, col_hi, p, sw, sg, perm, sems,
+):
+    copies = start_copies(((perm_h.at[0:2], perm), (p_h, p), (sw_h, sw), (sg_h, sg)), sems)
+    lane = iota((R, LANES), 1)
+    columns = jnp.zeros((R, LANES), f32)
+    wait_copies(copies[:1])
+    for l in range(L):
+        n = 3 * L + l
+        row_lo[n : n + 1, :] = perm[0, l, 0:16, :].astype(f32)[0:1]
+        row_hi[n : n + 1, :] = perm[0, l, R - 16 : R, :].astype(f32)[15:16]
+        k = perm[1, l].astype(f32)
+        columns = jnp.where(lane == n, k[:, 0:1], columns)
+        columns = jnp.where(lane == 4 * L + n, k[:, C - 1 : C], columns)
+    wait_copies(copies[1:])
+    for l in range(L):
+        for f, ref in enumerate((p, sw, sg)):
+            x = ref[l]
+            n = f * L + l
+            row_lo[n : n + 1, :] = x[0:1]
+            row_hi[n : n + 1, :] = x[R - 1 : R]
+            columns = jnp.where(lane == n, x[:, 0:1], columns)
+            columns = jnp.where(lane == 4 * L + n, x[:, C - 1 : C], columns)
+    pack_columns(columns, col_lo, col_hi)
+
+
 def start_kernel(
-    cell_h, well_h, index_h, pressure_h, rate_h, p_h, sw_h, sg_h, perm_h,
-    row_lo, row_hi, col_lo, col_hi, pay, perf, info, own,
-    cells, cell_in, well_in, index_in, pressure_in, rate_in, p, sw, sg, perm, rows, sems,
+    cell_h, well_h, index_h, pressure_h, rate_h, p, sw, sg,
+    pay, perf, info, own,
+    cells, cell_in, well_in, index_in, pressure_in, rate_in, rows, sems,
 ):
     copies = start_copies(
         (
             (cell_h, cells), (cell_h, cell_in), (well_h, well_in), (index_h, index_in),
             (pressure_h, pressure_in), (rate_h, rate_in),
-            (p_h, p), (sw_h, sw), (sg_h, sg), (perm_h.at[0:2], perm),
         ),
         sems,
     )
-    wait_copies(copies[:6])
+    wait_copies(copies)
     cell_row = cell_in[...]
     well_row = well_in[...]
     index_row = index_in[...]
@@ -225,24 +250,6 @@
     column = to_column(cell_float).astype(i32) & (C - 1)
     slot_column = to_column(well_float).astype(i32) & 15
     index_column = to_column(index_row)
-    wait_copies(copies[6:])
-    lane = iota((R, LANES), 1)
-    columns = jnp.zeros((R, LANES), f32)
-    for l in range(L):
-        for f, ref in enumerate((p, sw, sg)):
-            x = ref[l]
-            n = f * L + l
-            row_lo[n : n + 1, :] = x[0:1]
-            row_hi[n : n + 1, :] = x[R - 1 : R]
-            columns = jnp.where(lane == n, x[:, 0:1], columns)
-            columns = jnp.where(lane == 4 * L + n, x[:, C - 1 : C], columns)
-        n = 3 * L + l
-        row_lo[n : n + 1, :] = perm[0, l, 0:16, :].astype(f32)[0:1]
-        row_hi[n : n + 1, :] = perm[0, l, R - 16 : R, :].astype(f32)[15:16]
-        k = perm[1, l].astype(f32)
-        columns = jnp.where(lane == n, k[:, 0:1], columns)
-        columns = jnp.where(lane == 4 * L + n, k[:, C - 1 : C], columns)
-    pack_columns(columns, col_lo, col_hi)
     gather_cells(cells, (p, sw, sg), rows)
     here = [pick_columns(rows, n, column) for n in range(3)]
     coeffs = coeffs_of(*here)
@@ -274,14 +281,12 @@
 
 
 def setup_kernel(
-    me, info, row_lo, row_hi, col_lo, col_hi, p_h, sw_h, sg_h, por_h, mass_h, perm_h,
-    coef_row, coef_col, coef_h, tx_h, ty_h, tz_h, base_h, head_h, weight_h, res_h, diag_h,
-    p, sw, sg, por, mass, perm, coef, tx, ty, tz, base, head, weight, res, diag, index_sum,
+    me, info, row_lo, row_hi, col_lo, col_hi, p, sw, sg, por_h, mass_h, perm_h,
+    coef_row, coef_col, base, head, coef_h, tx_h, ty_h, tz_h, weight_h, res_h, diag_h,
+    por, mass, perm, coef, tx, ty, tz, weight, res, diag, index_sum,
     sems, sems_t, sems_out,
 ):
-    copies = start_copies(
-        ((p_h, p), (sw_h, sw), (sg_h, sg), (perm_h, perm), (por_h, por), (mass_h, mass)), sems
-    )
+    copies = start_copies(((perm_h, perm), (por_h, por), (mass_h, mass)), sems)
     index_sum[...] = scatter(info[0:1].astype(i32), info[2:3]).reshape(L, R, C)
     for side, ref in enumerate((row_lo, row_hi)):
         for a, c in enumerate(coeffs_of(ref[0:L], ref[L : 2 * L], ref[2 * L : 3 * L])):
@@ -295,7 +300,7 @@
     gx = me[0] >> 4
     gy = me[0] & 15
     inside = [jnp.where(t, 1.0, 0.0) for t in (gx > 0, gx < 7, gy > 0, gy < 15)]
-    wait_copies(copies[:4])
+    wait_copies(copies[:1])
 
     def first(l, carry):
         for a, c in enumerate(coeffs_of(p[l], sw[l], sg[l])):
@@ -321,11 +326,11 @@
     lax.fori_loop(0, L, first, 0)
     tz[L] = jnp.zeros((R, C), f32)
     saved = start_copies(((coef, coef_h), (tx, tx_h), (ty, ty_h), (tz, tz_h)), sems_t)
-    wait_copies(copies[4:])
+    wait_copies(copies[1:])
 
     def outs(l):
         return (
-            (base.at[l], base_h.at[l]), (head.at[l], head_h.at[l]), (weight.at[:, l], weight_h.at[:, l]),
+            (weight.at[:, l], weight_h.at[:, l]),
             (res.at[:, l], res_h.at[:, l]), (diag.at[:, l], diag_h.at[:, l]),
         )
 
@@ -374,11 +379,8 @@
 
 
 def first_kernel(
-    cells, me, got, info, own, perf, base_h, head_h,
-    row_lo, row_hi, col_lo, col_hi, pay, mine, well_residual, spread_h, step_h,
-    base, head, spread, step, rows, sems,
-):
-    copies = start_copies(((base_h, base), (head_h, head)), sems)
+    got, info, own, base, head, row_lo, row_hi, col_lo, col_hi, mine, well_residual, spread, step,
+):
     lane = iota((1, LANES), 1)
     sums = jnp.sum(got[...], axis=0, keepdims=True)
     total = jnp.where(lane < WELL_DEV, sums, 1.0)
@@ -391,34 +393,33 @@
     well_row = info[1:2].astype(i32)
     heads = gather_wells(got[...], well_row >> 4, (well_row & 15) + 32)
     spread[...] = scatter(cell_row, info[2:3] * heads).reshape(L, R, C)
-    wait_copies(copies)
     step[...] = base[...] + head[...] * spread[...]
-    copies = start_copies(((spread, spread_h), (step, step_h)), sems)
     write_faces(step, (row_lo, row_hi, col_lo, col_hi))
+
+
+def first_flow_kernel(cells, me, info, perf, mine, step, pay, rows):
     gather_cells(cells, (step,), rows)
+    well_row = info[1:2].astype(i32)
     column = to_column(info[0:1]).astype(i32) & (C - 1)
     here = to_row(pick_columns(rows, 0, column))
     parts = parts_by_offset(me[0], well_row, perf[0:1] * here)
     packed = parts[:, TAIL:]
+    residual = mine[0:1]
+    inverse = mine[1:2]
     for n, row in enumerate((residual * inverse, residual, inverse)):
         packed = packed + rolled_row(row, 16 * (n + 1))
     tiles = [parts[:, LANES * t : LANES * (t + 1)] for t in range(5)]
     pay[...] = to_everyone(jnp.concatenate(tiles + [packed, jnp.zeros((2, LANES), f32)], axis=0))
-    wait_copies(copies)
 
 
 def grid_kernel(
-    coef_row, coef_col, row_lo, row_hi, col_lo, col_hi,
-    coef_h, tx_h, ty_h, tz_h, head_h, weight_h, res_h, spread_h, step_h,
-    residual_h, gain_h, ahead_h,
-    coef, tx, ty, tz, head, weight, res, spread, step, residual, gain, ahead, sems, sems_out,
+    coef_row, coef_col, row_lo, row_hi, col_lo, col_hi, head, spread, step,
+    coef_h, tx_h, ty_h, tz_h, weight_h, res_h,
+    ahead, residual_h, gain_h,
+    coef, tx, ty, tz, weight, res, residual, gain, sems, sems_out,
 ):
     copies = start_copies(
-        (
-            (coef_h, coef), (tx_h, tx), (ty_h, ty), (tz_h, tz), (head_h, head), (weight_h, weight),
-            (res_h, res), (spread_h, spread), (step_h, step),
-        ),
-        sems,
+        ((coef_h, coef), (tx_h, tx), (ty_h, ty), (tz_h, tz), (weight_h, weight), (res_h, res)), sems
     )
     columns = unpack_columns(col_lo, col_hi)
     wait_copies(copies)
@@ -426,7 +427,6 @@
     def outs(l):
         return (
             (residual.at[:, l], residual_h.at[:, l]), (gain.at[:, l], gain_h.at[:, l]),
-            (ahead.at[l], ahead_h.at[l]),
         )
 
     def layer(l, carry):
@@ -454,21 +454,19 @@
         wait_copies(layer_copies(outs, sems_out, l))
 
 
-def second_kernel(got, info, ahead_h, head_h, row_lo, row_hi, col_lo, col_hi, step, ahead, head, sems):
-    copies = start_copies(((ahead_h, ahead), (head_h, head)), sems)
+def second_kernel(got, info, ahead, head, row_lo, row_hi, col_lo, col_hi, step):
     cell_row = info[0:1].astype(i32)
     well_row = info[1:2].astype(i32)
     moves = gather_wells(tile_of(got, 5), well_row >> 4, (well_row & 15) + 16)
     wells = scatter(cell_row, info[2:3] * moves).reshape(L, R, C)
-    wait_copies(copies)
     step[...] = ahead[...] + head[...] * wells
     write_faces(step, (row_lo, row_hi, col_lo, col_hi))
 
 
 def wells_kernel(
-    cells, me, got, info, perf, step, base_h, gain_h, head_h, table, parts, spread, base, gain, head, rows, sems,
-):
-    copies = start_copies(((base_h, base), (gain_h, gain), (head_h, head)), sems)
+    cells, me, got, info, perf, step, gain_h, table, parts, spread, gain, rows, sems,
+):
+    copies = start_copies(((gain_h, gain),), sems)
     tail = tile_of(got, 5)
     residuals = pltpu.roll(tail, LANES - 32, 1)
     inverses = pltpu.roll(tail, LANES - 48, 1)
@@ -490,8 +488,8 @@
 
 
 def third_kernel(
-    cells, info, perf, parts, spread, old, base, gain, head, row_lo, row_hi, col_lo, col_hi,
-    out_row_lo, out_row_hi, out_col_lo, out_col_hi, pay, step_h, step, rows, sems,
+    spread, old, base, gain, head, row_lo, row_hi, col_lo, col_hi,
+    out_row_lo, out_row_hi, out_col_lo, out_col_hi, step,
 ):
     columns = unpack_columns(col_lo, col_hi)
 
@@ -504,8 +502,10 @@
         return carry
 
     lax.fori_loop(0, L, layer, 0)
-    copies = start_copies(((step, step_h),), sems)
     write_faces(step, (out_row_lo, out_row_hi, out_col_lo, out_col_hi))
+
+
+def third_flow_kernel(cells, info, perf, parts, step, pay, rows):
     gather_cells(cells, (step,), rows)
     column = to_column(info[0:1]).astype(i32) & (C - 1)
     here = pick_columns(rows, 0, column)
@@ -515,19 +515,18 @@
     pay[pl.ds(6, DEVICES, stride=8), :] = to_holders(
         well_row >> 4, slot_column, ((0, to_column(perf[0:1]) * here),)
     )
-    wait_copies(copies)
 
 
 def last_grid_kernel(
-    coef_row, coef_col, row_lo, row_hi, col_lo, col_hi,
-    p_h, por_h, coef_h, tx_h, ty_h, tz_h, head_h, weight_h, diag_h, residual_h, step_h,
+    coef_row, coef_col, row_lo, row_hi, col_lo, col_hi, head, step,
+    p_h, por_h, coef_h, tx_h, ty_h, tz_h, weight_h, diag_h, residual_h,
     ahead_h, slope_h,
-    p, por, coef, tx, ty, tz, head, weight, diag, residual, step, ahead, slope, sems, sems_out,
+    p, por, coef, tx, ty, tz, weight, diag, residual, ahead, slope, sems, sems_out,
 ):
     copies = start_copies(
         (
-            (p_h, p), (por_h, por), (coef_h, coef), (tx_h, tx), (ty_h, ty), (tz_h, tz), (head_h, head),
-            (weight_h, weight), (diag_h, diag), (residual_h, residual), (step_h, step),
+            (p_h, p), (por_h, por), (coef_h, coef), (tx_h, tx), (ty_h, ty), (tz_h, tz),
+            (weight_h, weight), (diag_h, diag), (residual_h, residual),
         ),
         sems,
     )
@@ -570,9 +569,9 @@
 
 
 def final_kernel(
-    got, info, table, mine, ahead_h, head_h, slope_h, update_h, moved, ahead, head, slope, update, sems, sems_out,
-):
-    copies = start_copies(((head_h, head), (ahead_h, ahead), (slope_h, slope)), sems)
+    got, info, table, mine, head, ahead_h, slope_h, update_h, moved, ahead, slope, update, sems, sems_out,
+):
+    copies = start_copies(((ahead_h, ahead), (slope_h, slope)), sems)
     flow = jnp.sum(tile_of(got, 6), axis=0, keepdims=True)
     moved[...] = ((flow + mine[0:1]) * mine[1:2])[:, 0:WELL_DEV]
     cell_row = info[0:1].astype(i32)
@@ -650,97 +649,96 @@
 ):
     me = (lax.axis_index("gx") * lax.axis_size("gy") + lax.axis_index("gy")).astype(i32).reshape(1)
     cells = perf_cell.reshape(1, PERFS)
-    *faces, pay, perf, info, own = call(
+    *faces, p, sw, sg = call(
+        faces_kernel,
+        WIDE_FACES + ((FIELD, VM), (FIELD, VM), (FIELD, VM)),
+        [HB] * 4,
+        (pressure, sat_water, sat_gas, perm),
+        [pltpu.VMEM(TWO, bf16), sem((4,))],
+    )
+    halo = halo_of(faces)
+    pay, perf, info, own = call(
         start_kernel,
-        WIDE_FACES + (((DEVICES, LANES), None), ((8, PERFS), VM), ((8, PERFS), VM), (SMALL, VM)),
-        [HB] * 9,
+        (((DEVICES, LANES), None), ((8, PERFS), VM), ((8, PERFS), VM), (SMALL, VM)),
+        [HB] * 5 + [VM] * 3,
         (
             cells, perf_well.reshape(1, PERFS), perf_index.reshape(1, PERFS),
-            well_pressure.reshape(1, WELL_DEV), well_rate.reshape(1, WELL_DEV), pressure, sat_water, sat_gas, perm,
+            well_pressure.reshape(1, WELL_DEV), well_rate.reshape(1, WELL_DEV), p, sw, sg,
         ),
         [
             pltpu.SMEM((1, PERFS), i32), pltpu.VMEM((1, PERFS), i32), pltpu.VMEM((1, PERFS), i32), (1, PERFS),
-            (1, WELL_DEV), (1, WELL_DEV), FIELD, FIELD, FIELD, pltpu.VMEM(TWO, bf16), (3, PERFS, C), sem((10,)),
+            (1, WELL_DEV), (1, WELL_DEV), (3, PERFS, C), sem((6,)),
         ],
     )
-    halo = halo_of(faces)
     got = exchange(pay)
-    coef_row, coef_col, coef, tx, ty, tz, base, head, weight, res, diag = call(
+    coef_row, coef_col, base, head, coef, tx, ty, tz, weight, res, diag = call(
         setup_kernel,
         (
-            ((2, 3, L, C), VM), ((3, R, LANES), VM), (THREE, HB), (TWO, HB), (TWO, HB), (FACED, HB),
-            (FIELD, HB), (FIELD, HB), (THREE, HB), (THREE, HB), (TWO, HB),
+            ((2, 3, L, C), VM), ((3, R, LANES), VM), (FIELD, VM), (FIELD, VM), (THREE, HB), (TWO, HB), (TWO, HB),
+            (FACED, HB), (THREE, HB), (THREE, HB), (TWO, HB),
         ),
-        [SM] + [VM] * 5 + [HB] * 6,
-        (me, info, *halo, pressure, sat_water, sat_gas, porosity, old_mass, perm),
+        [SM] + [VM] * 8 + [HB] * 3,
+        (me, info, *halo, p, sw, sg, porosity, old_mass, perm),
         [
-            FIELD, FIELD, FIELD, FIELD, THREE, pltpu.VMEM(THREE, bf16), THREE, TWO, TWO, FACED,
-            FIELD, FIELD, THREE, THREE, TWO, FIELD, sem((6,)), sem((4,)), sem((5, L)),
+            FIELD, THREE, pltpu.VMEM(THREE, bf16), THREE, TWO, TWO, FACED,
+            THREE, THREE, TWO, FIELD, sem((3,)), sem((4,)), sem((3, L)),
         ],
         flops=400 * L * R * C,
     )
-    *faces, pay, mine, well_residual, spread, start = call(
+    *faces, mine, well_residual, spread, start = call(
         first_kernel,
-        FACES + (PAY, (SMALL, VM), ((1, WELL_DEV), None), (FIELD, HB), (FIELD, HB)),
-        [SM, SM] + [VM] * 4 + [HB] * 2,
-        (cells, me, got, info, own, perf, base, head),
-        [FIELD, FIELD, FIELD, FIELD, ROWS, sem((2,))],
+        FACES + ((SMALL, VM), ((1, WELL_DEV), None), (FIELD, VM), (FIELD, VM)),
+        [VM] * 5,
+        (got, info, own, base, head),
     )
     halo = halo_of(faces)
+    (pay,) = call(
+        first_flow_kernel, (PAY,), [SM] * 2 + [VM] * 4, (cells, me, info, perf, mine, start), [ROWS]
+    )
     got = exchange_tiles(pay)
-    fields = (coef, tx, ty, tz, head, weight)
-    residual, gain, ahead = call(
+    fields = (coef, tx, ty, tz, weight)
+    ahead, residual, gain = call(
         grid_kernel,
-        ((THREE, HB), (SIX, HB), (FIELD, HB)),
-        [VM] * 6 + [HB] * 9,
-        (coef_row, coef_col, *halo, *fields, res, spread, start),
-        [
-            THREE, TWO, TWO, FACED, FIELD, THREE, THREE, FIELD, FIELD, THREE, SIX, FIELD,
-            sem((9,)), sem((3, L)),
-        ],
+        ((FIELD, VM), (THREE, HB), (SIX, HB)),
+        [VM] * 9 + [HB] * 6,
+        (coef_row, coef_col, *halo, head, spread, start, *fields, res),
+        [THREE, TWO, TWO, FACED, THREE, THREE, THREE, SIX, sem((6,)), sem((2, L))],
         flops=100 * L * R * C,
     )
+    *faces, step = call(second_kernel, FACES + ((FIELD, VM),), [VM] * 4, (got, info, ahead, head))
+    halo = halo_of(faces)
+    table, parts, spread, gain_near = call(
+        wells_kernel,
+        (((2, DEVICES, LANES), VM), (SMALL, VM), (FIELD, VM), (SIX, VM)),
+        [SM, SM] + [VM] * 4 + [HB],
+        (cells, me, got, info, perf, step, gain),
+        [ROWS, sem((1,))],
+    )
     *faces, step = call(
-        second_kernel,
+        third_kernel,
         FACES + ((FIELD, VM),),
-        [VM] * 2 + [HB] * 2,
-        (got, info, ahead, head),
-        [FIELD, FIELD, sem((2,))],
+        [VM] * 9,
+        (spread, step, start, gain_near, head, *halo),
     )
     halo = halo_of(faces)
-    table, parts, spread, base, gain_near, head_near = call(
-        wells_kernel,
-        (((2, DEVICES, LANES), None), (SMALL, VM), (FIELD, VM), (FIELD, VM), (SIX, VM), (FIELD, VM)),
-        [SM, SM] + [VM] * 4 + [HB] * 3,
-        (cells, me, got, info, perf, step, start, gain, head),
-        [ROWS, sem((3,))],
-    )
-    *faces, pay, step = call(
-        third_kernel,
-        FACES + (PAY, (FIELD, HB)),
-        [SM] + [VM] * 12,
-        (cells, info, perf, parts, spread, step, base, gain_near, head_near, *halo),
-        [FIELD, ROWS, sem((1,))],
-    )
-    halo = halo_of(faces)
+    (pay,) = call(
+        third_flow_kernel, (PAY,), [SM] + [VM] * 4, (cells, info, perf, parts, step), [ROWS]
+    )
     got = exchange_tiles(pay)
     ahead, slope = call(
         last_grid_kernel,
         ((THREE, HB), (TWO, HB)),
-        [VM] * 6 + [HB] * 11,
-        (coef_row, coef_col, *halo, pressure, porosity, *fields, diag, residual, step),
-        [
-            FIELD, FIELD, THREE, TWO, TWO, FACED, FIELD, THREE, TWO, THREE, FIELD, THREE, TWO,
-            sem((11,)), sem((2, L)),
-        ],
+        [VM] * 8 + [HB] * 9,
+        (coef_row, coef_col, *halo, head, step, pressure, porosity, *fields, diag, residual),
+        [FIELD, FIELD, THREE, TWO, TWO, FACED, THREE, TWO, THREE, THREE, TWO, sem((9,)), sem((2, L))],
         flops=150 * L * R * C,
     )
     update, moved = call(
         final_kernel,
         ((THREE, HB), ((1, WELL_DEV), None)),
-        [VM] * 4 + [HB] * 3,
-        (got, info, table, mine, ahead, head, slope),
-        [THREE, FIELD, TWO, THREE, sem((3,)), sem((1, L))],
+        [VM] * 5 + [HB] * 2,
+        (got, info, table, mine, head, ahead, slope),
+        [THREE, TWO, THREE, sem((2,)), sem((1, L))],
     )
     return residual, well_residual.reshape(WELL_DEV), update, moved.reshape(WELL_DEV)
 

time: 120 us -> 117 us (0.975)
  Pallas kernels: 51.9 us -> 49.4 us
    pallas_call x9 -> x12, Pallas kernels: 51.9 us -> 49.4 us  [call(): pl.pallas_call(kernel, out_shape=shapes, in_specs=ins, out_specs=tuple((w...]
where the time goes in v4:
time: 117 us
  starting transfers between devices  57.8 us (49%)
  Pallas kernels  49.4 us (42%)
  waiting for transfers between devices  8.97 us (8%)
    pallas_call x12, Pallas kernels, call(): pl.pallas_call(kernel, out_shape=shapes, in_specs=ins, out_specs=tuple((w...  49.4 us
    all_to_all x3, starting transfers between devices, exchange(): return lax.all_to_all(array, AXES, split_axis=0, concat_axis=0, tiled=True)  29.9 us
    ppermute x8, starting transfers between devices, halo_of(): got.append(lax.ppermute(low, axis, [(j, i) for i, j in up]))  17.1 us
    ppermute x8, starting transfers between devices, halo_of(): got.append(lax.ppermute(high, axis, up))  10.8 us
    ppermute x8, waiting for transfers between devices, halo_of(): got.append(lax.ppermute(high, axis, up))  8.94 us
  transfers between devices with their start and end apart: 19, of which 3 were waited for; matrix products, arithmetic and copies ran while one was open for 0% of the time, Pallas kernels for 26%

profile of v4, /device:TPU:1, one launch (start us, length us, event | category | flops | bytes accessed | tf_op | source)
XLA Modules:
  0.0 117.0 jit_solution(11976472771878211133)
XLA Ops:
  0.6 2.2 %shard_map.138 = (f32[32,256]{1,0:T(8,128)S(1)}, f32[32,256]{1,0:T(8,128)S(1)}, f32[32,128]{1,0:T(8,128)S(1)}, f32[32,128]{1,0:T(8,128)S(1)}, f32[8,64,256]{2,1,...) custom-call(f32[8,64,256]{2,1,0:T(8,128)} %p_h.3, f32[8,64,256]{2,1,0:T(8,128)} %sw_h.1, ...), custom_call_target="tpu_custom_call" | custom-call | bytes 3145728 | tf_op jit(solution)/shard_map/pallas_call | solution.py:606
  2.8 3.7 %shard_map.139 = (f32[128,128]{1,0:T(8,128)}, f32[8,256]{1,0:T(8,128)S(1)}, f32[8,256]{1,0:T(8,128)S(1)}, f32[8,128]{1,0:T(8,128)S(1)}) custom-call(s32[1,256]{1,0:T(1,128)} %bitcast.20, s32[1,256]{1,0:T(1,128)} %bitcast.24, f32[1,256]{1,0:T(1,128)} %bitcast.25, f32[1,16]{1,0:T(1,128)} %bitcast.26, f32[1,16]{1,0:T(1,128)} %bitcast.27, ...), custom_call_target="tpu_custom_call" | custom-call | bytes 1576064 | tf_op jit(solution)/shard_map/pallas_call | solution.py:606
  6.5 11.5 %all-to-all-start = ((f32[128,1,128]{2,1,0:T(1,128)}), f32[128,1,128]{2,1,0:T(1,128)S(1)}, u32[]{:S(2)}, u32[]{:S(2)}) async-start(f32[128,1,128]{2,1,0:T(1,128)} %bitcast.7), calls=%async_computation | async-start | bytes 131072 | tf_op jit(solution)/shard_map/all_to_all | solution.py:628
  18.0 1.6 %collective-permute-start = (f32[32,256]{1,0:T(8,128)S(1)}, f32[32,256]{1,0:T(8,128)S(1)}, u32[]{:S(2)}, u32[]{:S(2)}) collective-permute-start(f32[32,256]{1,0:T(8,128)S(1)} %get-tuple-element.59), channel_id=1, source_target_pairs={{0,16},{16,32},{32,48},{48,64},{64,80},{80,96},{96,112},{112,0},{1... | collective-permute-start | bytes 98312 | tf_op jit(solution)/shard_map/ppermute | solution.py:641
  19.7 0.0 collective-permute-start.1
  19.7 1.2 %collective-permute-start.2 = (f32[32,128]{1,0:T(8,128)S(1)}, f32[32,128]{1,0:T(8,128)S(1)}, u32[]{:S(2)}, u32[]{:S(2)}) collective-permute-start(f32[32,128]{1,0:T(8,128)S(1)} %get-tuple-element.61), channel_id=1, source_target_pairs={{0,1},{1,2},{2,3},{3,4},{4,5},{5,6},{6,7},{7,8},{8,9},{9,10},{10,1... | collective-permute-start | bytes 49160 | tf_op jit(solution)/shard_map/ppermute | solution.py:641
  20.9 4.1 %collective-permute-start.3 = (f32[32,128]{1,0:T(8,128)S(1)}, f32[32,128]{1,0:T(8,128)S(1)}, u32[]{:S(2)}, u32[]{:S(2)}) collective-permute-start(f32[32,128]{1,0:T(8,128)S(1)} %get-tuple-element.62), channel_id=1, source_target_pairs={{1,0},{2,1},{3,2},{4,3},{5,4},{6,5},{7,6},{8,7},{9,8},{10,9},{11,1... | collective-permute-start | bytes 49160 | tf_op jit(solution)/shard_map/ppermute | solution.py:642
  25.0 1.4 %collective-permute-done.2.col_lo = f32[32,128]{1,0:T(8,128)S(1)} collective-permute-done((f32[32,128]{1,0:T(8,128)S(1)}, f32[32,128]{1,0:T(8,128)S(1)}, u32[]{:S(2)}, u32[]{:S(2)}) %collective-permute-start.2) | collective-permute-done | bytes 16416 | tf_op jit(solution)/shard_map/ppermute | solution.py:641
  26.4 0.0 collective-permute-done.3.col_hi
  26.4 0.0 collective-permute-done.row_lo
  26.4 0.0 collective-permute-done.1.row_hi
  26.4 0.0 copy-start
  26.4 9.7 %shard_map.140 = (f32[2,3,8,256]{3,2,1,0:T(8,128)S(1)}, f32[3,64,128]{2,1,0:T(8,128)S(1)}, f32[8,64,256]{2,1,0:T(8,128)S(1)}, f32[8,64,256]{2,1,0:T(8,128)S(1)},...) custom-call(s32[1]{0:T(128)} %bitcast.me, ...), custom_call_target="tpu_custom_call" | custom-call | flops 52428800 | bytes 5349380 | tf_op jit(solution)/shard_map/pallas_call | solution.py:606
  36.1 0.0 all-to-all-done
  36.1 1.2 %shard_map.141 = (f32[8,256]{1,0:T(8,128)S(1)}, f32[8,256]{1,0:T(8,128)S(1)}, f32[8,128]{1,0:T(8,128)S(1)}, f32[8,128]{1,0:T(8,128)S(1)}, f32[8,128]{1,0:T(8,128...) custom-call(f32[128,128]{1,0:T(8,128)S(1)} %bitcast.19, ...), custom_call_target="tpu_custom_call" | custom-call | bytes 1126400 | tf_op jit(solution)/shard_map/pallas_call | solution.py:606
  37.4 3.1 %shard_map.143 = f32[1024,128]{1,0:T(8,128)} custom-call(s32[1,256]{1,0:T(1,128)S(1)} %bitcast.21, s32[1]{0:T(128)} %bitcast.me, f32[8,256]{1,0:T(8,128)S(1)} %get-tuple-element.58.info, f32[8,256]{1,0:T(8,128)S(1)} %get-tuple-element.83.perf, f32[8,128]{1,0:T(8,128)S(1)} %get-tuple-element.84.mine, f32[8,64,256]{2,1,0:T(8,128)S(1)} %get-tuple-element.74.step.base), custom_call_target="tpu_custom_call" | custom-call | bytes 545796 | tf_op jit(solution)/shard_map/pallas_call | solution.py:606
  40.4 10.1 %all-to-all-start.1 = ((f32[128,8,128]{2,1,0:T(8,128)}), f32[128,8,128]{2,1,0:T(8,128)S(1)}, u32[]{:S(2)}, u32[]{:S(2)}) async-start(f32[128,8,128]{2,1,0:T(8,128)} %bitcast.10), calls=%async_computation.1 | async-start | bytes 1048576 | tf_op jit(solution)/shard_map/all_to_all | solution.py:628
  50.5 1.6 %collective-permute-start.4 = (f32[8,256]{1,0:T(8,128)S(1)}, f32[8,256]{1,0:T(8,128)S(1)}, u32[]{:S(2)}, u32[]{:S(2)}) collective-permute-start(f32[8,256]{1,0:T(8,128)S(1)} %get-tuple-element.69), channel_id=1, source_target_pairs={{0,16},{16,32},{32,48},{48,64},{64,80},{80,96},{96,112},{112,0},{1... | collective-permute-start | bytes 24584 | tf_op jit(solution)/shard_map/ppermute | solution.py:641
  52.2 0.0 collective-permute-start.5
  52.2 1.2 %collective-permute-start.6 = (f32[8,128]{1,0:T(8,128)S(1)}, f32[8,128]{1,0:T(8,128)S(1)}, u32[]{:S(2)}, u32[]{:S(2)}) collective-permute-start(f32[8,128]{1,0:T(8,128)S(1)} %get-tuple-element.71), channel_id=1, source_target_pairs={{0,1},{1,2},{2,3},{3,4},{4,5},{5,6},{6,7},{7,8},{8,9},{9,10},{10,1... | collective-permute-start | bytes 12296 | tf_op jit(solution)/shard_map/ppermute | solution.py:641
  53.4 4.1 %collective-permute-start.7 = (f32[8,128]{1,0:T(8,128)S(1)}, f32[8,128]{1,0:T(8,128)S(1)}, u32[]{:S(2)}, u32[]{:S(2)}) collective-permute-start(f32[8,128]{1,0:T(8,128)S(1)} %get-tuple-element.72), channel_id=1, source_target_pairs={{1,0},{2,1},{3,2},{4,3},{5,4},{6,5},{7,6},{8,7},{9,8},{10,9},{11,1... | collective-permute-start | bytes 12296 | tf_op jit(solution)/shard_map/ppermute | solution.py:642
  57.5 3.8 %collective-permute-done.6.col_lo = f32[8,128]{1,0:T(8,128)S(1)} collective-permute-done((f32[8,128]{1,0:T(8,128)S(1)}, f32[8,128]{1,0:T(8,128)S(1)}, u32[]{:S(2)}, u32[]{:S(2)}) %collective-permute-start.6) | collective-permute-done | bytes 4128 | tf_op jit(solution)/shard_map/ppermute | solution.py:641
  61.2 0.0 collective-permute-done.7.col_hi
  61.2 0.0 collective-permute-done.4.row_lo
  61.2 0.0 collective-permute-done.5.row_hi
  61.2 8.1 %shard_map.142 = (f32[8,64,256]{2,1,0:T(8,128)S(1)}, f32[3,8,64,256]{3,2,1,0:T(8,128)}, f32[6,8,64,256]{3,2,1,0:T(8,128)}) custom-call(f32[2,3,8,256]{3,2,1,0:T(8,128)S(1)} %get-tuple-element.63.coef_row, f32[3,64,128]{2,1,0:T(8,128)S(1)} %get-tuple-element.64.coef_col, f32[8,256]{1,0:T(8,128)S(1)} %collective-permute-done.4.row_lo, ...), custom_call_target="tpu_custom_call" | custom-call | flops 13107200 | bytes 9150464 | tf_op jit(solution)/shard_map/pallas_call | solution.py:606
  69.3 0.0 all-to-all-done.1
  69.4 0.9 shard_map.144
  70.2 2.3 %collective-permute-start.8 = (f32[8,256]{1,0:T(8,128)S(1)}, f32[8,256]{1,0:T(8,128)S(1)}, u32[]{:S(2)}, u32[]{:S(2)}) collective-permute-start(f32[8,256]{1,0:T(8,128)S(1)} %get-tuple-element.91), channel_id=1, source_target_pairs={{0,16},{16,32},{32,48},{48,64},{64,80},{80,96},{96,112},{112,0},{1... | collective-permute-start | bytes 24584 | tf_op jit(solution)/shard_map/ppermute | solution.py:641
  72.6 0.0 collective-permute-start.9
  72.6 0.0 collective-permute-start.10
  72.6 4.8 %collective-permute-start.11 = (f32[8,128]{1,0:T(8,128)S(1)}, f32[8,128]{1,0:T(8,128)S(1)}, u32[]{:S(2)}, u32[]{:S(2)}) collective-permute-start(f32[8,128]{1,0:T(8,128)S(1)} %get-tuple-element.94), channel_id=1, source_target_pairs={{1,0},{2,1},{3,2},{4,3},{5,4},{6,5},{7,6},{8,7},{9,8},{10,9},{11,1... | collective-permute-start | bytes 12296 | tf_op jit(solution)/shard_map/ppermute | solution.py:642
  77.4 3.2 %shard_map.145 = (f32[2,128,128]{2,1,0:T(8,128)S(1)}, f32[8,128]{1,0:T(8,128)S(1)}, f32[8,64,256]{2,1,0:T(8,128)S(1)}, f32[6,8,64,256]{3,2,1,0:T(8,128)S(1)}) custom-call(s32[1,256]{1,0:T(1,128)S(1)} %bitcast.22, s32[1]{0:T(128)} %bitcast.me, f32[1024,128]{1,0:T(8,128)S(1)} %bitcast.17, f32[8,256]{1,0:T(8,128)S(1)} %get-tuple-element.58.info, ...), custom_call_target="tpu_custom_call" | custom-call | bytes 4211716 | tf_op jit(solution)/shard_map/pallas_call | solution.py:606
  80.6 0.0 collective-permute-done.11.col_hi
  80.6 0.0 collective-permute-done.8.row_lo
  80.6 1.6 %shard_map.146 = (f32[8,256]{1,0:T(8,128)S(1)}, f32[8,256]{1,0:T(8,128)S(1)}, f32[8,128]{1,0:T(8,128)S(1)}, f32[8,128]{1,0:T(8,128)S(1)}, f32[8,64,256]{2,1,0:T(8,128)S(1)}) custom-call(f32[8,64,256]{2,1,0:T(8,128)S(1)} %get-tuple-element.89.spread, f32[8,64,256]{2,1,0:T(8,128)S(1)} %get-tuple-element.86.step.old, ...), custom_call_target="tpu_custom_call" | custom-call | bytes 5267456 | tf_op jit(solution)/shard_map/pallas_call | solution.py:606
  82.2 3.0 %shard_map.147 = f32[1024,128]{1,0:T(8,128)} custom-call(s32[1,256]{1,0:T(1,128)S(1)} %bitcast.23, f32[8,256]{1,0:T(8,128)S(1)} %get-tuple-element.58.info, f32[8,256]{1,0:T(8,128)S(1)} %get-tuple-element.83.perf, f32[8,128]{1,0:T(8,128)S(1)} %get-tuple-element.88.parts, f32[8,64,256]{2,1,0:T(8,128)S(1)} %get-tuple-element.95.step), custom_call_target="tpu_custom_call" | custom-call | bytes 545792 | tf_op jit(solution)/shard_map/pallas_call | solution.py:606
  85.3 8.3 %all-to-all-start.2 = ((f32[128,8,128]{2,1,0:T(8,128)}), f32[128,8,128]{2,1,0:T(8,128)S(1)}, u32[]{:S(2)}, u32[]{:S(2)}) async-start(f32[128,8,128]{2,1,0:T(8,128)} %bitcast.12), calls=%async_computation.2 | async-start | bytes 1048576 | tf_op jit(solution)/shard_map/all_to_all | solution.py:628
  93.6 1.6 %collective-permute-start.12 = (f32[8,256]{1,0:T(8,128)S(1)}, f32[8,256]{1,0:T(8,128)S(1)}, u32[]{:S(2)}, u32[]{:S(2)}) collective-permute-start(f32[8,256]{1,0:T(8,128)S(1)} %get-tuple-element.97), channel_id=1, source_target_pairs={{0,16},{16,32},{32,48},{48,64},{64,80},{80,96},{96,112},{112,0},{1... | collective-permute-start | bytes 24584 | tf_op jit(solution)/shard_map/ppermute | solution.py:641
  95.2 1.2 %collective-permute-start.14 = (f32[8,128]{1,0:T(8,128)S(1)}, f32[8,128]{1,0:T(8,128)S(1)}, u32[]{:S(2)}, u32[]{:S(2)}) collective-permute-start(f32[8,128]{1,0:T(8,128)S(1)} %get-tuple-element.99), channel_id=1, source_target_pairs={{0,1},{1,2},{2,3},{3,4},{4,5},{5,6},{6,7},{7,8},{8,9},{9,10},{10,1... | collective-permute-start | bytes 12296 | tf_op jit(solution)/shard_map/ppermute | solution.py:641
  96.4 4.1 %collective-permute-start.15 = (f32[8,128]{1,0:T(8,128)S(1)}, f32[8,128]{1,0:T(8,128)S(1)}, u32[]{:S(2)}, u32[]{:S(2)}) collective-permute-start(f32[8,128]{1,0:T(8,128)S(1)} %get-tuple-element.100), channel_id=1, source_target_pairs={{1,0},{2,1},{3,2},{4,3},{5,4},{6,5},{7,6},{8,7},{9,8},{10,9},{11,1... | collective-permute-start | bytes 12296 | tf_op jit(solution)/shard_map/ppermute | solution.py:642
  100.5 3.8 %collective-permute-done.14.col_lo = f32[8,128]{1,0:T(8,128)S(1)} collective-permute-done((f32[8,128]{1,0:T(8,128)S(1)}, f32[8,128]{1,0:T(8,128)S(1)}, u32[]{:S(2)}, u32[]{:S(2)}) %collective-permute-start.14) | collective-permute-done | bytes 4128 | tf_op jit(solution)/shard_map/ppermute | solution.py:641
  104.2 0.0 collective-permute-done.15.col_hi
  104.2 0.0 collective-permute-done.12.row_lo
  104.2 0.0 collective-permute-done.13.row_hi
  104.3 8.8 %shard_map.148 = (f32[3,8,64,256]{3,2,1,0:T(8,128)}, f32[2,8,64,256]{3,2,1,0:T(8,128)}) custom-call(f32[2,3,8,256]{3,2,1,0:T(8,128)S(1)} %get-tuple-element.63.coef_row, f32[3,64,128]{2,1,0:T(8,128)S(1)} %get-tuple-element.64.coef_col, f32[8,256]{1,0:T(8,128)S(1)} %collective-permute-done.12.row_lo, f32[8,256]{1,0:T(8,128)S(1)} %collective-permute-done.13.row_hi, ...), custom_call_target="tpu_custom_call" | custom-call | flops 19660800 | bytes 10723328 | tf_op jit(solution)/shard_map/pallas_call | solution.py:606
  113.1 0.0 all-to-all-done.2
  113.1 3.9 %shard_map.149 = (f32[3,8,64,256]{3,2,1,0:T(8,128)}, f32[1,16]{1,0:T(1,128)}) custom-call(f32[1024,128]{1,0:T(8,128)S(1)} %bitcast.18, f32[8,256]{1,0:T(8,128)S(1)} %get-tuple-element.58.info, f32[2,128,128]{2,1,0:T(8,128)S(1)} %get-tuple-element.96.table, f32[8,128]{1,0:T(8,128)S(1)} %get-tuple-element.84.mine, f32[8,64,256]{2,1,0:T(8,128)S(1)} %get-tuple-element.68.head, ...), custom_call_target="tpu_custom_call" | custom-call | bytes 3813376 | tf_op jit(solution)/shard_map/pallas_call | solution.py:606
  (4 shorter events, 0.0 us)
Async XLA Ops:
  6.5 29.6 %all-to-all-start = ((f32[128,1,128]{2,1,0:T(1,128)}), f32[128,1,128]{2,1,0:T(1,128)S(1)}, u32[]{:S(2)}, u32[]{:S(2)}) async-start(f32[128,1,128]{2,1,0:T(1,128)} %bitcast.7), calls=%async_computation | async-start | bytes 131072 | tf_op jit(solution)/shard_map/all_to_all | solution.py:628
  18.0 8.4 %collective-permute-start = (f32[32,256]{1,0:T(8,128)S(1)}, f32[32,256]{1,0:T(8,128)S(1)}, u32[]{:S(2)}, u32[]{:S(2)}) collective-permute-start(f32[32,256]{1,0:T(8,128)S(1)} %get-tuple-element.59), channel_id=1, source_target_pairs={{0,16},{16,32},{32,48},{48,64},{64,80},{80,96},{96,112},{112,0},{1... | collective-permute-start | bytes 98312 | tf_op jit(solution)/shard_map/ppermute | solution.py:641
  19.7 6.7 %collective-permute-start.1 = (f32[32,256]{1,0:T(8,128)S(1)}, f32[32,256]{1,0:T(8,128)S(1)}, u32[]{:S(2)}, u32[]{:S(2)}) collective-permute-start(f32[32,256]{1,0:T(8,128)S(1)} %get-tuple-element.60), channel_id=1, source_target_pairs={{16,0},{32,16},{48,32},{64,48},{80,64},{96,80},{112,96},{0,112},{1... | collective-permute-start | bytes 98312 | tf_op jit(solution)/shard_map/ppermute | solution.py:642
  19.7 6.7 %collective-permute-start.2 = (f32[32,128]{1,0:T(8,128)S(1)}, f32[32,128]{1,0:T(8,128)S(1)}, u32[]{:S(2)}, u32[]{:S(2)}) collective-permute-start(f32[32,128]{1,0:T(8,128)S(1)} %get-tuple-element.61), channel_id=1, source_target_pairs={{0,1},{1,2},{2,3},{3,4},{4,5},{5,6},{6,7},{7,8},{8,9},{9,10},{10,1... | collective-permute-start | bytes 49160 | tf_op jit(solution)/shard_map/ppermute | solution.py:641
  20.9 5.5 %collective-permute-start.3 = (f32[32,128]{1,0:T(8,128)S(1)}, f32[32,128]{1,0:T(8,128)S(1)}, u32[]{:S(2)}, u32[]{:S(2)}) collective-permute-start(f32[32,128]{1,0:T(8,128)S(1)} %get-tuple-element.62), channel_id=1, source_target_pairs={{1,0},{2,1},{3,2},{4,3},{5,4},{6,5},{7,6},{8,7},{9,8},{10,9},{11,1... | collective-permute-start | bytes 49160 | tf_op jit(solution)/shard_map/ppermute | solution.py:642
  26.4 11.0 %copy-start = (s32[256]{0:T(256)S(1)}, s32[256]{0:T(256)}, u32[]{:S(2)}) copy-start(s32[256]{0:T(256)} %param.18) | copy-start | bytes 3076
  40.4 28.9 %all-to-all-start.1 = ((f32[128,8,128]{2,1,0:T(8,128)}), f32[128,8,128]{2,1,0:T(8,128)S(1)}, u32[]{:S(2)}, u32[]{:S(2)}) async-start(f32[128,8,128]{2,1,0:T(8,128)} %bitcast.10), calls=%async_computation.1 | async-start | bytes 1048576 | tf_op jit(solution)/shard_map/all_to_all | solution.py:628
  50.5 10.7 %collective-permute-start.4 = (f32[8,256]{1,0:T(8,128)S(1)}, f32[8,256]{1,0:T(8,128)S(1)}, u32[]{:S(2)}, u32[]{:S(2)}) collective-permute-start(f32[8,256]{1,0:T(8,128)S(1)} %get-tuple-element.69), channel_id=1, source_target_pairs={{0,16},{16,32},{32,48},{48,64},{64,80},{80,96},{96,112},{112,0},{1... | collective-permute-start | bytes 24584 | tf_op jit(solution)/shard_map/ppermute | solution.py:641
  52.2 9.1 %collective-permute-start.5 = (f32[8,256]{1,0:T(8,128)S(1)}, f32[8,256]{1,0:T(8,128)S(1)}, u32[]{:S(2)}, u32[]{:S(2)}) collective-permute-start(f32[8,256]{1,0:T(8,128)S(1)} %get-tuple-element.70), channel_id=1, source_target_pairs={{16,0},{32,16},{48,32},{64,48},{80,64},{96,80},{112,96},{0,112},{1... | collective-permute-start | bytes 24584 | tf_op jit(solution)/shard_map/ppermute | solution.py:642
  52.2 9.0 %collective-permute-start.6 = (f32[8,128]{1,0:T(8,128)S(1)}, f32[8,128]{1,0:T(8,128)S(1)}, u32[]{:S(2)}, u32[]{:S(2)}) collective-permute-start(f32[8,128]{1,0:T(8,128)S(1)} %get-tuple-element.71), channel_id=1, source_target_pairs={{0,1},{1,2},{2,3},{3,4},{4,5},{5,6},{6,7},{7,8},{8,9},{9,10},{10,1... | collective-permute-start | bytes 12296 | tf_op jit(solution)/shard_map/ppermute | solution.py:641
  53.4 7.9 %collective-permute-start.7 = (f32[8,128]{1,0:T(8,128)S(1)}, f32[8,128]{1,0:T(8,128)S(1)}, u32[]{:S(2)}, u32[]{:S(2)}) collective-permute-start(f32[8,128]{1,0:T(8,128)S(1)} %get-tuple-element.72), channel_id=1, source_target_pairs={{1,0},{2,1},{3,2},{4,3},{5,4},{6,5},{7,6},{8,7},{9,8},{10,9},{11,1... | collective-permute-start | bytes 12296 | tf_op jit(solution)/shard_map/ppermute | solution.py:642
  70.2 10.3 %collective-permute-start.8 = (f32[8,256]{1,0:T(8,128)S(1)}, f32[8,256]{1,0:T(8,128)S(1)}, u32[]{:S(2)}, u32[]{:S(2)}) collective-permute-start(f32[8,256]{1,0:T(8,128)S(1)} %get-tuple-element.91), channel_id=1, source_target_pairs={{0,16},{16,32},{32,48},{48,64},{64,80},{80,96},{96,112},{112,0},{1... | collective-permute-start | bytes 24584 | tf_op jit(solution)/shard_map/ppermute | solution.py:641
  72.6 8.0 %collective-permute-start.9 = (f32[8,256]{1,0:T(8,128)S(1)}, f32[8,256]{1,0:T(8,128)S(1)}, u32[]{:S(2)}, u32[]{:S(2)}) collective-permute-start(f32[8,256]{1,0:T(8,128)S(1)} %get-tuple-element.92), channel_id=1, source_target_pairs={{16,0},{32,16},{48,32},{64,48},{80,64},{96,80},{112,96},{0,112},{1... | collective-permute-start | bytes 24584 | tf_op jit(solution)/shard_map/ppermute | solution.py:642
  72.6 8.0 %collective-permute-start.10 = (f32[8,128]{1,0:T(8,128)S(1)}, f32[8,128]{1,0:T(8,128)S(1)}, u32[]{:S(2)}, u32[]{:S(2)}) collective-permute-start(f32[8,128]{1,0:T(8,128)S(1)} %get-tuple-element.93), channel_id=1, source_target_pairs={{0,1},{1,2},{2,3},{3,4},{4,5},{5,6},{6,7},{7,8},{8,9},{9,10},{10,1... | collective-permute-start | bytes 12296 | tf_op jit(solution)/shard_map/ppermute | solution.py:641
  72.6 8.0 %collective-permute-start.11 = (f32[8,128]{1,0:T(8,128)S(1)}, f32[8,128]{1,0:T(8,128)S(1)}, u32[]{:S(2)}, u32[]{:S(2)}) collective-permute-start(f32[8,128]{1,0:T(8,128)S(1)} %get-tuple-element.94), channel_id=1, source_target_pairs={{1,0},{2,1},{3,2},{4,3},{5,4},{6,5},{7,6},{8,7},{9,8},{10,9},{11,1... | collective-permute-start | bytes 12296 | tf_op jit(solution)/shard_map/ppermute | solution.py:642
  85.3 27.8 %all-to-all-start.2 = ((f32[128,8,128]{2,1,0:T(8,128)}), f32[128,8,128]{2,1,0:T(8,128)S(1)}, u32[]{:S(2)}, u32[]{:S(2)}) async-start(f32[128,8,128]{2,1,0:T(8,128)} %bitcast.12), calls=%async_computation.2 | async-start | bytes 1048576 | tf_op jit(solution)/shard_map/all_to_all | solution.py:628
  93.6 10.7 %collective-permute-start.12 = (f32[8,256]{1,0:T(8,128)S(1)}, f32[8,256]{1,0:T(8,128)S(1)}, u32[]{:S(2)}, u32[]{:S(2)}) collective-permute-start(f32[8,256]{1,0:T(8,128)S(1)} %get-tuple-element.97), channel_id=1, source_target_pairs={{0,16},{16,32},{32,48},{48,64},{64,80},{80,96},{96,112},{112,0},{1... | collective-permute-start | bytes 24584 | tf_op jit(solution)/shard_map/ppermute | solution.py:641
  95.2 9.1 %collective-permute-start.13 = (f32[8,256]{1,0:T(8,128)S(1)}, f32[8,256]{1,0:T(8,128)S(1)}, u32[]{:S(2)}, u32[]{:S(2)}) collective-permute-start(f32[8,256]{1,0:T(8,128)S(1)} %get-tuple-element.98), channel_id=1, source_target_pairs={{16,0},{32,16},{48,32},{64,48},{80,64},{96,80},{112,96},{0,112},{1... | collective-permute-start | bytes 24584 | tf_op jit(solution)/shard_map/ppermute | solution.py:642
  95.2 9.0 %collective-permute-start.14 = (f32[8,128]{1,0:T(8,128)S(1)}, f32[8,128]{1,0:T(8,128)S(1)}, u32[]{:S(2)}, u32[]{:S(2)}) collective-permute-start(f32[8,128]{1,0:T(8,128)S(1)} %get-tuple-element.99), channel_id=1, source_target_pairs={{0,1},{1,2},{2,3},{3,4},{4,5},{5,6},{6,7},{7,8},{8,9},{9,10},{10,1... | collective-permute-start | bytes 12296 | tf_op jit(solution)/shard_map/ppermute | solution.py:641
  96.4 7.9 %collective-permute-start.15 = (f32[8,128]{1,0:T(8,128)S(1)}, f32[8,128]{1,0:T(8,128)S(1)}, u32[]{:S(2)}, u32[]{:S(2)}) collective-permute-start(f32[8,128]{1,0:T(8,128)S(1)} %get-tuple-element.100), channel_id=1, source_target_pairs={{1,0},{2,1},{3,2},{4,3},{5,4},{6,5},{7,6},{8,7},{9,8},{10,9},{11,1... | collective-permute-start | bytes 12296 | tf_op jit(solution)/shard_map/ppermute | solution.py:642

commit v5 on v4

--- a/solution.py
+++ b/solution.py
@@ -24,7 +24,6 @@
 L, R, C = 8, 64, 256
 PERFS = 256
 VM = pl.BlockSpec(memory_space=pltpu.VMEM)
-SM = pl.BlockSpec(memory_space=pltpu.SMEM)
 HB = pl.BlockSpec(memory_space=pltpu.HBM)
 
 
@@ -70,22 +69,18 @@
     )
 
 
-def gather_cells(cells, refs, rows):
-    def body(block, carry):
-        for u in range(8):
-            k = block * 8 + u
-            cell = cells[0, k]
-            layer = cell >> 14
-            line = (cell >> 8) & (R - 1)
-            for n, ref in enumerate(refs):
-                rows[n, pl.ds(k, 1), :] = ref[layer, pl.ds(line, 1), :]
-        return carry
-
-    lax.fori_loop(0, PERFS // 8, body, 0)
-
-
-def pick_columns(rows, n, column):
-    return jnp.sum(jnp.where(iota((PERFS, C), 1) == column, rows[n], 0.0), axis=1, keepdims=True)
+def gather_cells(cell_column, fields):
+    onehot = (iota((PERFS, L * R), 1) == (cell_column >> 8)).astype(bf16)
+    here = iota((PERFS, C), 1) == (cell_column & (C - 1))
+    picked = []
+    for field in fields:
+        rows = sum(dot(onehot, part) for part in split3(field))
+        picked.append(jnp.sum(jnp.where(here, rows, 0.0), axis=1, keepdims=True))
+    return picked
+
+
+def flat(field):
+    return field[...].reshape(L * R, C)
 
 
 def gather_wells(table, holder, slot):
@@ -227,36 +222,38 @@
 def start_kernel(
     cell_h, well_h, index_h, pressure_h, rate_h, p, sw, sg,
     pay, perf, info, own,
-    cells, cell_in, well_in, index_in, pressure_in, rate_in, rows, sems,
+    cell_in, well_in, index_in, pressure_in, rate_in, sems,
 ):
     copies = start_copies(
         (
-            (cell_h, cells), (cell_h, cell_in), (well_h, well_in), (index_h, index_in),
+            (cell_h, cell_in), (well_h, well_in), (index_h, index_in),
             (pressure_h, pressure_in), (rate_h, rate_in),
         ),
         sems,
     )
+    me = lax.axis_index("gx") * 16 + lax.axis_index("gy")
+    device = jnp.full((1, PERFS), me, i32).astype(f32)
     wait_copies(copies)
-    cell_row = cell_in[...]
     well_row = well_in[...]
     index_row = index_in[...]
-    cell_float = cell_row.astype(f32)
+    cell_float = cell_in[...].astype(f32)
     well_float = well_row.astype(f32)
-    info[...] = jnp.concatenate([cell_float, well_float, index_row, jnp.zeros((5, PERFS), f32)], axis=0)
+    info[...] = jnp.concatenate([cell_float, well_float, index_row, device, jnp.zeros((4, PERFS), f32)], axis=0)
     blank = jnp.zeros((1, LANES - WELL_DEV), f32)
     heads = jnp.concatenate([pressure_in[...], blank], axis=1)
     rates = jnp.concatenate([rate_in[...], blank], axis=1)
     own[...] = jnp.concatenate([heads, rates, jnp.zeros((6, LANES), f32)], axis=0)
-    column = to_column(cell_float).astype(i32) & (C - 1)
     slot_column = to_column(well_float).astype(i32) & 15
-    index_column = to_column(index_row)
-    gather_cells(cells, (p, sw, sg), rows)
-    here = [pick_columns(rows, n, column) for n in range(3)]
+    here = gather_cells(to_column(cell_float).astype(i32), (flat(p), flat(sw), flat(sg)))
     coeffs = coeffs_of(*here)
-    total = index_column * (coeffs[0] + coeffs[1] + coeffs[2])
+    total = to_column(index_row) * (coeffs[0] + coeffs[1] + coeffs[2])
     sums = to_holders(well_row >> 4, slot_column, ((0, total), (1, total * here[0])))
     pay[...] = sums + rolled_row(heads, 32)
     perf[...] = jnp.broadcast_to(to_row(total), (8, PERFS))
+
+
+def after_kernel(pay, *refs):
+    pass
 
 
 def transmit(k, k_next):
@@ -275,13 +272,33 @@
     return neighbours(lambda m: coef[a, m], l, rows, coef_col[a], l, 4 * L + l)
 
 
+def inner_neighbours(step, l):
+    blank = jnp.zeros((1, C), f32)
+    here = step[l]
+    nexts = shift_rows(here, blank, blank) + shift_columns(here, 0.0, 0.0)
+    return nexts + (step[jnp.maximum(l - 1, 0)], step[jnp.minimum(l + 1, L - 1)])
+
+
 def step_neighbours(step, row_lo, row_hi, columns, l):
     rows = (row_lo[pl.ds(l, 1), :], row_hi[pl.ds(l, 1), :])
     return neighbours(lambda m: step[m], l, rows, columns, l, L + l)
 
 
+def add_faces(field, l, low, high, columns):
+    lane = iota((R, LANES), 1)
+    field[l, :, 0:LANES] += jnp.where(lane == 0, columns[:, l : l + 1], 0.0)
+    field[l, :, C - LANES : C] += jnp.where(lane == LANES - 1, columns[:, L + l : L + l + 1], 0.0)
+    field[l, 0:1, :] += low
+    field[l, R - 1 : R, :] += high
+
+
+def end_columns(columns, l, first, last):
+    lane = iota((R, LANES), 1)
+    return jnp.where(lane == l, first, jnp.where(lane == L + l, last, columns))
+
+
 def setup_kernel(
-    me, info, row_lo, row_hi, col_lo, col_hi, p, sw, sg, por_h, mass_h, perm_h,
+    info, row_lo, row_hi, col_lo, col_hi, p, sw, sg, por_h, mass_h, perm_h,
     coef_row, coef_col, base, head, coef_h, tx_h, ty_h, tz_h, weight_h, res_h, diag_h,
     por, mass, perm, coef, tx, ty, tz, weight, res, diag, index_sum,
     sems, sems_t, sems_out,
@@ -297,8 +314,9 @@
     ):
         coef_col[a] = c
     lane = iota((R, C), 1)
-    gx = me[0] >> 4
-    gy = me[0] & 15
+    me = info[3:4, 0:1].astype(i32)
+    gx = me >> 4
+    gy = me & 15
     inside = [jnp.where(t, 1.0, 0.0) for t in (gx > 0, gx < 7, gy > 0, gy < 15)]
     wait_copies(copies[:1])
 
@@ -397,12 +415,10 @@
     write_faces(step, (row_lo, row_hi, col_lo, col_hi))
 
 
-def first_flow_kernel(cells, me, info, perf, mine, step, pay, rows):
-    gather_cells(cells, (step,), rows)
+def first_flow_kernel(info, perf, mine, step, pay):
     well_row = info[1:2].astype(i32)
-    column = to_column(info[0:1]).astype(i32) & (C - 1)
-    here = to_row(pick_columns(rows, 0, column))
-    parts = parts_by_offset(me[0], well_row, perf[0:1] * here)
+    here = to_row(gather_cells(to_column(info[0:1]).astype(i32), (flat(step),))[0])
+    parts = parts_by_offset(info[3:4].astype(i32), well_row, perf[0:1] * here)
     packed = parts[:, TAIL:]
     residual = mine[0:1]
     inverse = mine[1:2]
@@ -413,15 +429,14 @@
 
 
 def grid_kernel(
-    coef_row, coef_col, row_lo, row_hi, col_lo, col_hi, head, spread, step,
+    coef_row, coef_col, head, spread, step,
     coef_h, tx_h, ty_h, tz_h, weight_h, res_h,
-    ahead, residual_h, gain_h,
+    ahead, end_row, end_col, residual_h, gain_h,
     coef, tx, ty, tz, weight, res, residual, gain, sems, sems_out,
 ):
     copies = start_copies(
         ((coef_h, coef), (tx_h, tx), (ty_h, ty), (tz_h, tz), (weight_h, weight), (res_h, res)), sems
     )
-    columns = unpack_columns(col_lo, col_hi)
     wait_copies(copies)
 
     def outs(l):
@@ -429,8 +444,8 @@
             (residual.at[:, l], residual_h.at[:, l]), (gain.at[:, l], gain_h.at[:, l]),
         )
 
-    def layer(l, carry):
-        nexts = step_neighbours(step, row_lo, row_hi, columns, l)
+    def layer(l, ends):
+        nexts = inner_neighbours(step, l)
         faces = (tx[0, l], tx[1, l], ty[0, l], ty[1, l], tz[l], tz[l + 1])
         wells = spread[l]
         mixes = [head[l]] * 6
@@ -440,31 +455,43 @@
             mixes = [m + w * s for m, s in zip(mixes, sides)]
             residual[a, l] = res[a, l] - coef[a, l] * wells
         total = step[l]
+        gains = []
         for j in range(6):
             g = faces[j] * mixes[j]
             gain[j, l] = g
             total = total + g * nexts[j]
+            gains.append(g)
         ahead[l] = total
+        end_row[0, pl.ds(l, 1), :] = gains[0][0:1]
+        end_row[1, pl.ds(l, 1), :] = gains[1][R - 1 : R]
         for c in layer_copies(outs, sems_out, l):
             c.start()
-        return carry
-
-    lax.fori_loop(0, L, layer, 0)
+        return end_columns(ends, l, gains[2][:, 0:1], gains[3][:, C - 1 : C])
+
+    end_col[...] = lax.fori_loop(0, L, layer, jnp.zeros((R, LANES), f32))
     for l in range(L):
         wait_copies(layer_copies(outs, sems_out, l))
 
 
-def second_kernel(got, info, ahead, head, row_lo, row_hi, col_lo, col_hi, step):
+def second_kernel(
+    got, info, ahead, head, end_row, end_col, row_lo, row_hi, col_lo, col_hi,
+    out_row_lo, out_row_hi, out_col_lo, out_col_hi, step,
+):
     cell_row = info[0:1].astype(i32)
     well_row = info[1:2].astype(i32)
     moves = gather_wells(tile_of(got, 5), well_row >> 4, (well_row & 15) + 16)
     wells = scatter(cell_row, info[2:3] * moves).reshape(L, R, C)
     step[...] = ahead[...] + head[...] * wells
-    write_faces(step, (row_lo, row_hi, col_lo, col_hi))
+    columns = end_col[...] * unpack_columns(col_lo, col_hi)
+    for l in range(L):
+        low = end_row[0, l : l + 1, :] * row_lo[l : l + 1, :]
+        high = end_row[1, l : l + 1, :] * row_hi[l : l + 1, :]
+        add_faces(step, l, low, high, columns)
+    write_faces(step, (out_row_lo, out_row_hi, out_col_lo, out_col_hi))
 
 
 def wells_kernel(
-    cells, me, got, info, perf, step, gain_h, table, parts, spread, gain, rows, sems,
+    got, info, perf, step, gain_h, table, parts, spread, gain, sems,
 ):
     copies = start_copies(((gain_h, gain),), sems)
     tail = tile_of(got, 5)
@@ -478,10 +505,8 @@
     moves = jnp.where(valid, (sum_parts(got) + residuals) * inverses, 0.0)
     values = gather_wells(moves, well_row >> 4, well_row & 15)
     spread[...] = scatter(cell_row, info[2:3] * values).reshape(L, R, C)
-    gather_cells(cells, (step,), rows)
-    column = to_column(info[0:1]).astype(i32) & (C - 1)
-    here = to_row(pick_columns(rows, 0, column))
-    flows = parts_by_offset(me[0], well_row, perf[0:1] * here)
+    here = to_row(gather_cells(to_column(info[0:1]).astype(i32), (flat(step),))[0])
+    flows = parts_by_offset(info[3:4].astype(i32), well_row, perf[0:1] * here)
     tiles = [flows[:, LANES * t : LANES * (t + 1)] for t in range(6)]
     parts[...] = jnp.concatenate(tiles + [jnp.zeros((2, LANES), f32)], axis=0)
     wait_copies(copies)
@@ -505,10 +530,8 @@
     write_faces(step, (out_row_lo, out_row_hi, out_col_lo, out_col_hi))
 
 
-def third_flow_kernel(cells, info, perf, parts, step, pay, rows):
-    gather_cells(cells, (step,), rows)
-    column = to_column(info[0:1]).astype(i32) & (C - 1)
-    here = pick_columns(rows, 0, column)
+def third_flow_kernel(info, perf, parts, step, pay):
+    here = gather_cells(to_column(info[0:1]).astype(i32), (flat(step),))[0]
     well_row = info[1:2].astype(i32)
     slot_column = to_column(info[1:2]).astype(i32) & 15
     pay[...] = to_everyone(parts[...])
@@ -518,9 +541,9 @@
 
 
 def last_grid_kernel(
-    coef_row, coef_col, row_lo, row_hi, col_lo, col_hi, head, step,
+    coef_row, coef_col, head, step, gain_row, gain_col,
     p_h, por_h, coef_h, tx_h, ty_h, tz_h, weight_h, diag_h, residual_h,
-    ahead_h, slope_h,
+    end_row, end_col, ahead_h, slope_h,
     p, por, coef, tx, ty, tz, weight, diag, residual, ahead, slope, sems, sems_out,
 ):
     copies = start_copies(
@@ -530,22 +553,22 @@
         ),
         sems,
     )
-    columns = unpack_columns(col_lo, col_hi)
     wait_copies(copies)
 
     def outs(l):
         return ((ahead.at[:, l], ahead_h.at[:, l]), (slope.at[:, l], slope_h.at[:, l]))
 
-    def layer(l, carry):
-        nexts = step_neighbours(step, row_lo, row_hi, columns, l)
+    def layer(l, ends):
+        nexts = inner_neighbours(step, l)
         faces = (tx[0, l], tx[1, l], ty[0, l], ty[1, l], tz[l], tz[l + 1])
         flows = [t * q for t, q in zip(faces, nexts)]
         flow_sum = sum(flows)
-        rights, cs = [], []
+        rights, cs, sides = [], [], []
         for a in range(3):
             c = coef[a, l]
             total = c * flow_sum - residual[a, l]
-            for v, s in zip(flows, coeff_neighbours(coef, coef_row, coef_col, a, l)):
+            sides.append(coeff_neighbours(coef, coef_row, coef_col, a, l))
+            for v, s in zip(flows, sides[a]):
                 total = total + v * s
             rights.append(total)
             cs.append(c)
@@ -561,15 +584,31 @@
         slope[1, l] = (cs[2] - diag[1, l] * h) * inverse_gas
         for c in layer_copies(outs, sems_out, l):
             c.start()
-        return carry
-
-    lax.fori_loop(0, L, layer, 0)
+        columns = lane_of(gain_col[...], l), lane_of(gain_col[...], L + l)
+        done = []
+        for n, (a, inverse) in enumerate(((0, inverse_water), (2, inverse_gas))):
+            d = diag[n, l]
+            for side, row in enumerate((slice(0, 1), slice(R - 1, R))):
+                face = faces[side][row] * (cs[a][row] + sides[a][side][row])
+                end_row[side, n, pl.ds(l, 1), :] = (
+                    face - d[row] * gain_row[side, pl.ds(l, 1), :]
+                ) * inverse[row]
+            pair = []
+            for side, col in enumerate((slice(0, 1), slice(C - 1, C))):
+                face = faces[2 + side][:, col] * (cs[a][:, col] + sides[a][2 + side][:, col])
+                pair.append((face - d[:, col] * columns[side]) * inverse[:, col])
+            done.append(end_columns(ends[n], l, *pair))
+        return tuple(done)
+
+    blank = jnp.zeros((R, LANES), f32)
+    end_col[0], end_col[1] = lax.fori_loop(0, L, layer, (blank, blank))
     for l in range(L):
         wait_copies(layer_copies(outs, sems_out, l))
 
 
 def final_kernel(
-    got, info, table, mine, head, ahead_h, slope_h, update_h, moved, ahead, slope, update, sems, sems_out,
+    got, info, table, mine, head, gain_row, gain_col, end_row, end_col, row_lo, row_hi, col_lo, col_hi,
+    ahead_h, slope_h, update_h, moved, ahead, slope, update, sems, sems_out,
 ):
     copies = start_copies(((ahead_h, ahead), (slope_h, slope)), sems)
     flow = jnp.sum(tile_of(got, 6), axis=0, keepdims=True)
@@ -580,15 +619,20 @@
     moves = jnp.where(valid, (sum_parts(got) + table[0]) * table[1], 0.0)
     values = gather_wells(moves, well_row >> 4, well_row & 15)
     wells = scatter(cell_row, info[2:3] * values).reshape(L, R, C)
+    halo = unpack_columns(col_lo, col_hi)
+    columns = (gain_col[...] * halo, end_col[0] * halo, end_col[1] * halo)
     wait_copies(copies)
 
     def outs(l):
         return ((update.at[:, l], update_h.at[:, l]),)
 
     for l in range(L):
-        update[0, l] = ahead[0, l] + head[l] * wells[l]
-        update[1, l] = ahead[1, l] + slope[0, l] * wells[l]
-        update[2, l] = ahead[2, l] + slope[1, l] * wells[l]
+        low = row_lo[l : l + 1, :]
+        high = row_hi[l : l + 1, :]
+        for n in range(3):
+            rows = [gain_row[side, l : l + 1, :] if n == 0 else end_row[side, n - 1, l : l + 1, :] for side in range(2)]
+            update[n, l] = ahead[n, l] + (head[l] if n == 0 else slope[n - 1, l]) * wells[l]
+            add_faces(update.at[n], l, rows[0] * low, rows[1] * high, columns[n])
         layer_copies(outs, sems_out, l)[0].start()
     for l in range(L):
         wait_copies(layer_copies(outs, sems_out, l))
@@ -619,7 +663,6 @@
 FACES = (((L, C), VM), ((L, C), VM), ((L, LANES), VM), ((L, LANES), VM))
 WIDE_FACES = (((4 * L, C), VM), ((4 * L, C), VM), ((4 * L, LANES), VM), ((4 * L, LANES), VM))
 SMALL = (8, LANES)
-ROWS = (1, PERFS, C)
 PAY = ((8 * DEVICES, LANES), None)
 sem = pltpu.SemaphoreType.DMA
 
@@ -647,8 +690,6 @@
     pressure, sat_water, sat_gas, old_mass, perm, porosity,
     perf_well, perf_cell, perf_index, well_pressure, well_rate,
 ):
-    me = (lax.axis_index("gx") * lax.axis_size("gy") + lax.axis_index("gy")).astype(i32).reshape(1)
-    cells = perf_cell.reshape(1, PERFS)
     *faces, p, sw, sg = call(
         faces_kernel,
         WIDE_FACES + ((FIELD, VM), (FIELD, VM), (FIELD, VM)),
@@ -662,14 +703,21 @@
         (((DEVICES, LANES), None), ((8, PERFS), VM), ((8, PERFS), VM), (SMALL, VM)),
         [HB] * 5 + [VM] * 3,
         (
-            cells, perf_well.reshape(1, PERFS), perf_index.reshape(1, PERFS),
+            perf_cell.reshape(1, PERFS), perf_well.reshape(1, PERFS), perf_index.reshape(1, PERFS),
             well_pressure.reshape(1, WELL_DEV), well_rate.reshape(1, WELL_DEV), p, sw, sg,
         ),
         [
-            pltpu.SMEM((1, PERFS), i32), pltpu.VMEM((1, PERFS), i32), pltpu.VMEM((1, PERFS), i32), (1, PERFS),
-            (1, WELL_DEV), (1, WELL_DEV), (3, PERFS, C), sem((6,)),
+            pltpu.VMEM((1, PERFS), i32), pltpu.VMEM((1, PERFS), i32), (1, PERFS),
+            (1, WELL_DEV), (1, WELL_DEV), sem((5,)),
         ],
     )
+    pay = pl.pallas_call(
+        after_kernel,
+        out_shape=jax.ShapeDtypeStruct(pay.shape, f32),
+        in_specs=[pl.BlockSpec(memory_space=pl.ANY)] * 5,
+        out_specs=pl.BlockSpec(memory_space=pl.ANY),
+        input_output_aliases={0: 0},
+    )(pay, *halo)
     got = exchange(pay)
     coef_row, coef_col, base, head, coef, tx, ty, tz, weight, res, diag = call(
         setup_kernel,
@@ -677,8 +725,8 @@
             ((2, 3, L, C), VM), ((3, R, LANES), VM), (FIELD, VM), (FIELD, VM), (THREE, HB), (TWO, HB), (TWO, HB),
             (FACED, HB), (THREE, HB), (THREE, HB), (TWO, HB),
         ),
-        [SM] + [VM] * 8 + [HB] * 3,
-        (me, info, *halo, p, sw, sg, porosity, old_mass, perm),
+        [VM] * 8 + [HB] * 3,
+        (info, *halo, p, sw, sg, porosity, old_mass, perm),
         [
             FIELD, THREE, pltpu.VMEM(THREE, bf16), THREE, TWO, TWO, FACED,
             THREE, THREE, TWO, FIELD, sem((3,)), sem((4,)), sem((3, L)),
@@ -692,27 +740,30 @@
         (got, info, own, base, head),
     )
     halo = halo_of(faces)
-    (pay,) = call(
-        first_flow_kernel, (PAY,), [SM] * 2 + [VM] * 4, (cells, me, info, perf, mine, start), [ROWS]
-    )
+    (pay,) = call(first_flow_kernel, (PAY,), [VM] * 4, (info, perf, mine, start))
     got = exchange_tiles(pay)
     fields = (coef, tx, ty, tz, weight)
-    ahead, residual, gain = call(
+    ahead, gain_row, gain_col, residual, gain = call(
         grid_kernel,
-        ((FIELD, VM), (THREE, HB), (SIX, HB)),
-        [VM] * 9 + [HB] * 6,
-        (coef_row, coef_col, *halo, head, spread, start, *fields, res),
+        ((FIELD, VM), ((2, L, C), VM), ((R, LANES), VM), (THREE, HB), (SIX, HB)),
+        [VM] * 5 + [HB] * 6,
+        (coef_row, coef_col, head, spread, start, *fields, res),
         [THREE, TWO, TWO, FACED, THREE, THREE, THREE, SIX, sem((6,)), sem((2, L))],
         flops=100 * L * R * C,
     )
-    *faces, step = call(second_kernel, FACES + ((FIELD, VM),), [VM] * 4, (got, info, ahead, head))
+    *faces, step = call(
+        second_kernel,
+        FACES + ((FIELD, VM),),
+        [VM] * 10,
+        (got, info, ahead, head, gain_row, gain_col, *halo),
+    )
     halo = halo_of(faces)
     table, parts, spread, gain_near = call(
         wells_kernel,
         (((2, DEVICES, LANES), VM), (SMALL, VM), (FIELD, VM), (SIX, VM)),
-        [SM, SM] + [VM] * 4 + [HB],
-        (cells, me, got, info, perf, step, gain),
-        [ROWS, sem((1,))],
+        [VM] * 4 + [HB],
+        (got, info, perf, step, gain),
+        [sem((1,))],
     )
     *faces, step = call(
         third_kernel,
@@ -721,23 +772,21 @@
         (spread, step, start, gain_near, head, *halo),
     )
     halo = halo_of(faces)
-    (pay,) = call(
-        third_flow_kernel, (PAY,), [SM] + [VM] * 4, (cells, info, perf, parts, step), [ROWS]
-    )
+    (pay,) = call(third_flow_kernel, (PAY,), [VM] * 4, (info, perf, parts, step))
     got = exchange_tiles(pay)
-    ahead, slope = call(
+    end_row, end_col, ahead, slope = call(
         last_grid_kernel,
-        ((THREE, HB), (TWO, HB)),
-        [VM] * 8 + [HB] * 9,
-        (coef_row, coef_col, *halo, head, step, pressure, porosity, *fields, diag, residual),
+        (((2, 2, L, C), VM), ((2, R, LANES), VM), (THREE, HB), (TWO, HB)),
+        [VM] * 6 + [HB] * 9,
+        (coef_row, coef_col, head, step, gain_row, gain_col, pressure, porosity, *fields, diag, residual),
         [FIELD, FIELD, THREE, TWO, TWO, FACED, THREE, TWO, THREE, THREE, TWO, sem((9,)), sem((2, L))],
         flops=150 * L * R * C,
     )
     update, moved = call(
         final_kernel,
         ((THREE, HB), ((1, WELL_DEV), None)),
-        [VM] * 5 + [HB] * 2,
-        (got, info, table, mine, head, ahead, slope),
+        [VM] * 13 + [HB] * 2,
+        (got, info, table, mine, head, gain_row, gain_col, end_row, end_col, *halo, ahead, slope),
         [THREE, TWO, THREE, sem((2,)), sem((1, L))],
     )
     return residual, well_residual.reshape(WELL_DEV), update, moved.reshape(WELL_DEV)

time: 117 us -> 111 us (0.949); the launches traced: 117 us -> 109 us
  waiting for transfers between devices: 8.97 us -> 0.05 us
  local copies, waits for them, and re-layouts: 0.01 us -> 4.17 us
  Pallas kernels: 49.4 us -> 45.9 us
    ppermute x8, waiting for transfers between devices: 8.94 us -> 0.02 us  [halo_of(): got.append(lax.ppermute(high, axis, up))]
    unnamed x2 -> x18, local copies, waits for them, and re-layouts: 0.01 us -> 4.17 us
    pallas_call x12, Pallas kernels: 49.4 us -> 45.9 us  [call(): pl.pallas_call(kernel, out_shape=shapes, in_specs=ins, out_specs=tuple((w...]
    all_to_all x3, starting transfers between devices: 29.9 us -> 27.9 us  [exchange(): return lax.all_to_all(array, AXES, split_axis=0, concat_axis=0, tiled=True)]
  transfers between devices with their start and end apart: 19 -> 19, of which waited for: 3 -> 0; matrix products, arithmetic and copies ran while one was open for 0% -> 0% of each run, Pallas kernels for 26% -> 30%
where the time goes in v5:
time: 111 us; the launch traced here: 109 us
  starting transfers between devices  57.7 us (52%)
  Pallas kernels  45.9 us (41%)
  local copies, waits for them, and re-layouts  4.17 us (4%)
    pallas_call x12, Pallas kernels, call(): pl.pallas_call(kernel, out_shape=shapes, in_specs=ins, out_specs=tuple((w...  45.9 us
    all_to_all x3, starting transfers between devices, exchange(): return lax.all_to_all(array, AXES, split_axis=0, concat_axis=0, tiled=True)  27.9 us
    ppermute x8, starting transfers between devices, halo_of(): got.append(lax.ppermute(low, axis, [(j, i) for i, j in up]))  18.2 us
    ppermute x8, starting transfers between devices, halo_of(): got.append(lax.ppermute(high, axis, up))  11.6 us
    unnamed x18, local copies, waits for them, and re-layouts  4.17 us
  transfers between devices with their start and end apart: 19, of which 0 were waited for; matrix products, arithmetic and copies ran while one was open for 0% of the time, Pallas kernels for 30%

profile of v5, /device:TPU:1, one launch (start us, length us, event | category | flops | bytes accessed | tf_op | source)
XLA Modules:
  0.0 108.9 jit_solution(17828593179832859460)
XLA Ops:
  0.6 2.2 %shard_map.138 = (f32[32,256]{1,0:T(8,128)S(1)}, f32[32,256]{1,0:T(8,128)S(1)}, f32[32,128]{1,0:T(8,128)S(1)}, f32[32,128]{1,0:T(8,128)S(1)}, f32[8,64,256]{2,1,...) custom-call(f32[8,64,256]{2,1,0:T(8,128)} %p_h.3, f32[8,64,256]{2,1,0:T(8,128)} %sw_h.1, ...), custom_call_target="tpu_custom_call" | custom-call | bytes 3145728 | tf_op jit(solution)/shard_map/pallas_call | solution.py:650
  2.8 2.7 %collective-permute-start = (f32[32,256]{1,0:T(8,128)S(1)}, f32[32,256]{1,0:T(8,128)S(1)}, u32[]{:S(2)}, u32[]{:S(2)}) collective-permute-start(f32[32,256]{1,0:T(8,128)S(1)} %get-tuple-element.63), channel_id=1, source_target_pairs={{0,16},{16,32},{32,48},{48,64},{64,80},{80,96},{96,112},{112,0},{1... | collective-permute-start | bytes 98312 | tf_op jit(solution)/shard_map/ppermute | solution.py:684
  5.5 0.0 collective-permute-start.1
  5.5 1.2 %collective-permute-start.2 = (f32[32,128]{1,0:T(8,128)S(1)}, f32[32,128]{1,0:T(8,128)S(1)}, u32[]{:S(2)}, u32[]{:S(2)}) collective-permute-start(f32[32,128]{1,0:T(8,128)S(1)} %get-tuple-element.65), channel_id=1, source_target_pairs={{0,1},{1,2},{2,3},{3,4},{4,5},{5,6},{6,7},{7,8},{8,9},{9,10},{10,1... | collective-permute-start | bytes 49160 | tf_op jit(solution)/shard_map/ppermute | solution.py:684
  6.7 4.7 %collective-permute-start.3 = (f32[32,128]{1,0:T(8,128)S(1)}, f32[32,128]{1,0:T(8,128)S(1)}, u32[]{:S(2)}, u32[]{:S(2)}) collective-permute-start(f32[32,128]{1,0:T(8,128)S(1)} %get-tuple-element.66), channel_id=1, source_target_pairs={{1,0},{2,1},{3,2},{4,3},{5,4},{6,5},{7,6},{8,7},{9,8},{10,9},{11,1... | collective-permute-start | bytes 49160 | tf_op jit(solution)/shard_map/ppermute | solution.py:685
  11.5 2.1 %shard_map.139 = (f32[128,128]{1,0:T(8,128)S(1)}, f32[8,256]{1,0:T(8,128)S(1)}, f32[8,256]{1,0:T(8,128)S(1)}, f32[8,128]{1,0:T(8,128)S(1)}) custom-call(s32[1,256]{1,0:T(1,128)} %bitcast.20, s32[1,256]{1,0:T(1,128)} %bitcast.21, f32[1,256]{1,0:T(1,128)} %bitcast.22, f32[1,16]{1,0:T(1,128)} %bitcast.23, f32[1,16]{1,0:T(1,128)} %bitcast.24, ...), custom_call_target="tpu_custom_call" | custom-call | bytes 1576064 | tf_op jit(solution)/shard_map/pallas_call | solution.py:650
  13.5 0.0 copy-start
  13.5 0.6 copy-done
  14.2 0.0 collective-permute-done.2.col_lo.refs_2_
  14.2 0.0 collective-permute-done.3.col_hi.refs_3_
  14.2 0.0 copy-start.1
  14.2 0.0 collective-permute-done.1.row_hi.refs_1_
  14.2 0.5 copy-done.5
  14.8 0.0 copy-done.1
  14.8 0.0 copy-done.3
  14.8 8.8 %all-to-all-start = ((f32[128,1,128]{2,1,0:T(1,128)}), f32[128,1,128]{2,1,0:T(1,128)S(1)}, u32[]{:S(2)}, u32[]{:S(2)}) async-start(f32[128,1,128]{2,1,0:T(1,128)} %bitcast.19), calls=%async_computation | async-start | bytes 131072 | tf_op jit(solution)/shard_map/all_to_all | solution.py:671
  23.7 0.0 copy-start.2
  23.7 0.7 copy-done.2
  24.4 0.8 copy-done.4
  25.2 0.7 copy-done.6
  25.9 0.7 copy-done.8
  26.6 10.3 %shard_map.140 = (f32[2,3,8,256]{3,2,1,0:T(8,128)S(1)}, f32[3,64,128]{2,1,0:T(8,128)S(1)}, f32[8,64,256]{2,1,0:T(8,128)S(1)}, f32[8,64,256]{2,1,0:T(8,128)S(1)},...) custom-call(f32[8,256]{1,0:T(8,128)S(1)} %get-tuple-element.62.info,, ...), custom_call_target="tpu_custom_call" | custom-call | flops 52428800 | bytes 5349376 | tf_op jit(solution)/shard_map/pallas_call | solution.py:650
  37.0 1.2 %shard_map.142 = (f32[8,256]{1,0:T(8,128)S(1)}, f32[8,256]{1,0:T(8,128)S(1)}, f32[8,128]{1,0:T(8,128)S(1)}, f32[8,128]{1,0:T(8,128)S(1)}, f32[8,128]{1,0:T(8,128...) custom-call(f32[128,128]{1,0:T(8,128)S(1)} %bitcast.18, ...), custom_call_target="tpu_custom_call" | custom-call | bytes 1126400 | tf_op jit(solution)/shard_map/pallas_call | solution.py:650
  38.2 1.7 %shard_map.144 = f32[1024,128]{1,0:T(8,128)} custom-call(f32[8,256]{1,0:T(8,128)S(1)} %get-tuple-element.62.info, f32[8,256]{1,0:T(8,128)S(1)} %get-tuple-element.83.perf, f32[8,128]{1,0:T(8,128)S(1)} %get-tuple-element.84.mine, f32[8,64,256]{2,1,0:T(8,128)S(1)} %get-tuple-element.74.step.base), custom_call_target="tpu_custom_call" | custom-call | bytes 544768 | tf_op jit(solution)/shard_map/pallas_call | solution.py:650
  39.9 9.8 %all-to-all-start.1 = ((f32[128,8,128]{2,1,0:T(8,128)}), f32[128,8,128]{2,1,0:T(8,128)S(1)}, u32[]{:S(2)}, u32[]{:S(2)}) async-start(f32[128,8,128]{2,1,0:T(8,128)} %bitcast.9), calls=%async_computation.1 | async-start | bytes 1048576 | tf_op jit(solution)/shard_map/all_to_all | solution.py:671
  49.6 1.6 %collective-permute-start.4 = (f32[8,256]{1,0:T(8,128)S(1)}, f32[8,256]{1,0:T(8,128)S(1)}, u32[]{:S(2)}, u32[]{:S(2)}) collective-permute-start(f32[8,256]{1,0:T(8,128)S(1)} %get-tuple-element.88), channel_id=1, source_target_pairs={{0,16},{16,32},{32,48},{48,64},{64,80},{80,96},{96,112},{112,0},{1... | collective-permute-start | bytes 24584 | tf_op jit(solution)/shard_map/ppermute | solution.py:684
  51.3 0.0 collective-permute-start.5
  51.3 1.2 %collective-permute-start.6 = (f32[8,128]{1,0:T(8,128)S(1)}, f32[8,128]{1,0:T(8,128)S(1)}, u32[]{:S(2)}, u32[]{:S(2)}) collective-permute-start(f32[8,128]{1,0:T(8,128)S(1)} %get-tuple-element.90), channel_id=1, source_target_pairs={{0,1},{1,2},{2,3},{3,4},{4,5},{5,6},{6,7},{7,8},{8,9},{9,10},{10,1... | collective-permute-start | bytes 12296 | tf_op jit(solution)/shard_map/ppermute | solution.py:684
  52.5 4.1 %collective-permute-start.7 = (f32[8,128]{1,0:T(8,128)S(1)}, f32[8,128]{1,0:T(8,128)S(1)}, u32[]{:S(2)}, u32[]{:S(2)}) collective-permute-start(f32[8,128]{1,0:T(8,128)S(1)} %get-tuple-element.91), channel_id=1, source_target_pairs={{1,0},{2,1},{3,2},{4,3},{5,4},{6,5},{7,6},{8,7},{9,8},{10,9},{11,1... | collective-permute-start | bytes 12296 | tf_op jit(solution)/shard_map/ppermute | solution.py:685
  56.6 8.6 %shard_map.143 = (f32[8,64,256]{2,1,0:T(8,128)S(1)}, f32[2,8,256]{2,1,0:T(8,128)S(1)}, f32[64,128]{1,0:T(8,128)S(1)}, f32[3,8,64,256]{3,2,1,0:T(8,128)}, f32[6,8,64,256]{3,2,1,0:T(8,128)}) custom-call(f32[2,3,8,256]{3,2,1,0:T(8,128)S(1)} %get-tuple-element.67.coef_row, f32[3,64,128]{2,1,0:T(8,128)S(1)} %get-tuple-element.68.coef_col, ...), custom_call_target="tpu_custom_call" | custom-call | flops 13107200 | bytes 9125888 | tf_op jit(solution)/shard_map/pallas_call | solution.py:650
  65.1 0.0 collective-permute-done.6.col_lo
  65.2 0.0 collective-permute-done.7.col_hi
  65.2 0.0 all-to-all-done.1
  65.2 0.9 shard_map.145
  66.1 2.1 %collective-permute-start.8 = (f32[8,256]{1,0:T(8,128)S(1)}, f32[8,256]{1,0:T(8,128)S(1)}, u32[]{:S(2)}, u32[]{:S(2)}) collective-permute-start(f32[8,256]{1,0:T(8,128)S(1)} %get-tuple-element.97), channel_id=1, source_target_pairs={{0,16},{16,32},{32,48},{48,64},{64,80},{80,96},{96,112},{112,0},{1... | collective-permute-start | bytes 24584 | tf_op jit(solution)/shard_map/ppermute | solution.py:684
  68.2 0.4 collective-permute-start.9
  68.6 0.0 collective-permute-start.10
  68.6 4.8 %collective-permute-start.11 = (f32[8,128]{1,0:T(8,128)S(1)}, f32[8,128]{1,0:T(8,128)S(1)}, u32[]{:S(2)}, u32[]{:S(2)}) collective-permute-start(f32[8,128]{1,0:T(8,128)S(1)} %get-tuple-element.100), channel_id=1, source_target_pairs={{1,0},{2,1},{3,2},{4,3},{5,4},{6,5},{7,6},{8,7},{9,8},{10,9},{11,1... | collective-permute-start | bytes 12296 | tf_op jit(solution)/shard_map/ppermute | solution.py:685
  73.4 1.9 %shard_map.146 = (f32[2,128,128]{2,1,0:T(8,128)S(1)}, f32[8,128]{1,0:T(8,128)S(1)}, f32[8,64,256]{2,1,0:T(8,128)S(1)}, f32[6,8,64,256]{3,2,1,0:T(8,128)S(1)}) custom-call(f32[1024,128]{1,0:T(8,128)S(1)} %bitcast.16, f32[8,256]{1,0:T(8,128)S(1)} %get-tuple-element.62.info, f32[8,256]{1,0:T(8,128)S(1)} %get-tuple-element.83.perf, ...), custom_call_target="tpu_custom_call" | custom-call | bytes 4210688 | tf_op jit(solution)/shard_map/pallas_call | solution.py:650
  75.4 0.0 collective-permute-done.11.col_hi
  75.4 1.7 %shard_map.147 = (f32[8,256]{1,0:T(8,128)S(1)}, f32[8,256]{1,0:T(8,128)S(1)}, f32[8,128]{1,0:T(8,128)S(1)}, f32[8,128]{1,0:T(8,128)S(1)}, f32[8,64,256]{2,1,0:T(8,128)S(1)}) custom-call(f32[8,64,256]{2,1,0:T(8,128)S(1)} %get-tuple-element.95.spread, f32[8,64,256]{2,1,0:T(8,128)S(1)} %get-tuple-element.92.step.old, ...), custom_call_target="tpu_custom_call" | custom-call | bytes 5267456 | tf_op jit(solution)/shard_map/pallas_call | solution.py:650
  77.0 1.6 %shard_map.148 = f32[1024,128]{1,0:T(8,128)} custom-call(f32[8,256]{1,0:T(8,128)S(1)} %get-tuple-element.62.info, f32[8,256]{1,0:T(8,128)S(1)} %get-tuple-element.83.perf, f32[8,128]{1,0:T(8,128)S(1)} %get-tuple-element.94.parts, f32[8,64,256]{2,1,0:T(8,128)S(1)} %get-tuple-element.101.step), custom_call_target="tpu_custom_call" | custom-call | bytes 544768 | tf_op jit(solution)/shard_map/pallas_call | solution.py:650
  78.7 9.3 %all-to-all-start.2 = ((f32[128,8,128]{2,1,0:T(8,128)}), f32[128,8,128]{2,1,0:T(8,128)S(1)}, u32[]{:S(2)}, u32[]{:S(2)}) async-start(f32[128,8,128]{2,1,0:T(8,128)} %bitcast.11), calls=%async_computation.2 | async-start | bytes 1048576 | tf_op jit(solution)/shard_map/all_to_all | solution.py:671
  88.0 1.6 %collective-permute-start.12 = (f32[8,256]{1,0:T(8,128)S(1)}, f32[8,256]{1,0:T(8,128)S(1)}, u32[]{:S(2)}, u32[]{:S(2)}) collective-permute-start(f32[8,256]{1,0:T(8,128)S(1)} %get-tuple-element.106), channel_id=1, source_target_pairs={{0,16},{16,32},{32,48},{48,64},{64,80},{80,96},{96,112},{112,0},{1... | collective-permute-start | bytes 24584 | tf_op jit(solution)/shard_map/ppermute | solution.py:684
  89.7 1.2 %collective-permute-start.14 = (f32[8,128]{1,0:T(8,128)S(1)}, f32[8,128]{1,0:T(8,128)S(1)}, u32[]{:S(2)}, u32[]{:S(2)}) collective-permute-start(f32[8,128]{1,0:T(8,128)S(1)} %get-tuple-element.108), channel_id=1, source_target_pairs={{0,1},{1,2},{2,3},{3,4},{4,5},{5,6},{6,7},{7,8},{8,9},{9,10},{10,1... | collective-permute-start | bytes 12296 | tf_op jit(solution)/shard_map/ppermute | solution.py:684
  90.9 4.1 %collective-permute-start.15 = (f32[8,128]{1,0:T(8,128)S(1)}, f32[8,128]{1,0:T(8,128)S(1)}, u32[]{:S(2)}, u32[]{:S(2)}) collective-permute-start(f32[8,128]{1,0:T(8,128)S(1)} %get-tuple-element.109), channel_id=1, source_target_pairs={{1,0},{2,1},{3,2},{4,3},{5,4},{6,5},{7,6},{8,7},{9,8},{10,9},{11,1... | collective-permute-start | bytes 12296 | tf_op jit(solution)/shard_map/ppermute | solution.py:685
  95.0 9.9 %shard_map.149 = (f32[2,2,8,256]{3,2,1,0:T(8,128)S(1)}, f32[2,64,128]{2,1,0:T(8,128)S(1)}, f32[3,8,64,256]{3,2,1,0:T(8,128)}, f32[2,8,64,256]{3,2,1,0:T(8,128)}) custom-call(f32[2,3,8,256]{3,2,1,0:T(8,128)S(1)} %get-tuple-element.67.coef_row, f32[3,64,128]{2,1,0:T(8,128)S(1)} %get-tuple-element.68.coef_col, f32[8,64,256]{2,1,0:T(8,128)S(1)} %get-tuple-element.69.head, ...), custom_call_target="tpu_custom_call" | custom-call | flops 19660800 | bytes 10747904 | tf_op jit(solution)/shard_map/pallas_call | solution.py:650
  104.9 3.8 %shard_map.150 = (f32[3,8,64,256]{3,2,1,0:T(8,128)}, f32[1,16]{1,0:T(1,128)}) custom-call(f32[1024,128]{1,0:T(8,128)S(1)} %bitcast.17, f32[8,256]{1,0:T(8,128)S(1)} %get-tuple-element.62.info, f32[2,128,128]{2,1,0:T(8,128)S(1)} %get-tuple-element.102.table, f32[8,128]{1,0:T(8,128)S(1)} %get-tuple-element.84.mine, f32[8,64,256]{2,1,0:T(8,128)S(1)} %get-tuple-element.69.head, ...), custom_call_target="tpu_custom_call" | custom-call | bytes 3985408 | tf_op jit(solution)/shard_map/pallas_call | solution.py:650
  (21 shorter events, 0.0 us)
Async XLA Ops:
  2.8 11.4 %collective-permute-start = (f32[32,256]{1,0:T(8,128)S(1)}, f32[32,256]{1,0:T(8,128)S(1)}, u32[]{:S(2)}, u32[]{:S(2)}) collective-permute-start(f32[32,256]{1,0:T(8,128)S(1)} %get-tuple-element.63), channel_id=1, source_target_pairs={{0,16},{16,32},{32,48},{48,64},{64,80},{80,96},{96,112},{112,0},{1... | collective-permute-start | bytes 98312 | tf_op jit(solution)/shard_map/ppermute | solution.py:684
  5.5 8.7 %collective-permute-start.1 = (f32[32,256]{1,0:T(8,128)S(1)}, f32[32,256]{1,0:T(8,128)S(1)}, u32[]{:S(2)}, u32[]{:S(2)}) collective-permute-start(f32[32,256]{1,0:T(8,128)S(1)} %get-tuple-element.64), channel_id=1, source_target_pairs={{16,0},{32,16},{48,32},{64,48},{80,64},{96,80},{112,96},{0,112},{1... | collective-permute-start | bytes 98312 | tf_op jit(solution)/shard_map/ppermute | solution.py:685
  5.5 8.7 %collective-permute-start.2 = (f32[32,128]{1,0:T(8,128)S(1)}, f32[32,128]{1,0:T(8,128)S(1)}, u32[]{:S(2)}, u32[]{:S(2)}) collective-permute-start(f32[32,128]{1,0:T(8,128)S(1)} %get-tuple-element.65), channel_id=1, source_target_pairs={{0,1},{1,2},{2,3},{3,4},{4,5},{5,6},{6,7},{7,8},{8,9},{9,10},{10,1... | collective-permute-start | bytes 49160 | tf_op jit(solution)/shard_map/ppermute | solution.py:684
  6.7 7.4 %collective-permute-start.3 = (f32[32,128]{1,0:T(8,128)S(1)}, f32[32,128]{1,0:T(8,128)S(1)}, u32[]{:S(2)}, u32[]{:S(2)}) collective-permute-start(f32[32,128]{1,0:T(8,128)S(1)} %get-tuple-element.66), channel_id=1, source_target_pairs={{1,0},{2,1},{3,2},{4,3},{5,4},{6,5},{7,6},{8,7},{9,8},{10,9},{11,1... | collective-permute-start | bytes 49160 | tf_op jit(solution)/shard_map/ppermute | solution.py:685
  13.5 0.6 copy-start
  14.2 0.6 copy-start.5
  14.2 0.6 copy-start.7
  14.2 0.6 copy-start.1
  14.2 0.6 copy-start.3
  14.8 22.1 %all-to-all-start = ((f32[128,1,128]{2,1,0:T(1,128)}), f32[128,1,128]{2,1,0:T(1,128)S(1)}, u32[]{:S(2)}, u32[]{:S(2)}) async-start(f32[128,1,128]{2,1,0:T(1,128)} %bitcast.19), calls=%async_computation | async-start | bytes 131072 | tf_op jit(solution)/shard_map/all_to_all | solution.py:671
  23.7 0.8 copy-start.2
  24.4 0.8 copy-start.4
  25.2 0.7 copy-start.6
  25.9 0.7 copy-start.8
  39.9 25.3 %all-to-all-start.1 = ((f32[128,8,128]{2,1,0:T(8,128)}), f32[128,8,128]{2,1,0:T(8,128)S(1)}, u32[]{:S(2)}, u32[]{:S(2)}) async-start(f32[128,8,128]{2,1,0:T(8,128)} %bitcast.9), calls=%async_computation.1 | async-start | bytes 1048576 | tf_op jit(solution)/shard_map/all_to_all | solution.py:671
  49.6 15.5 %collective-permute-start.4 = (f32[8,256]{1,0:T(8,128)S(1)}, f32[8,256]{1,0:T(8,128)S(1)}, u32[]{:S(2)}, u32[]{:S(2)}) collective-permute-start(f32[8,256]{1,0:T(8,128)S(1)} %get-tuple-element.88), channel_id=1, source_target_pairs={{0,16},{16,32},{32,48},{48,64},{64,80},{80,96},{96,112},{112,0},{1... | collective-permute-start | bytes 24584 | tf_op jit(solution)/shard_map/ppermute | solution.py:684
  51.3 13.9 %collective-permute-start.5 = (f32[8,256]{1,0:T(8,128)S(1)}, f32[8,256]{1,0:T(8,128)S(1)}, u32[]{:S(2)}, u32[]{:S(2)}) collective-permute-start(f32[8,256]{1,0:T(8,128)S(1)} %get-tuple-element.89), channel_id=1, source_target_pairs={{16,0},{32,16},{48,32},{64,48},{80,64},{96,80},{112,96},{0,112},{1... | collective-permute-start | bytes 24584 | tf_op jit(solution)/shard_map/ppermute | solution.py:685
  51.3 13.8 %collective-permute-start.6 = (f32[8,128]{1,0:T(8,128)S(1)}, f32[8,128]{1,0:T(8,128)S(1)}, u32[]{:S(2)}, u32[]{:S(2)}) collective-permute-start(f32[8,128]{1,0:T(8,128)S(1)} %get-tuple-element.90), channel_id=1, source_target_pairs={{0,1},{1,2},{2,3},{3,4},{4,5},{5,6},{6,7},{7,8},{8,9},{9,10},{10,1... | collective-permute-start | bytes 12296 | tf_op jit(solution)/shard_map/ppermute | solution.py:684
  52.5 12.7 %collective-permute-start.7 = (f32[8,128]{1,0:T(8,128)S(1)}, f32[8,128]{1,0:T(8,128)S(1)}, u32[]{:S(2)}, u32[]{:S(2)}) collective-permute-start(f32[8,128]{1,0:T(8,128)S(1)} %get-tuple-element.91), channel_id=1, source_target_pairs={{1,0},{2,1},{3,2},{4,3},{5,4},{6,5},{7,6},{8,7},{9,8},{10,9},{11,1... | collective-permute-start | bytes 12296 | tf_op jit(solution)/shard_map/ppermute | solution.py:685
  66.1 9.2 %collective-permute-start.8 = (f32[8,256]{1,0:T(8,128)S(1)}, f32[8,256]{1,0:T(8,128)S(1)}, u32[]{:S(2)}, u32[]{:S(2)}) collective-permute-start(f32[8,256]{1,0:T(8,128)S(1)} %get-tuple-element.97), channel_id=1, source_target_pairs={{0,16},{16,32},{32,48},{48,64},{64,80},{80,96},{96,112},{112,0},{1... | collective-permute-start | bytes 24584 | tf_op jit(solution)/shard_map/ppermute | solution.py:684
  68.2 7.2 %collective-permute-start.9 = (f32[8,256]{1,0:T(8,128)S(1)}, f32[8,256]{1,0:T(8,128)S(1)}, u32[]{:S(2)}, u32[]{:S(2)}) collective-permute-start(f32[8,256]{1,0:T(8,128)S(1)} %get-tuple-element.98), channel_id=1, source_target_pairs={{16,0},{32,16},{48,32},{64,48},{80,64},{96,80},{112,96},{0,112},{1... | collective-permute-start | bytes 24584 | tf_op jit(solution)/shard_map/ppermute | solution.py:685
  68.6 6.7 %collective-permute-start.10 = (f32[8,128]{1,0:T(8,128)S(1)}, f32[8,128]{1,0:T(8,128)S(1)}, u32[]{:S(2)}, u32[]{:S(2)}) collective-permute-start(f32[8,128]{1,0:T(8,128)S(1)} %get-tuple-element.99), channel_id=1, source_target_pairs={{0,1},{1,2},{2,3},{3,4},{4,5},{5,6},{6,7},{7,8},{8,9},{9,10},{10,1... | collective-permute-start | bytes 12296 | tf_op jit(solution)/shard_map/ppermute | solution.py:684
  68.6 6.7 %collective-permute-start.11 = (f32[8,128]{1,0:T(8,128)S(1)}, f32[8,128]{1,0:T(8,128)S(1)}, u32[]{:S(2)}, u32[]{:S(2)}) collective-permute-start(f32[8,128]{1,0:T(8,128)S(1)} %get-tuple-element.100), channel_id=1, source_target_pairs={{1,0},{2,1},{3,2},{4,3},{5,4},{6,5},{7,6},{8,7},{9,8},{10,9},{11,1... | collective-permute-start | bytes 12296 | tf_op jit(solution)/shard_map/ppermute | solution.py:685
  78.7 26.2 %all-to-all-start.2 = ((f32[128,8,128]{2,1,0:T(8,128)}), f32[128,8,128]{2,1,0:T(8,128)S(1)}, u32[]{:S(2)}, u32[]{:S(2)}) async-start(f32[128,8,128]{2,1,0:T(8,128)} %bitcast.11), calls=%async_computation.2 | async-start | bytes 1048576 | tf_op jit(solution)/shard_map/all_to_all | solution.py:671
  88.0 16.9 %collective-permute-start.12 = (f32[8,256]{1,0:T(8,128)S(1)}, f32[8,256]{1,0:T(8,128)S(1)}, u32[]{:S(2)}, u32[]{:S(2)}) collective-permute-start(f32[8,256]{1,0:T(8,128)S(1)} %get-tuple-element.106), channel_id=1, source_target_pairs={{0,16},{16,32},{32,48},{48,64},{64,80},{80,96},{96,112},{112,0},{1... | collective-permute-start | bytes 24584 | tf_op jit(solution)/shard_map/ppermute | solution.py:684
  89.7 15.2 %collective-permute-start.13 = (f32[8,256]{1,0:T(8,128)S(1)}, f32[8,256]{1,0:T(8,128)S(1)}, u32[]{:S(2)}, u32[]{:S(2)}) collective-permute-start(f32[8,256]{1,0:T(8,128)S(1)} %get-tuple-element.107), channel_id=1, source_target_pairs={{16,0},{32,16},{48,32},{64,48},{80,64},{96,80},{112,96},{0,112},{1... | collective-permute-start | bytes 24584 | tf_op jit(solution)/shard_map/ppermute | solution.py:685
  89.7 15.2 %collective-permute-start.14 = (f32[8,128]{1,0:T(8,128)S(1)}, f32[8,128]{1,0:T(8,128)S(1)}, u32[]{:S(2)}, u32[]{:S(2)}) collective-permute-start(f32[8,128]{1,0:T(8,128)S(1)} %get-tuple-element.108), channel_id=1, source_target_pairs={{0,1},{1,2},{2,3},{3,4},{4,5},{5,6},{6,7},{7,8},{8,9},{9,10},{10,1... | collective-permute-start | bytes 12296 | tf_op jit(solution)/shard_map/ppermute | solution.py:684
  90.9 14.0 %collective-permute-start.15 = (f32[8,128]{1,0:T(8,128)S(1)}, f32[8,128]{1,0:T(8,128)S(1)}, u32[]{:S(2)}, u32[]{:S(2)}) collective-permute-start(f32[8,128]{1,0:T(8,128)S(1)} %get-tuple-element.109), channel_id=1, source_target_pairs={{1,0},{2,1},{3,2},{4,3},{5,4},{6,5},{7,6},{8,7},{9,8},{10,9},{11,1... | collective-permute-start | bytes 12296 | tf_op jit(solution)/shard_map/ppermute | solution.py:685

commit v6 on v5

--- a/solution.py
+++ b/solution.py
@@ -23,6 +23,7 @@
 LANES = 128
 L, R, C = 8, 64, 256
 PERFS = 256
+BLOCK = 8
 VM = pl.BlockSpec(memory_space=pltpu.VMEM)
 HB = pl.BlockSpec(memory_space=pltpu.HBM)
 
@@ -151,30 +152,44 @@
     return pltpu.roll(x, (LANES - index) % LANES, 1)[:, 0:1]
 
 
-def pack_columns(columns, low, high):
-    n = low.shape[0]
+def is_even(axis):
+    return lax.axis_index(axis) % 2 == 0
+
+
+def by_partner(axis, low, high):
+    even = is_even(axis)
+    return jnp.where(even, high, low), jnp.where(even, low, high)
+
+
+def from_partner(axis, first, second):
+    even = is_even(axis)
+    return jnp.where(even, second, first), jnp.where(even, first, second)
+
+
+def pack_columns(columns, first, second):
+    n = first.shape[0]
     turned = jnp.concatenate([columns, jnp.zeros((LANES - R, LANES), f32)], axis=0).T
-    low[...] = turned[0:n]
-    high[...] = turned[n : 2 * n]
-
-
-def unpack_columns(low, high):
-    n = low.shape[0]
-    rows = jnp.concatenate([low[...], high[...], jnp.zeros((LANES - 2 * n, LANES), f32)], axis=0)
+    first[...], second[...] = by_partner("gy", turned[0:n], turned[n : 2 * n])
+
+
+def unpack_columns(first, second):
+    n = first.shape[0]
+    low, high = from_partner("gy", first[...], second[...])
+    rows = jnp.concatenate([low, high, jnp.zeros((LANES - 2 * n, LANES), f32)], axis=0)
     return rows.T[0:R]
 
 
 def write_faces(step, outs):
-    row_lo, row_hi, col_lo, col_hi = outs
+    row_first, row_second, col_first, col_second = outs
     lane = iota((R, LANES), 1)
     columns = jnp.zeros((R, LANES), f32)
     for l in range(L):
         x = step[l]
-        row_lo[l : l + 1, :] = x[0:1]
-        row_hi[l : l + 1, :] = x[R - 1 : R]
+        pair = by_partner("gx", x[0:1], x[R - 1 : R])
+        row_first[l : l + 1, :], row_second[l : l + 1, :] = pair
         columns = jnp.where(lane == l, x[:, 0:1], columns)
         columns = jnp.where(lane == L + l, x[:, C - 1 : C], columns)
-    pack_columns(columns, col_lo, col_hi)
+    pack_columns(columns, col_first, col_second)
 
 
 def start_copies(pairs, sems):
@@ -194,7 +209,7 @@
 
 
 def faces_kernel(
-    p_h, sw_h, sg_h, perm_h, row_lo, row_hi, col_lo, col_hi, p, sw, sg, perm, sems,
+    p_h, sw_h, sg_h, perm_h, row_first, row_second, col_first, col_second, p, sw, sg, perm, sems,
 ):
     copies = start_copies(((perm_h.at[0:2], perm), (p_h, p), (sw_h, sw), (sg_h, sg)), sems)
     lane = iota((R, LANES), 1)
@@ -202,8 +217,9 @@
     wait_copies(copies[:1])
     for l in range(L):
         n = 3 * L + l
-        row_lo[n : n + 1, :] = perm[0, l, 0:16, :].astype(f32)[0:1]
-        row_hi[n : n + 1, :] = perm[0, l, R - 16 : R, :].astype(f32)[15:16]
+        low = perm[0, l, 0:16, :].astype(f32)[0:1]
+        high = perm[0, l, R - 16 : R, :].astype(f32)[15:16]
+        row_first[n : n + 1, :], row_second[n : n + 1, :] = by_partner("gx", low, high)
         k = perm[1, l].astype(f32)
         columns = jnp.where(lane == n, k[:, 0:1], columns)
         columns = jnp.where(lane == 4 * L + n, k[:, C - 1 : C], columns)
@@ -212,11 +228,11 @@
         for f, ref in enumerate((p, sw, sg)):
             x = ref[l]
             n = f * L + l
-            row_lo[n : n + 1, :] = x[0:1]
-            row_hi[n : n + 1, :] = x[R - 1 : R]
+            pair = by_partner("gx", x[0:1], x[R - 1 : R])
+            row_first[n : n + 1, :], row_second[n : n + 1, :] = pair
             columns = jnp.where(lane == n, x[:, 0:1], columns)
             columns = jnp.where(lane == 4 * L + n, x[:, C - 1 : C], columns)
-    pack_columns(columns, col_lo, col_hi)
+    pack_columns(columns, col_first, col_second)
 
 
 def start_kernel(
@@ -256,32 +272,65 @@
     pass
 
 
+def reciprocal(x):
+    r = pl.reciprocal(x, approx=True)
+    return r * (2.0 - x * r)
+
+
 def transmit(k, k_next):
-    return k * k_next / (k + k_next)
-
-
-def neighbours(field, l, rows, columns, first, last):
-    here = field(l)
-    nexts = shift_rows(here, *rows)
-    nexts += shift_columns(here, lane_of(columns, first), lane_of(columns, last))
-    return nexts + (field(jnp.maximum(l - 1, 0)), field(jnp.minimum(l + 1, L - 1)))
-
-
-def coeff_neighbours(coef, coef_row, coef_col, a, l):
+    return k * k_next * reciprocal(k + k_next)
+
+
+def neighbours(field, l, lo, rows, columns):
+    hi = lo + BLOCK
+    here = field[l, lo:hi, :]
+    if lo > 0:
+        before = field[l, lo - 1 : hi - 1, :]
+    else:
+        before = jnp.concatenate([rows[0], field[l, 0 : hi - 1, :]], axis=0)
+    if hi < R:
+        after = field[l, lo + 1 : hi + 1, :]
+    else:
+        after = jnp.concatenate([field[l, lo + 1 : R, :], rows[1]], axis=0)
+    sides = (field[jnp.maximum(l - 1, 0), lo:hi, :], field[jnp.minimum(l + 1, L - 1), lo:hi, :])
+    return (before, after) + shift_columns(here, *columns) + sides
+
+
+def coeff_neighbours(coef, coef_row, a, l, lo, columns):
     rows = (coef_row[0, a, pl.ds(l, 1), :], coef_row[1, a, pl.ds(l, 1), :])
-    return neighbours(lambda m: coef[a, m], l, rows, coef_col[a], l, 4 * L + l)
-
-
-def inner_neighbours(step, l):
+    ends = [c[lo : lo + BLOCK] for c in columns[a]]
+    return neighbours(coef.at[a], l, lo, rows, ends)
+
+
+def coeff_columns(coef_col, l):
+    return [(lane_of(coef_col[a], l), lane_of(coef_col[a], 4 * L + l)) for a in range(3)]
+
+
+def inner_neighbours(step, l, lo):
     blank = jnp.zeros((1, C), f32)
-    here = step[l]
-    nexts = shift_rows(here, blank, blank) + shift_columns(here, 0.0, 0.0)
-    return nexts + (step[jnp.maximum(l - 1, 0)], step[jnp.minimum(l + 1, L - 1)])
-
-
-def step_neighbours(step, row_lo, row_hi, columns, l):
+    return neighbours(step, l, lo, (blank, blank), (0.0, 0.0))
+
+
+def step_neighbours(step, row_lo, row_hi, columns, l, lo):
     rows = (row_lo[pl.ds(l, 1), :], row_hi[pl.ds(l, 1), :])
-    return neighbours(lambda m: step[m], l, rows, columns, l, L + l)
+    ends = [lane_of(columns, n)[lo : lo + BLOCK] for n in (l, L + l)]
+    return neighbours(step, l, lo, rows, ends)
+
+
+def face_terms(tx, ty, tz, l, rows):
+    return (tx[0, l, rows, :], tx[1, l, rows, :], ty[0, l, rows, :], ty[1, l, rows, :], tz[l, rows, :], tz[l + 1, rows, :])
+
+
+def halves(pairs):
+    parts = []
+    for half in range(2):
+        for a, b, dim in pairs:
+            count = a.shape[dim]
+            middle = L // 2 + 1
+            span = pl.ds(0, middle) if half == 0 else pl.ds(middle, count - middle)
+            index = (slice(None),) * dim + (span,)
+            parts.append((a.at[index], b.at[index]))
+    return parts
 
 
 def add_faces(field, l, low, high, columns):
@@ -298,17 +347,18 @@
 
 
 def setup_kernel(
-    info, row_lo, row_hi, col_lo, col_hi, p, sw, sg, por_h, mass_h, perm_h,
+    info, row_first, row_second, col_first, col_second, p, sw, sg, por_h, mass_h, perm_h,
     coef_row, coef_col, base, head, coef_h, tx_h, ty_h, tz_h, weight_h, res_h, diag_h,
-    por, mass, perm, coef, tx, ty, tz, weight, res, diag, index_sum,
+    por, mass, perm, coef, tx, ty, tz, weight, res, diag, index_sum, row_lo, row_hi,
     sems, sems_t, sems_out,
 ):
     copies = start_copies(((perm_h, perm), (por_h, por), (mass_h, mass)), sems)
     index_sum[...] = scatter(info[0:1].astype(i32), info[2:3]).reshape(L, R, C)
+    row_lo[...], row_hi[...] = from_partner("gx", row_first[...], row_second[...])
     for side, ref in enumerate((row_lo, row_hi)):
         for a, c in enumerate(coeffs_of(ref[0:L], ref[L : 2 * L], ref[2 * L : 3 * L])):
             coef_row[side, a] = c
-    columns = unpack_columns(col_lo, col_hi)
+    columns = unpack_columns(col_first, col_second)
     for a, c in enumerate(
         coeffs_of(columns, pltpu.roll(columns, LANES - L, 1), pltpu.roll(columns, LANES - 2 * L, 1))
     ):
@@ -353,39 +403,44 @@
         )
 
     def second(l, carry):
-        here = p[l]
         rows = (row_lo[pl.ds(l, 1), :], row_hi[pl.ds(l, 1), :])
-        nexts = neighbours(lambda m: p[m], l, rows, columns, l, 4 * L + l)
-        faces = (tx[0, l], tx[1, l], ty[0, l], ty[1, l], tz[l], tz[l + 1])
-        drops = [t * (here - q) for t, q in zip(faces, nexts)]
-        face_sum = sum(faces)
-        drop_sum = sum(drops)
-        porous = volume_scale * por[l]
-        sats = (sw[l], 1.0 - sw[l] - sg[l], sg[l])
-        indices = index_sum[l]
-        diagonals, residuals, inverses, cs = [], [], [], []
-        for a in range(3):
-            c = coef[a, l]
-            ab = c * face_sum
-            net = c * drop_sum
-            for t, d, s in zip(faces, drops, coeff_neighbours(coef, coef_row, coef_col, a, l)):
-                ab = ab + t * s
-                net = net + d * s
-            b = 1.0 + compress[a] * here
-            stored = porous * sats[a]
-            diagonals.append(compress[a] * stored + ab + c * indices)
-            residuals.append(b * stored - volume_scale * mass[a, l] + net + c * (indices * here))
-            inverses.append(1.0 / (porous * b))
-            cs.append(c)
-        inverse_total = 1.0 / sum(d * v for d, v in zip(diagonals, inverses))
-        weights = [v * inverse_total for v in inverses]
-        base[l] = -sum(w * r for w, r in zip(weights, residuals))
-        head[l] = sum(w * c for w, c in zip(weights, cs))
-        for a in range(3):
-            weight[a, l] = weights[a]
-            res[a, l] = residuals[a]
-        diag[0, l] = diagonals[0]
-        diag[1, l] = diagonals[2]
+        ends = lane_of(columns, l), lane_of(columns, 4 * L + l)
+        sides_of = coeff_columns(coef_col, l)
+        for lo in range(0, R, BLOCK):
+            at = slice(lo, lo + BLOCK)
+            here = p[l, at, :]
+            nexts = neighbours(p, l, lo, rows, [e[at] for e in ends])
+            faces = face_terms(tx, ty, tz, l, at)
+            drops = [t * (here - q) for t, q in zip(faces, nexts)]
+            face_sum = sum(faces)
+            drop_sum = sum(drops)
+            porous = volume_scale * por[l, at, :]
+            water, gas = (sw[l, at, :], sg[l, at, :])
+            sats = (water, 1.0 - water - gas, gas)
+            indices = index_sum[l, at, :]
+            diagonals, residuals, inverses, cs = [], [], [], []
+            for a in range(3):
+                c = coef[a, l, at, :]
+                ab = c * face_sum
+                net = c * drop_sum
+                for t, d, s in zip(faces, drops, coeff_neighbours(coef, coef_row, a, l, lo, sides_of)):
+                    ab = ab + t * s
+                    net = net + d * s
+                b = 1.0 + compress[a] * here
+                stored = porous * sats[a]
+                diagonals.append(compress[a] * stored + ab + c * indices)
+                residuals.append(b * stored - volume_scale * mass[a, l, at, :] + net + c * (indices * here))
+                inverses.append(reciprocal(porous * b))
+                cs.append(c)
+            inverse_total = reciprocal(sum(d * v for d, v in zip(diagonals, inverses)))
+            weights = [v * inverse_total for v in inverses]
+            base[l, at, :] = -sum(w * r for w, r in zip(weights, residuals))
+            head[l, at, :] = sum(w * c for w, c in zip(weights, cs))
+            for a in range(3):
+                weight[a, l, at, :] = weights[a]
+                res[a, l, at, :] = residuals[a]
+            diag[0, l, at, :] = diagonals[0]
+            diag[1, l, at, :] = diagonals[2]
         for c in layer_copies(outs, sems_out, l):
             c.start()
         return carry
@@ -397,7 +452,7 @@
 
 
 def first_kernel(
-    got, info, own, base, head, row_lo, row_hi, col_lo, col_hi, mine, well_residual, spread, step,
+    got, info, own, base, head, row_first, row_second, col_first, col_second, mine, well_residual, spread, step,
 ):
     lane = iota((1, LANES), 1)
     sums = jnp.sum(got[...], axis=0, keepdims=True)
@@ -412,7 +467,7 @@
     heads = gather_wells(got[...], well_row >> 4, (well_row & 15) + 32)
     spread[...] = scatter(cell_row, info[2:3] * heads).reshape(L, R, C)
     step[...] = base[...] + head[...] * spread[...]
-    write_faces(step, (row_lo, row_hi, col_lo, col_hi))
+    write_faces(step, (row_first, row_second, col_first, col_second))
 
 
 def first_flow_kernel(info, perf, mine, step, pay):
@@ -435,9 +490,10 @@
     coef, tx, ty, tz, weight, res, residual, gain, sems, sems_out,
 ):
     copies = start_copies(
-        ((coef_h, coef), (tx_h, tx), (ty_h, ty), (tz_h, tz), (weight_h, weight), (res_h, res)), sems
-    )
-    wait_copies(copies)
+        halves(((coef_h, coef, 1), (tx_h, tx, 1), (ty_h, ty, 1), (tz_h, tz, 0), (weight_h, weight, 1), (res_h, res, 1))),
+        sems,
+    )
+    wait_copies(copies[:6])
 
     def outs(l):
         return (
@@ -445,49 +501,53 @@
         )
 
     def layer(l, ends):
-        nexts = inner_neighbours(step, l)
-        faces = (tx[0, l], tx[1, l], ty[0, l], ty[1, l], tz[l], tz[l + 1])
-        wells = spread[l]
-        mixes = [head[l]] * 6
-        for a in range(3):
-            w = weight[a, l]
-            sides = coeff_neighbours(coef, coef_row, coef_col, a, l)
-            mixes = [m + w * s for m, s in zip(mixes, sides)]
-            residual[a, l] = res[a, l] - coef[a, l] * wells
-        total = step[l]
-        gains = []
-        for j in range(6):
-            g = faces[j] * mixes[j]
-            gain[j, l] = g
-            total = total + g * nexts[j]
-            gains.append(g)
-        ahead[l] = total
-        end_row[0, pl.ds(l, 1), :] = gains[0][0:1]
-        end_row[1, pl.ds(l, 1), :] = gains[1][R - 1 : R]
+        sides_of = coeff_columns(coef_col, l)
+        for lo in range(0, R, BLOCK):
+            at = slice(lo, lo + BLOCK)
+            nexts = inner_neighbours(step, l, lo)
+            faces = face_terms(tx, ty, tz, l, at)
+            wells = spread[l, at, :]
+            mixes = [head[l, at, :]] * 6
+            for a in range(3):
+                w = weight[a, l, at, :]
+                sides = coeff_neighbours(coef, coef_row, a, l, lo, sides_of)
+                mixes = [m + w * s for m, s in zip(mixes, sides)]
+                residual[a, l, at, :] = res[a, l, at, :] - coef[a, l, at, :] * wells
+            total = step[l, at, :]
+            for j in range(6):
+                g = faces[j] * mixes[j]
+                gain[j, l, at, :] = g
+                total = total + g * nexts[j]
+            ahead[l, at, :] = total
+        end_row[0, pl.ds(l, 1), :] = gain[0, l, 0:1, :]
+        end_row[1, pl.ds(l, 1), :] = gain[1, l, R - 1 : R, :]
         for c in layer_copies(outs, sems_out, l):
             c.start()
-        return end_columns(ends, l, gains[2][:, 0:1], gains[3][:, C - 1 : C])
-
-    end_col[...] = lax.fori_loop(0, L, layer, jnp.zeros((R, LANES), f32))
+        return end_columns(ends, l, gain[2, l, :, 0:LANES][:, 0:1], gain[3, l, :, C - LANES : C][:, LANES - 1 : LANES])
+
+    ends = lax.fori_loop(0, L // 2, layer, jnp.zeros((R, LANES), f32))
+    wait_copies(copies[6:])
+    end_col[...] = lax.fori_loop(L // 2, L, layer, ends)
     for l in range(L):
         wait_copies(layer_copies(outs, sems_out, l))
 
 
 def second_kernel(
-    got, info, ahead, head, end_row, end_col, row_lo, row_hi, col_lo, col_hi,
-    out_row_lo, out_row_hi, out_col_lo, out_col_hi, step,
+    got, info, ahead, head, end_row, end_col, row_first, row_second, col_first, col_second,
+    out_row_first, out_row_second, out_col_first, out_col_second, step,
 ):
     cell_row = info[0:1].astype(i32)
     well_row = info[1:2].astype(i32)
     moves = gather_wells(tile_of(got, 5), well_row >> 4, (well_row & 15) + 16)
     wells = scatter(cell_row, info[2:3] * moves).reshape(L, R, C)
     step[...] = ahead[...] + head[...] * wells
-    columns = end_col[...] * unpack_columns(col_lo, col_hi)
+    columns = end_col[...] * unpack_columns(col_first, col_second)
+    low, high = from_partner("gx", row_first[...], row_second[...])
+    low = end_row[0] * low
+    high = end_row[1] * high
     for l in range(L):
-        low = end_row[0, l : l + 1, :] * row_lo[l : l + 1, :]
-        high = end_row[1, l : l + 1, :] * row_hi[l : l + 1, :]
-        add_faces(step, l, low, high, columns)
-    write_faces(step, (out_row_lo, out_row_hi, out_col_lo, out_col_hi))
+        add_faces(step, l, low[l : l + 1], high[l : l + 1], columns)
+    write_faces(step, (out_row_first, out_row_second, out_col_first, out_col_second))
 
 
 def wells_kernel(
@@ -513,21 +573,24 @@
 
 
 def third_kernel(
-    spread, old, base, gain, head, row_lo, row_hi, col_lo, col_hi,
-    out_row_lo, out_row_hi, out_col_lo, out_col_hi, step,
-):
-    columns = unpack_columns(col_lo, col_hi)
+    spread, old, base, gain, head, row_first, row_second, col_first, col_second,
+    out_row_first, out_row_second, out_col_first, out_col_second, step, row_lo, row_hi,
+):
+    columns = unpack_columns(col_first, col_second)
+    row_lo[...], row_hi[...] = from_partner("gx", row_first[...], row_second[...])
 
     def layer(l, carry):
-        nexts = step_neighbours(old, row_lo, row_hi, columns, l)
-        total = base[l] + head[l] * spread[l]
-        for j in range(6):
-            total = total + gain[j, l] * nexts[j]
-        step[l] = total
+        for lo in range(0, R, BLOCK):
+            at = slice(lo, lo + BLOCK)
+            nexts = step_neighbours(old, row_lo, row_hi, columns, l, lo)
+            total = base[l, at, :] + head[l, at, :] * spread[l, at, :]
+            for j in range(6):
+                total = total + gain[j, l, at, :] * nexts[j]
+            step[l, at, :] = total
         return carry
 
     lax.fori_loop(0, L, layer, 0)
-    write_faces(step, (out_row_lo, out_row_hi, out_col_lo, out_col_hi))
+    write_faces(step, (out_row_first, out_row_second, out_col_first, out_col_second))
 
 
 def third_flow_kernel(info, perf, parts, step, pay):
@@ -547,67 +610,74 @@
     p, por, coef, tx, ty, tz, weight, diag, residual, ahead, slope, sems, sems_out,
 ):
     copies = start_copies(
-        (
-            (p_h, p), (por_h, por), (coef_h, coef), (tx_h, tx), (ty_h, ty), (tz_h, tz),
-            (weight_h, weight), (diag_h, diag), (residual_h, residual),
+        halves(
+            (
+                (p_h, p, 0), (por_h, por, 0), (coef_h, coef, 1), (tx_h, tx, 1), (ty_h, ty, 1), (tz_h, tz, 0),
+                (weight_h, weight, 1), (diag_h, diag, 1), (residual_h, residual, 1),
+            )
         ),
         sems,
     )
-    wait_copies(copies)
+    wait_copies(copies[:9])
 
     def outs(l):
         return ((ahead.at[:, l], ahead_h.at[:, l]), (slope.at[:, l], slope_h.at[:, l]))
 
     def layer(l, ends):
-        nexts = inner_neighbours(step, l)
-        faces = (tx[0, l], tx[1, l], ty[0, l], ty[1, l], tz[l], tz[l + 1])
-        flows = [t * q for t, q in zip(faces, nexts)]
-        flow_sum = sum(flows)
-        rights, cs, sides = [], [], []
-        for a in range(3):
-            c = coef[a, l]
-            total = c * flow_sum - residual[a, l]
-            sides.append(coeff_neighbours(coef, coef_row, coef_col, a, l))
-            for v, s in zip(flows, sides[a]):
-                total = total + v * s
-            rights.append(total)
-            cs.append(c)
-        z = sum(weight[a, l] * rights[a] for a in range(3))
-        h = head[l]
-        porous = volume_scale * por[l]
-        inverse_water = 1.0 / (porous * (1.0 + compress[0] * p[l]))
-        inverse_gas = 1.0 / (porous * (1.0 + compress[2] * p[l]))
-        ahead[0, l] = z
-        ahead[1, l] = (rights[0] - diag[0, l] * z) * inverse_water
-        ahead[2, l] = (rights[2] - diag[1, l] * z) * inverse_gas
-        slope[0, l] = (cs[0] - diag[0, l] * h) * inverse_water
-        slope[1, l] = (cs[2] - diag[1, l] * h) * inverse_gas
+        sides_of = coeff_columns(coef_col, l)
+        gains = lane_of(gain_col[...], l), lane_of(gain_col[...], L + l)
+        pairs = [([], []), ([], [])]
+        for lo in range(0, R, BLOCK):
+            at = slice(lo, lo + BLOCK)
+            nexts = inner_neighbours(step, l, lo)
+            faces = face_terms(tx, ty, tz, l, at)
+            flows = [t * q for t, q in zip(faces, nexts)]
+            flow_sum = sum(flows)
+            rights, cs, sides = [], [], []
+            for a in range(3):
+                c = coef[a, l, at, :]
+                total = c * flow_sum - residual[a, l, at, :]
+                sides.append(coeff_neighbours(coef, coef_row, a, l, lo, sides_of))
+                for v, s in zip(flows, sides[a]):
+                    total = total + v * s
+                rights.append(total)
+                cs.append(c)
+            z = sum(weight[a, l, at, :] * rights[a] for a in range(3))
+            h = head[l, at, :]
+            porous = volume_scale * por[l, at, :]
+            inverses = [reciprocal(porous * (1.0 + compress[a] * p[l, at, :])) for a in (0, 2)]
+            ahead[0, l, at, :] = z
+            for n, a in enumerate((0, 2)):
+                d = diag[n, l, at, :]
+                inverse = inverses[n]
+                ahead[1 + n, l, at, :] = (rights[a] - d * z) * inverse
+                slope[n, l, at, :] = (cs[a] - d * h) * inverse
+                for side in range(2):
+                    if lo == (0, R - BLOCK)[side]:
+                        row = slice(0, 1) if side == 0 else slice(BLOCK - 1, BLOCK)
+                        face = faces[side][row] * (cs[a][row] + sides[a][side][row])
+                        end_row[side, n, pl.ds(l, 1), :] = (
+                            face - d[row] * gain_row[side, pl.ds(l, 1), :]
+                        ) * inverse[row]
+                    col = slice(0, 1) if side == 0 else slice(C - 1, C)
+                    face = faces[2 + side][:, col] * (cs[a][:, col] + sides_of[a][side][at])
+                    pairs[n][side].append((face - d[:, col] * gains[side][at]) * inverse[:, col])
         for c in layer_copies(outs, sems_out, l):
             c.start()
-        columns = lane_of(gain_col[...], l), lane_of(gain_col[...], L + l)
-        done = []
-        for n, (a, inverse) in enumerate(((0, inverse_water), (2, inverse_gas))):
-            d = diag[n, l]
-            for side, row in enumerate((slice(0, 1), slice(R - 1, R))):
-                face = faces[side][row] * (cs[a][row] + sides[a][side][row])
-                end_row[side, n, pl.ds(l, 1), :] = (
-                    face - d[row] * gain_row[side, pl.ds(l, 1), :]
-                ) * inverse[row]
-            pair = []
-            for side, col in enumerate((slice(0, 1), slice(C - 1, C))):
-                face = faces[2 + side][:, col] * (cs[a][:, col] + sides[a][2 + side][:, col])
-                pair.append((face - d[:, col] * columns[side]) * inverse[:, col])
-            done.append(end_columns(ends[n], l, *pair))
-        return tuple(done)
+        return tuple(
+            end_columns(ends[n], l, *(jnp.concatenate(part, axis=0) for part in pairs[n])) for n in range(2)
+        )
 
     blank = jnp.zeros((R, LANES), f32)
-    end_col[0], end_col[1] = lax.fori_loop(0, L, layer, (blank, blank))
+    ends = lax.fori_loop(0, L // 2, layer, (blank, blank))
+    wait_copies(copies[9:])
+    end_col[0], end_col[1] = lax.fori_loop(L // 2, L, layer, ends)
     for l in range(L):
         wait_copies(layer_copies(outs, sems_out, l))
 
 
 def final_kernel(
-    got, info, table, mine, head, gain_row, gain_col, end_row, end_col, row_lo, row_hi, col_lo, col_hi,
+    got, info, table, mine, head, gain_row, gain_col, end_row, end_col, row_first, row_second, col_first, col_second,
     ahead_h, slope_h, update_h, moved, ahead, slope, update, sems, sems_out,
 ):
     copies = start_copies(((ahead_h, ahead), (slope_h, slope)), sems)
@@ -619,7 +689,8 @@
     moves = jnp.where(valid, (sum_parts(got) + table[0]) * table[1], 0.0)
     values = gather_wells(moves, well_row >> 4, well_row & 15)
     wells = scatter(cell_row, info[2:3] * values).reshape(L, R, C)
-    halo = unpack_columns(col_lo, col_hi)
+    halo = unpack_columns(col_first, col_second)
+    lows, highs = from_partner("gx", row_first[...], row_second[...])
     columns = (gain_col[...] * halo, end_col[0] * halo, end_col[1] * halo)
     wait_copies(copies)
 
@@ -627,8 +698,8 @@
         return ((update.at[:, l], update_h.at[:, l]),)
 
     for l in range(L):
-        low = row_lo[l : l + 1, :]
-        high = row_hi[l : l + 1, :]
+        low = lows[l : l + 1]
+        high = highs[l : l + 1]
         for n in range(3):
             rows = [gain_row[side, l : l + 1, :] if n == 0 else end_row[side, n - 1, l : l + 1, :] for side in range(2)]
             update[n, l] = ahead[n, l] + (head[l] if n == 0 else slope[n - 1, l]) * wells[l]
@@ -676,13 +747,12 @@
 
 
 def halo_of(faces):
-    row_lo, row_hi, col_lo, col_hi = faces
+    row_first, row_second, col_first, col_second = faces
     got = []
-    for axis, low, high in (("gx", row_lo, row_hi), ("gy", col_lo, col_hi)):
+    for axis, first, second in (("gx", row_first, row_second), ("gy", col_first, col_second)):
         count = lax.axis_size(axis)
-        up = [(i, (i + 1) % count) for i in range(count)]
-        got.append(lax.ppermute(high, axis, up))
-        got.append(lax.ppermute(low, axis, [(j, i) for i, j in up]))
+        got.append(lax.ppermute(first, axis, [(i, i ^ 1) for i in range(count)]))
+        got.append(lax.ppermute(second, axis, [(i, (i - 1 + 2 * (i % 2)) % count) for i in range(count)]))
     return got
 
 
@@ -700,7 +770,7 @@
     halo = halo_of(faces)
     pay, perf, info, own = call(
         start_kernel,
-        (((DEVICES, LANES), None), ((8, PERFS), VM), ((8, PERFS), VM), (SMALL, VM)),
+        (((DEVICES, LANES), VM), ((8, PERFS), VM), ((8, PERFS), VM), (SMALL, VM)),
         [HB] * 5 + [VM] * 3,
         (
             perf_cell.reshape(1, PERFS), perf_well.reshape(1, PERFS), perf_index.reshape(1, PERFS),
@@ -711,12 +781,12 @@
             (1, WELL_DEV), (1, WELL_DEV), sem((5,)),
         ],
     )
-    pay = pl.pallas_call(
+    pay, *halo = pl.pallas_call(
         after_kernel,
-        out_shape=jax.ShapeDtypeStruct(pay.shape, f32),
+        out_shape=tuple(pltpu.VMEM(x.shape, f32) for x in (pay, *halo)),
         in_specs=[pl.BlockSpec(memory_space=pl.ANY)] * 5,
-        out_specs=pl.BlockSpec(memory_space=pl.ANY),
-        input_output_aliases={0: 0},
+        out_specs=(pl.BlockSpec(memory_space=pl.ANY),) * 5,
+        input_output_aliases={n: n for n in range(5)},
     )(pay, *halo)
     got = exchange(pay)
     coef_row, coef_col, base, head, coef, tx, ty, tz, weight, res, diag = call(
@@ -729,7 +799,7 @@
         (info, *halo, p, sw, sg, porosity, old_mass, perm),
         [
             FIELD, THREE, pltpu.VMEM(THREE, bf16), THREE, TWO, TWO, FACED,
-            THREE, THREE, TWO, FIELD, sem((3,)), sem((4,)), sem((3, L)),
+            THREE, THREE, TWO, FIELD, (4 * L, C), (4 * L, C), sem((3,)), sem((4,)), sem((3, L)),
         ],
         flops=400 * L * R * C,
     )
@@ -748,7 +818,7 @@
         ((FIELD, VM), ((2, L, C), VM), ((R, LANES), VM), (THREE, HB), (SIX, HB)),
         [VM] * 5 + [HB] * 6,
         (coef_row, coef_col, head, spread, start, *fields, res),
-        [THREE, TWO, TWO, FACED, THREE, THREE, THREE, SIX, sem((6,)), sem((2, L))],
+        [THREE, TWO, TWO, FACED, THREE, THREE, THREE, SIX, sem((12,)), sem((2, L))],
         flops=100 * L * R * C,
     )
     *faces, step = call(
@@ -770,6 +840,7 @@
         FACES + ((FIELD, VM),),
         [VM] * 9,
         (spread, step, start, gain_near, head, *halo),
+        [(L, C), (L, C)],
     )
     halo = halo_of(faces)
     (pay,) = call(third_flow_kernel, (PAY,), [VM] * 4, (info, perf, parts, step))
@@ -779,7 +850,7 @@
         (((2, 2, L, C), VM), ((2, R, LANES), VM), (THREE, HB), (TWO, HB)),
         [VM] * 6 + [HB] * 9,
         (coef_row, coef_col, head, step, gain_row, gain_col, pressure, porosity, *fields, diag, residual),
-        [FIELD, FIELD, THREE, TWO, TWO, FACED, THREE, TWO, THREE, THREE, TWO, sem((9,)), sem((2, L))],
+        [FIELD, FIELD, THREE, TWO, TWO, FACED, THREE, TWO, THREE, THREE, TWO, sem((18,)), sem((2, L))],
         flops=150 * L * R * C,
     )
     update, moved = call(

time: 111 us -> 97.8 us (0.88)
  starting transfers between devices: 57.7 us -> 50.2 us
  Pallas kernels: 45.9 us -> 41.4 us
  local copies, waits for them, and re-layouts: 4.17 us -> 0 us
  waiting for transfers between devices: 0.05 us -> 3.91 us
    all_to_all x3, starting transfers between devices: 27.9 us -> 22.4 us  [exchange(): return lax.all_to_all(array, AXES, split_axis=0, concat_axis=0, tiled=True)]
    pallas_call x12, Pallas kernels: 45.9 us -> 41.4 us  [call(): pl.pallas_call(kernel, out_shape=shapes, in_specs=ins, out_specs=tuple((w...]
    unnamed x18 -> x0, local copies, waits for them, and re-layouts: 4.17 us -> none
    ppermute x16, waiting for transfers between devices: 0.04 us -> 3.25 us  [the longest x8 3.23 us: halo_of(): lax.ppermute(second, axis, [(i, (i - 1 + 2 * (i % 2)) % count) for i in r...]
    ppermute x16, starting transfers between devices: 29.8 us -> 27.9 us  [the longest x8 18 us: halo_of(): lax.ppermute(second, axis, [(i, (i - 1 + 2 * (i % 2)) % count) for i in r...]
  transfers between devices with their start and end apart: 19 -> 19, of which waited for: 0 -> 2; matrix products, arithmetic and copies ran while one was open for 0% -> 0% of each run, Pallas kernels for 30% -> 29%
where the time goes in v6:
time: 97.8 us; the launch traced here: 96.5 us
  starting transfers between devices  50.2 us (51%)
  Pallas kernels  41.4 us (42%)
  waiting for transfers between devices  3.91 us (4%)
  between operations  1 us (1%)
    pallas_call x12, Pallas kernels, call(): pl.pallas_call(kernel, out_shape=shapes, in_specs=ins, out_specs=tuple((w...  41.4 us
    all_to_all x3, starting transfers between devices, exchange(): return lax.all_to_all(array, AXES, split_axis=0, concat_axis=0, tiled=True)  22.4 us
    ppermute x8, starting transfers between devices, halo_of(): lax.ppermute(second, axis, [(i, (i - 1 + 2 * (i % 2)) % count) for i in r...  18 us
    ppermute x8, starting transfers between devices, halo_of(): got.append(lax.ppermute(first, axis, [(i, i ^ 1) for i in range(count)]))  9.85 us
    ppermute x8, waiting for transfers between devices, halo_of(): lax.ppermute(second, axis, [(i, (i - 1 + 2 * (i % 2)) % count) for i in r...  3.23 us
  transfers between devices with their start and end apart: 19, of which 2 were waited for; matrix products, arithmetic and copies ran while one was open for 0% of the time, Pallas kernels for 29%

profile of v6, /device:TPU:1, one launch (start us, length us, event | category | flops | bytes accessed | tf_op | source)
XLA Modules:
  0.0 96.5 jit_solution(13176192533645567520)
XLA Ops:
  0.6 2.2 %shard_map.138 = (f32[32,256]{1,0:T(8,128)S(1)}, f32[32,256]{1,0:T(8,128)S(1)}, f32[32,128]{1,0:T(8,128)S(1)}, f32[32,128]{1,0:T(8,128)S(1)}, f32[8,64,256]{2,1,...) custom-call(f32[8,64,256]{2,1,0:T(8,128)} %p_h.3, f32[8,64,256]{2,1,0:T(8,128)} %sw_h.1, ...), custom_call_target="tpu_custom_call" | custom-call | bytes 3145728 | tf_op jit(solution)/shard_map/pallas_call | solution.py:721
  2.8 1.5 %collective-permute-start = (f32[32,256]{1,0:T(8,128)S(1)}, f32[32,256]{1,0:T(8,128)S(1)}, u32[]{:S(2)}, u32[]{:S(2)}) collective-permute-start(f32[32,256]{1,0:T(8,128)S(1)} %get-tuple-element.69), channel_id=1, source_target_pairs={{0,16},{16,0},{32,48},{48,32},{64,80},{80,64},{96,112},{112,96},{1... | collective-permute-start | bytes 98312 | tf_op jit(solution)/shard_map/ppermute | solution.py:754
  4.3 1.4 %collective-permute-start.1 = (f32[32,256]{1,0:T(8,128)S(1)}, f32[32,256]{1,0:T(8,128)S(1)}, u32[]{:S(2)}, u32[]{:S(2)}) collective-permute-start(f32[32,256]{1,0:T(8,128)S(1)} %get-tuple-element.70), channel_id=1, source_target_pairs={{0,112},{16,32},{32,16},{48,64},{64,48},{80,96},{96,80},{112,0},{1... | collective-permute-start | bytes 98312 | tf_op jit(solution)/shard_map/ppermute | solution.py:755
  5.7 1.2 %collective-permute-start.2 = (f32[32,128]{1,0:T(8,128)S(1)}, f32[32,128]{1,0:T(8,128)S(1)}, u32[]{:S(2)}, u32[]{:S(2)}) collective-permute-start(f32[32,128]{1,0:T(8,128)S(1)} %get-tuple-element.71), channel_id=1, source_target_pairs={{0,1},{1,0},{2,3},{3,2},{4,5},{5,4},{6,7},{7,6},{8,9},{9,8},{10,11... | collective-permute-start | bytes 49160 | tf_op jit(solution)/shard_map/ppermute | solution.py:754
  6.9 5.3 %collective-permute-start.3 = (f32[32,128]{1,0:T(8,128)S(1)}, f32[32,128]{1,0:T(8,128)S(1)}, u32[]{:S(2)}, u32[]{:S(2)}) collective-permute-start(f32[32,128]{1,0:T(8,128)S(1)} %get-tuple-element.72), channel_id=1, source_target_pairs={{0,15},{1,2},{2,1},{3,4},{4,3},{5,6},{6,5},{7,8},{8,7},{9,10},{10,... | collective-permute-start | bytes 49160 | tf_op jit(solution)/shard_map/ppermute | solution.py:755
  12.2 2.7 %shard_map.139 = (f32[128,128]{1,0:T(8,128)}, f32[8,256]{1,0:T(8,128)S(1)}, f32[8,256]{1,0:T(8,128)S(1)}, f32[8,128]{1,0:T(8,128)S(1)}) custom-call(s32[1,256]{1,0:T(1,128)} %bitcast.19, s32[1,256]{1,0:T(1,128)} %bitcast.20, f32[1,256]{1,0:T(1,128)} %bitcast.21, f32[1,16]{1,0:T(1,128)} %bitcast.22, f32[1,16]{1,0:T(1,128)} %bitcast.23, ...), custom_call_target="tpu_custom_call" | custom-call | bytes 1576064 | tf_op jit(solution)/shard_map/pallas_call | solution.py:721
  14.8 0.0 collective-permute-done.2.refs_2_
  14.9 0.0 collective-permute-done.3.refs_3_
  14.9 0.0 collective-permute-done.refs_0_
  14.9 0.0 collective-permute-done.1.refs_1_
  14.9 7.8 %all-to-all-start = ((f32[128,1,128]{2,1,0:T(1,128)}), f32[128,1,128]{2,1,0:T(1,128)S(1)}, u32[]{:S(2)}, u32[]{:S(2)}) async-start(f32[128,1,128]{2,1,0:T(1,128)} %bitcast.6), calls=%async_computation | async-start | bytes 131072 | tf_op jit(solution)/shard_map/all_to_all | solution.py:742
  22.7 9.0 %shard_map.141 = (f32[2,3,8,256]{3,2,1,0:T(8,128)S(1)}, f32[3,64,128]{2,1,0:T(8,128)S(1)}, f32[8,64,256]{2,1,0:T(8,128)S(1)}, f32[8,64,256]{2,1,0:T(8,128)S(1)},...) custom-call(f32[8,256]{1,0:T(8,128)S(1)} %get-tuple-element.67.info,, ...), custom_call_target="tpu_custom_call" | custom-call | flops 52428800 | bytes 5349376 | tf_op jit(solution)/shard_map/pallas_call | solution.py:721
  31.8 0.7 all-to-all-done
  32.4 1.2 %shard_map.142 = (f32[8,256]{1,0:T(8,128)S(1)}, f32[8,256]{1,0:T(8,128)S(1)}, f32[8,128]{1,0:T(8,128)S(1)}, f32[8,128]{1,0:T(8,128)S(1)}, f32[8,128]{1,0:T(8,128...) custom-call(f32[128,128]{1,0:T(8,128)S(1)} %bitcast.18, ...), custom_call_target="tpu_custom_call" | custom-call | bytes 1126400 | tf_op jit(solution)/shard_map/pallas_call | solution.py:721
  33.6 1.7 %shard_map.144 = f32[1024,128]{1,0:T(8,128)} custom-call(f32[8,256]{1,0:T(8,128)S(1)} %get-tuple-element.67.info, f32[8,256]{1,0:T(8,128)S(1)} %get-tuple-element.93.perf, f32[8,128]{1,0:T(8,128)S(1)} %get-tuple-element.94.mine, f32[8,64,256]{2,1,0:T(8,128)S(1)} %get-tuple-element.84.step.base), custom_call_target="tpu_custom_call" | custom-call | bytes 544768 | tf_op jit(solution)/shard_map/pallas_call | solution.py:721
  35.3 9.1 %all-to-all-start.1 = ((f32[128,8,128]{2,1,0:T(8,128)}), f32[128,8,128]{2,1,0:T(8,128)S(1)}, u32[]{:S(2)}, u32[]{:S(2)}) async-start(f32[128,8,128]{2,1,0:T(8,128)} %bitcast.9), calls=%async_computation.1 | async-start | bytes 1048576 | tf_op jit(solution)/shard_map/all_to_all | solution.py:742
  44.4 1.1 %collective-permute-start.4 = (f32[8,256]{1,0:T(8,128)S(1)}, f32[8,256]{1,0:T(8,128)S(1)}, u32[]{:S(2)}, u32[]{:S(2)}) collective-permute-start(f32[8,256]{1,0:T(8,128)S(1)} %get-tuple-element.98), channel_id=1, source_target_pairs={{0,16},{16,0},{32,48},{48,32},{64,80},{80,64},{96,112},{112,96},{1... | collective-permute-start | bytes 24584 | tf_op jit(solution)/shard_map/ppermute | solution.py:754
  45.6 0.7 collective-permute-start.5
  46.3 1.2 %collective-permute-start.6 = (f32[8,128]{1,0:T(8,128)S(1)}, f32[8,128]{1,0:T(8,128)S(1)}, u32[]{:S(2)}, u32[]{:S(2)}) collective-permute-start(f32[8,128]{1,0:T(8,128)S(1)} %get-tuple-element.100), channel_id=1, source_target_pairs={{0,1},{1,0},{2,3},{3,2},{4,5},{5,4},{6,7},{7,6},{8,9},{9,8},{10,11... | collective-permute-start | bytes 12296 | tf_op jit(solution)/shard_map/ppermute | solution.py:754
  47.5 4.7 %collective-permute-start.7 = (f32[8,128]{1,0:T(8,128)S(1)}, f32[8,128]{1,0:T(8,128)S(1)}, u32[]{:S(2)}, u32[]{:S(2)}) collective-permute-start(f32[8,128]{1,0:T(8,128)S(1)} %get-tuple-element.101), channel_id=1, source_target_pairs={{0,15},{1,2},{2,1},{3,4},{4,3},{5,6},{6,5},{7,8},{8,7},{9,10},{10,... | collective-permute-start | bytes 12296 | tf_op jit(solution)/shard_map/ppermute | solution.py:755
  52.1 6.7 %shard_map.143 = (f32[8,64,256]{2,1,0:T(8,128)S(1)}, f32[2,8,256]{2,1,0:T(8,128)S(1)}, f32[64,128]{1,0:T(8,128)S(1)}, f32[3,8,64,256]{3,2,1,0:T(8,128)}, f32[6,8,64,256]{3,2,1,0:T(8,128)}) custom-call(f32[2,3,8,256]{3,2,1,0:T(8,128)S(1)} %get-tuple-element.77.coef_row, f32[3,64,128]{2,1,0:T(8,128)S(1)} %get-tuple-element.78.coef_col, ...), custom_call_target="tpu_custom_call" | custom-call | flops 13107200 | bytes 9125888 | tf_op jit(solution)/shard_map/pallas_call | solution.py:721
  58.9 0.0 collective-permute-done.6.col_first
  58.9 0.0 collective-permute-done.7.col_second
  58.9 0.0 collective-permute-done.4.row_first
  58.9 0.0 collective-permute-done.5.row_second
  58.9 0.0 all-to-all-done.1
  58.9 0.9 shard_map.145
  59.8 2.3 %collective-permute-start.8 = (f32[8,256]{1,0:T(8,128)S(1)}, f32[8,256]{1,0:T(8,128)S(1)}, u32[]{:S(2)}, u32[]{:S(2)}) collective-permute-start(f32[8,256]{1,0:T(8,128)S(1)} %get-tuple-element.107), channel_id=1, source_target_pairs={{0,16},{16,0},{32,48},{48,32},{64,80},{80,64},{96,112},{112,96},{1... | collective-permute-start | bytes 24584 | tf_op jit(solution)/shard_map/ppermute | solution.py:754
  62.1 0.0 collective-permute-start.9
  62.1 0.0 collective-permute-start.10
  62.1 0.6 collective-permute-start.11
  62.8 1.9 %shard_map.146 = (f32[2,128,128]{2,1,0:T(8,128)S(1)}, f32[8,128]{1,0:T(8,128)S(1)}, f32[8,64,256]{2,1,0:T(8,128)S(1)}, f32[6,8,64,256]{3,2,1,0:T(8,128)S(1)}) custom-call(f32[1024,128]{1,0:T(8,128)S(1)} %bitcast.16, f32[8,256]{1,0:T(8,128)S(1)} %get-tuple-element.67.info, f32[8,256]{1,0:T(8,128)S(1)} %get-tuple-element.93.perf, ...), custom_call_target="tpu_custom_call" | custom-call | bytes 4210688 | tf_op jit(solution)/shard_map/pallas_call | solution.py:721
  64.7 0.0 collective-permute-done.10.col_first
  64.7 3.2 %collective-permute-done.11.col_second = f32[8,128]{1,0:T(8,128)S(1)} collective-permute-done((f32[8,128]{1,0:T(8,128)S(1)}, f32[8,128]{1,0:T(8,128)S(1)}, u32[]{:S(2)}, u32[]{:S(2)}) %collective-permute-start.11) | collective-permute-done | bytes 4128 | tf_op jit(solution)/shard_map/ppermute | solution.py:755
  67.9 0.0 collective-permute-done.8.row_first
  67.9 0.0 collective-permute-done.9.row_second
  67.9 1.7 %shard_map.147 = (f32[8,256]{1,0:T(8,128)S(1)}, f32[8,256]{1,0:T(8,128)S(1)}, f32[8,128]{1,0:T(8,128)S(1)}, f32[8,128]{1,0:T(8,128)S(1)}, f32[8,64,256]{2,1,0:T(8,128)S(1)}) custom-call(f32[8,64,256]{2,1,0:T(8,128)S(1)} %get-tuple-element.105.spread, f32[8,64,256]{2,1,0:T(8,128)S(1)} %get-tuple-element.102.step.old, ...), custom_call_target="tpu_custom_call" | custom-call | bytes 5267456 | tf_op jit(solution)/shard_map/pallas_call | solution.py:721
  69.6 1.6 %shard_map.148 = f32[1024,128]{1,0:T(8,128)} custom-call(f32[8,256]{1,0:T(8,128)S(1)} %get-tuple-element.67.info, f32[8,256]{1,0:T(8,128)S(1)} %get-tuple-element.93.perf, f32[8,128]{1,0:T(8,128)S(1)} %get-tuple-element.104.parts, f32[8,64,256]{2,1,0:T(8,128)S(1)} %get-tuple-element.111.step), custom_call_target="tpu_custom_call" | custom-call | bytes 544768 | tf_op jit(solution)/shard_map/pallas_call | solution.py:721
  71.2 5.4 %all-to-all-start.2 = ((f32[128,8,128]{2,1,0:T(8,128)}), f32[128,8,128]{2,1,0:T(8,128)S(1)}, u32[]{:S(2)}, u32[]{:S(2)}) async-start(f32[128,8,128]{2,1,0:T(8,128)} %bitcast.11), calls=%async_computation.2 | async-start | bytes 1048576 | tf_op jit(solution)/shard_map/all_to_all | solution.py:742
  76.7 1.3 %collective-permute-start.12 = (f32[8,256]{1,0:T(8,128)S(1)}, f32[8,256]{1,0:T(8,128)S(1)}, u32[]{:S(2)}, u32[]{:S(2)}) collective-permute-start(f32[8,256]{1,0:T(8,128)S(1)} %get-tuple-element.116), channel_id=1, source_target_pairs={{0,16},{16,0},{32,48},{48,32},{64,80},{80,64},{96,112},{112,96},{1... | collective-permute-start | bytes 24584 | tf_op jit(solution)/shard_map/ppermute | solution.py:754
  78.0 0.6 collective-permute-start.13
  78.6 1.2 %collective-permute-start.14 = (f32[8,128]{1,0:T(8,128)S(1)}, f32[8,128]{1,0:T(8,128)S(1)}, u32[]{:S(2)}, u32[]{:S(2)}) collective-permute-start(f32[8,128]{1,0:T(8,128)S(1)} %get-tuple-element.118), channel_id=1, source_target_pairs={{0,1},{1,0},{2,3},{3,2},{4,5},{5,4},{6,7},{7,6},{8,9},{9,8},{10,11... | collective-permute-start | bytes 12296 | tf_op jit(solution)/shard_map/ppermute | solution.py:754
  79.8 4.7 %collective-permute-start.15 = (f32[8,128]{1,0:T(8,128)S(1)}, f32[8,128]{1,0:T(8,128)S(1)}, u32[]{:S(2)}, u32[]{:S(2)}) collective-permute-start(f32[8,128]{1,0:T(8,128)S(1)} %get-tuple-element.119), channel_id=1, source_target_pairs={{0,15},{1,2},{2,1},{3,4},{4,3},{5,6},{6,5},{7,8},{8,7},{9,10},{10,... | collective-permute-start | bytes 12296 | tf_op jit(solution)/shard_map/ppermute | solution.py:755
  84.5 7.8 %shard_map.149 = (f32[2,2,8,256]{3,2,1,0:T(8,128)S(1)}, f32[2,64,128]{2,1,0:T(8,128)S(1)}, f32[3,8,64,256]{3,2,1,0:T(8,128)}, f32[2,8,64,256]{3,2,1,0:T(8,128)}) custom-call(f32[2,3,8,256]{3,2,1,0:T(8,128)S(1)} %get-tuple-element.77.coef_row, f32[3,64,128]{2,1,0:T(8,128)S(1)} %get-tuple-element.78.coef_col, f32[8,64,256]{2,1,0:T(8,128)S(1)} %get-tuple-element.79.head, ...), custom_call_target="tpu_custom_call" | custom-call | flops 19660800 | bytes 10747904 | tf_op jit(solution)/shard_map/pallas_call | solution.py:721
  92.4 0.0 collective-permute-done.14.col_first
  92.4 0.0 collective-permute-done.15.col_second
  92.4 0.0 collective-permute-done.12.row_first
  92.4 4.0 %shard_map.150 = (f32[3,8,64,256]{3,2,1,0:T(8,128)}, f32[1,16]{1,0:T(1,128)}) custom-call(f32[1024,128]{1,0:T(8,128)S(1)} %bitcast.17, f32[8,256]{1,0:T(8,128)S(1)} %get-tuple-element.67.info, f32[2,128,128]{2,1,0:T(8,128)S(1)} %get-tuple-element.112.table, f32[8,128]{1,0:T(8,128)S(1)} %get-tuple-element.94.mine, f32[8,64,256]{2,1,0:T(8,128)S(1)} %get-tuple-element.79.head, ...), custom_call_target="tpu_custom_call" | custom-call | bytes 3985408 | tf_op jit(solution)/shard_map/pallas_call | solution.py:721
  (3 shorter events, 0.0 us)
Async XLA Ops:
  2.8 12.1 %collective-permute-start = (f32[32,256]{1,0:T(8,128)S(1)}, f32[32,256]{1,0:T(8,128)S(1)}, u32[]{:S(2)}, u32[]{:S(2)}) collective-permute-start(f32[32,256]{1,0:T(8,128)S(1)} %get-tuple-element.69), channel_id=1, source_target_pairs={{0,16},{16,0},{32,48},{48,32},{64,80},{80,64},{96,112},{112,96},{1... | collective-permute-start | bytes 98312 | tf_op jit(solution)/shard_map/ppermute | solution.py:754
  4.3 10.6 %collective-permute-start.1 = (f32[32,256]{1,0:T(8,128)S(1)}, f32[32,256]{1,0:T(8,128)S(1)}, u32[]{:S(2)}, u32[]{:S(2)}) collective-permute-start(f32[32,256]{1,0:T(8,128)S(1)} %get-tuple-element.70), channel_id=1, source_target_pairs={{0,112},{16,32},{32,16},{48,64},{64,48},{80,96},{96,80},{112,0},{1... | collective-permute-start | bytes 98312 | tf_op jit(solution)/shard_map/ppermute | solution.py:755
  5.7 9.2 %collective-permute-start.2 = (f32[32,128]{1,0:T(8,128)S(1)}, f32[32,128]{1,0:T(8,128)S(1)}, u32[]{:S(2)}, u32[]{:S(2)}) collective-permute-start(f32[32,128]{1,0:T(8,128)S(1)} %get-tuple-element.71), channel_id=1, source_target_pairs={{0,1},{1,0},{2,3},{3,2},{4,5},{5,4},{6,7},{7,6},{8,9},{9,8},{10,11... | collective-permute-start | bytes 49160 | tf_op jit(solution)/shard_map/ppermute | solution.py:754
  6.9 8.0 %collective-permute-start.3 = (f32[32,128]{1,0:T(8,128)S(1)}, f32[32,128]{1,0:T(8,128)S(1)}, u32[]{:S(2)}, u32[]{:S(2)}) collective-permute-start(f32[32,128]{1,0:T(8,128)S(1)} %get-tuple-element.72), channel_id=1, source_target_pairs={{0,15},{1,2},{2,1},{3,4},{4,3},{5,6},{6,5},{7,8},{8,7},{9,10},{10,... | collective-permute-start | bytes 49160 | tf_op jit(solution)/shard_map/ppermute | solution.py:755
  14.9 17.5 %all-to-all-start = ((f32[128,1,128]{2,1,0:T(1,128)}), f32[128,1,128]{2,1,0:T(1,128)S(1)}, u32[]{:S(2)}, u32[]{:S(2)}) async-start(f32[128,1,128]{2,1,0:T(1,128)} %bitcast.6), calls=%async_computation | async-start | bytes 131072 | tf_op jit(solution)/shard_map/all_to_all | solution.py:742
  35.3 23.6 %all-to-all-start.1 = ((f32[128,8,128]{2,1,0:T(8,128)}), f32[128,8,128]{2,1,0:T(8,128)S(1)}, u32[]{:S(2)}, u32[]{:S(2)}) async-start(f32[128,8,128]{2,1,0:T(8,128)} %bitcast.9), calls=%async_computation.1 | async-start | bytes 1048576 | tf_op jit(solution)/shard_map/all_to_all | solution.py:742
  44.4 14.5 %collective-permute-start.4 = (f32[8,256]{1,0:T(8,128)S(1)}, f32[8,256]{1,0:T(8,128)S(1)}, u32[]{:S(2)}, u32[]{:S(2)}) collective-permute-start(f32[8,256]{1,0:T(8,128)S(1)} %get-tuple-element.98), channel_id=1, source_target_pairs={{0,16},{16,0},{32,48},{48,32},{64,80},{80,64},{96,112},{112,96},{1... | collective-permute-start | bytes 24584 | tf_op jit(solution)/shard_map/ppermute | solution.py:754
  45.6 13.3 %collective-permute-start.5 = (f32[8,256]{1,0:T(8,128)S(1)}, f32[8,256]{1,0:T(8,128)S(1)}, u32[]{:S(2)}, u32[]{:S(2)}) collective-permute-start(f32[8,256]{1,0:T(8,128)S(1)} %get-tuple-element.99), channel_id=1, source_target_pairs={{0,112},{16,32},{32,16},{48,64},{64,48},{80,96},{96,80},{112,0},{1... | collective-permute-start | bytes 24584 | tf_op jit(solution)/shard_map/ppermute | solution.py:755
  46.3 12.6 %collective-permute-start.6 = (f32[8,128]{1,0:T(8,128)S(1)}, f32[8,128]{1,0:T(8,128)S(1)}, u32[]{:S(2)}, u32[]{:S(2)}) collective-permute-start(f32[8,128]{1,0:T(8,128)S(1)} %get-tuple-element.100), channel_id=1, source_target_pairs={{0,1},{1,0},{2,3},{3,2},{4,5},{5,4},{6,7},{7,6},{8,9},{9,8},{10,11... | collective-permute-start | bytes 12296 | tf_op jit(solution)/shard_map/ppermute | solution.py:754
  47.5 11.4 %collective-permute-start.7 = (f32[8,128]{1,0:T(8,128)S(1)}, f32[8,128]{1,0:T(8,128)S(1)}, u32[]{:S(2)}, u32[]{:S(2)}) collective-permute-start(f32[8,128]{1,0:T(8,128)S(1)} %get-tuple-element.101), channel_id=1, source_target_pairs={{0,15},{1,2},{2,1},{3,4},{4,3},{5,6},{6,5},{7,8},{8,7},{9,10},{10,... | collective-permute-start | bytes 12296 | tf_op jit(solution)/shard_map/ppermute | solution.py:755
  59.8 8.1 %collective-permute-start.8 = (f32[8,256]{1,0:T(8,128)S(1)}, f32[8,256]{1,0:T(8,128)S(1)}, u32[]{:S(2)}, u32[]{:S(2)}) collective-permute-start(f32[8,256]{1,0:T(8,128)S(1)} %get-tuple-element.107), channel_id=1, source_target_pairs={{0,16},{16,0},{32,48},{48,32},{64,80},{80,64},{96,112},{112,96},{1... | collective-permute-start | bytes 24584 | tf_op jit(solution)/shard_map/ppermute | solution.py:754
  62.1 5.8 %collective-permute-start.9 = (f32[8,256]{1,0:T(8,128)S(1)}, f32[8,256]{1,0:T(8,128)S(1)}, u32[]{:S(2)}, u32[]{:S(2)}) collective-permute-start(f32[8,256]{1,0:T(8,128)S(1)} %get-tuple-element.108), channel_id=1, source_target_pairs={{0,112},{16,32},{32,16},{48,64},{64,48},{80,96},{96,80},{112,0},{1... | collective-permute-start | bytes 24584 | tf_op jit(solution)/shard_map/ppermute | solution.py:755
  62.1 2.6 %collective-permute-start.10 = (f32[8,128]{1,0:T(8,128)S(1)}, f32[8,128]{1,0:T(8,128)S(1)}, u32[]{:S(2)}, u32[]{:S(2)}) collective-permute-start(f32[8,128]{1,0:T(8,128)S(1)} %get-tuple-element.109), channel_id=1, source_target_pairs={{0,1},{1,0},{2,3},{3,2},{4,5},{5,4},{6,7},{7,6},{8,9},{9,8},{10,11... | collective-permute-start | bytes 12296 | tf_op jit(solution)/shard_map/ppermute | solution.py:754
  62.1 5.8 %collective-permute-start.11 = (f32[8,128]{1,0:T(8,128)S(1)}, f32[8,128]{1,0:T(8,128)S(1)}, u32[]{:S(2)}, u32[]{:S(2)}) collective-permute-start(f32[8,128]{1,0:T(8,128)S(1)} %get-tuple-element.110), channel_id=1, source_target_pairs={{0,15},{1,2},{2,1},{3,4},{4,3},{5,6},{6,5},{7,8},{8,7},{9,10},{10,... | collective-permute-start | bytes 12296 | tf_op jit(solution)/shard_map/ppermute | solution.py:755
  71.2 21.2 %all-to-all-start.2 = ((f32[128,8,128]{2,1,0:T(8,128)}), f32[128,8,128]{2,1,0:T(8,128)S(1)}, u32[]{:S(2)}, u32[]{:S(2)}) async-start(f32[128,8,128]{2,1,0:T(8,128)} %bitcast.11), calls=%async_computation.2 | async-start | bytes 1048576 | tf_op jit(solution)/shard_map/all_to_all | solution.py:742
  76.7 15.7 %collective-permute-start.12 = (f32[8,256]{1,0:T(8,128)S(1)}, f32[8,256]{1,0:T(8,128)S(1)}, u32[]{:S(2)}, u32[]{:S(2)}) collective-permute-start(f32[8,256]{1,0:T(8,128)S(1)} %get-tuple-element.116), channel_id=1, source_target_pairs={{0,16},{16,0},{32,48},{48,32},{64,80},{80,64},{96,112},{112,96},{1... | collective-permute-start | bytes 24584 | tf_op jit(solution)/shard_map/ppermute | solution.py:754
  78.0 14.4 %collective-permute-start.13 = (f32[8,256]{1,0:T(8,128)S(1)}, f32[8,256]{1,0:T(8,128)S(1)}, u32[]{:S(2)}, u32[]{:S(2)}) collective-permute-start(f32[8,256]{1,0:T(8,128)S(1)} %get-tuple-element.117), channel_id=1, source_target_pairs={{0,112},{16,32},{32,16},{48,64},{64,48},{80,96},{96,80},{112,0},{1... | collective-permute-start | bytes 24584 | tf_op jit(solution)/shard_map/ppermute | solution.py:755
  78.6 13.7 %collective-permute-start.14 = (f32[8,128]{1,0:T(8,128)S(1)}, f32[8,128]{1,0:T(8,128)S(1)}, u32[]{:S(2)}, u32[]{:S(2)}) collective-permute-start(f32[8,128]{1,0:T(8,128)S(1)} %get-tuple-element.118), channel_id=1, source_target_pairs={{0,1},{1,0},{2,3},{3,2},{4,5},{5,4},{6,7},{7,6},{8,9},{9,8},{10,11... | collective-permute-start | bytes 12296 | tf_op jit(solution)/shard_map/ppermute | solution.py:754
  79.8 12.5 %collective-permute-start.15 = (f32[8,128]{1,0:T(8,128)S(1)}, f32[8,128]{1,0:T(8,128)S(1)}, u32[]{:S(2)}, u32[]{:S(2)}) collective-permute-start(f32[8,128]{1,0:T(8,128)S(1)} %get-tuple-element.119), channel_id=1, source_target_pairs={{0,15},{1,2},{2,1},{3,4},{4,3},{5,6},{6,5},{7,8},{8,7},{9,10},{10,... | collective-permute-start | bytes 12296 | tf_op jit(solution)/shard_map/ppermute | solution.py:755

commit v7 on v6

--- a/solution.py
+++ b/solution.py
@@ -746,14 +746,25 @@
     return exchange(array.reshape(DEVICES, 8, LANES)).reshape(8 * DEVICES, LANES)
 
 
+def partners():
+    rows, columns = (lax.axis_size(axis) for axis in AXES)
+    swaps = [[], [], [], []]
+    for x in range(rows):
+        for y in range(columns):
+            here = x * columns + y
+            x_next = x - 1 + 2 * (x % 2)
+            y_next = y - 1 + 2 * (y % 2)
+            swaps[0].append((here, (x ^ 1) * columns + y))
+            swaps[1].append((here, x_next * columns + y if 0 <= x_next < rows else x * columns + (y ^ 1)))
+            swaps[2].append((here, x * columns + (y ^ 1)))
+            swaps[3].append((here, x * columns + y_next if 0 <= y_next < columns else (x ^ 1) * columns + y))
+    return swaps
+
+
 def halo_of(faces):
-    row_first, row_second, col_first, col_second = faces
-    got = []
-    for axis, first, second in (("gx", row_first, row_second), ("gy", col_first, col_second)):
-        count = lax.axis_size(axis)
-        got.append(lax.ppermute(first, axis, [(i, i ^ 1) for i in range(count)]))
-        got.append(lax.ppermute(second, axis, [(i, (i - 1 + 2 * (i % 2)) % count) for i in range(count)]))
-    return got
+    swaps = partners()
+    got = {n: lax.ppermute(faces[n], AXES, swaps[n]) for n in (3, 1, 2, 0)}
+    return [got[n] for n in range(4)]
 
 
 def local(

time: 97.8 us -> 92.4 us (0.945)
  starting transfers between devices: 50.2 us -> 41.7 us
  waiting for transfers between devices: 3.91 us -> 7.87 us
    ppermute x16, starting transfers between devices: 27.9 us -> 13.3 us  [halo_of(): got = {n: lax.ppermute(faces[n], AXES, swaps[n]) for n in (3, 1, 2, 0)}]
    all_to_all x3, waiting for transfers between devices: 0.66 us -> 7.83 us  [exchange(): return lax.all_to_all(array, AXES, split_axis=0, concat_axis=0, tiled=True)]
    all_to_all x3, starting transfers between devices: 22.4 us -> 28.4 us  [exchange(): return lax.all_to_all(array, AXES, split_axis=0, concat_axis=0, tiled=True)]
    ppermute x16, waiting for transfers between devices: 3.25 us -> 0.04 us  [halo_of(): got = {n: lax.ppermute(faces[n], AXES, swaps[n]) for n in (3, 1, 2, 0)}]
  transfers between devices with their start and end apart: 19 -> 19, of which waited for: 2 -> 3; matrix products, arithmetic and copies ran while one was open for 0% -> 0% of each run, Pallas kernels for 29% -> 31%
where the time goes in v7:
time: 92.4 us; the launch traced here: 92 us
  starting transfers between devices  41.7 us (45%)
  Pallas kernels  41.4 us (45%)
  waiting for transfers between devices  7.87 us (9%)
  between operations  1.01 us (1%)
    pallas_call x12, Pallas kernels, call(): pl.pallas_call(kernel, out_shape=shapes, in_specs=ins, out_specs=tuple((w...  41.4 us
    all_to_all x3, starting transfers between devices, exchange(): return lax.all_to_all(array, AXES, split_axis=0, concat_axis=0, tiled=True)  28.4 us
    ppermute x16, starting transfers between devices, halo_of(): got = {n: lax.ppermute(faces[n], AXES, swaps[n]) for n in (3, 1, 2, 0)}  13.3 us
    all_to_all x3, waiting for transfers between devices, exchange(): return lax.all_to_all(array, AXES, split_axis=0, concat_axis=0, tiled=True)  7.83 us
  transfers between devices with their start and end apart: 19, of which 3 were waited for; matrix products, arithmetic and copies ran while one was open for 0% of the time, Pallas kernels for 31%

profile of v7, /device:TPU:1, one launch (start us, length us, event | category | flops | bytes accessed | tf_op | source)
XLA Modules:
  0.0 92.0 jit_solution(174024978374681177)
XLA Ops:
  0.6 2.2 %shard_map.138 = (f32[32,256]{1,0:T(8,128)S(1)}, f32[32,256]{1,0:T(8,128)S(1)}, f32[32,128]{1,0:T(8,128)S(1)}, f32[32,128]{1,0:T(8,128)S(1)}, f32[8,64,256]{2,1,...) custom-call(f32[8,64,256]{2,1,0:T(8,128)} %p_h.3, f32[8,64,256]{2,1,0:T(8,128)} %sw_h.1, ...), custom_call_target="tpu_custom_call" | custom-call | bytes 3145728 | tf_op jit(solution)/shard_map/pallas_call | solution.py:721
  2.8 1.5 %collective-permute-start = (f32[32,256]{1,0:T(8,128)S(1)}, f32[32,256]{1,0:T(8,128)S(1)}, u32[]{:S(2)}, u32[]{:S(2)}) collective-permute-start(f32[32,256]{1,0:T(8,128)S(1)} %get-tuple-element.69), channel_id=1, source_target_pairs={{0,16},{1,17},{2,18},{3,19},{4,20},{5,21},{6,22},{7,23},{8,24},{9,... | collective-permute-start | bytes 98312 | tf_op jit(solution)/shard_map/ppermute | solution.py:766
  4.3 1.4 %collective-permute-start.1 = (f32[32,256]{1,0:T(8,128)S(1)}, f32[32,256]{1,0:T(8,128)S(1)}, u32[]{:S(2)}, u32[]{:S(2)}) collective-permute-start(f32[32,256]{1,0:T(8,128)S(1)} %get-tuple-element.70), channel_id=1, source_target_pairs={{0,1},{1,0},{2,3},{3,2},{4,5},{5,4},{6,7},{7,6},{8,9},{9,8},{10,11... | collective-permute-start | bytes 98312 | tf_op jit(solution)/shard_map/ppermute | solution.py:766
  5.7 1.2 %collective-permute-start.2 = (f32[32,128]{1,0:T(8,128)S(1)}, f32[32,128]{1,0:T(8,128)S(1)}, u32[]{:S(2)}, u32[]{:S(2)}) collective-permute-start(f32[32,128]{1,0:T(8,128)S(1)} %get-tuple-element.71), channel_id=1, source_target_pairs={{0,1},{1,0},{2,3},{3,2},{4,5},{5,4},{6,7},{7,6},{8,9},{9,8},{10,11... | collective-permute-start | bytes 49160 | tf_op jit(solution)/shard_map/ppermute | solution.py:766
  6.9 0.0 collective-permute-start.3
  6.9 2.7 %shard_map.139 = (f32[128,128]{1,0:T(8,128)}, f32[8,256]{1,0:T(8,128)S(1)}, f32[8,256]{1,0:T(8,128)S(1)}, f32[8,128]{1,0:T(8,128)S(1)}) custom-call(s32[1,256]{1,0:T(1,128)} %bitcast.19, s32[1,256]{1,0:T(1,128)} %bitcast.20, f32[1,256]{1,0:T(1,128)} %bitcast.21, f32[1,16]{1,0:T(1,128)} %bitcast.22, f32[1,16]{1,0:T(1,128)} %bitcast.23, ...), custom_call_target="tpu_custom_call" | custom-call | bytes 1576064 | tf_op jit(solution)/shard_map/pallas_call | solution.py:721
  9.6 0.0 collective-permute-done.2.refs_2_
  9.6 0.0 collective-permute-done.3.refs_3_
  9.6 0.0 collective-permute-done.refs_0_
  9.6 0.0 collective-permute-done.1.refs_1_
  9.6 11.7 %all-to-all-start = ((f32[128,1,128]{2,1,0:T(1,128)}), f32[128,1,128]{2,1,0:T(1,128)S(1)}, u32[]{:S(2)}, u32[]{:S(2)}) async-start(f32[128,1,128]{2,1,0:T(1,128)} %bitcast.6), calls=%async_computation | async-start | bytes 131072 | tf_op jit(solution)/shard_map/all_to_all | solution.py:742
  21.3 9.0 %shard_map.141 = (f32[2,3,8,256]{3,2,1,0:T(8,128)S(1)}, f32[3,64,128]{2,1,0:T(8,128)S(1)}, f32[8,64,256]{2,1,0:T(8,128)S(1)}, f32[8,64,256]{2,1,0:T(8,128)S(1)},...) custom-call(f32[8,256]{1,0:T(8,128)S(1)} %get-tuple-element.67.info,, ...), custom_call_target="tpu_custom_call" | custom-call | flops 52428800 | bytes 5349376 | tf_op jit(solution)/shard_map/pallas_call | solution.py:721
  30.4 0.7 all-to-all-done
  31.0 1.2 %shard_map.142 = (f32[8,256]{1,0:T(8,128)S(1)}, f32[8,256]{1,0:T(8,128)S(1)}, f32[8,128]{1,0:T(8,128)S(1)}, f32[8,128]{1,0:T(8,128)S(1)}, f32[8,128]{1,0:T(8,128...) custom-call(f32[128,128]{1,0:T(8,128)S(1)} %bitcast.18, ...), custom_call_target="tpu_custom_call" | custom-call | bytes 1126400 | tf_op jit(solution)/shard_map/pallas_call | solution.py:721
  32.3 1.7 %shard_map.144 = f32[1024,128]{1,0:T(8,128)} custom-call(f32[8,256]{1,0:T(8,128)S(1)} %get-tuple-element.67.info, f32[8,256]{1,0:T(8,128)S(1)} %get-tuple-element.93.perf, f32[8,128]{1,0:T(8,128)S(1)} %get-tuple-element.94.mine, f32[8,64,256]{2,1,0:T(8,128)S(1)} %get-tuple-element.84.step.base), custom_call_target="tpu_custom_call" | custom-call | bytes 544768 | tf_op jit(solution)/shard_map/pallas_call | solution.py:721
  33.9 9.1 %all-to-all-start.1 = ((f32[128,8,128]{2,1,0:T(8,128)}), f32[128,8,128]{2,1,0:T(8,128)S(1)}, u32[]{:S(2)}, u32[]{:S(2)}) async-start(f32[128,8,128]{2,1,0:T(8,128)} %bitcast.9), calls=%async_computation.1 | async-start | bytes 1048576 | tf_op jit(solution)/shard_map/all_to_all | solution.py:742
  43.1 1.1 %collective-permute-start.4 = (f32[8,256]{1,0:T(8,128)S(1)}, f32[8,256]{1,0:T(8,128)S(1)}, u32[]{:S(2)}, u32[]{:S(2)}) collective-permute-start(f32[8,256]{1,0:T(8,128)S(1)} %get-tuple-element.98), channel_id=1, source_target_pairs={{0,16},{1,17},{2,18},{3,19},{4,20},{5,21},{6,22},{7,23},{8,24},{9,... | collective-permute-start | bytes 24584 | tf_op jit(solution)/shard_map/ppermute | solution.py:766
  44.2 0.7 collective-permute-start.5
  44.9 1.2 %collective-permute-start.6 = (f32[8,128]{1,0:T(8,128)S(1)}, f32[8,128]{1,0:T(8,128)S(1)}, u32[]{:S(2)}, u32[]{:S(2)}) collective-permute-start(f32[8,128]{1,0:T(8,128)S(1)} %get-tuple-element.100), channel_id=1, source_target_pairs={{0,1},{1,0},{2,3},{3,2},{4,5},{5,4},{6,7},{7,6},{8,9},{9,8},{10,11... | collective-permute-start | bytes 12296 | tf_op jit(solution)/shard_map/ppermute | solution.py:766
  46.1 0.2 collective-permute-start.7
  46.3 6.7 %shard_map.143 = (f32[8,64,256]{2,1,0:T(8,128)S(1)}, f32[2,8,256]{2,1,0:T(8,128)S(1)}, f32[64,128]{1,0:T(8,128)S(1)}, f32[3,8,64,256]{3,2,1,0:T(8,128)}, f32[6,8,64,256]{3,2,1,0:T(8,128)}) custom-call(f32[2,3,8,256]{3,2,1,0:T(8,128)S(1)} %get-tuple-element.77.coef_row, f32[3,64,128]{2,1,0:T(8,128)S(1)} %get-tuple-element.78.coef_col, ...), custom_call_target="tpu_custom_call" | custom-call | flops 13107200 | bytes 9125888 | tf_op jit(solution)/shard_map/pallas_call | solution.py:721
  53.1 0.0 collective-permute-done.6.col_first
  53.1 0.0 collective-permute-done.7.col_second
  53.1 0.0 collective-permute-done.4.row_first
  53.1 0.0 collective-permute-done.5.row_second
  53.1 4.1 %all-to-all-done.1 = f32[128,8,128]{2,1,0:T(8,128)S(1)} async-done(((f32[128,8,128]{2,1,0:T(8,128)}), f32[128,8,128]{2,1,0:T(8,128)S(1)}, u32[]{:S(2)}, u32[]{:S(2)}) %all-to-all-start.1) | async-done | bytes 524320 | tf_op jit(solution)/shard_map/all_to_all | solution.py:742
  57.2 0.9 shard_map.145
  58.1 0.6 collective-permute-start.8
  58.7 0.4 collective-permute-start.9
  59.2 0.3 collective-permute-start.10
  59.5 1.4 %collective-permute-start.11 = (f32[8,128]{1,0:T(8,128)S(1)}, f32[8,128]{1,0:T(8,128)S(1)}, u32[]{:S(2)}, u32[]{:S(2)}) collective-permute-start(f32[8,128]{1,0:T(8,128)S(1)} %get-tuple-element.110), channel_id=1, source_target_pairs={{0,16},{1,2},{2,1},{3,4},{4,3},{5,6},{6,5},{7,8},{8,7},{9,10},{10,... | collective-permute-start | bytes 12296 | tf_op jit(solution)/shard_map/ppermute | solution.py:766
  60.9 1.9 %shard_map.146 = (f32[2,128,128]{2,1,0:T(8,128)S(1)}, f32[8,128]{1,0:T(8,128)S(1)}, f32[8,64,256]{2,1,0:T(8,128)S(1)}, f32[6,8,64,256]{3,2,1,0:T(8,128)S(1)}) custom-call(f32[1024,128]{1,0:T(8,128)S(1)} %bitcast.16, f32[8,256]{1,0:T(8,128)S(1)} %get-tuple-element.67.info, f32[8,256]{1,0:T(8,128)S(1)} %get-tuple-element.93.perf, ...), custom_call_target="tpu_custom_call" | custom-call | bytes 4210688 | tf_op jit(solution)/shard_map/pallas_call | solution.py:721
  62.8 0.0 collective-permute-done.10.col_first
  62.8 0.0 collective-permute-done.11.col_second
  62.8 0.0 collective-permute-done.8.row_first
  62.8 0.0 collective-permute-done.9.row_second
  62.8 1.7 %shard_map.147 = (f32[8,256]{1,0:T(8,128)S(1)}, f32[8,256]{1,0:T(8,128)S(1)}, f32[8,128]{1,0:T(8,128)S(1)}, f32[8,128]{1,0:T(8,128)S(1)}, f32[8,64,256]{2,1,0:T(8,128)S(1)}) custom-call(f32[8,64,256]{2,1,0:T(8,128)S(1)} %get-tuple-element.105.spread, f32[8,64,256]{2,1,0:T(8,128)S(1)} %get-tuple-element.102.step.old, ...), custom_call_target="tpu_custom_call" | custom-call | bytes 5267456 | tf_op jit(solution)/shard_map/pallas_call | solution.py:721
  64.5 1.6 %shard_map.148 = f32[1024,128]{1,0:T(8,128)} custom-call(f32[8,256]{1,0:T(8,128)S(1)} %get-tuple-element.67.info, f32[8,256]{1,0:T(8,128)S(1)} %get-tuple-element.93.perf, f32[8,128]{1,0:T(8,128)S(1)} %get-tuple-element.104.parts, f32[8,64,256]{2,1,0:T(8,128)S(1)} %get-tuple-element.111.step), custom_call_target="tpu_custom_call" | custom-call | bytes 544768 | tf_op jit(solution)/shard_map/pallas_call | solution.py:721
  66.2 7.5 %all-to-all-start.2 = ((f32[128,8,128]{2,1,0:T(8,128)}), f32[128,8,128]{2,1,0:T(8,128)S(1)}, u32[]{:S(2)}, u32[]{:S(2)}) async-start(f32[128,8,128]{2,1,0:T(8,128)} %bitcast.11), calls=%async_computation.2 | async-start | bytes 1048576 | tf_op jit(solution)/shard_map/all_to_all | solution.py:742
  73.7 1.1 %collective-permute-start.12 = (f32[8,256]{1,0:T(8,128)S(1)}, f32[8,256]{1,0:T(8,128)S(1)}, u32[]{:S(2)}, u32[]{:S(2)}) collective-permute-start(f32[8,256]{1,0:T(8,128)S(1)} %get-tuple-element.116), channel_id=1, source_target_pairs={{0,16},{1,17},{2,18},{3,19},{4,20},{5,21},{6,22},{7,23},{8,24},{9,... | collective-permute-start | bytes 24584 | tf_op jit(solution)/shard_map/ppermute | solution.py:766
  74.9 0.7 collective-permute-start.13
  75.6 1.2 %collective-permute-start.14 = (f32[8,128]{1,0:T(8,128)S(1)}, f32[8,128]{1,0:T(8,128)S(1)}, u32[]{:S(2)}, u32[]{:S(2)}) collective-permute-start(f32[8,128]{1,0:T(8,128)S(1)} %get-tuple-element.118), channel_id=1, source_target_pairs={{0,1},{1,0},{2,3},{3,2},{4,5},{5,4},{6,7},{7,6},{8,9},{9,8},{10,11... | collective-permute-start | bytes 12296 | tf_op jit(solution)/shard_map/ppermute | solution.py:766
  76.8 0.2 collective-permute-start.15
  77.0 7.8 %shard_map.149 = (f32[2,2,8,256]{3,2,1,0:T(8,128)S(1)}, f32[2,64,128]{2,1,0:T(8,128)S(1)}, f32[3,8,64,256]{3,2,1,0:T(8,128)}, f32[2,8,64,256]{3,2,1,0:T(8,128)}) custom-call(f32[2,3,8,256]{3,2,1,0:T(8,128)S(1)} %get-tuple-element.77.coef_row, f32[3,64,128]{2,1,0:T(8,128)S(1)} %get-tuple-element.78.coef_col, f32[8,64,256]{2,1,0:T(8,128)S(1)} %get-tuple-element.79.head, ...), custom_call_target="tpu_custom_call" | custom-call | flops 19660800 | bytes 10747904 | tf_op jit(solution)/shard_map/pallas_call | solution.py:721
  84.8 0.0 collective-permute-done.14.col_first
  84.8 0.0 collective-permute-done.15.col_second
  84.8 3.0 %all-to-all-done.2 = f32[128,8,128]{2,1,0:T(8,128)S(1)} async-done(((f32[128,8,128]{2,1,0:T(8,128)}), f32[128,8,128]{2,1,0:T(8,128)S(1)}, u32[]{:S(2)}, u32[]{:S(2)}) %all-to-all-start.2) | async-done | bytes 524320 | tf_op jit(solution)/shard_map/all_to_all | solution.py:742
  87.9 4.0 %shard_map.150 = (f32[3,8,64,256]{3,2,1,0:T(8,128)}, f32[1,16]{1,0:T(1,128)}) custom-call(f32[1024,128]{1,0:T(8,128)S(1)} %bitcast.17, f32[8,256]{1,0:T(8,128)S(1)} %get-tuple-element.67.info, f32[2,128,128]{2,1,0:T(8,128)S(1)} %get-tuple-element.112.table, f32[8,128]{1,0:T(8,128)S(1)} %get-tuple-element.94.mine, f32[8,64,256]{2,1,0:T(8,128)S(1)} %get-tuple-element.79.head, ...), custom_call_target="tpu_custom_call" | custom-call | bytes 3985408 | tf_op jit(solution)/shard_map/pallas_call | solution.py:721
  (3 shorter events, 0.0 us)
Async XLA Ops:
  2.8 6.8 %collective-permute-start = (f32[32,256]{1,0:T(8,128)S(1)}, f32[32,256]{1,0:T(8,128)S(1)}, u32[]{:S(2)}, u32[]{:S(2)}) collective-permute-start(f32[32,256]{1,0:T(8,128)S(1)} %get-tuple-element.69), channel_id=1, source_target_pairs={{0,16},{1,17},{2,18},{3,19},{4,20},{5,21},{6,22},{7,23},{8,24},{9,... | collective-permute-start | bytes 98312 | tf_op jit(solution)/shard_map/ppermute | solution.py:766
  4.3 5.3 %collective-permute-start.1 = (f32[32,256]{1,0:T(8,128)S(1)}, f32[32,256]{1,0:T(8,128)S(1)}, u32[]{:S(2)}, u32[]{:S(2)}) collective-permute-start(f32[32,256]{1,0:T(8,128)S(1)} %get-tuple-element.70), channel_id=1, source_target_pairs={{0,1},{1,0},{2,3},{3,2},{4,5},{5,4},{6,7},{7,6},{8,9},{9,8},{10,11... | collective-permute-start | bytes 98312 | tf_op jit(solution)/shard_map/ppermute | solution.py:766
  5.7 3.9 %collective-permute-start.2 = (f32[32,128]{1,0:T(8,128)S(1)}, f32[32,128]{1,0:T(8,128)S(1)}, u32[]{:S(2)}, u32[]{:S(2)}) collective-permute-start(f32[32,128]{1,0:T(8,128)S(1)} %get-tuple-element.71), channel_id=1, source_target_pairs={{0,1},{1,0},{2,3},{3,2},{4,5},{5,4},{6,7},{7,6},{8,9},{9,8},{10,11... | collective-permute-start | bytes 49160 | tf_op jit(solution)/shard_map/ppermute | solution.py:766
  6.9 2.7 %collective-permute-start.3 = (f32[32,128]{1,0:T(8,128)S(1)}, f32[32,128]{1,0:T(8,128)S(1)}, u32[]{:S(2)}, u32[]{:S(2)}) collective-permute-start(f32[32,128]{1,0:T(8,128)S(1)} %get-tuple-element.72), channel_id=1, source_target_pairs={{0,16},{1,2},{2,1},{3,4},{4,3},{5,6},{6,5},{7,8},{8,7},{9,10},{10,... | collective-permute-start | bytes 49160 | tf_op jit(solution)/shard_map/ppermute | solution.py:766
  9.6 21.4 %all-to-all-start = ((f32[128,1,128]{2,1,0:T(1,128)}), f32[128,1,128]{2,1,0:T(1,128)S(1)}, u32[]{:S(2)}, u32[]{:S(2)}) async-start(f32[128,1,128]{2,1,0:T(1,128)} %bitcast.6), calls=%async_computation | async-start | bytes 131072 | tf_op jit(solution)/shard_map/all_to_all | solution.py:742
  33.9 23.3 %all-to-all-start.1 = ((f32[128,8,128]{2,1,0:T(8,128)}), f32[128,8,128]{2,1,0:T(8,128)S(1)}, u32[]{:S(2)}, u32[]{:S(2)}) async-start(f32[128,8,128]{2,1,0:T(8,128)} %bitcast.9), calls=%async_computation.1 | async-start | bytes 1048576 | tf_op jit(solution)/shard_map/all_to_all | solution.py:742
  43.1 10.0 %collective-permute-start.4 = (f32[8,256]{1,0:T(8,128)S(1)}, f32[8,256]{1,0:T(8,128)S(1)}, u32[]{:S(2)}, u32[]{:S(2)}) collective-permute-start(f32[8,256]{1,0:T(8,128)S(1)} %get-tuple-element.98), channel_id=1, source_target_pairs={{0,16},{1,17},{2,18},{3,19},{4,20},{5,21},{6,22},{7,23},{8,24},{9,... | collective-permute-start | bytes 24584 | tf_op jit(solution)/shard_map/ppermute | solution.py:766
  44.2 8.9 %collective-permute-start.5 = (f32[8,256]{1,0:T(8,128)S(1)}, f32[8,256]{1,0:T(8,128)S(1)}, u32[]{:S(2)}, u32[]{:S(2)}) collective-permute-start(f32[8,256]{1,0:T(8,128)S(1)} %get-tuple-element.99), channel_id=1, source_target_pairs={{0,1},{1,0},{2,3},{3,2},{4,5},{5,4},{6,7},{7,6},{8,9},{9,8},{10,11... | collective-permute-start | bytes 24584 | tf_op jit(solution)/shard_map/ppermute | solution.py:766
  44.9 8.1 %collective-permute-start.6 = (f32[8,128]{1,0:T(8,128)S(1)}, f32[8,128]{1,0:T(8,128)S(1)}, u32[]{:S(2)}, u32[]{:S(2)}) collective-permute-start(f32[8,128]{1,0:T(8,128)S(1)} %get-tuple-element.100), channel_id=1, source_target_pairs={{0,1},{1,0},{2,3},{3,2},{4,5},{5,4},{6,7},{7,6},{8,9},{9,8},{10,11... | collective-permute-start | bytes 12296 | tf_op jit(solution)/shard_map/ppermute | solution.py:766
  46.1 7.0 %collective-permute-start.7 = (f32[8,128]{1,0:T(8,128)S(1)}, f32[8,128]{1,0:T(8,128)S(1)}, u32[]{:S(2)}, u32[]{:S(2)}) collective-permute-start(f32[8,128]{1,0:T(8,128)S(1)} %get-tuple-element.101), channel_id=1, source_target_pairs={{0,16},{1,2},{2,1},{3,4},{4,3},{5,6},{6,5},{7,8},{8,7},{9,10},{10,... | collective-permute-start | bytes 12296 | tf_op jit(solution)/shard_map/ppermute | solution.py:766
  58.1 4.7 %collective-permute-start.8 = (f32[8,256]{1,0:T(8,128)S(1)}, f32[8,256]{1,0:T(8,128)S(1)}, u32[]{:S(2)}, u32[]{:S(2)}) collective-permute-start(f32[8,256]{1,0:T(8,128)S(1)} %get-tuple-element.107), channel_id=1, source_target_pairs={{0,16},{1,17},{2,18},{3,19},{4,20},{5,21},{6,22},{7,23},{8,24},{9,... | collective-permute-start | bytes 24584 | tf_op jit(solution)/shard_map/ppermute | solution.py:766
  58.7 4.1 %collective-permute-start.9 = (f32[8,256]{1,0:T(8,128)S(1)}, f32[8,256]{1,0:T(8,128)S(1)}, u32[]{:S(2)}, u32[]{:S(2)}) collective-permute-start(f32[8,256]{1,0:T(8,128)S(1)} %get-tuple-element.108), channel_id=1, source_target_pairs={{0,1},{1,0},{2,3},{3,2},{4,5},{5,4},{6,7},{7,6},{8,9},{9,8},{10,11... | collective-permute-start | bytes 24584 | tf_op jit(solution)/shard_map/ppermute | solution.py:766
  59.2 3.6 %collective-permute-start.10 = (f32[8,128]{1,0:T(8,128)S(1)}, f32[8,128]{1,0:T(8,128)S(1)}, u32[]{:S(2)}, u32[]{:S(2)}) collective-permute-start(f32[8,128]{1,0:T(8,128)S(1)} %get-tuple-element.109), channel_id=1, source_target_pairs={{0,1},{1,0},{2,3},{3,2},{4,5},{5,4},{6,7},{7,6},{8,9},{9,8},{10,11... | collective-permute-start | bytes 12296 | tf_op jit(solution)/shard_map/ppermute | solution.py:766
  59.5 3.3 %collective-permute-start.11 = (f32[8,128]{1,0:T(8,128)S(1)}, f32[8,128]{1,0:T(8,128)S(1)}, u32[]{:S(2)}, u32[]{:S(2)}) collective-permute-start(f32[8,128]{1,0:T(8,128)S(1)} %get-tuple-element.110), channel_id=1, source_target_pairs={{0,16},{1,2},{2,1},{3,4},{4,3},{5,6},{6,5},{7,8},{8,7},{9,10},{10,... | collective-permute-start | bytes 12296 | tf_op jit(solution)/shard_map/ppermute | solution.py:766
  66.2 21.7 %all-to-all-start.2 = ((f32[128,8,128]{2,1,0:T(8,128)}), f32[128,8,128]{2,1,0:T(8,128)S(1)}, u32[]{:S(2)}, u32[]{:S(2)}) async-start(f32[128,8,128]{2,1,0:T(8,128)} %bitcast.11), calls=%async_computation.2 | async-start | bytes 1048576 | tf_op jit(solution)/shard_map/all_to_all | solution.py:742
  73.7 11.1 %collective-permute-start.12 = (f32[8,256]{1,0:T(8,128)S(1)}, f32[8,256]{1,0:T(8,128)S(1)}, u32[]{:S(2)}, u32[]{:S(2)}) collective-permute-start(f32[8,256]{1,0:T(8,128)S(1)} %get-tuple-element.116), channel_id=1, source_target_pairs={{0,16},{1,17},{2,18},{3,19},{4,20},{5,21},{6,22},{7,23},{8,24},{9,... | collective-permute-start | bytes 24584 | tf_op jit(solution)/shard_map/ppermute | solution.py:766
  74.9 10.0 %collective-permute-start.13 = (f32[8,256]{1,0:T(8,128)S(1)}, f32[8,256]{1,0:T(8,128)S(1)}, u32[]{:S(2)}, u32[]{:S(2)}) collective-permute-start(f32[8,256]{1,0:T(8,128)S(1)} %get-tuple-element.117), channel_id=1, source_target_pairs={{0,1},{1,0},{2,3},{3,2},{4,5},{5,4},{6,7},{7,6},{8,9},{9,8},{10,11... | collective-permute-start | bytes 24584 | tf_op jit(solution)/shard_map/ppermute | solution.py:766
  75.6 9.2 %collective-permute-start.14 = (f32[8,128]{1,0:T(8,128)S(1)}, f32[8,128]{1,0:T(8,128)S(1)}, u32[]{:S(2)}, u32[]{:S(2)}) collective-permute-start(f32[8,128]{1,0:T(8,128)S(1)} %get-tuple-element.118), channel_id=1, source_target_pairs={{0,1},{1,0},{2,3},{3,2},{4,5},{5,4},{6,7},{7,6},{8,9},{9,8},{10,11... | collective-permute-start | bytes 12296 | tf_op jit(solution)/shard_map/ppermute | solution.py:766
  76.8 8.0 %collective-permute-start.15 = (f32[8,128]{1,0:T(8,128)S(1)}, f32[8,128]{1,0:T(8,128)S(1)}, u32[]{:S(2)}, u32[]{:S(2)}) collective-permute-start(f32[8,128]{1,0:T(8,128)S(1)} %get-tuple-element.119), channel_id=1, source_target_pairs={{0,16},{1,2},{2,1},{3,4},{4,3},{5,6},{6,5},{7,8},{8,7},{9,10},{10,... | collective-permute-start | bytes 12296 | tf_op jit(solution)/shard_map/ppermute | solution.py:766

commit v8 on v7

--- a/solution.py
+++ b/solution.py
@@ -20,6 +20,7 @@
 FAR = 64
 TAIL = REACH * WELL_DEV
 WIDTH = TAIL + 128
+TILES = WIDTH // 128
 LANES = 128
 L, R, C = 8, 64, 256
 PERFS = 256
@@ -112,7 +113,7 @@
 
 
 def tile_of(got, t):
-    return got[pl.ds(t, DEVICES, stride=8), :]
+    return got[pl.ds(t, DEVICES, stride=TILES), :]
 
 
 def sum_parts(got):
@@ -125,8 +126,9 @@
     return total
 
 
-def to_everyone(tile):
-    return jnp.broadcast_to(tile[None], (DEVICES, 8, LANES)).reshape(8 * DEVICES, LANES)
+def to_everyone(pay, rows):
+    four = jnp.concatenate([rows] * 4, axis=0)
+    pay[...] = jnp.broadcast_to(four[None], (DEVICES // 4, 4 * TILES, LANES)).reshape(TILES * DEVICES, LANES)
 
 
 def rolled_row(row, shift):
@@ -209,9 +211,27 @@
 
 
 def faces_kernel(
-    p_h, sw_h, sg_h, perm_h, row_first, row_second, col_first, col_second, p, sw, sg, perm, sems,
+    cell_h, well_h, index_h, pressure_h, rate_h, p_h, sw_h, sg_h, perm_h,
+    row_first, row_second, col_first, col_second, p, sw, sg, info, own,
+    cell_in, well_in, index_in, pressure_in, rate_in, perm, sems, sems_in,
 ):
     copies = start_copies(((perm_h.at[0:2], perm), (p_h, p), (sw_h, sw), (sg_h, sg)), sems)
+    small = start_copies(
+        (
+            (cell_h, cell_in), (well_h, well_in), (index_h, index_in),
+            (pressure_h, pressure_in), (rate_h, rate_in),
+        ),
+        sems_in,
+    )
+    me = lax.axis_index("gx") * 16 + lax.axis_index("gy")
+    device = jnp.full((1, PERFS), me, i32).astype(f32)
+    wait_copies(small)
+    numbers = [cell_in[...].astype(f32), well_in[...].astype(f32), index_in[...], device]
+    info[...] = jnp.concatenate(numbers + [jnp.zeros((4, PERFS), f32)], axis=0)
+    blank = jnp.zeros((1, LANES - WELL_DEV), f32)
+    heads = jnp.concatenate([pressure_in[...], blank], axis=1)
+    rates = jnp.concatenate([rate_in[...], blank], axis=1)
+    own[...] = jnp.concatenate([heads, rates, jnp.zeros((6, LANES), f32)], axis=0)
     lane = iota((R, LANES), 1)
     columns = jnp.zeros((R, LANES), f32)
     wait_copies(copies[:1])
@@ -235,36 +255,14 @@
     pack_columns(columns, col_first, col_second)
 
 
-def start_kernel(
-    cell_h, well_h, index_h, pressure_h, rate_h, p, sw, sg,
-    pay, perf, info, own,
-    cell_in, well_in, index_in, pressure_in, rate_in, sems,
-):
-    copies = start_copies(
-        (
-            (cell_h, cell_in), (well_h, well_in), (index_h, index_in),
-            (pressure_h, pressure_in), (rate_h, rate_in),
-        ),
-        sems,
-    )
-    me = lax.axis_index("gx") * 16 + lax.axis_index("gy")
-    device = jnp.full((1, PERFS), me, i32).astype(f32)
-    wait_copies(copies)
-    well_row = well_in[...]
-    index_row = index_in[...]
-    cell_float = cell_in[...].astype(f32)
-    well_float = well_row.astype(f32)
-    info[...] = jnp.concatenate([cell_float, well_float, index_row, device, jnp.zeros((4, PERFS), f32)], axis=0)
-    blank = jnp.zeros((1, LANES - WELL_DEV), f32)
-    heads = jnp.concatenate([pressure_in[...], blank], axis=1)
-    rates = jnp.concatenate([rate_in[...], blank], axis=1)
-    own[...] = jnp.concatenate([heads, rates, jnp.zeros((6, LANES), f32)], axis=0)
-    slot_column = to_column(well_float).astype(i32) & 15
-    here = gather_cells(to_column(cell_float).astype(i32), (flat(p), flat(sw), flat(sg)))
+def start_kernel(info, own, p, sw, sg, pay, perf):
+    well_row = info[1:2].astype(i32)
+    slot_column = to_column(info[1:2]).astype(i32) & 15
+    here = gather_cells(to_column(info[0:1]).astype(i32), (flat(p), flat(sw), flat(sg)))
     coeffs = coeffs_of(*here)
-    total = to_column(index_row) * (coeffs[0] + coeffs[1] + coeffs[2])
+    total = to_column(info[2:3]) * (coeffs[0] + coeffs[1] + coeffs[2])
     sums = to_holders(well_row >> 4, slot_column, ((0, total), (1, total * here[0])))
-    pay[...] = sums + rolled_row(heads, 32)
+    pay[...] = sums + rolled_row(own[0:1], 32)
     perf[...] = jnp.broadcast_to(to_row(total), (8, PERFS))
 
 
@@ -452,7 +450,7 @@
 
 
 def first_kernel(
-    got, info, own, base, head, row_first, row_second, col_first, col_second, mine, well_residual, spread, step,
+    got, info, own, perf, base, head, mine, well_residual, spread, step, pay,
 ):
     lane = iota((1, LANES), 1)
     sums = jnp.sum(got[...], axis=0, keepdims=True)
@@ -467,20 +465,17 @@
     heads = gather_wells(got[...], well_row >> 4, (well_row & 15) + 32)
     spread[...] = scatter(cell_row, info[2:3] * heads).reshape(L, R, C)
     step[...] = base[...] + head[...] * spread[...]
-    write_faces(step, (row_first, row_second, col_first, col_second))
-
-
-def first_flow_kernel(info, perf, mine, step, pay):
-    well_row = info[1:2].astype(i32)
     here = to_row(gather_cells(to_column(info[0:1]).astype(i32), (flat(step),))[0])
     parts = parts_by_offset(info[3:4].astype(i32), well_row, perf[0:1] * here)
     packed = parts[:, TAIL:]
-    residual = mine[0:1]
-    inverse = mine[1:2]
     for n, row in enumerate((residual * inverse, residual, inverse)):
         packed = packed + rolled_row(row, 16 * (n + 1))
     tiles = [parts[:, LANES * t : LANES * (t + 1)] for t in range(5)]
-    pay[...] = to_everyone(jnp.concatenate(tiles + [packed, jnp.zeros((2, LANES), f32)], axis=0))
+    to_everyone(pay, jnp.concatenate(tiles + [packed], axis=0))
+
+
+def step_faces_kernel(step, row_first, row_second, col_first, col_second):
+    write_faces(step, (row_first, row_second, col_first, col_second))
 
 
 def grid_kernel(
@@ -573,8 +568,8 @@
 
 
 def third_kernel(
-    spread, old, base, gain, head, row_first, row_second, col_first, col_second,
-    out_row_first, out_row_second, out_col_first, out_col_second, step, row_lo, row_hi,
+    info, perf, parts, spread, old, base, gain, head, row_first, row_second, col_first, col_second,
+    step, pay, row_lo, row_hi,
 ):
     columns = unpack_columns(col_first, col_second)
     row_lo[...], row_hi[...] = from_partner("gx", row_first[...], row_second[...])
@@ -590,17 +585,12 @@
         return carry
 
     lax.fori_loop(0, L, layer, 0)
-    write_faces(step, (out_row_first, out_row_second, out_col_first, out_col_second))
-
-
-def third_flow_kernel(info, perf, parts, step, pay):
     here = gather_cells(to_column(info[0:1]).astype(i32), (flat(step),))[0]
     well_row = info[1:2].astype(i32)
     slot_column = to_column(info[1:2]).astype(i32) & 15
-    pay[...] = to_everyone(parts[...])
-    pay[pl.ds(6, DEVICES, stride=8), :] = to_holders(
-        well_row >> 4, slot_column, ((0, to_column(perf[0:1]) * here),)
-    )
+    sums = to_holders(well_row >> 4, slot_column, ((1, to_column(perf[0:1]) * here),))
+    to_everyone(pay, parts[0:TILES])
+    pay[pl.ds(TILES - 1, DEVICES, stride=TILES), :] = sums + parts[TILES - 1 : TILES]
 
 
 def last_grid_kernel(
@@ -681,7 +671,7 @@
     ahead_h, slope_h, update_h, moved, ahead, slope, update, sems, sems_out,
 ):
     copies = start_copies(((ahead_h, ahead), (slope_h, slope)), sems)
-    flow = jnp.sum(tile_of(got, 6), axis=0, keepdims=True)
+    flow = rolled_row(jnp.sum(tile_of(got, TILES - 1), axis=0, keepdims=True), LANES - 16)
     moved[...] = ((flow + mine[0:1]) * mine[1:2])[:, 0:WELL_DEV]
     cell_row = info[0:1].astype(i32)
     well_row = info[1:2].astype(i32)
@@ -734,7 +724,7 @@
 FACES = (((L, C), VM), ((L, C), VM), ((L, LANES), VM), ((L, LANES), VM))
 WIDE_FACES = (((4 * L, C), VM), ((4 * L, C), VM), ((4 * L, LANES), VM), ((4 * L, LANES), VM))
 SMALL = (8, LANES)
-PAY = ((8 * DEVICES, LANES), None)
+PAY = ((TILES * DEVICES, LANES), None)
 sem = pltpu.SemaphoreType.DMA
 
 
@@ -743,7 +733,7 @@
 
 
 def exchange_tiles(array):
-    return exchange(array.reshape(DEVICES, 8, LANES)).reshape(8 * DEVICES, LANES)
+    return exchange(array.reshape(DEVICES, WIDTH)).reshape(TILES * DEVICES, LANES)
 
 
 def partners():
@@ -771,26 +761,22 @@
     pressure, sat_water, sat_gas, old_mass, perm, porosity,
     perf_well, perf_cell, perf_index, well_pressure, well_rate,
 ):
-    *faces, p, sw, sg = call(
+    *faces, p, sw, sg, info, own = call(
         faces_kernel,
-        WIDE_FACES + ((FIELD, VM), (FIELD, VM), (FIELD, VM)),
-        [HB] * 4,
-        (pressure, sat_water, sat_gas, perm),
-        [pltpu.VMEM(TWO, bf16), sem((4,))],
-    )
-    halo = halo_of(faces)
-    pay, perf, info, own = call(
-        start_kernel,
-        (((DEVICES, LANES), VM), ((8, PERFS), VM), ((8, PERFS), VM), (SMALL, VM)),
-        [HB] * 5 + [VM] * 3,
+        WIDE_FACES + ((FIELD, VM), (FIELD, VM), (FIELD, VM), ((8, PERFS), VM), (SMALL, VM)),
+        [HB] * 9,
         (
             perf_cell.reshape(1, PERFS), perf_well.reshape(1, PERFS), perf_index.reshape(1, PERFS),
-            well_pressure.reshape(1, WELL_DEV), well_rate.reshape(1, WELL_DEV), p, sw, sg,
+            well_pressure.reshape(1, WELL_DEV), well_rate.reshape(1, WELL_DEV), pressure, sat_water, sat_gas, perm,
         ),
         [
             pltpu.VMEM((1, PERFS), i32), pltpu.VMEM((1, PERFS), i32), (1, PERFS),
-            (1, WELL_DEV), (1, WELL_DEV), sem((5,)),
+            (1, WELL_DEV), (1, WELL_DEV), pltpu.VMEM(TWO, bf16), sem((4,)), sem((5,)),
         ],
+    )
+    halo = halo_of(faces)
+    pay, perf = call(
+        start_kernel, (((DEVICES, LANES), VM), ((8, PERFS), VM)), [VM] * 5, (info, own, p, sw, sg)
     )
     pay, *halo = pl.pallas_call(
         after_kernel,
@@ -814,15 +800,14 @@
         ],
         flops=400 * L * R * C,
     )
-    *faces, mine, well_residual, spread, start = call(
+    mine, well_residual, spread, start, pay = call(
         first_kernel,
-        FACES + ((SMALL, VM), ((1, WELL_DEV), None), (FIELD, VM), (FIELD, VM)),
-        [VM] * 5,
-        (got, info, own, base, head),
-    )
-    halo = halo_of(faces)
-    (pay,) = call(first_flow_kernel, (PAY,), [VM] * 4, (info, perf, mine, start))
+        ((SMALL, VM), ((1, WELL_DEV), None), (FIELD, VM), (FIELD, VM), PAY),
+        [VM] * 6,
+        (got, info, own, perf, base, head),
+    )
     got = exchange_tiles(pay)
+    halo = halo_of(call(step_faces_kernel, FACES, [VM], (start,)))
     fields = (coef, tx, ty, tz, weight)
     ahead, gain_row, gain_col, residual, gain = call(
         grid_kernel,
@@ -846,16 +831,15 @@
         (got, info, perf, step, gain),
         [sem((1,))],
     )
-    *faces, step = call(
+    step, pay = call(
         third_kernel,
-        FACES + ((FIELD, VM),),
-        [VM] * 9,
-        (spread, step, start, gain_near, head, *halo),
+        ((FIELD, VM), PAY),
+        [VM] * 12,
+        (info, perf, parts, spread, step, start, gain_near, head, *halo),
         [(L, C), (L, C)],
     )
-    halo = halo_of(faces)
-    (pay,) = call(third_flow_kernel, (PAY,), [VM] * 4, (info, perf, parts, step))
     got = exchange_tiles(pay)
+    halo = halo_of(call(step_faces_kernel, FACES, [VM], (step,)))
     end_row, end_col, ahead, slope = call(
         last_grid_kernel,
         (((2, 2, L, C), VM), ((2, R, LANES), VM), (THREE, HB), (TWO, HB)),

time: 92.4 us -> 91 us (0.985)
  waiting for transfers between devices: 7.87 us -> 4.8 us
  starting transfers between devices: 41.7 us -> 43.9 us
    all_to_all x3, waiting for transfers between devices: 7.83 us -> 4.76 us  [exchange(): return lax.all_to_all(array, AXES, split_axis=0, concat_axis=0, tiled=True)]
    all_to_all x3, starting transfers between devices: 28.4 us -> 30.6 us  [exchange(): return lax.all_to_all(array, AXES, split_axis=0, concat_axis=0, tiled=True)]
where the time goes in v8:
time: 91 us; the launch traced here: 90.7 us
  starting transfers between devices  43.9 us (48%)
  Pallas kernels  41 us (45%)
  waiting for transfers between devices  4.8 us (5%)
  between operations  0.99 us (1%)
    pallas_call x12, Pallas kernels, call(): pl.pallas_call(kernel, out_shape=shapes, in_specs=ins, out_specs=tuple((w...  41 us
    all_to_all x3, starting transfers between devices, exchange(): return lax.all_to_all(array, AXES, split_axis=0, concat_axis=0, tiled=True)  30.6 us
    ppermute x16, starting transfers between devices, halo_of(): got = {n: lax.ppermute(faces[n], AXES, swaps[n]) for n in (3, 1, 2, 0)}  13.3 us
    all_to_all x3, waiting for transfers between devices, exchange(): return lax.all_to_all(array, AXES, split_axis=0, concat_axis=0, tiled=True)  4.76 us
  transfers between devices with their start and end apart: 19, of which 3 were waited for; matrix products, arithmetic and copies ran while one was open for 0% of the time, Pallas kernels for 31%

profile of v8, /device:TPU:1, one launch (start us, length us, event | category | flops | bytes accessed | tf_op | source)
XLA Modules:
  0.0 90.7 jit_solution(9579787469914041100)
XLA Ops:
  0.6 2.3 %shard_map.138 = (f32[32,256]{1,0:T(8,128)S(1)}, f32[32,256]{1,0:T(8,128)S(1)}, f32[32,128]{1,0:T(8,128)S(1)}, f32[32,128]{1,0:T(8,128)S(1)}, f32[8,64,256]{2,1,...) custom-call(s32[1,256]{1,0:T(1,128)} %bitcast.19, ...), custom_call_target="tpu_custom_call" | custom-call | bytes 3148928 | tf_op jit(solution)/shard_map/pallas_call | solution.py:711
  2.9 1.5 %collective-permute-start = (f32[32,256]{1,0:T(8,128)S(1)}, f32[32,256]{1,0:T(8,128)S(1)}, u32[]{:S(2)}, u32[]{:S(2)}) collective-permute-start(f32[32,256]{1,0:T(8,128)S(1)} %get-tuple-element.72), channel_id=1, source_target_pairs={{0,16},{1,17},{2,18},{3,19},{4,20},{5,21},{6,22},{7,23},{8,24},{9,... | collective-permute-start | bytes 98312 | tf_op jit(solution)/shard_map/ppermute | solution.py:756
  4.4 1.4 %collective-permute-start.1 = (f32[32,256]{1,0:T(8,128)S(1)}, f32[32,256]{1,0:T(8,128)S(1)}, u32[]{:S(2)}, u32[]{:S(2)}) collective-permute-start(f32[32,256]{1,0:T(8,128)S(1)} %get-tuple-element.73), channel_id=1, source_target_pairs={{0,1},{1,0},{2,3},{3,2},{4,5},{5,4},{6,7},{7,6},{8,9},{9,8},{10,11... | collective-permute-start | bytes 98312 | tf_op jit(solution)/shard_map/ppermute | solution.py:756
  5.8 1.2 %collective-permute-start.2 = (f32[32,128]{1,0:T(8,128)S(1)}, f32[32,128]{1,0:T(8,128)S(1)}, u32[]{:S(2)}, u32[]{:S(2)}) collective-permute-start(f32[32,128]{1,0:T(8,128)S(1)} %get-tuple-element.74), channel_id=1, source_target_pairs={{0,1},{1,0},{2,3},{3,2},{4,5},{5,4},{6,7},{7,6},{8,9},{9,8},{10,11... | collective-permute-start | bytes 49160 | tf_op jit(solution)/shard_map/ppermute | solution.py:756
  7.0 0.0 collective-permute-start.3
  7.0 1.9 %shard_map.139 = (f32[128,128]{1,0:T(8,128)}, f32[8,256]{1,0:T(8,128)S(1)}) custom-call(f32[8,256]{1,0:T(8,128)S(1)} %get-tuple-element.66.info, f32[8,128]{1,0:T(8,128)S(1)} %get-tuple-element.67.own, f32[8,64,256]{2,1,0:T(8,128)S(1)} %get-tuple-element.68.p, f32[8,64,256]{2,1,0:T(8,128)S(1)} %get-tuple-element.69.sw, f32[8,64,256]{2,1,0:T(8,128)S(1)} %get-tuple-element.70.sg), custom_call_target="tpu_custom_call" | custom-call | bytes 1585152 | tf_op jit(solution)/shard_map/pallas_call | solution.py:711
  8.9 0.0 collective-permute-done.2.refs_2_
  8.9 0.0 collective-permute-done.3.refs_3_
  8.9 0.0 collective-permute-done.refs_0_
  8.9 0.0 collective-permute-done.1.refs_1_
  8.9 12.5 %all-to-all-start = ((f32[128,1,128]{2,1,0:T(1,128)}), f32[128,1,128]{2,1,0:T(1,128)S(1)}, u32[]{:S(2)}, u32[]{:S(2)}) async-start(f32[128,1,128]{2,1,0:T(1,128)} %bitcast.6), calls=%async_computation | async-start | bytes 131072 | tf_op jit(solution)/shard_map/all_to_all | solution.py:732
  21.4 9.0 %shard_map.141 = (f32[2,3,8,256]{3,2,1,0:T(8,128)S(1)}, f32[3,64,128]{2,1,0:T(8,128)S(1)}, f32[8,64,256]{2,1,0:T(8,128)S(1)}, f32[8,64,256]{2,1,0:T(8,128)S(1)},...) custom-call(f32[8,256]{1,0:T(8,128)S(1)} %get-tuple-element.66.info,, ...), custom_call_target="tpu_custom_call" | custom-call | flops 52428800 | bytes 5349376 | tf_op jit(solution)/shard_map/pallas_call | solution.py:711
  30.5 0.7 all-to-all-done
  31.2 2.5 %shard_map.142 = (f32[8,128]{1,0:T(8,128)S(1)}, f32[1,16]{1,0:T(1,128)}, f32[8,64,256]{2,1,0:T(8,128)S(1)}, f32[8,64,256]{2,1,0:T(8,128)S(1)}, f32[768,128]{1,0:T(8,128)}) custom-call(f32[128,128]{1,0:T(8,128)S(1)} %bitcast.18, f32[8,256]{1,0:T(8,128)S(1)} %get-tuple-element.66.info, f32[8,128]{1,0:T(8,128)S(1)} %get-tuple-element.67.own, ...), custom_call_target="tpu_custom_call" | custom-call | bytes 1134592 | tf_op jit(solution)/shard_map/pallas_call | solution.py:711
  33.6 9.1 %all-to-all-start.1 = ((f32[128,1,768]{2,1,0:T(1,128)}), f32[128,1,768]{2,1,0:T(1,128)S(1)}, u32[]{:S(2)}, u32[]{:S(2)}) async-start(f32[128,1,768]{2,1,0:T(1,128)} %bitcast.9), calls=%async_computation.1 | async-start | bytes 786432 | tf_op jit(solution)/shard_map/all_to_all | solution.py:732
  42.7 0.3 shard_map.144
  43.0 1.1 %collective-permute-start.4 = (f32[8,256]{1,0:T(8,128)S(1)}, f32[8,256]{1,0:T(8,128)S(1)}, u32[]{:S(2)}, u32[]{:S(2)}) collective-permute-start(f32[8,256]{1,0:T(8,128)S(1)} %get-tuple-element.100), channel_id=1, source_target_pairs={{0,16},{1,17},{2,18},{3,19},{4,20},{5,21},{6,22},{7,23},{8,24},{9,... | collective-permute-start | bytes 24584 | tf_op jit(solution)/shard_map/ppermute | solution.py:756
  44.1 0.7 collective-permute-start.5
  44.8 1.2 %collective-permute-start.6 = (f32[8,128]{1,0:T(8,128)S(1)}, f32[8,128]{1,0:T(8,128)S(1)}, u32[]{:S(2)}, u32[]{:S(2)}) collective-permute-start(f32[8,128]{1,0:T(8,128)S(1)} %get-tuple-element.102), channel_id=1, source_target_pairs={{0,1},{1,0},{2,3},{3,2},{4,5},{5,4},{6,7},{7,6},{8,9},{9,8},{10,11... | collective-permute-start | bytes 12296 | tf_op jit(solution)/shard_map/ppermute | solution.py:756
  46.0 0.2 collective-permute-start.7
  46.2 6.7 %shard_map.143 = (f32[8,64,256]{2,1,0:T(8,128)S(1)}, f32[2,8,256]{2,1,0:T(8,128)S(1)}, f32[64,128]{1,0:T(8,128)S(1)}, f32[3,8,64,256]{3,2,1,0:T(8,128)}, f32[6,8,64,256]{3,2,1,0:T(8,128)}) custom-call(f32[2,3,8,256]{3,2,1,0:T(8,128)S(1)} %get-tuple-element.80.coef_row, f32[3,64,128]{2,1,0:T(8,128)S(1)} %get-tuple-element.81.coef_col, ...), custom_call_target="tpu_custom_call" | custom-call | flops 13107200 | bytes 9125888 | tf_op jit(solution)/shard_map/pallas_call | solution.py:711
  52.9 0.0 collective-permute-done.6.col_first
  53.0 0.0 collective-permute-done.7.col_second
  53.0 0.0 collective-permute-done.4.row_first
  53.0 0.0 collective-permute-done.5.row_second
  53.0 2.6 %all-to-all-done.1 = f32[128,1,768]{2,1,0:T(1,128)S(1)} async-done(((f32[128,1,768]{2,1,0:T(1,128)}), f32[128,1,768]{2,1,0:T(1,128)S(1)}, u32[]{:S(2)}, u32[]{:S(2)}) %all-to-all-start.1) | async-done | bytes 393248 | tf_op jit(solution)/shard_map/all_to_all | solution.py:732
  55.6 0.9 %shard_map.145 = (f32[8,256]{1,0:T(8,128)S(1)}, f32[8,256]{1,0:T(8,128)S(1)}, f32[8,128]{1,0:T(8,128)S(1)}, f32[8,128]{1,0:T(8,128)S(1)}, f32[8,64,256]{2,1,0:T(8,128)S(1)}) custom-call(f32[768,128]{1,0:T(8,128)S(1)} %bitcast.15, f32[8,256]{1,0:T(8,128)S(1)} %get-tuple-element.66.info, f32[8,64,256]{2,1,0:T(8,128)S(1)} %get-tuple-element.97.ahead, ...), custom_call_target="tpu_custom_call" | custom-call | bytes 1523712 | tf_op jit(solution)/shard_map/pallas_call | solution.py:711
  56.5 0.6 collective-permute-start.8
  57.1 0.4 collective-permute-start.9
  57.5 0.3 collective-permute-start.10
  57.8 1.4 %collective-permute-start.11 = (f32[8,128]{1,0:T(8,128)S(1)}, f32[8,128]{1,0:T(8,128)S(1)}, u32[]{:S(2)}, u32[]{:S(2)}) collective-permute-start(f32[8,128]{1,0:T(8,128)S(1)} %get-tuple-element.112), channel_id=1, source_target_pairs={{0,16},{1,2},{2,1},{3,4},{4,3},{5,6},{6,5},{7,8},{8,7},{9,10},{10,... | collective-permute-start | bytes 12296 | tf_op jit(solution)/shard_map/ppermute | solution.py:756
  59.2 2.1 %shard_map.146 = (f32[2,128,128]{2,1,0:T(8,128)S(1)}, f32[8,128]{1,0:T(8,128)S(1)}, f32[8,64,256]{2,1,0:T(8,128)S(1)}, f32[6,8,64,256]{3,2,1,0:T(8,128)S(1)}) custom-call(f32[768,128]{1,0:T(8,128)S(1)} %bitcast.16, f32[8,256]{1,0:T(8,128)S(1)} %get-tuple-element.66.info, f32[8,256]{1,0:T(8,128)S(1)} %get-tuple-element.84.perf, ...), custom_call_target="tpu_custom_call" | custom-call | bytes 4079616 | tf_op jit(solution)/shard_map/pallas_call | solution.py:711
  61.3 0.0 collective-permute-done.10.col_first
  61.3 0.0 collective-permute-done.11.col_second
  61.3 0.0 collective-permute-done.8.row_first
  61.3 0.0 collective-permute-done.9.row_second
  61.3 3.1 %shard_map.147 = (f32[8,64,256]{2,1,0:T(8,128)S(1)}, f32[768,128]{1,0:T(8,128)}) custom-call(f32[8,256]{1,0:T(8,128)S(1)} %get-tuple-element.66.info, f32[8,256]{1,0:T(8,128)S(1)} %get-tuple-element.84.perf, f32[8,128]{1,0:T(8,128)S(1)} %get-tuple-element.106.parts, f32[8,64,256]{2,1,0:T(8,128)S(1)} %get-tuple-element.107.spread, ...), custom_call_target="tpu_custom_call" | custom-call | bytes 5287936 | tf_op jit(solution)/shard_map/pallas_call | solution.py:711
  64.4 9.0 %all-to-all-start.2 = ((f32[128,1,768]{2,1,0:T(1,128)}), f32[128,1,768]{2,1,0:T(1,128)S(1)}, u32[]{:S(2)}, u32[]{:S(2)}) async-start(f32[128,1,768]{2,1,0:T(1,128)} %bitcast.11), calls=%async_computation.2 | async-start | bytes 786432 | tf_op jit(solution)/shard_map/all_to_all | solution.py:732
  73.4 0.3 shard_map.149
  73.6 1.1 %collective-permute-start.12 = (f32[8,256]{1,0:T(8,128)S(1)}, f32[8,256]{1,0:T(8,128)S(1)}, u32[]{:S(2)}, u32[]{:S(2)}) collective-permute-start(f32[8,256]{1,0:T(8,128)S(1)} %get-tuple-element.120), channel_id=1, source_target_pairs={{0,16},{1,17},{2,18},{3,19},{4,20},{5,21},{6,22},{7,23},{8,24},{9,... | collective-permute-start | bytes 24584 | tf_op jit(solution)/shard_map/ppermute | solution.py:756
  74.8 0.7 collective-permute-start.13
  75.5 1.2 %collective-permute-start.14 = (f32[8,128]{1,0:T(8,128)S(1)}, f32[8,128]{1,0:T(8,128)S(1)}, u32[]{:S(2)}, u32[]{:S(2)}) collective-permute-start(f32[8,128]{1,0:T(8,128)S(1)} %get-tuple-element.122), channel_id=1, source_target_pairs={{0,1},{1,0},{2,3},{3,2},{4,5},{5,4},{6,7},{7,6},{8,9},{9,8},{10,11... | collective-permute-start | bytes 12296 | tf_op jit(solution)/shard_map/ppermute | solution.py:756
  76.7 0.2 collective-permute-start.15
  76.9 7.8 %shard_map.148 = (f32[2,2,8,256]{3,2,1,0:T(8,128)S(1)}, f32[2,64,128]{2,1,0:T(8,128)S(1)}, f32[3,8,64,256]{3,2,1,0:T(8,128)}, f32[2,8,64,256]{3,2,1,0:T(8,128)}) custom-call(f32[2,3,8,256]{3,2,1,0:T(8,128)S(1)} %get-tuple-element.80.coef_row, f32[3,64,128]{2,1,0:T(8,128)S(1)} %get-tuple-element.81.coef_col, f32[8,64,256]{2,1,0:T(8,128)S(1)} %get-tuple-element.82.head, ...), custom_call_target="tpu_custom_call" | custom-call | flops 19660800 | bytes 10747904 | tf_op jit(solution)/shard_map/pallas_call | solution.py:711
  84.7 0.0 collective-permute-done.14.col_first
  84.7 0.0 collective-permute-done.12.row_first
  84.7 1.5 %all-to-all-done.2 = f32[128,1,768]{2,1,0:T(1,128)S(1)} async-done(((f32[128,1,768]{2,1,0:T(1,128)}), f32[128,1,768]{2,1,0:T(1,128)S(1)}, u32[]{:S(2)}, u32[]{:S(2)}) %all-to-all-start.2) | async-done | bytes 393248 | tf_op jit(solution)/shard_map/all_to_all | solution.py:732
  86.2 4.3 %shard_map.150 = (f32[3,8,64,256]{3,2,1,0:T(8,128)}, f32[1,16]{1,0:T(1,128)}) custom-call(f32[768,128]{1,0:T(8,128)S(1)} %bitcast.17, f32[8,256]{1,0:T(8,128)S(1)} %get-tuple-element.66.info, f32[2,128,128]{2,1,0:T(8,128)S(1)} %get-tuple-element.114.table, f32[8,128]{1,0:T(8,128)S(1)} %get-tuple-element.115.mine, f32[8,64,256]{2,1,0:T(8,128)S(1)} %get-tuple-element.82.head, ...), custom_call_target="tpu_custom_call" | custom-call | bytes 3854336 | tf_op jit(solution)/shard_map/pallas_call | solution.py:711
  (3 shorter events, 0.0 us)
Async XLA Ops:
  2.9 6.0 %collective-permute-start = (f32[32,256]{1,0:T(8,128)S(1)}, f32[32,256]{1,0:T(8,128)S(1)}, u32[]{:S(2)}, u32[]{:S(2)}) collective-permute-start(f32[32,256]{1,0:T(8,128)S(1)} %get-tuple-element.72), channel_id=1, source_target_pairs={{0,16},{1,17},{2,18},{3,19},{4,20},{5,21},{6,22},{7,23},{8,24},{9,... | collective-permute-start | bytes 98312 | tf_op jit(solution)/shard_map/ppermute | solution.py:756
  4.4 4.5 %collective-permute-start.1 = (f32[32,256]{1,0:T(8,128)S(1)}, f32[32,256]{1,0:T(8,128)S(1)}, u32[]{:S(2)}, u32[]{:S(2)}) collective-permute-start(f32[32,256]{1,0:T(8,128)S(1)} %get-tuple-element.73), channel_id=1, source_target_pairs={{0,1},{1,0},{2,3},{3,2},{4,5},{5,4},{6,7},{7,6},{8,9},{9,8},{10,11... | collective-permute-start | bytes 98312 | tf_op jit(solution)/shard_map/ppermute | solution.py:756
  5.8 3.1 %collective-permute-start.2 = (f32[32,128]{1,0:T(8,128)S(1)}, f32[32,128]{1,0:T(8,128)S(1)}, u32[]{:S(2)}, u32[]{:S(2)}) collective-permute-start(f32[32,128]{1,0:T(8,128)S(1)} %get-tuple-element.74), channel_id=1, source_target_pairs={{0,1},{1,0},{2,3},{3,2},{4,5},{5,4},{6,7},{7,6},{8,9},{9,8},{10,11... | collective-permute-start | bytes 49160 | tf_op jit(solution)/shard_map/ppermute | solution.py:756
  7.0 1.9 %collective-permute-start.3 = (f32[32,128]{1,0:T(8,128)S(1)}, f32[32,128]{1,0:T(8,128)S(1)}, u32[]{:S(2)}, u32[]{:S(2)}) collective-permute-start(f32[32,128]{1,0:T(8,128)S(1)} %get-tuple-element.75), channel_id=1, source_target_pairs={{0,16},{1,2},{2,1},{3,4},{4,3},{5,6},{6,5},{7,8},{8,7},{9,10},{10,... | collective-permute-start | bytes 49160 | tf_op jit(solution)/shard_map/ppermute | solution.py:756
  8.9 22.2 %all-to-all-start = ((f32[128,1,128]{2,1,0:T(1,128)}), f32[128,1,128]{2,1,0:T(1,128)S(1)}, u32[]{:S(2)}, u32[]{:S(2)}) async-start(f32[128,1,128]{2,1,0:T(1,128)} %bitcast.6), calls=%async_computation | async-start | bytes 131072 | tf_op jit(solution)/shard_map/all_to_all | solution.py:732
  33.6 22.0 %all-to-all-start.1 = ((f32[128,1,768]{2,1,0:T(1,128)}), f32[128,1,768]{2,1,0:T(1,128)S(1)}, u32[]{:S(2)}, u32[]{:S(2)}) async-start(f32[128,1,768]{2,1,0:T(1,128)} %bitcast.9), calls=%async_computation.1 | async-start | bytes 786432 | tf_op jit(solution)/shard_map/all_to_all | solution.py:732
  43.0 10.0 %collective-permute-start.4 = (f32[8,256]{1,0:T(8,128)S(1)}, f32[8,256]{1,0:T(8,128)S(1)}, u32[]{:S(2)}, u32[]{:S(2)}) collective-permute-start(f32[8,256]{1,0:T(8,128)S(1)} %get-tuple-element.100), channel_id=1, source_target_pairs={{0,16},{1,17},{2,18},{3,19},{4,20},{5,21},{6,22},{7,23},{8,24},{9,... | collective-permute-start | bytes 24584 | tf_op jit(solution)/shard_map/ppermute | solution.py:756
  44.1 8.9 %collective-permute-start.5 = (f32[8,256]{1,0:T(8,128)S(1)}, f32[8,256]{1,0:T(8,128)S(1)}, u32[]{:S(2)}, u32[]{:S(2)}) collective-permute-start(f32[8,256]{1,0:T(8,128)S(1)} %get-tuple-element.101), channel_id=1, source_target_pairs={{0,1},{1,0},{2,3},{3,2},{4,5},{5,4},{6,7},{7,6},{8,9},{9,8},{10,11... | collective-permute-start | bytes 24584 | tf_op jit(solution)/shard_map/ppermute | solution.py:756
  44.8 8.1 %collective-permute-start.6 = (f32[8,128]{1,0:T(8,128)S(1)}, f32[8,128]{1,0:T(8,128)S(1)}, u32[]{:S(2)}, u32[]{:S(2)}) collective-permute-start(f32[8,128]{1,0:T(8,128)S(1)} %get-tuple-element.102), channel_id=1, source_target_pairs={{0,1},{1,0},{2,3},{3,2},{4,5},{5,4},{6,7},{7,6},{8,9},{9,8},{10,11... | collective-permute-start | bytes 12296 | tf_op jit(solution)/shard_map/ppermute | solution.py:756
  46.0 7.0 %collective-permute-start.7 = (f32[8,128]{1,0:T(8,128)S(1)}, f32[8,128]{1,0:T(8,128)S(1)}, u32[]{:S(2)}, u32[]{:S(2)}) collective-permute-start(f32[8,128]{1,0:T(8,128)S(1)} %get-tuple-element.103), channel_id=1, source_target_pairs={{0,16},{1,2},{2,1},{3,4},{4,3},{5,6},{6,5},{7,8},{8,7},{9,10},{10,... | collective-permute-start | bytes 12296 | tf_op jit(solution)/shard_map/ppermute | solution.py:756
  56.5 4.8 %collective-permute-start.8 = (f32[8,256]{1,0:T(8,128)S(1)}, f32[8,256]{1,0:T(8,128)S(1)}, u32[]{:S(2)}, u32[]{:S(2)}) collective-permute-start(f32[8,256]{1,0:T(8,128)S(1)} %get-tuple-element.109), channel_id=1, source_target_pairs={{0,16},{1,17},{2,18},{3,19},{4,20},{5,21},{6,22},{7,23},{8,24},{9,... | collective-permute-start | bytes 24584 | tf_op jit(solution)/shard_map/ppermute | solution.py:756
  57.1 4.2 %collective-permute-start.9 = (f32[8,256]{1,0:T(8,128)S(1)}, f32[8,256]{1,0:T(8,128)S(1)}, u32[]{:S(2)}, u32[]{:S(2)}) collective-permute-start(f32[8,256]{1,0:T(8,128)S(1)} %get-tuple-element.110), channel_id=1, source_target_pairs={{0,1},{1,0},{2,3},{3,2},{4,5},{5,4},{6,7},{7,6},{8,9},{9,8},{10,11... | collective-permute-start | bytes 24584 | tf_op jit(solution)/shard_map/ppermute | solution.py:756
  57.5 3.8 %collective-permute-start.10 = (f32[8,128]{1,0:T(8,128)S(1)}, f32[8,128]{1,0:T(8,128)S(1)}, u32[]{:S(2)}, u32[]{:S(2)}) collective-permute-start(f32[8,128]{1,0:T(8,128)S(1)} %get-tuple-element.111), channel_id=1, source_target_pairs={{0,1},{1,0},{2,3},{3,2},{4,5},{5,4},{6,7},{7,6},{8,9},{9,8},{10,11... | collective-permute-start | bytes 12296 | tf_op jit(solution)/shard_map/ppermute | solution.py:756
  57.8 3.5 %collective-permute-start.11 = (f32[8,128]{1,0:T(8,128)S(1)}, f32[8,128]{1,0:T(8,128)S(1)}, u32[]{:S(2)}, u32[]{:S(2)}) collective-permute-start(f32[8,128]{1,0:T(8,128)S(1)} %get-tuple-element.112), channel_id=1, source_target_pairs={{0,16},{1,2},{2,1},{3,4},{4,3},{5,6},{6,5},{7,8},{8,7},{9,10},{10,... | collective-permute-start | bytes 12296 | tf_op jit(solution)/shard_map/ppermute | solution.py:756
  64.4 21.8 %all-to-all-start.2 = ((f32[128,1,768]{2,1,0:T(1,128)}), f32[128,1,768]{2,1,0:T(1,128)S(1)}, u32[]{:S(2)}, u32[]{:S(2)}) async-start(f32[128,1,768]{2,1,0:T(1,128)} %bitcast.11), calls=%async_computation.2 | async-start | bytes 786432 | tf_op jit(solution)/shard_map/all_to_all | solution.py:732
  73.6 11.0 %collective-permute-start.12 = (f32[8,256]{1,0:T(8,128)S(1)}, f32[8,256]{1,0:T(8,128)S(1)}, u32[]{:S(2)}, u32[]{:S(2)}) collective-permute-start(f32[8,256]{1,0:T(8,128)S(1)} %get-tuple-element.120), channel_id=1, source_target_pairs={{0,16},{1,17},{2,18},{3,19},{4,20},{5,21},{6,22},{7,23},{8,24},{9,... | collective-permute-start | bytes 24584 | tf_op jit(solution)/shard_map/ppermute | solution.py:756
  74.8 9.9 %collective-permute-start.13 = (f32[8,256]{1,0:T(8,128)S(1)}, f32[8,256]{1,0:T(8,128)S(1)}, u32[]{:S(2)}, u32[]{:S(2)}) collective-permute-start(f32[8,256]{1,0:T(8,128)S(1)} %get-tuple-element.121), channel_id=1, source_target_pairs={{0,1},{1,0},{2,3},{3,2},{4,5},{5,4},{6,7},{7,6},{8,9},{9,8},{10,11... | collective-permute-start | bytes 24584 | tf_op jit(solution)/shard_map/ppermute | solution.py:756
  75.5 9.2 %collective-permute-start.14 = (f32[8,128]{1,0:T(8,128)S(1)}, f32[8,128]{1,0:T(8,128)S(1)}, u32[]{:S(2)}, u32[]{:S(2)}) collective-permute-start(f32[8,128]{1,0:T(8,128)S(1)} %get-tuple-element.122), channel_id=1, source_target_pairs={{0,1},{1,0},{2,3},{3,2},{4,5},{5,4},{6,7},{7,6},{8,9},{9,8},{10,11... | collective-permute-start | bytes 12296 | tf_op jit(solution)/shard_map/ppermute | solution.py:756
  76.7 8.0 %collective-permute-start.15 = (f32[8,128]{1,0:T(8,128)S(1)}, f32[8,128]{1,0:T(8,128)S(1)}, u32[]{:S(2)}, u32[]{:S(2)}) collective-permute-start(f32[8,128]{1,0:T(8,128)S(1)} %get-tuple-element.123), channel_id=1, source_target_pairs={{0,16},{1,2},{2,1},{3,4},{4,3},{5,6},{6,5},{7,8},{8,7},{9,10},{10,... | collective-permute-start | bytes 12296 | tf_op jit(solution)/shard_map/ppermute | solution.py:756

commit v9 on v8

--- a/solution.py
+++ b/solution.py
@@ -309,12 +309,6 @@
     return neighbours(step, l, lo, (blank, blank), (0.0, 0.0))
 
 
-def step_neighbours(step, row_lo, row_hi, columns, l, lo):
-    rows = (row_lo[pl.ds(l, 1), :], row_hi[pl.ds(l, 1), :])
-    ends = [lane_of(columns, n)[lo : lo + BLOCK] for n in (l, L + l)]
-    return neighbours(step, l, lo, rows, ends)
-
-
 def face_terms(tx, ty, tz, l, rows):
     return (tx[0, l, rows, :], tx[1, l, rows, :], ty[0, l, rows, :], ty[1, l, rows, :], tz[l, rows, :], tz[l + 1, rows, :])
 
@@ -331,10 +325,10 @@
     return parts
 
 
-def add_faces(field, l, low, high, columns):
+def put_with_faces(field, l, x, low, high, columns):
     lane = iota((R, LANES), 1)
-    field[l, :, 0:LANES] += jnp.where(lane == 0, columns[:, l : l + 1], 0.0)
-    field[l, :, C - LANES : C] += jnp.where(lane == LANES - 1, columns[:, L + l : L + l + 1], 0.0)
+    field[l, :, 0:LANES] = x[:, 0:LANES] + jnp.where(lane == 0, columns[:, l : l + 1], 0.0)
+    field[l, :, LANES:C] = x[:, LANES:C] + jnp.where(lane == LANES - 1, columns[:, L + l : L + l + 1], 0.0)
     field[l, 0:1, :] += low
     field[l, R - 1 : R, :] += high
 
@@ -535,18 +529,17 @@
     well_row = info[1:2].astype(i32)
     moves = gather_wells(tile_of(got, 5), well_row >> 4, (well_row & 15) + 16)
     wells = scatter(cell_row, info[2:3] * moves).reshape(L, R, C)
-    step[...] = ahead[...] + head[...] * wells
     columns = end_col[...] * unpack_columns(col_first, col_second)
     low, high = from_partner("gx", row_first[...], row_second[...])
     low = end_row[0] * low
     high = end_row[1] * high
     for l in range(L):
-        add_faces(step, l, low[l : l + 1], high[l : l + 1], columns)
+        put_with_faces(step, l, ahead[l] + head[l] * wells[l], low[l : l + 1], high[l : l + 1], columns)
     write_faces(step, (out_row_first, out_row_second, out_col_first, out_col_second))
 
 
 def wells_kernel(
-    got, info, perf, step, gain_h, table, parts, spread, gain, sems,
+    got, info, perf, step, base, head, gain_h, table, parts, near, gain, spread, sems,
 ):
     copies = start_copies(((gain_h, gain),), sems)
     tail = tile_of(got, 5)
@@ -566,25 +559,25 @@
     parts[...] = jnp.concatenate(tiles + [jnp.zeros((2, LANES), f32)], axis=0)
     wait_copies(copies)
 
-
-def third_kernel(
-    info, perf, parts, spread, old, base, gain, head, row_first, row_second, col_first, col_second,
-    step, pay, row_lo, row_hi,
-):
-    columns = unpack_columns(col_first, col_second)
-    row_lo[...], row_hi[...] = from_partner("gx", row_first[...], row_second[...])
-
     def layer(l, carry):
         for lo in range(0, R, BLOCK):
             at = slice(lo, lo + BLOCK)
-            nexts = step_neighbours(old, row_lo, row_hi, columns, l, lo)
             total = base[l, at, :] + head[l, at, :] * spread[l, at, :]
-            for j in range(6):
-                total = total + gain[j, l, at, :] * nexts[j]
-            step[l, at, :] = total
+            for j, q in enumerate(inner_neighbours(step, l, lo)):
+                total = total + gain[j, l, at, :] * q
+            near[l, at, :] = total
         return carry
 
     lax.fori_loop(0, L, layer, 0)
+
+
+def third_kernel(info, perf, parts, near, end_row, end_col, row_first, row_second, col_first, col_second, step, pay):
+    columns = end_col[...] * unpack_columns(col_first, col_second)
+    low, high = from_partner("gx", row_first[...], row_second[...])
+    low = end_row[0] * low
+    high = end_row[1] * high
+    for l in range(L):
+        put_with_faces(step, l, near[l], low[l : l + 1], high[l : l + 1], columns)
     here = gather_cells(to_column(info[0:1]).astype(i32), (flat(step),))[0]
     well_row = info[1:2].astype(i32)
     slot_column = to_column(info[1:2]).astype(i32) & 15
@@ -692,8 +685,8 @@
         high = highs[l : l + 1]
         for n in range(3):
             rows = [gain_row[side, l : l + 1, :] if n == 0 else end_row[side, n - 1, l : l + 1, :] for side in range(2)]
-            update[n, l] = ahead[n, l] + (head[l] if n == 0 else slope[n - 1, l]) * wells[l]
-            add_faces(update.at[n], l, rows[0] * low, rows[1] * high, columns[n])
+            x = ahead[n, l] + (head[l] if n == 0 else slope[n - 1, l]) * wells[l]
+            put_with_faces(update.at[n], l, x, rows[0] * low, rows[1] * high, columns[n])
         layer_copies(outs, sems_out, l)[0].start()
     for l in range(L):
         wait_copies(layer_copies(outs, sems_out, l))
@@ -824,19 +817,18 @@
         (got, info, ahead, head, gain_row, gain_col, *halo),
     )
     halo = halo_of(faces)
-    table, parts, spread, gain_near = call(
+    table, parts, near = call(
         wells_kernel,
-        (((2, DEVICES, LANES), VM), (SMALL, VM), (FIELD, VM), (SIX, VM)),
-        [VM] * 4 + [HB],
-        (got, info, perf, step, gain),
-        [sem((1,))],
+        (((2, DEVICES, LANES), VM), (SMALL, VM), (FIELD, VM)),
+        [VM] * 6 + [HB],
+        (got, info, perf, step, start, head, gain),
+        [SIX, FIELD, sem((1,))],
     )
     step, pay = call(
         third_kernel,
         ((FIELD, VM), PAY),
-        [VM] * 12,
-        (info, perf, parts, spread, step, start, gain_near, head, *halo),
-        [(L, C), (L, C)],
+        [VM] * 10,
+        (info, perf, parts, near, gain_row, gain_col, *halo),
     )
     got = exchange_tiles(pay)
     halo = halo_of(call(step_faces_kernel, FACES, [VM], (step,)))

time: 91 us -> 90.8 us (level)
  starting transfers between devices: 43.9 us -> 42.9 us
    all_to_all x3, starting transfers between devices: 30.6 us -> 29.7 us  [exchange(): return lax.all_to_all(array, AXES, split_axis=0, concat_axis=0, tiled=True)]
  transfers between devices with their start and end apart: 19 -> 19, of which waited for: 3 -> 3; matrix products, arithmetic and copies ran while one was open for 0% -> 0% of each run, Pallas kernels for 31% -> 33%
where the time goes in v9:
time: 90.8 us; the launch traced here: 90.4 us
  starting transfers between devices  42.9 us (47%)
  Pallas kernels  41.7 us (46%)
  waiting for transfers between devices  4.81 us (5%)
  between operations  0.99 us (1%)
    pallas_call x12, Pallas kernels, call(): pl.pallas_call(kernel, out_shape=shapes, in_specs=ins, out_specs=tuple((w...  41.7 us
    all_to_all x3, starting transfers between devices, exchange(): return lax.all_to_all(array, AXES, split_axis=0, concat_axis=0, tiled=True)  29.7 us
    ppermute x16, starting transfers between devices, halo_of(): got = {n: lax.ppermute(faces[n], AXES, swaps[n]) for n in (3, 1, 2, 0)}  13.3 us
    all_to_all x3, waiting for transfers between devices, exchange(): return lax.all_to_all(array, AXES, split_axis=0, concat_axis=0, tiled=True)  4.77 us
  transfers between devices with their start and end apart: 19, of which 3 were waited for; matrix products, arithmetic and copies ran while one was open for 0% of the time, Pallas kernels for 33%

profile of v9, /device:TPU:1, one launch (start us, length us, event | category | flops | bytes accessed | tf_op | source)
XLA Modules:
  0.0 90.4 jit_solution(11329840503293378493)
XLA Ops:
  0.6 2.3 %shard_map.138 = (f32[32,256]{1,0:T(8,128)S(1)}, f32[32,256]{1,0:T(8,128)S(1)}, f32[32,128]{1,0:T(8,128)S(1)}, f32[32,128]{1,0:T(8,128)S(1)}, f32[8,64,256]{2,1,...) custom-call(s32[1,256]{1,0:T(1,128)} %bitcast.19, ...), custom_call_target="tpu_custom_call" | custom-call | bytes 3148928 | tf_op jit(solution)/shard_map/pallas_call | solution.py:704
  2.9 1.5 %collective-permute-start = (f32[32,256]{1,0:T(8,128)S(1)}, f32[32,256]{1,0:T(8,128)S(1)}, u32[]{:S(2)}, u32[]{:S(2)}) collective-permute-start(f32[32,256]{1,0:T(8,128)S(1)} %get-tuple-element.71), channel_id=1, source_target_pairs={{0,16},{1,17},{2,18},{3,19},{4,20},{5,21},{6,22},{7,23},{8,24},{9,... | collective-permute-start | bytes 98312 | tf_op jit(solution)/shard_map/ppermute | solution.py:749
  4.4 1.4 %collective-permute-start.1 = (f32[32,256]{1,0:T(8,128)S(1)}, f32[32,256]{1,0:T(8,128)S(1)}, u32[]{:S(2)}, u32[]{:S(2)}) collective-permute-start(f32[32,256]{1,0:T(8,128)S(1)} %get-tuple-element.72), channel_id=1, source_target_pairs={{0,1},{1,0},{2,3},{3,2},{4,5},{5,4},{6,7},{7,6},{8,9},{9,8},{10,11... | collective-permute-start | bytes 98312 | tf_op jit(solution)/shard_map/ppermute | solution.py:749
  5.8 1.2 %collective-permute-start.2 = (f32[32,128]{1,0:T(8,128)S(1)}, f32[32,128]{1,0:T(8,128)S(1)}, u32[]{:S(2)}, u32[]{:S(2)}) collective-permute-start(f32[32,128]{1,0:T(8,128)S(1)} %get-tuple-element.73), channel_id=1, source_target_pairs={{0,1},{1,0},{2,3},{3,2},{4,5},{5,4},{6,7},{7,6},{8,9},{9,8},{10,11... | collective-permute-start | bytes 49160 | tf_op jit(solution)/shard_map/ppermute | solution.py:749
  7.0 0.0 collective-permute-start.3
  7.0 1.9 %shard_map.139 = (f32[128,128]{1,0:T(8,128)}, f32[8,256]{1,0:T(8,128)S(1)}) custom-call(f32[8,256]{1,0:T(8,128)S(1)} %get-tuple-element.65.info, f32[8,128]{1,0:T(8,128)S(1)} %get-tuple-element.66.own, f32[8,64,256]{2,1,0:T(8,128)S(1)} %get-tuple-element.67.p, f32[8,64,256]{2,1,0:T(8,128)S(1)} %get-tuple-element.68.sw, f32[8,64,256]{2,1,0:T(8,128)S(1)} %get-tuple-element.69.sg), custom_call_target="tpu_custom_call" | custom-call | bytes 1585152 | tf_op jit(solution)/shard_map/pallas_call | solution.py:704
  8.9 0.0 collective-permute-done.2.refs_2_
  8.9 0.0 collective-permute-done.3.refs_3_
  8.9 0.0 collective-permute-done.refs_0_
  8.9 0.0 collective-permute-done.1.refs_1_
  8.9 12.5 %all-to-all-start = ((f32[128,1,128]{2,1,0:T(1,128)}), f32[128,1,128]{2,1,0:T(1,128)S(1)}, u32[]{:S(2)}, u32[]{:S(2)}) async-start(f32[128,1,128]{2,1,0:T(1,128)} %bitcast.6), calls=%async_computation | async-start | bytes 131072 | tf_op jit(solution)/shard_map/all_to_all | solution.py:725
  21.4 9.0 %shard_map.141 = (f32[2,3,8,256]{3,2,1,0:T(8,128)S(1)}, f32[3,64,128]{2,1,0:T(8,128)S(1)}, f32[8,64,256]{2,1,0:T(8,128)S(1)}, f32[8,64,256]{2,1,0:T(8,128)S(1)},...) custom-call(f32[8,256]{1,0:T(8,128)S(1)} %get-tuple-element.65.info,, ...), custom_call_target="tpu_custom_call" | custom-call | flops 52428800 | bytes 5349376 | tf_op jit(solution)/shard_map/pallas_call | solution.py:704
  30.5 0.7 all-to-all-done
  31.2 2.5 %shard_map.142 = (f32[8,128]{1,0:T(8,128)S(1)}, f32[1,16]{1,0:T(1,128)}, f32[8,64,256]{2,1,0:T(8,128)S(1)}, f32[8,64,256]{2,1,0:T(8,128)S(1)}, f32[768,128]{1,0:T(8,128)}) custom-call(f32[128,128]{1,0:T(8,128)S(1)} %bitcast.18, f32[8,256]{1,0:T(8,128)S(1)} %get-tuple-element.65.info, f32[8,128]{1,0:T(8,128)S(1)} %get-tuple-element.66.own, ...), custom_call_target="tpu_custom_call" | custom-call | bytes 1134592 | tf_op jit(solution)/shard_map/pallas_call | solution.py:704
  33.6 9.1 %all-to-all-start.1 = ((f32[128,1,768]{2,1,0:T(1,128)}), f32[128,1,768]{2,1,0:T(1,128)S(1)}, u32[]{:S(2)}, u32[]{:S(2)}) async-start(f32[128,1,768]{2,1,0:T(1,128)} %bitcast.9), calls=%async_computation.1 | async-start | bytes 786432 | tf_op jit(solution)/shard_map/all_to_all | solution.py:725
  42.7 0.3 shard_map.144
  43.0 1.1 %collective-permute-start.4 = (f32[8,256]{1,0:T(8,128)S(1)}, f32[8,256]{1,0:T(8,128)S(1)}, u32[]{:S(2)}, u32[]{:S(2)}) collective-permute-start(f32[8,256]{1,0:T(8,128)S(1)} %get-tuple-element.99), channel_id=1, source_target_pairs={{0,16},{1,17},{2,18},{3,19},{4,20},{5,21},{6,22},{7,23},{8,24},{9,... | collective-permute-start | bytes 24584 | tf_op jit(solution)/shard_map/ppermute | solution.py:749
  44.1 0.7 collective-permute-start.5
  44.8 1.2 %collective-permute-start.6 = (f32[8,128]{1,0:T(8,128)S(1)}, f32[8,128]{1,0:T(8,128)S(1)}, u32[]{:S(2)}, u32[]{:S(2)}) collective-permute-start(f32[8,128]{1,0:T(8,128)S(1)} %get-tuple-element.101), channel_id=1, source_target_pairs={{0,1},{1,0},{2,3},{3,2},{4,5},{5,4},{6,7},{7,6},{8,9},{9,8},{10,11... | collective-permute-start | bytes 12296 | tf_op jit(solution)/shard_map/ppermute | solution.py:749
  46.0 0.2 collective-permute-start.7
  46.2 6.7 %shard_map.143 = (f32[8,64,256]{2,1,0:T(8,128)S(1)}, f32[2,8,256]{2,1,0:T(8,128)S(1)}, f32[64,128]{1,0:T(8,128)S(1)}, f32[3,8,64,256]{3,2,1,0:T(8,128)}, f32[6,8,64,256]{3,2,1,0:T(8,128)}) custom-call(f32[2,3,8,256]{3,2,1,0:T(8,128)S(1)} %get-tuple-element.79.coef_row, f32[3,64,128]{2,1,0:T(8,128)S(1)} %get-tuple-element.80.coef_col, ...), custom_call_target="tpu_custom_call" | custom-call | flops 13107200 | bytes 9125888 | tf_op jit(solution)/shard_map/pallas_call | solution.py:704
  52.9 0.0 collective-permute-done.6.col_first
  53.0 0.0 collective-permute-done.7.col_second
  53.0 0.0 collective-permute-done.4.row_first
  53.0 0.0 collective-permute-done.5.row_second
  53.0 2.6 %all-to-all-done.1 = f32[128,1,768]{2,1,0:T(1,128)S(1)} async-done(((f32[128,1,768]{2,1,0:T(1,128)}), f32[128,1,768]{2,1,0:T(1,128)S(1)}, u32[]{:S(2)}, u32[]{:S(2)}) %all-to-all-start.1) | async-done | bytes 393248 | tf_op jit(solution)/shard_map/all_to_all | solution.py:725
  55.6 0.9 shard_map.145
  56.5 0.6 collective-permute-start.8
  57.1 0.4 collective-permute-start.9
  57.5 0.3 collective-permute-start.10
  57.8 1.4 %collective-permute-start.11 = (f32[8,128]{1,0:T(8,128)S(1)}, f32[8,128]{1,0:T(8,128)S(1)}, u32[]{:S(2)}, u32[]{:S(2)}) collective-permute-start(f32[8,128]{1,0:T(8,128)S(1)} %get-tuple-element.110), channel_id=1, source_target_pairs={{0,16},{1,2},{2,1},{3,4},{4,3},{5,6},{6,5},{7,8},{8,7},{9,10},{10,... | collective-permute-start | bytes 12296 | tf_op jit(solution)/shard_map/ppermute | solution.py:749
  59.2 3.7 %shard_map.146 = (f32[2,128,128]{2,1,0:T(8,128)S(1)}, f32[8,128]{1,0:T(8,128)S(1)}, f32[8,64,256]{2,1,0:T(8,128)S(1)}) custom-call(f32[768,128]{1,0:T(8,128)S(1)} %bitcast.16, f32[8,256]{1,0:T(8,128)S(1)} %get-tuple-element.65.info, f32[8,256]{1,0:T(8,128)S(1)} %get-tuple-element.83.perf, f32[8,64,256]{2,1,0:T(8,128)S(1)} %get-tuple-element.103.step, ...), custom_call_target="tpu_custom_call" | custom-call | bytes 5128192 | tf_op jit(solution)/shard_map/pallas_call | solution.py:704
  62.9 0.0 collective-permute-done.10.col_first
  63.0 0.0 collective-permute-done.11.col_second
  63.0 0.0 collective-permute-done.8.row_first
  63.0 2.1 %shard_map.147 = (f32[8,64,256]{2,1,0:T(8,128)S(1)}, f32[768,128]{1,0:T(8,128)}) custom-call(f32[8,256]{1,0:T(8,128)S(1)} %get-tuple-element.65.info, f32[8,256]{1,0:T(8,128)S(1)} %get-tuple-element.83.perf, f32[8,128]{1,0:T(8,128)S(1)} %get-tuple-element.105.parts, f32[8,64,256]{2,1,0:T(8,128)S(1)} %get-tuple-element.106.near, ...), custom_call_target="tpu_custom_call" | custom-call | bytes 618496 | tf_op jit(solution)/shard_map/pallas_call | solution.py:704
  65.1 8.0 %all-to-all-start.2 = ((f32[128,1,768]{2,1,0:T(1,128)}), f32[128,1,768]{2,1,0:T(1,128)S(1)}, u32[]{:S(2)}, u32[]{:S(2)}) async-start(f32[128,1,768]{2,1,0:T(1,128)} %bitcast.11), calls=%async_computation.2 | async-start | bytes 786432 | tf_op jit(solution)/shard_map/all_to_all | solution.py:725
  73.1 0.3 shard_map.149
  73.4 1.1 %collective-permute-start.12 = (f32[8,256]{1,0:T(8,128)S(1)}, f32[8,256]{1,0:T(8,128)S(1)}, u32[]{:S(2)}, u32[]{:S(2)}) collective-permute-start(f32[8,256]{1,0:T(8,128)S(1)} %get-tuple-element.118), channel_id=1, source_target_pairs={{0,16},{1,17},{2,18},{3,19},{4,20},{5,21},{6,22},{7,23},{8,24},{9,... | collective-permute-start | bytes 24584 | tf_op jit(solution)/shard_map/ppermute | solution.py:749
  74.5 0.7 collective-permute-start.13
  75.2 1.2 %collective-permute-start.14 = (f32[8,128]{1,0:T(8,128)S(1)}, f32[8,128]{1,0:T(8,128)S(1)}, u32[]{:S(2)}, u32[]{:S(2)}) collective-permute-start(f32[8,128]{1,0:T(8,128)S(1)} %get-tuple-element.120), channel_id=1, source_target_pairs={{0,1},{1,0},{2,3},{3,2},{4,5},{5,4},{6,7},{7,6},{8,9},{9,8},{10,11... | collective-permute-start | bytes 12296 | tf_op jit(solution)/shard_map/ppermute | solution.py:749
  76.4 0.2 collective-permute-start.15
  76.6 7.8 %shard_map.148 = (f32[2,2,8,256]{3,2,1,0:T(8,128)S(1)}, f32[2,64,128]{2,1,0:T(8,128)S(1)}, f32[3,8,64,256]{3,2,1,0:T(8,128)}, f32[2,8,64,256]{3,2,1,0:T(8,128)}) custom-call(f32[2,3,8,256]{3,2,1,0:T(8,128)S(1)} %get-tuple-element.79.coef_row, f32[3,64,128]{2,1,0:T(8,128)S(1)} %get-tuple-element.80.coef_col, f32[8,64,256]{2,1,0:T(8,128)S(1)} %get-tuple-element.81.head, ...), custom_call_target="tpu_custom_call" | custom-call | flops 19660800 | bytes 10747904 | tf_op jit(solution)/shard_map/pallas_call | solution.py:704
  84.4 0.0 collective-permute-done.14.col_first
  84.4 0.0 collective-permute-done.12.row_first
  84.4 0.0 collective-permute-done.13.row_second
  84.4 1.5 %all-to-all-done.2 = f32[128,1,768]{2,1,0:T(1,128)S(1)} async-done(((f32[128,1,768]{2,1,0:T(1,128)}), f32[128,1,768]{2,1,0:T(1,128)S(1)}, u32[]{:S(2)}, u32[]{:S(2)}) %all-to-all-start.2) | async-done | bytes 393248 | tf_op jit(solution)/shard_map/all_to_all | solution.py:725
  85.9 4.3 %shard_map.150 = (f32[3,8,64,256]{3,2,1,0:T(8,128)}, f32[1,16]{1,0:T(1,128)}) custom-call(f32[768,128]{1,0:T(8,128)S(1)} %bitcast.17, f32[8,256]{1,0:T(8,128)S(1)} %get-tuple-element.65.info, f32[2,128,128]{2,1,0:T(8,128)S(1)} %get-tuple-element.112.table, f32[8,128]{1,0:T(8,128)S(1)} %get-tuple-element.113.mine, f32[8,64,256]{2,1,0:T(8,128)S(1)} %get-tuple-element.81.head, ...), custom_call_target="tpu_custom_call" | custom-call | bytes 3854336 | tf_op jit(solution)/shard_map/pallas_call | solution.py:704
  (3 shorter events, 0.0 us)
Async XLA Ops:
  2.9 6.0 %collective-permute-start = (f32[32,256]{1,0:T(8,128)S(1)}, f32[32,256]{1,0:T(8,128)S(1)}, u32[]{:S(2)}, u32[]{:S(2)}) collective-permute-start(f32[32,256]{1,0:T(8,128)S(1)} %get-tuple-element.71), channel_id=1, source_target_pairs={{0,16},{1,17},{2,18},{3,19},{4,20},{5,21},{6,22},{7,23},{8,24},{9,... | collective-permute-start | bytes 98312 | tf_op jit(solution)/shard_map/ppermute | solution.py:749
  4.4 4.5 %collective-permute-start.1 = (f32[32,256]{1,0:T(8,128)S(1)}, f32[32,256]{1,0:T(8,128)S(1)}, u32[]{:S(2)}, u32[]{:S(2)}) collective-permute-start(f32[32,256]{1,0:T(8,128)S(1)} %get-tuple-element.72), channel_id=1, source_target_pairs={{0,1},{1,0},{2,3},{3,2},{4,5},{5,4},{6,7},{7,6},{8,9},{9,8},{10,11... | collective-permute-start | bytes 98312 | tf_op jit(solution)/shard_map/ppermute | solution.py:749
  5.8 3.1 %collective-permute-start.2 = (f32[32,128]{1,0:T(8,128)S(1)}, f32[32,128]{1,0:T(8,128)S(1)}, u32[]{:S(2)}, u32[]{:S(2)}) collective-permute-start(f32[32,128]{1,0:T(8,128)S(1)} %get-tuple-element.73), channel_id=1, source_target_pairs={{0,1},{1,0},{2,3},{3,2},{4,5},{5,4},{6,7},{7,6},{8,9},{9,8},{10,11... | collective-permute-start | bytes 49160 | tf_op jit(solution)/shard_map/ppermute | solution.py:749
  7.0 1.9 %collective-permute-start.3 = (f32[32,128]{1,0:T(8,128)S(1)}, f32[32,128]{1,0:T(8,128)S(1)}, u32[]{:S(2)}, u32[]{:S(2)}) collective-permute-start(f32[32,128]{1,0:T(8,128)S(1)} %get-tuple-element.74), channel_id=1, source_target_pairs={{0,16},{1,2},{2,1},{3,4},{4,3},{5,6},{6,5},{7,8},{8,7},{9,10},{10,... | collective-permute-start | bytes 49160 | tf_op jit(solution)/shard_map/ppermute | solution.py:749
  8.9 22.2 %all-to-all-start = ((f32[128,1,128]{2,1,0:T(1,128)}), f32[128,1,128]{2,1,0:T(1,128)S(1)}, u32[]{:S(2)}, u32[]{:S(2)}) async-start(f32[128,1,128]{2,1,0:T(1,128)} %bitcast.6), calls=%async_computation | async-start | bytes 131072 | tf_op jit(solution)/shard_map/all_to_all | solution.py:725
  33.6 22.0 %all-to-all-start.1 = ((f32[128,1,768]{2,1,0:T(1,128)}), f32[128,1,768]{2,1,0:T(1,128)S(1)}, u32[]{:S(2)}, u32[]{:S(2)}) async-start(f32[128,1,768]{2,1,0:T(1,128)} %bitcast.9), calls=%async_computation.1 | async-start | bytes 786432 | tf_op jit(solution)/shard_map/all_to_all | solution.py:725
  43.0 10.0 %collective-permute-start.4 = (f32[8,256]{1,0:T(8,128)S(1)}, f32[8,256]{1,0:T(8,128)S(1)}, u32[]{:S(2)}, u32[]{:S(2)}) collective-permute-start(f32[8,256]{1,0:T(8,128)S(1)} %get-tuple-element.99), channel_id=1, source_target_pairs={{0,16},{1,17},{2,18},{3,19},{4,20},{5,21},{6,22},{7,23},{8,24},{9,... | collective-permute-start | bytes 24584 | tf_op jit(solution)/shard_map/ppermute | solution.py:749
  44.1 8.9 %collective-permute-start.5 = (f32[8,256]{1,0:T(8,128)S(1)}, f32[8,256]{1,0:T(8,128)S(1)}, u32[]{:S(2)}, u32[]{:S(2)}) collective-permute-start(f32[8,256]{1,0:T(8,128)S(1)} %get-tuple-element.100), channel_id=1, source_target_pairs={{0,1},{1,0},{2,3},{3,2},{4,5},{5,4},{6,7},{7,6},{8,9},{9,8},{10,11... | collective-permute-start | bytes 24584 | tf_op jit(solution)/shard_map/ppermute | solution.py:749
  44.8 8.1 %collective-permute-start.6 = (f32[8,128]{1,0:T(8,128)S(1)}, f32[8,128]{1,0:T(8,128)S(1)}, u32[]{:S(2)}, u32[]{:S(2)}) collective-permute-start(f32[8,128]{1,0:T(8,128)S(1)} %get-tuple-element.101), channel_id=1, source_target_pairs={{0,1},{1,0},{2,3},{3,2},{4,5},{5,4},{6,7},{7,6},{8,9},{9,8},{10,11... | collective-permute-start | bytes 12296 | tf_op jit(solution)/shard_map/ppermute | solution.py:749
  46.0 7.0 %collective-permute-start.7 = (f32[8,128]{1,0:T(8,128)S(1)}, f32[8,128]{1,0:T(8,128)S(1)}, u32[]{:S(2)}, u32[]{:S(2)}) collective-permute-start(f32[8,128]{1,0:T(8,128)S(1)} %get-tuple-element.102), channel_id=1, source_target_pairs={{0,16},{1,2},{2,1},{3,4},{4,3},{5,6},{6,5},{7,8},{8,7},{9,10},{10,... | collective-permute-start | bytes 12296 | tf_op jit(solution)/shard_map/ppermute | solution.py:749
  56.5 6.5 %collective-permute-start.8 = (f32[8,256]{1,0:T(8,128)S(1)}, f32[8,256]{1,0:T(8,128)S(1)}, u32[]{:S(2)}, u32[]{:S(2)}) collective-permute-start(f32[8,256]{1,0:T(8,128)S(1)} %get-tuple-element.107), channel_id=1, source_target_pairs={{0,16},{1,17},{2,18},{3,19},{4,20},{5,21},{6,22},{7,23},{8,24},{9,... | collective-permute-start | bytes 24584 | tf_op jit(solution)/shard_map/ppermute | solution.py:749
  57.1 5.9 %collective-permute-start.9 = (f32[8,256]{1,0:T(8,128)S(1)}, f32[8,256]{1,0:T(8,128)S(1)}, u32[]{:S(2)}, u32[]{:S(2)}) collective-permute-start(f32[8,256]{1,0:T(8,128)S(1)} %get-tuple-element.108), channel_id=1, source_target_pairs={{0,1},{1,0},{2,3},{3,2},{4,5},{5,4},{6,7},{7,6},{8,9},{9,8},{10,11... | collective-permute-start | bytes 24584 | tf_op jit(solution)/shard_map/ppermute | solution.py:749
  57.5 5.5 %collective-permute-start.10 = (f32[8,128]{1,0:T(8,128)S(1)}, f32[8,128]{1,0:T(8,128)S(1)}, u32[]{:S(2)}, u32[]{:S(2)}) collective-permute-start(f32[8,128]{1,0:T(8,128)S(1)} %get-tuple-element.109), channel_id=1, source_target_pairs={{0,1},{1,0},{2,3},{3,2},{4,5},{5,4},{6,7},{7,6},{8,9},{9,8},{10,11... | collective-permute-start | bytes 12296 | tf_op jit(solution)/shard_map/ppermute | solution.py:749
  57.8 5.2 %collective-permute-start.11 = (f32[8,128]{1,0:T(8,128)S(1)}, f32[8,128]{1,0:T(8,128)S(1)}, u32[]{:S(2)}, u32[]{:S(2)}) collective-permute-start(f32[8,128]{1,0:T(8,128)S(1)} %get-tuple-element.110), channel_id=1, source_target_pairs={{0,16},{1,2},{2,1},{3,4},{4,3},{5,6},{6,5},{7,8},{8,7},{9,10},{10,... | collective-permute-start | bytes 12296 | tf_op jit(solution)/shard_map/ppermute | solution.py:749
  65.1 20.9 %all-to-all-start.2 = ((f32[128,1,768]{2,1,0:T(1,128)}), f32[128,1,768]{2,1,0:T(1,128)S(1)}, u32[]{:S(2)}, u32[]{:S(2)}) async-start(f32[128,1,768]{2,1,0:T(1,128)} %bitcast.11), calls=%async_computation.2 | async-start | bytes 786432 | tf_op jit(solution)/shard_map/all_to_all | solution.py:725
  73.4 11.0 %collective-permute-start.12 = (f32[8,256]{1,0:T(8,128)S(1)}, f32[8,256]{1,0:T(8,128)S(1)}, u32[]{:S(2)}, u32[]{:S(2)}) collective-permute-start(f32[8,256]{1,0:T(8,128)S(1)} %get-tuple-element.118), channel_id=1, source_target_pairs={{0,16},{1,17},{2,18},{3,19},{4,20},{5,21},{6,22},{7,23},{8,24},{9,... | collective-permute-start | bytes 24584 | tf_op jit(solution)/shard_map/ppermute | solution.py:749
  74.5 9.9 %collective-permute-start.13 = (f32[8,256]{1,0:T(8,128)S(1)}, f32[8,256]{1,0:T(8,128)S(1)}, u32[]{:S(2)}, u32[]{:S(2)}) collective-permute-start(f32[8,256]{1,0:T(8,128)S(1)} %get-tuple-element.119), channel_id=1, source_target_pairs={{0,1},{1,0},{2,3},{3,2},{4,5},{5,4},{6,7},{7,6},{8,9},{9,8},{10,11... | collective-permute-start | bytes 24584 | tf_op jit(solution)/shard_map/ppermute | solution.py:749
  75.2 9.2 %collective-permute-start.14 = (f32[8,128]{1,0:T(8,128)S(1)}, f32[8,128]{1,0:T(8,128)S(1)}, u32[]{:S(2)}, u32[]{:S(2)}) collective-permute-start(f32[8,128]{1,0:T(8,128)S(1)} %get-tuple-element.120), channel_id=1, source_target_pairs={{0,1},{1,0},{2,3},{3,2},{4,5},{5,4},{6,7},{7,6},{8,9},{9,8},{10,11... | collective-permute-start | bytes 12296 | tf_op jit(solution)/shard_map/ppermute | solution.py:749
  76.4 8.0 %collective-permute-start.15 = (f32[8,128]{1,0:T(8,128)S(1)}, f32[8,128]{1,0:T(8,128)S(1)}, u32[]{:S(2)}, u32[]{:S(2)}) collective-permute-start(f32[8,128]{1,0:T(8,128)S(1)} %get-tuple-element.121), channel_id=1, source_target_pairs={{0,16},{1,2},{2,1},{3,4},{4,3},{5,6},{6,5},{7,8},{8,7},{9,10},{10,... | collective-permute-start | bytes 12296 | tf_op jit(solution)/shard_map/ppermute | solution.py:749

commit v10 on v9

--- a/solution.py
+++ b/solution.py
@@ -66,17 +66,17 @@
     match = iota((L * R, PERFS), 0) == (cell_row >> 8)
     column = to_column(cell_row.astype(f32)).astype(i32) & (C - 1)
     spread = (iota((PERFS, C), 1) == column).astype(bf16)
-    return sum(
-        dot(jnp.where(match, part.astype(f32), 0.0).astype(bf16), spread) for part in split3(values)
-    )
+    parts = [jnp.where(match, part.astype(f32), 0.0).astype(bf16) for part in split3(values)]
+    return dot(jnp.concatenate(parts, axis=1), jnp.concatenate([spread] * 3, axis=0))
 
 
 def gather_cells(cell_column, fields):
     onehot = (iota((PERFS, L * R), 1) == (cell_column >> 8)).astype(bf16)
+    onehot = jnp.concatenate([onehot] * 3, axis=1)
     here = iota((PERFS, C), 1) == (cell_column & (C - 1))
     picked = []
     for field in fields:
-        rows = sum(dot(onehot, part) for part in split3(field))
+        rows = dot(onehot, jnp.concatenate(split3(field), axis=0))
         picked.append(jnp.sum(jnp.where(here, rows, 0.0), axis=1, keepdims=True))
     return picked
 
@@ -87,7 +87,7 @@
 
 def gather_wells(table, holder, slot):
     onehot = (iota((DEVICES, PERFS), 0) == holder).astype(bf16)
-    wide = sum(dot(part, onehot) for part in split3(table.T))
+    wide = dot(jnp.concatenate(split3(table.T), axis=1), jnp.concatenate([onehot] * 3, axis=0))
     return jnp.sum(jnp.where(iota((LANES, PERFS), 0) == slot, wide, 0.0), axis=0, keepdims=True)
 
 
@@ -99,7 +99,7 @@
         values = jnp.where(group == g, column, values)
     values = jnp.where((lane & 15) == slot_column, values, 0.0)
     onehot = (iota((DEVICES, PERFS), 0) == holder).astype(bf16)
-    return sum(dot(onehot, part) for part in split3(values))
+    return dot(jnp.concatenate([onehot] * 3, axis=1), jnp.concatenate(split3(values), axis=0))
 
 
 def parts_by_offset(me, well_row, values):

time: 90.8 us -> 90.3 us (level)
  no operation moved by 1% of the time
where the time goes in v10:
time: 90.3 us; the launch traced here: 89.9 us
  starting transfers between devices  42.9 us (48%)
  Pallas kernels  41.2 us (46%)
  waiting for transfers between devices  4.81 us (5%)
  between operations  0.99 us (1%)
    pallas_call x12, Pallas kernels, call(): pl.pallas_call(kernel, out_shape=shapes, in_specs=ins, out_specs=tuple((w...  41.2 us
    all_to_all x3, starting transfers between devices, exchange(): return lax.all_to_all(array, AXES, split_axis=0, concat_axis=0, tiled=True)  29.6 us
    ppermute x16, starting transfers between devices, halo_of(): got = {n: lax.ppermute(faces[n], AXES, swaps[n]) for n in (3, 1, 2, 0)}  13.3 us
    all_to_all x3, waiting for transfers between devices, exchange(): return lax.all_to_all(array, AXES, split_axis=0, concat_axis=0, tiled=True)  4.77 us
  transfers between devices with their start and end apart: 19, of which 3 were waited for; matrix products, arithmetic and copies ran while one was open for 0% of the time, Pallas kernels for 33%

profile of v10, /device:TPU:1, one launch (start us, length us, event | category | flops | bytes accessed | tf_op | source)
XLA Modules:
  0.0 89.9 jit_solution(10995643998713839623)
XLA Ops:
  0.6 2.3 %shard_map.138 = (f32[32,256]{1,0:T(8,128)S(1)}, f32[32,256]{1,0:T(8,128)S(1)}, f32[32,128]{1,0:T(8,128)S(1)}, f32[32,128]{1,0:T(8,128)S(1)}, f32[8,64,256]{2,1,...) custom-call(s32[1,256]{1,0:T(1,128)} %bitcast.19, ...), custom_call_target="tpu_custom_call" | custom-call | bytes 3148928 | tf_op jit(solution)/shard_map/pallas_call | solution.py:704
  2.9 1.5 %collective-permute-start = (f32[32,256]{1,0:T(8,128)S(1)}, f32[32,256]{1,0:T(8,128)S(1)}, u32[]{:S(2)}, u32[]{:S(2)}) collective-permute-start(f32[32,256]{1,0:T(8,128)S(1)} %get-tuple-element.71), channel_id=1, source_target_pairs={{0,16},{1,17},{2,18},{3,19},{4,20},{5,21},{6,22},{7,23},{8,24},{9,... | collective-permute-start | bytes 98312 | tf_op jit(solution)/shard_map/ppermute | solution.py:749
  4.4 1.4 %collective-permute-start.1 = (f32[32,256]{1,0:T(8,128)S(1)}, f32[32,256]{1,0:T(8,128)S(1)}, u32[]{:S(2)}, u32[]{:S(2)}) collective-permute-start(f32[32,256]{1,0:T(8,128)S(1)} %get-tuple-element.72), channel_id=1, source_target_pairs={{0,1},{1,0},{2,3},{3,2},{4,5},{5,4},{6,7},{7,6},{8,9},{9,8},{10,11... | collective-permute-start | bytes 98312 | tf_op jit(solution)/shard_map/ppermute | solution.py:749
  5.8 1.2 %collective-permute-start.2 = (f32[32,128]{1,0:T(8,128)S(1)}, f32[32,128]{1,0:T(8,128)S(1)}, u32[]{:S(2)}, u32[]{:S(2)}) collective-permute-start(f32[32,128]{1,0:T(8,128)S(1)} %get-tuple-element.73), channel_id=1, source_target_pairs={{0,1},{1,0},{2,3},{3,2},{4,5},{5,4},{6,7},{7,6},{8,9},{9,8},{10,11... | collective-permute-start | bytes 49160 | tf_op jit(solution)/shard_map/ppermute | solution.py:749
  7.0 0.0 collective-permute-start.3
  7.0 1.9 %shard_map.139 = (f32[128,128]{1,0:T(8,128)}, f32[8,256]{1,0:T(8,128)S(1)}) custom-call(f32[8,256]{1,0:T(8,128)S(1)} %get-tuple-element.65.info, f32[8,128]{1,0:T(8,128)S(1)} %get-tuple-element.66.own, f32[8,64,256]{2,1,0:T(8,128)S(1)} %get-tuple-element.67.p, f32[8,64,256]{2,1,0:T(8,128)S(1)} %get-tuple-element.68.sw, f32[8,64,256]{2,1,0:T(8,128)S(1)} %get-tuple-element.69.sg), custom_call_target="tpu_custom_call" | custom-call | bytes 1585152 | tf_op jit(solution)/shard_map/pallas_call | solution.py:704
  8.9 0.0 collective-permute-done.2.refs_2_
  8.9 0.0 collective-permute-done.3.refs_3_
  8.9 0.0 collective-permute-done.refs_0_
  8.9 0.0 collective-permute-done.1.refs_1_
  8.9 12.5 %all-to-all-start = ((f32[128,1,128]{2,1,0:T(1,128)}), f32[128,1,128]{2,1,0:T(1,128)S(1)}, u32[]{:S(2)}, u32[]{:S(2)}) async-start(f32[128,1,128]{2,1,0:T(1,128)} %bitcast.6), calls=%async_computation | async-start | bytes 131072 | tf_op jit(solution)/shard_map/all_to_all | solution.py:725
  21.4 9.0 %shard_map.141 = (f32[2,3,8,256]{3,2,1,0:T(8,128)S(1)}, f32[3,64,128]{2,1,0:T(8,128)S(1)}, f32[8,64,256]{2,1,0:T(8,128)S(1)}, f32[8,64,256]{2,1,0:T(8,128)S(1)},...) custom-call(f32[8,256]{1,0:T(8,128)S(1)} %get-tuple-element.65.info,, ...), custom_call_target="tpu_custom_call" | custom-call | flops 52428800 | bytes 5349376 | tf_op jit(solution)/shard_map/pallas_call | solution.py:704
  30.5 0.7 all-to-all-done
  31.2 2.3 %shard_map.142 = (f32[8,128]{1,0:T(8,128)S(1)}, f32[1,16]{1,0:T(1,128)}, f32[8,64,256]{2,1,0:T(8,128)S(1)}, f32[8,64,256]{2,1,0:T(8,128)S(1)}, f32[768,128]{1,0:T(8,128)}) custom-call(f32[128,128]{1,0:T(8,128)S(1)} %bitcast.18, f32[8,256]{1,0:T(8,128)S(1)} %get-tuple-element.65.info, f32[8,128]{1,0:T(8,128)S(1)} %get-tuple-element.66.own, ...), custom_call_target="tpu_custom_call" | custom-call | bytes 1134592 | tf_op jit(solution)/shard_map/pallas_call | solution.py:704
  33.5 9.1 %all-to-all-start.1 = ((f32[128,1,768]{2,1,0:T(1,128)}), f32[128,1,768]{2,1,0:T(1,128)S(1)}, u32[]{:S(2)}, u32[]{:S(2)}) async-start(f32[128,1,768]{2,1,0:T(1,128)} %bitcast.9), calls=%async_computation.1 | async-start | bytes 786432 | tf_op jit(solution)/shard_map/all_to_all | solution.py:725
  42.6 0.3 shard_map.144
  42.9 1.1 %collective-permute-start.4 = (f32[8,256]{1,0:T(8,128)S(1)}, f32[8,256]{1,0:T(8,128)S(1)}, u32[]{:S(2)}, u32[]{:S(2)}) collective-permute-start(f32[8,256]{1,0:T(8,128)S(1)} %get-tuple-element.99), channel_id=1, source_target_pairs={{0,16},{1,17},{2,18},{3,19},{4,20},{5,21},{6,22},{7,23},{8,24},{9,... | collective-permute-start | bytes 24584 | tf_op jit(solution)/shard_map/ppermute | solution.py:749
  44.0 0.7 collective-permute-start.5
  44.7 1.2 %collective-permute-start.6 = (f32[8,128]{1,0:T(8,128)S(1)}, f32[8,128]{1,0:T(8,128)S(1)}, u32[]{:S(2)}, u32[]{:S(2)}) collective-permute-start(f32[8,128]{1,0:T(8,128)S(1)} %get-tuple-element.101), channel_id=1, source_target_pairs={{0,1},{1,0},{2,3},{3,2},{4,5},{5,4},{6,7},{7,6},{8,9},{9,8},{10,11... | collective-permute-start | bytes 12296 | tf_op jit(solution)/shard_map/ppermute | solution.py:749
  45.9 0.2 collective-permute-start.7
  46.1 6.7 %shard_map.143 = (f32[8,64,256]{2,1,0:T(8,128)S(1)}, f32[2,8,256]{2,1,0:T(8,128)S(1)}, f32[64,128]{1,0:T(8,128)S(1)}, f32[3,8,64,256]{3,2,1,0:T(8,128)}, f32[6,8,64,256]{3,2,1,0:T(8,128)}) custom-call(f32[2,3,8,256]{3,2,1,0:T(8,128)S(1)} %get-tuple-element.79.coef_row, f32[3,64,128]{2,1,0:T(8,128)S(1)} %get-tuple-element.80.coef_col, ...), custom_call_target="tpu_custom_call" | custom-call | flops 13107200 | bytes 9125888 | tf_op jit(solution)/shard_map/pallas_call | solution.py:704
  52.8 0.0 collective-permute-done.6.col_first
  52.8 0.0 collective-permute-done.7.col_second
  52.8 0.0 collective-permute-done.4.row_first
  52.8 0.0 collective-permute-done.5.row_second
  52.9 2.6 %all-to-all-done.1 = f32[128,1,768]{2,1,0:T(1,128)S(1)} async-done(((f32[128,1,768]{2,1,0:T(1,128)}), f32[128,1,768]{2,1,0:T(1,128)S(1)}, u32[]{:S(2)}, u32[]{:S(2)}) %all-to-all-start.1) | async-done | bytes 393248 | tf_op jit(solution)/shard_map/all_to_all | solution.py:725
  55.4 0.9 shard_map.145
  56.3 0.6 collective-permute-start.8
  56.9 0.4 collective-permute-start.9
  57.3 0.3 collective-permute-start.10
  57.6 1.4 %collective-permute-start.11 = (f32[8,128]{1,0:T(8,128)S(1)}, f32[8,128]{1,0:T(8,128)S(1)}, u32[]{:S(2)}, u32[]{:S(2)}) collective-permute-start(f32[8,128]{1,0:T(8,128)S(1)} %get-tuple-element.110), channel_id=1, source_target_pairs={{0,16},{1,2},{2,1},{3,4},{4,3},{5,6},{6,5},{7,8},{8,7},{9,10},{10,... | collective-permute-start | bytes 12296 | tf_op jit(solution)/shard_map/ppermute | solution.py:749
  59.0 3.7 %shard_map.146 = (f32[2,128,128]{2,1,0:T(8,128)S(1)}, f32[8,128]{1,0:T(8,128)S(1)}, f32[8,64,256]{2,1,0:T(8,128)S(1)}) custom-call(f32[768,128]{1,0:T(8,128)S(1)} %bitcast.16, f32[8,256]{1,0:T(8,128)S(1)} %get-tuple-element.65.info, f32[8,256]{1,0:T(8,128)S(1)} %get-tuple-element.83.perf, f32[8,64,256]{2,1,0:T(8,128)S(1)} %get-tuple-element.103.step, ...), custom_call_target="tpu_custom_call" | custom-call | bytes 5128192 | tf_op jit(solution)/shard_map/pallas_call | solution.py:704
  62.7 0.0 collective-permute-done.10.col_first
  62.7 0.0 collective-permute-done.11.col_second
  62.7 0.0 collective-permute-done.8.row_first
  62.7 0.0 collective-permute-done.9.row_second
  62.8 2.0 %shard_map.147 = (f32[8,64,256]{2,1,0:T(8,128)S(1)}, f32[768,128]{1,0:T(8,128)}) custom-call(f32[8,256]{1,0:T(8,128)S(1)} %get-tuple-element.65.info, f32[8,256]{1,0:T(8,128)S(1)} %get-tuple-element.83.perf, f32[8,128]{1,0:T(8,128)S(1)} %get-tuple-element.105.parts, f32[8,64,256]{2,1,0:T(8,128)S(1)} %get-tuple-element.106.near, ...), custom_call_target="tpu_custom_call" | custom-call | bytes 618496 | tf_op jit(solution)/shard_map/pallas_call | solution.py:704
  64.8 8.1 %all-to-all-start.2 = ((f32[128,1,768]{2,1,0:T(1,128)}), f32[128,1,768]{2,1,0:T(1,128)S(1)}, u32[]{:S(2)}, u32[]{:S(2)}) async-start(f32[128,1,768]{2,1,0:T(1,128)} %bitcast.11), calls=%async_computation.2 | async-start | bytes 786432 | tf_op jit(solution)/shard_map/all_to_all | solution.py:725
  72.9 0.3 shard_map.149
  73.1 1.1 %collective-permute-start.12 = (f32[8,256]{1,0:T(8,128)S(1)}, f32[8,256]{1,0:T(8,128)S(1)}, u32[]{:S(2)}, u32[]{:S(2)}) collective-permute-start(f32[8,256]{1,0:T(8,128)S(1)} %get-tuple-element.118), channel_id=1, source_target_pairs={{0,16},{1,17},{2,18},{3,19},{4,20},{5,21},{6,22},{7,23},{8,24},{9,... | collective-permute-start | bytes 24584 | tf_op jit(solution)/shard_map/ppermute | solution.py:749
  74.2 0.7 collective-permute-start.13
  75.0 1.2 %collective-permute-start.14 = (f32[8,128]{1,0:T(8,128)S(1)}, f32[8,128]{1,0:T(8,128)S(1)}, u32[]{:S(2)}, u32[]{:S(2)}) collective-permute-start(f32[8,128]{1,0:T(8,128)S(1)} %get-tuple-element.120), channel_id=1, source_target_pairs={{0,1},{1,0},{2,3},{3,2},{4,5},{5,4},{6,7},{7,6},{8,9},{9,8},{10,11... | collective-permute-start | bytes 12296 | tf_op jit(solution)/shard_map/ppermute | solution.py:749
  76.1 0.2 collective-permute-start.15
  76.4 7.8 %shard_map.148 = (f32[2,2,8,256]{3,2,1,0:T(8,128)S(1)}, f32[2,64,128]{2,1,0:T(8,128)S(1)}, f32[3,8,64,256]{3,2,1,0:T(8,128)}, f32[2,8,64,256]{3,2,1,0:T(8,128)}) custom-call(f32[2,3,8,256]{3,2,1,0:T(8,128)S(1)} %get-tuple-element.79.coef_row, f32[3,64,128]{2,1,0:T(8,128)S(1)} %get-tuple-element.80.coef_col, f32[8,64,256]{2,1,0:T(8,128)S(1)} %get-tuple-element.81.head, ...), custom_call_target="tpu_custom_call" | custom-call | flops 19660800 | bytes 10747904 | tf_op jit(solution)/shard_map/pallas_call | solution.py:704
  84.1 0.0 collective-permute-done.14.col_first
  84.2 0.0 collective-permute-done.13.row_second
  84.2 1.5 %all-to-all-done.2 = f32[128,1,768]{2,1,0:T(1,128)S(1)} async-done(((f32[128,1,768]{2,1,0:T(1,128)}), f32[128,1,768]{2,1,0:T(1,128)S(1)}, u32[]{:S(2)}, u32[]{:S(2)}) %all-to-all-start.2) | async-done | bytes 393248 | tf_op jit(solution)/shard_map/all_to_all | solution.py:725
  85.7 4.1 %shard_map.150 = (f32[3,8,64,256]{3,2,1,0:T(8,128)}, f32[1,16]{1,0:T(1,128)}) custom-call(f32[768,128]{1,0:T(8,128)S(1)} %bitcast.17, f32[8,256]{1,0:T(8,128)S(1)} %get-tuple-element.65.info, f32[2,128,128]{2,1,0:T(8,128)S(1)} %get-tuple-element.112.table, f32[8,128]{1,0:T(8,128)S(1)} %get-tuple-element.113.mine, f32[8,64,256]{2,1,0:T(8,128)S(1)} %get-tuple-element.81.head, ...), custom_call_target="tpu_custom_call" | custom-call | bytes 3854336 | tf_op jit(solution)/shard_map/pallas_call | solution.py:704
  (3 shorter events, 0.0 us)
Async XLA Ops:
  2.9 6.0 %collective-permute-start = (f32[32,256]{1,0:T(8,128)S(1)}, f32[32,256]{1,0:T(8,128)S(1)}, u32[]{:S(2)}, u32[]{:S(2)}) collective-permute-start(f32[32,256]{1,0:T(8,128)S(1)} %get-tuple-element.71), channel_id=1, source_target_pairs={{0,16},{1,17},{2,18},{3,19},{4,20},{5,21},{6,22},{7,23},{8,24},{9,... | collective-permute-start | bytes 98312 | tf_op jit(solution)/shard_map/ppermute | solution.py:749
  4.4 4.5 %collective-permute-start.1 = (f32[32,256]{1,0:T(8,128)S(1)}, f32[32,256]{1,0:T(8,128)S(1)}, u32[]{:S(2)}, u32[]{:S(2)}) collective-permute-start(f32[32,256]{1,0:T(8,128)S(1)} %get-tuple-element.72), channel_id=1, source_target_pairs={{0,1},{1,0},{2,3},{3,2},{4,5},{5,4},{6,7},{7,6},{8,9},{9,8},{10,11... | collective-permute-start | bytes 98312 | tf_op jit(solution)/shard_map/ppermute | solution.py:749
  5.8 3.1 %collective-permute-start.2 = (f32[32,128]{1,0:T(8,128)S(1)}, f32[32,128]{1,0:T(8,128)S(1)}, u32[]{:S(2)}, u32[]{:S(2)}) collective-permute-start(f32[32,128]{1,0:T(8,128)S(1)} %get-tuple-element.73), channel_id=1, source_target_pairs={{0,1},{1,0},{2,3},{3,2},{4,5},{5,4},{6,7},{7,6},{8,9},{9,8},{10,11... | collective-permute-start | bytes 49160 | tf_op jit(solution)/shard_map/ppermute | solution.py:749
  7.0 1.9 %collective-permute-start.3 = (f32[32,128]{1,0:T(8,128)S(1)}, f32[32,128]{1,0:T(8,128)S(1)}, u32[]{:S(2)}, u32[]{:S(2)}) collective-permute-start(f32[32,128]{1,0:T(8,128)S(1)} %get-tuple-element.74), channel_id=1, source_target_pairs={{0,16},{1,2},{2,1},{3,4},{4,3},{5,6},{6,5},{7,8},{8,7},{9,10},{10,... | collective-permute-start | bytes 49160 | tf_op jit(solution)/shard_map/ppermute | solution.py:749
  8.9 22.2 %all-to-all-start = ((f32[128,1,128]{2,1,0:T(1,128)}), f32[128,1,128]{2,1,0:T(1,128)S(1)}, u32[]{:S(2)}, u32[]{:S(2)}) async-start(f32[128,1,128]{2,1,0:T(1,128)} %bitcast.6), calls=%async_computation | async-start | bytes 131072 | tf_op jit(solution)/shard_map/all_to_all | solution.py:725
  33.5 22.0 %all-to-all-start.1 = ((f32[128,1,768]{2,1,0:T(1,128)}), f32[128,1,768]{2,1,0:T(1,128)S(1)}, u32[]{:S(2)}, u32[]{:S(2)}) async-start(f32[128,1,768]{2,1,0:T(1,128)} %bitcast.9), calls=%async_computation.1 | async-start | bytes 786432 | tf_op jit(solution)/shard_map/all_to_all | solution.py:725
  42.9 10.0 %collective-permute-start.4 = (f32[8,256]{1,0:T(8,128)S(1)}, f32[8,256]{1,0:T(8,128)S(1)}, u32[]{:S(2)}, u32[]{:S(2)}) collective-permute-start(f32[8,256]{1,0:T(8,128)S(1)} %get-tuple-element.99), channel_id=1, source_target_pairs={{0,16},{1,17},{2,18},{3,19},{4,20},{5,21},{6,22},{7,23},{8,24},{9,... | collective-permute-start | bytes 24584 | tf_op jit(solution)/shard_map/ppermute | solution.py:749
  44.0 8.9 %collective-permute-start.5 = (f32[8,256]{1,0:T(8,128)S(1)}, f32[8,256]{1,0:T(8,128)S(1)}, u32[]{:S(2)}, u32[]{:S(2)}) collective-permute-start(f32[8,256]{1,0:T(8,128)S(1)} %get-tuple-element.100), channel_id=1, source_target_pairs={{0,1},{1,0},{2,3},{3,2},{4,5},{5,4},{6,7},{7,6},{8,9},{9,8},{10,11... | collective-permute-start | bytes 24584 | tf_op jit(solution)/shard_map/ppermute | solution.py:749
  44.7 8.1 %collective-permute-start.6 = (f32[8,128]{1,0:T(8,128)S(1)}, f32[8,128]{1,0:T(8,128)S(1)}, u32[]{:S(2)}, u32[]{:S(2)}) collective-permute-start(f32[8,128]{1,0:T(8,128)S(1)} %get-tuple-element.101), channel_id=1, source_target_pairs={{0,1},{1,0},{2,3},{3,2},{4,5},{5,4},{6,7},{7,6},{8,9},{9,8},{10,11... | collective-permute-start | bytes 12296 | tf_op jit(solution)/shard_map/ppermute | solution.py:749
  45.9 7.0 %collective-permute-start.7 = (f32[8,128]{1,0:T(8,128)S(1)}, f32[8,128]{1,0:T(8,128)S(1)}, u32[]{:S(2)}, u32[]{:S(2)}) collective-permute-start(f32[8,128]{1,0:T(8,128)S(1)} %get-tuple-element.102), channel_id=1, source_target_pairs={{0,16},{1,2},{2,1},{3,4},{4,3},{5,6},{6,5},{7,8},{8,7},{9,10},{10,... | collective-permute-start | bytes 12296 | tf_op jit(solution)/shard_map/ppermute | solution.py:749
  56.3 6.4 %collective-permute-start.8 = (f32[8,256]{1,0:T(8,128)S(1)}, f32[8,256]{1,0:T(8,128)S(1)}, u32[]{:S(2)}, u32[]{:S(2)}) collective-permute-start(f32[8,256]{1,0:T(8,128)S(1)} %get-tuple-element.107), channel_id=1, source_target_pairs={{0,16},{1,17},{2,18},{3,19},{4,20},{5,21},{6,22},{7,23},{8,24},{9,... | collective-permute-start | bytes 24584 | tf_op jit(solution)/shard_map/ppermute | solution.py:749
  56.9 5.8 %collective-permute-start.9 = (f32[8,256]{1,0:T(8,128)S(1)}, f32[8,256]{1,0:T(8,128)S(1)}, u32[]{:S(2)}, u32[]{:S(2)}) collective-permute-start(f32[8,256]{1,0:T(8,128)S(1)} %get-tuple-element.108), channel_id=1, source_target_pairs={{0,1},{1,0},{2,3},{3,2},{4,5},{5,4},{6,7},{7,6},{8,9},{9,8},{10,11... | collective-permute-start | bytes 24584 | tf_op jit(solution)/shard_map/ppermute | solution.py:749
  57.3 5.4 %collective-permute-start.10 = (f32[8,128]{1,0:T(8,128)S(1)}, f32[8,128]{1,0:T(8,128)S(1)}, u32[]{:S(2)}, u32[]{:S(2)}) collective-permute-start(f32[8,128]{1,0:T(8,128)S(1)} %get-tuple-element.109), channel_id=1, source_target_pairs={{0,1},{1,0},{2,3},{3,2},{4,5},{5,4},{6,7},{7,6},{8,9},{9,8},{10,11... | collective-permute-start | bytes 12296 | tf_op jit(solution)/shard_map/ppermute | solution.py:749
  57.6 5.1 %collective-permute-start.11 = (f32[8,128]{1,0:T(8,128)S(1)}, f32[8,128]{1,0:T(8,128)S(1)}, u32[]{:S(2)}, u32[]{:S(2)}) collective-permute-start(f32[8,128]{1,0:T(8,128)S(1)} %get-tuple-element.110), channel_id=1, source_target_pairs={{0,16},{1,2},{2,1},{3,4},{4,3},{5,6},{6,5},{7,8},{8,7},{9,10},{10,... | collective-permute-start | bytes 12296 | tf_op jit(solution)/shard_map/ppermute | solution.py:749
  64.8 20.9 %all-to-all-start.2 = ((f32[128,1,768]{2,1,0:T(1,128)}), f32[128,1,768]{2,1,0:T(1,128)S(1)}, u32[]{:S(2)}, u32[]{:S(2)}) async-start(f32[128,1,768]{2,1,0:T(1,128)} %bitcast.11), calls=%async_computation.2 | async-start | bytes 786432 | tf_op jit(solution)/shard_map/all_to_all | solution.py:725
  73.1 11.0 %collective-permute-start.12 = (f32[8,256]{1,0:T(8,128)S(1)}, f32[8,256]{1,0:T(8,128)S(1)}, u32[]{:S(2)}, u32[]{:S(2)}) collective-permute-start(f32[8,256]{1,0:T(8,128)S(1)} %get-tuple-element.118), channel_id=1, source_target_pairs={{0,16},{1,17},{2,18},{3,19},{4,20},{5,21},{6,22},{7,23},{8,24},{9,... | collective-permute-start | bytes 24584 | tf_op jit(solution)/shard_map/ppermute | solution.py:749
  74.2 9.9 %collective-permute-start.13 = (f32[8,256]{1,0:T(8,128)S(1)}, f32[8,256]{1,0:T(8,128)S(1)}, u32[]{:S(2)}, u32[]{:S(2)}) collective-permute-start(f32[8,256]{1,0:T(8,128)S(1)} %get-tuple-element.119), channel_id=1, source_target_pairs={{0,1},{1,0},{2,3},{3,2},{4,5},{5,4},{6,7},{7,6},{8,9},{9,8},{10,11... | collective-permute-start | bytes 24584 | tf_op jit(solution)/shard_map/ppermute | solution.py:749
  75.0 9.2 %collective-permute-start.14 = (f32[8,128]{1,0:T(8,128)S(1)}, f32[8,128]{1,0:T(8,128)S(1)}, u32[]{:S(2)}, u32[]{:S(2)}) collective-permute-start(f32[8,128]{1,0:T(8,128)S(1)} %get-tuple-element.120), channel_id=1, source_target_pairs={{0,1},{1,0},{2,3},{3,2},{4,5},{5,4},{6,7},{7,6},{8,9},{9,8},{10,11... | collective-permute-start | bytes 12296 | tf_op jit(solution)/shard_map/ppermute | solution.py:749
  76.1 8.0 %collective-permute-start.15 = (f32[8,128]{1,0:T(8,128)S(1)}, f32[8,128]{1,0:T(8,128)S(1)}, u32[]{:S(2)}, u32[]{:S(2)}) collective-permute-start(f32[8,128]{1,0:T(8,128)S(1)} %get-tuple-element.121), channel_id=1, source_target_pairs={{0,16},{1,2},{2,1},{3,4},{4,3},{5,6},{6,5},{7,8},{8,7},{9,10},{10,... | collective-permute-start | bytes 12296 | tf_op jit(solution)/shard_map/ppermute | solution.py:749

commit v11 on v10

--- a/solution.py
+++ b/solution.py
@@ -24,7 +24,7 @@
 LANES = 128
 L, R, C = 8, 64, 256
 PERFS = 256
-BLOCK = 8
+BLOCK = 32
 VM = pl.BlockSpec(memory_space=pltpu.VMEM)
 HB = pl.BlockSpec(memory_space=pltpu.HBM)
 

time: 90.3 us -> 90.1 us (level)
  no operation moved by 1% of the time
where the time goes in v11:
time: 90.1 us; the launch traced here: 89.7 us
  starting transfers between devices  42.7 us (47%)
  Pallas kernels  41.1 us (46%)
  waiting for transfers between devices  5.01 us (6%)
  between operations  0.99 us (1%)
    pallas_call x12, Pallas kernels, call(): pl.pallas_call(kernel, out_shape=shapes, in_specs=ins, out_specs=tuple((w...  41 us
    all_to_all x3, starting transfers between devices, exchange(): return lax.all_to_all(array, AXES, split_axis=0, concat_axis=0, tiled=True)  29.4 us
    ppermute x16, starting transfers between devices, halo_of(): got = {n: lax.ppermute(faces[n], AXES, swaps[n]) for n in (3, 1, 2, 0)}  13.3 us
    all_to_all x3, waiting for transfers between devices, exchange(): return lax.all_to_all(array, AXES, split_axis=0, concat_axis=0, tiled=True)  4.96 us
  transfers between devices with their start and end apart: 19, of which 3 were waited for; matrix products, arithmetic and copies ran while one was open for 0% of the time, Pallas kernels for 33%

profile of v11, /device:TPU:1, one launch (start us, length us, event | category | flops | bytes accessed | tf_op | source)
XLA Modules:
  0.0 89.7 jit_solution(13805404046704121747)
XLA Ops:
  0.6 2.3 %shard_map.138 = (f32[32,256]{1,0:T(8,128)S(1)}, f32[32,256]{1,0:T(8,128)S(1)}, f32[32,128]{1,0:T(8,128)S(1)}, f32[32,128]{1,0:T(8,128)S(1)}, f32[8,64,256]{2,1,...) custom-call(s32[1,256]{1,0:T(1,128)} %bitcast.19, ...), custom_call_target="tpu_custom_call" | custom-call | bytes 3148928 | tf_op jit(solution)/shard_map/pallas_call | solution.py:704
  2.9 1.5 %collective-permute-start = (f32[32,256]{1,0:T(8,128)S(1)}, f32[32,256]{1,0:T(8,128)S(1)}, u32[]{:S(2)}, u32[]{:S(2)}) collective-permute-start(f32[32,256]{1,0:T(8,128)S(1)} %get-tuple-element.71), channel_id=1, source_target_pairs={{0,16},{1,17},{2,18},{3,19},{4,20},{5,21},{6,22},{7,23},{8,24},{9,... | collective-permute-start | bytes 98312 | tf_op jit(solution)/shard_map/ppermute | solution.py:749
  4.4 1.4 %collective-permute-start.1 = (f32[32,256]{1,0:T(8,128)S(1)}, f32[32,256]{1,0:T(8,128)S(1)}, u32[]{:S(2)}, u32[]{:S(2)}) collective-permute-start(f32[32,256]{1,0:T(8,128)S(1)} %get-tuple-element.72), channel_id=1, source_target_pairs={{0,1},{1,0},{2,3},{3,2},{4,5},{5,4},{6,7},{7,6},{8,9},{9,8},{10,11... | collective-permute-start | bytes 98312 | tf_op jit(solution)/shard_map/ppermute | solution.py:749
  5.8 1.2 %collective-permute-start.2 = (f32[32,128]{1,0:T(8,128)S(1)}, f32[32,128]{1,0:T(8,128)S(1)}, u32[]{:S(2)}, u32[]{:S(2)}) collective-permute-start(f32[32,128]{1,0:T(8,128)S(1)} %get-tuple-element.73), channel_id=1, source_target_pairs={{0,1},{1,0},{2,3},{3,2},{4,5},{5,4},{6,7},{7,6},{8,9},{9,8},{10,11... | collective-permute-start | bytes 49160 | tf_op jit(solution)/shard_map/ppermute | solution.py:749
  7.0 0.0 collective-permute-start.3
  7.0 1.9 %shard_map.139 = (f32[128,128]{1,0:T(8,128)}, f32[8,256]{1,0:T(8,128)S(1)}) custom-call(f32[8,256]{1,0:T(8,128)S(1)} %get-tuple-element.65.info, f32[8,128]{1,0:T(8,128)S(1)} %get-tuple-element.66.own, f32[8,64,256]{2,1,0:T(8,128)S(1)} %get-tuple-element.67.p, f32[8,64,256]{2,1,0:T(8,128)S(1)} %get-tuple-element.68.sw, f32[8,64,256]{2,1,0:T(8,128)S(1)} %get-tuple-element.69.sg), custom_call_target="tpu_custom_call" | custom-call | bytes 1585152 | tf_op jit(solution)/shard_map/pallas_call | solution.py:704
  8.9 0.0 collective-permute-done.2.refs_2_
  8.9 0.0 collective-permute-done.3.refs_3_
  8.9 0.0 collective-permute-done.refs_0_
  8.9 0.0 collective-permute-done.1.refs_1_
  8.9 12.5 %all-to-all-start = ((f32[128,1,128]{2,1,0:T(1,128)}), f32[128,1,128]{2,1,0:T(1,128)S(1)}, u32[]{:S(2)}, u32[]{:S(2)}) async-start(f32[128,1,128]{2,1,0:T(1,128)} %bitcast.6), calls=%async_computation | async-start | bytes 131072 | tf_op jit(solution)/shard_map/all_to_all | solution.py:725
  21.4 9.0 %shard_map.141 = (f32[2,3,8,256]{3,2,1,0:T(8,128)S(1)}, f32[3,64,128]{2,1,0:T(8,128)S(1)}, f32[8,64,256]{2,1,0:T(8,128)S(1)}, f32[8,64,256]{2,1,0:T(8,128)S(1)},...) custom-call(f32[8,256]{1,0:T(8,128)S(1)} %get-tuple-element.65.info,, ...), custom_call_target="tpu_custom_call" | custom-call | flops 52428800 | bytes 5349376 | tf_op jit(solution)/shard_map/pallas_call | solution.py:704
  30.4 0.7 all-to-all-done
  31.2 2.3 %shard_map.142 = (f32[8,128]{1,0:T(8,128)S(1)}, f32[1,16]{1,0:T(1,128)}, f32[8,64,256]{2,1,0:T(8,128)S(1)}, f32[8,64,256]{2,1,0:T(8,128)S(1)}, f32[768,128]{1,0:T(8,128)}) custom-call(f32[128,128]{1,0:T(8,128)S(1)} %bitcast.18, f32[8,256]{1,0:T(8,128)S(1)} %get-tuple-element.65.info, f32[8,128]{1,0:T(8,128)S(1)} %get-tuple-element.66.own, ...), custom_call_target="tpu_custom_call" | custom-call | bytes 1134592 | tf_op jit(solution)/shard_map/pallas_call | solution.py:704
  33.5 9.0 %all-to-all-start.1 = ((f32[128,1,768]{2,1,0:T(1,128)}), f32[128,1,768]{2,1,0:T(1,128)S(1)}, u32[]{:S(2)}, u32[]{:S(2)}) async-start(f32[128,1,768]{2,1,0:T(1,128)} %bitcast.9), calls=%async_computation.1 | async-start | bytes 786432 | tf_op jit(solution)/shard_map/all_to_all | solution.py:725
  42.5 0.3 shard_map.144
  42.8 1.1 %collective-permute-start.4 = (f32[8,256]{1,0:T(8,128)S(1)}, f32[8,256]{1,0:T(8,128)S(1)}, u32[]{:S(2)}, u32[]{:S(2)}) collective-permute-start(f32[8,256]{1,0:T(8,128)S(1)} %get-tuple-element.99), channel_id=1, source_target_pairs={{0,16},{1,17},{2,18},{3,19},{4,20},{5,21},{6,22},{7,23},{8,24},{9,... | collective-permute-start | bytes 24584 | tf_op jit(solution)/shard_map/ppermute | solution.py:749
  43.9 0.7 collective-permute-start.5
  44.6 1.2 %collective-permute-start.6 = (f32[8,128]{1,0:T(8,128)S(1)}, f32[8,128]{1,0:T(8,128)S(1)}, u32[]{:S(2)}, u32[]{:S(2)}) collective-permute-start(f32[8,128]{1,0:T(8,128)S(1)} %get-tuple-element.101), channel_id=1, source_target_pairs={{0,1},{1,0},{2,3},{3,2},{4,5},{5,4},{6,7},{7,6},{8,9},{9,8},{10,11... | collective-permute-start | bytes 12296 | tf_op jit(solution)/shard_map/ppermute | solution.py:749
  45.8 0.2 collective-permute-start.7
  46.0 6.5 %shard_map.143 = (f32[8,64,256]{2,1,0:T(8,128)S(1)}, f32[2,8,256]{2,1,0:T(8,128)S(1)}, f32[64,128]{1,0:T(8,128)S(1)}, f32[3,8,64,256]{3,2,1,0:T(8,128)}, f32[6,8,64,256]{3,2,1,0:T(8,128)}) custom-call(f32[2,3,8,256]{3,2,1,0:T(8,128)S(1)} %get-tuple-element.79.coef_row, f32[3,64,128]{2,1,0:T(8,128)S(1)} %get-tuple-element.80.coef_col, ...), custom_call_target="tpu_custom_call" | custom-call | flops 13107200 | bytes 9125888 | tf_op jit(solution)/shard_map/pallas_call | solution.py:704
  52.6 0.0 collective-permute-done.6.col_first
  52.6 0.0 collective-permute-done.7.col_second
  52.6 0.0 collective-permute-done.4.row_first
  52.6 0.0 collective-permute-done.5.row_second
  52.6 2.7 %all-to-all-done.1 = f32[128,1,768]{2,1,0:T(1,128)S(1)} async-done(((f32[128,1,768]{2,1,0:T(1,128)}), f32[128,1,768]{2,1,0:T(1,128)S(1)}, u32[]{:S(2)}, u32[]{:S(2)}) %all-to-all-start.1) | async-done | bytes 393248 | tf_op jit(solution)/shard_map/all_to_all | solution.py:725
  55.4 0.9 shard_map.145
  56.2 0.6 collective-permute-start.8
  56.8 0.4 collective-permute-start.9
  57.2 0.3 collective-permute-start.10
  57.6 1.4 %collective-permute-start.11 = (f32[8,128]{1,0:T(8,128)S(1)}, f32[8,128]{1,0:T(8,128)S(1)}, u32[]{:S(2)}, u32[]{:S(2)}) collective-permute-start(f32[8,128]{1,0:T(8,128)S(1)} %get-tuple-element.110), channel_id=1, source_target_pairs={{0,16},{1,2},{2,1},{3,4},{4,3},{5,6},{6,5},{7,8},{8,7},{9,10},{10,... | collective-permute-start | bytes 12296 | tf_op jit(solution)/shard_map/ppermute | solution.py:749
  59.0 3.7 %shard_map.146 = (f32[2,128,128]{2,1,0:T(8,128)S(1)}, f32[8,128]{1,0:T(8,128)S(1)}, f32[8,64,256]{2,1,0:T(8,128)S(1)}) custom-call(f32[768,128]{1,0:T(8,128)S(1)} %bitcast.16, f32[8,256]{1,0:T(8,128)S(1)} %get-tuple-element.65.info, f32[8,256]{1,0:T(8,128)S(1)} %get-tuple-element.83.perf, f32[8,64,256]{2,1,0:T(8,128)S(1)} %get-tuple-element.103.step, ...), custom_call_target="tpu_custom_call" | custom-call | bytes 5128192 | tf_op jit(solution)/shard_map/pallas_call | solution.py:704
  62.7 0.0 collective-permute-done.10.col_first
  62.7 0.0 collective-permute-done.11.col_second
  62.7 0.0 collective-permute-done.8.row_first
  62.7 0.0 collective-permute-done.9.row_second
  62.7 2.0 %shard_map.147 = (f32[8,64,256]{2,1,0:T(8,128)S(1)}, f32[768,128]{1,0:T(8,128)}) custom-call(f32[8,256]{1,0:T(8,128)S(1)} %get-tuple-element.65.info, f32[8,256]{1,0:T(8,128)S(1)} %get-tuple-element.83.perf, f32[8,128]{1,0:T(8,128)S(1)} %get-tuple-element.105.parts, f32[8,64,256]{2,1,0:T(8,128)S(1)} %get-tuple-element.106.near, ...), custom_call_target="tpu_custom_call" | custom-call | bytes 618496 | tf_op jit(solution)/shard_map/pallas_call | solution.py:704
  64.8 7.9 %all-to-all-start.2 = ((f32[128,1,768]{2,1,0:T(1,128)}), f32[128,1,768]{2,1,0:T(1,128)S(1)}, u32[]{:S(2)}, u32[]{:S(2)}) async-start(f32[128,1,768]{2,1,0:T(1,128)} %bitcast.11), calls=%async_computation.2 | async-start | bytes 786432 | tf_op jit(solution)/shard_map/all_to_all | solution.py:725
  72.6 0.3 shard_map.149
  72.9 1.1 %collective-permute-start.12 = (f32[8,256]{1,0:T(8,128)S(1)}, f32[8,256]{1,0:T(8,128)S(1)}, u32[]{:S(2)}, u32[]{:S(2)}) collective-permute-start(f32[8,256]{1,0:T(8,128)S(1)} %get-tuple-element.118), channel_id=1, source_target_pairs={{0,16},{1,17},{2,18},{3,19},{4,20},{5,21},{6,22},{7,23},{8,24},{9,... | collective-permute-start | bytes 24584 | tf_op jit(solution)/shard_map/ppermute | solution.py:749
  74.0 0.7 collective-permute-start.13
  74.7 1.2 %collective-permute-start.14 = (f32[8,128]{1,0:T(8,128)S(1)}, f32[8,128]{1,0:T(8,128)S(1)}, u32[]{:S(2)}, u32[]{:S(2)}) collective-permute-start(f32[8,128]{1,0:T(8,128)S(1)} %get-tuple-element.120), channel_id=1, source_target_pairs={{0,1},{1,0},{2,3},{3,2},{4,5},{5,4},{6,7},{7,6},{8,9},{9,8},{10,11... | collective-permute-start | bytes 12296 | tf_op jit(solution)/shard_map/ppermute | solution.py:749
  75.9 0.2 collective-permute-start.15
  76.1 7.8 %shard_map.148 = (f32[2,2,8,256]{3,2,1,0:T(8,128)S(1)}, f32[2,64,128]{2,1,0:T(8,128)S(1)}, f32[3,8,64,256]{3,2,1,0:T(8,128)}, f32[2,8,64,256]{3,2,1,0:T(8,128)}) custom-call(f32[2,3,8,256]{3,2,1,0:T(8,128)S(1)} %get-tuple-element.79.coef_row, f32[3,64,128]{2,1,0:T(8,128)S(1)} %get-tuple-element.80.coef_col, f32[8,64,256]{2,1,0:T(8,128)S(1)} %get-tuple-element.81.head, ...), custom_call_target="tpu_custom_call" | custom-call | flops 19660800 | bytes 10747904 | tf_op jit(solution)/shard_map/pallas_call | solution.py:704
  84.0 0.0 collective-permute-done.12.row_first
  84.0 0.0 collective-permute-done.13.row_second
  84.0 1.5 %all-to-all-done.2 = f32[128,1,768]{2,1,0:T(1,128)S(1)} async-done(((f32[128,1,768]{2,1,0:T(1,128)}), f32[128,1,768]{2,1,0:T(1,128)S(1)}, u32[]{:S(2)}, u32[]{:S(2)}) %all-to-all-start.2) | async-done | bytes 393248 | tf_op jit(solution)/shard_map/all_to_all | solution.py:725
  85.5 4.1 %shard_map.150 = (f32[3,8,64,256]{3,2,1,0:T(8,128)}, f32[1,16]{1,0:T(1,128)}) custom-call(f32[768,128]{1,0:T(8,128)S(1)} %bitcast.17, f32[8,256]{1,0:T(8,128)S(1)} %get-tuple-element.65.info, f32[2,128,128]{2,1,0:T(8,128)S(1)} %get-tuple-element.112.table, f32[8,128]{1,0:T(8,128)S(1)} %get-tuple-element.113.mine, f32[8,64,256]{2,1,0:T(8,128)S(1)} %get-tuple-element.81.head, ...), custom_call_target="tpu_custom_call" | custom-call | bytes 3854336 | tf_op jit(solution)/shard_map/pallas_call | solution.py:704
  (3 shorter events, 0.0 us)
Async XLA Ops:
  2.9 6.0 %collective-permute-start = (f32[32,256]{1,0:T(8,128)S(1)}, f32[32,256]{1,0:T(8,128)S(1)}, u32[]{:S(2)}, u32[]{:S(2)}) collective-permute-start(f32[32,256]{1,0:T(8,128)S(1)} %get-tuple-element.71), channel_id=1, source_target_pairs={{0,16},{1,17},{2,18},{3,19},{4,20},{5,21},{6,22},{7,23},{8,24},{9,... | collective-permute-start | bytes 98312 | tf_op jit(solution)/shard_map/ppermute | solution.py:749
  4.4 4.5 %collective-permute-start.1 = (f32[32,256]{1,0:T(8,128)S(1)}, f32[32,256]{1,0:T(8,128)S(1)}, u32[]{:S(2)}, u32[]{:S(2)}) collective-permute-start(f32[32,256]{1,0:T(8,128)S(1)} %get-tuple-element.72), channel_id=1, source_target_pairs={{0,1},{1,0},{2,3},{3,2},{4,5},{5,4},{6,7},{7,6},{8,9},{9,8},{10,11... | collective-permute-start | bytes 98312 | tf_op jit(solution)/shard_map/ppermute | solution.py:749
  5.8 3.1 %collective-permute-start.2 = (f32[32,128]{1,0:T(8,128)S(1)}, f32[32,128]{1,0:T(8,128)S(1)}, u32[]{:S(2)}, u32[]{:S(2)}) collective-permute-start(f32[32,128]{1,0:T(8,128)S(1)} %get-tuple-element.73), channel_id=1, source_target_pairs={{0,1},{1,0},{2,3},{3,2},{4,5},{5,4},{6,7},{7,6},{8,9},{9,8},{10,11... | collective-permute-start | bytes 49160 | tf_op jit(solution)/shard_map/ppermute | solution.py:749
  7.0 1.9 %collective-permute-start.3 = (f32[32,128]{1,0:T(8,128)S(1)}, f32[32,128]{1,0:T(8,128)S(1)}, u32[]{:S(2)}, u32[]{:S(2)}) collective-permute-start(f32[32,128]{1,0:T(8,128)S(1)} %get-tuple-element.74), channel_id=1, source_target_pairs={{0,16},{1,2},{2,1},{3,4},{4,3},{5,6},{6,5},{7,8},{8,7},{9,10},{10,... | collective-permute-start | bytes 49160 | tf_op jit(solution)/shard_map/ppermute | solution.py:749
  8.9 22.2 %all-to-all-start = ((f32[128,1,128]{2,1,0:T(1,128)}), f32[128,1,128]{2,1,0:T(1,128)S(1)}, u32[]{:S(2)}, u32[]{:S(2)}) async-start(f32[128,1,128]{2,1,0:T(1,128)} %bitcast.6), calls=%async_computation | async-start | bytes 131072 | tf_op jit(solution)/shard_map/all_to_all | solution.py:725
  33.5 21.9 %all-to-all-start.1 = ((f32[128,1,768]{2,1,0:T(1,128)}), f32[128,1,768]{2,1,0:T(1,128)S(1)}, u32[]{:S(2)}, u32[]{:S(2)}) async-start(f32[128,1,768]{2,1,0:T(1,128)} %bitcast.9), calls=%async_computation.1 | async-start | bytes 786432 | tf_op jit(solution)/shard_map/all_to_all | solution.py:725
  42.8 9.8 %collective-permute-start.4 = (f32[8,256]{1,0:T(8,128)S(1)}, f32[8,256]{1,0:T(8,128)S(1)}, u32[]{:S(2)}, u32[]{:S(2)}) collective-permute-start(f32[8,256]{1,0:T(8,128)S(1)} %get-tuple-element.99), channel_id=1, source_target_pairs={{0,16},{1,17},{2,18},{3,19},{4,20},{5,21},{6,22},{7,23},{8,24},{9,... | collective-permute-start | bytes 24584 | tf_op jit(solution)/shard_map/ppermute | solution.py:749
  43.9 8.7 %collective-permute-start.5 = (f32[8,256]{1,0:T(8,128)S(1)}, f32[8,256]{1,0:T(8,128)S(1)}, u32[]{:S(2)}, u32[]{:S(2)}) collective-permute-start(f32[8,256]{1,0:T(8,128)S(1)} %get-tuple-element.100), channel_id=1, source_target_pairs={{0,1},{1,0},{2,3},{3,2},{4,5},{5,4},{6,7},{7,6},{8,9},{9,8},{10,11... | collective-permute-start | bytes 24584 | tf_op jit(solution)/shard_map/ppermute | solution.py:749
  44.6 8.0 %collective-permute-start.6 = (f32[8,128]{1,0:T(8,128)S(1)}, f32[8,128]{1,0:T(8,128)S(1)}, u32[]{:S(2)}, u32[]{:S(2)}) collective-permute-start(f32[8,128]{1,0:T(8,128)S(1)} %get-tuple-element.101), channel_id=1, source_target_pairs={{0,1},{1,0},{2,3},{3,2},{4,5},{5,4},{6,7},{7,6},{8,9},{9,8},{10,11... | collective-permute-start | bytes 12296 | tf_op jit(solution)/shard_map/ppermute | solution.py:749
  45.8 6.8 %collective-permute-start.7 = (f32[8,128]{1,0:T(8,128)S(1)}, f32[8,128]{1,0:T(8,128)S(1)}, u32[]{:S(2)}, u32[]{:S(2)}) collective-permute-start(f32[8,128]{1,0:T(8,128)S(1)} %get-tuple-element.102), channel_id=1, source_target_pairs={{0,16},{1,2},{2,1},{3,4},{4,3},{5,6},{6,5},{7,8},{8,7},{9,10},{10,... | collective-permute-start | bytes 12296 | tf_op jit(solution)/shard_map/ppermute | solution.py:749
  56.2 6.5 %collective-permute-start.8 = (f32[8,256]{1,0:T(8,128)S(1)}, f32[8,256]{1,0:T(8,128)S(1)}, u32[]{:S(2)}, u32[]{:S(2)}) collective-permute-start(f32[8,256]{1,0:T(8,128)S(1)} %get-tuple-element.107), channel_id=1, source_target_pairs={{0,16},{1,17},{2,18},{3,19},{4,20},{5,21},{6,22},{7,23},{8,24},{9,... | collective-permute-start | bytes 24584 | tf_op jit(solution)/shard_map/ppermute | solution.py:749
  56.8 5.9 %collective-permute-start.9 = (f32[8,256]{1,0:T(8,128)S(1)}, f32[8,256]{1,0:T(8,128)S(1)}, u32[]{:S(2)}, u32[]{:S(2)}) collective-permute-start(f32[8,256]{1,0:T(8,128)S(1)} %get-tuple-element.108), channel_id=1, source_target_pairs={{0,1},{1,0},{2,3},{3,2},{4,5},{5,4},{6,7},{7,6},{8,9},{9,8},{10,11... | collective-permute-start | bytes 24584 | tf_op jit(solution)/shard_map/ppermute | solution.py:749
  57.2 5.5 %collective-permute-start.10 = (f32[8,128]{1,0:T(8,128)S(1)}, f32[8,128]{1,0:T(8,128)S(1)}, u32[]{:S(2)}, u32[]{:S(2)}) collective-permute-start(f32[8,128]{1,0:T(8,128)S(1)} %get-tuple-element.109), channel_id=1, source_target_pairs={{0,1},{1,0},{2,3},{3,2},{4,5},{5,4},{6,7},{7,6},{8,9},{9,8},{10,11... | collective-permute-start | bytes 12296 | tf_op jit(solution)/shard_map/ppermute | solution.py:749
  57.6 5.1 %collective-permute-start.11 = (f32[8,128]{1,0:T(8,128)S(1)}, f32[8,128]{1,0:T(8,128)S(1)}, u32[]{:S(2)}, u32[]{:S(2)}) collective-permute-start(f32[8,128]{1,0:T(8,128)S(1)} %get-tuple-element.110), channel_id=1, source_target_pairs={{0,16},{1,2},{2,1},{3,4},{4,3},{5,6},{6,5},{7,8},{8,7},{9,10},{10,... | collective-permute-start | bytes 12296 | tf_op jit(solution)/shard_map/ppermute | solution.py:749
  64.8 20.7 %all-to-all-start.2 = ((f32[128,1,768]{2,1,0:T(1,128)}), f32[128,1,768]{2,1,0:T(1,128)S(1)}, u32[]{:S(2)}, u32[]{:S(2)}) async-start(f32[128,1,768]{2,1,0:T(1,128)} %bitcast.11), calls=%async_computation.2 | async-start | bytes 786432 | tf_op jit(solution)/shard_map/all_to_all | solution.py:725
  72.9 11.1 %collective-permute-start.12 = (f32[8,256]{1,0:T(8,128)S(1)}, f32[8,256]{1,0:T(8,128)S(1)}, u32[]{:S(2)}, u32[]{:S(2)}) collective-permute-start(f32[8,256]{1,0:T(8,128)S(1)} %get-tuple-element.118), channel_id=1, source_target_pairs={{0,16},{1,17},{2,18},{3,19},{4,20},{5,21},{6,22},{7,23},{8,24},{9,... | collective-permute-start | bytes 24584 | tf_op jit(solution)/shard_map/ppermute | solution.py:749
  74.0 10.0 %collective-permute-start.13 = (f32[8,256]{1,0:T(8,128)S(1)}, f32[8,256]{1,0:T(8,128)S(1)}, u32[]{:S(2)}, u32[]{:S(2)}) collective-permute-start(f32[8,256]{1,0:T(8,128)S(1)} %get-tuple-element.119), channel_id=1, source_target_pairs={{0,1},{1,0},{2,3},{3,2},{4,5},{5,4},{6,7},{7,6},{8,9},{9,8},{10,11... | collective-permute-start | bytes 24584 | tf_op jit(solution)/shard_map/ppermute | solution.py:749
  74.7 9.2 %collective-permute-start.14 = (f32[8,128]{1,0:T(8,128)S(1)}, f32[8,128]{1,0:T(8,128)S(1)}, u32[]{:S(2)}, u32[]{:S(2)}) collective-permute-start(f32[8,128]{1,0:T(8,128)S(1)} %get-tuple-element.120), channel_id=1, source_target_pairs={{0,1},{1,0},{2,3},{3,2},{4,5},{5,4},{6,7},{7,6},{8,9},{9,8},{10,11... | collective-permute-start | bytes 12296 | tf_op jit(solution)/shard_map/ppermute | solution.py:749
  75.9 8.1 %collective-permute-start.15 = (f32[8,128]{1,0:T(8,128)S(1)}, f32[8,128]{1,0:T(8,128)S(1)}, u32[]{:S(2)}, u32[]{:S(2)}) collective-permute-start(f32[8,128]{1,0:T(8,128)S(1)} %get-tuple-element.121), channel_id=1, source_target_pairs={{0,16},{1,2},{2,1},{3,4},{4,3},{5,6},{6,5},{7,8},{8,7},{9,10},{10,... | collective-permute-start | bytes 12296 | tf_op jit(solution)/shard_map/ppermute | solution.py:749
